TPU v7x, 32 devices: a whole 2x2x4 slice. The times are simulated.
32 devices in a mesh: node: 8 (over z, y), samp: 4 (over x, core).
Axes of the slice: x: 2, y: 2, z: 4, core: 2. Of those that a mesh axis runs over, the one named last changes fastest.
Arguments:
- snapshots: bfloat16 [65536, 2048], P('node', 'samp'), may hold values from -330 to 330
- sketch_matrix: bfloat16 [2048, 160], P('samp'), may hold values from -0.125 to 0.125
Outputs:
- core_rows: float32 [65536, 160], P(('node', 'samp'))
- next_rows: float32 [10240, 32], P('node', 'samp')
All inputs are finite; a program needn't handle non-finite values.
Results may differ from a plain program's by a relative error of at most 0.00045.
Values may be sent and summed in bfloat16 or wider, within the bound.
No kernel may reach another device: no remote copies, remote signals or barrier semaphores. Data moves between devices by JAX's collectives and lax.ppermute only.
A program may use at most 64 MiB of HBM per device.

v0:
```python
import jax
import jax.numpy as jnp
from jax import lax
from jax.sharding import PartitionSpec as P

P1 = 64
P2 = 32


highest_precision = lax.Precision.HIGHEST


def triangle_inverse(gram_matrix):
    factor_lower = jnp.linalg.cholesky(gram_matrix)
    identity = jnp.eye(gram_matrix.shape[0], dtype=jnp.float32)
    return lax.linalg.triangular_solve(factor_lower, identity, left_side=True, lower=True)


def body(snapshots, sketch_matrix):
    row_count = snapshots.shape[0]
    rank_size = sketch_matrix.shape[1]
    samp_size = lax.axis_size("samp")
    node_size = lax.axis_size("node")
    node_total = row_count * node_size
    quarter = row_count // samp_size
    partial_value = jnp.dot(snapshots, sketch_matrix, preferred_element_type=jnp.float32)
    sketched = lax.psum(partial_value, "samp")
    local_gram = jnp.dot(
        sketched.T, sketched, precision=highest_precision, preferred_element_type=jnp.float32
    )
    gram_matrix = lax.psum(local_gram, "node") / node_total
    inverse = triangle_inverse(gram_matrix)
    core_all = jnp.dot(
        sketched, inverse.T, precision=highest_precision, preferred_element_type=jnp.float32
    )
    basis_all = core_all.astype(jnp.bfloat16)
    core_rows = lax.dynamic_slice_in_dim(core_all, lax.axis_index("samp") * quarter, quarter, 0)
    coeff_part = jnp.einsum("nr,nc->rc", basis_all, snapshots, preferred_element_type=jnp.float32)
    block_values = P1 // samp_size
    per_node = P1 // node_size
    width_cols = P2 // samp_size
    coeff_cube = coeff_part.reshape(rank_size, block_values, P2)
    regrouped = lax.all_to_all(coeff_cube, "samp", split_axis=2, concat_axis=1, tiled=True)
    summed = lax.psum_scatter(regrouped, "node", scatter_dimension=1, tiled=True)
    scaled = summed / node_total
    next_rows = jnp.transpose(scaled, (1, 0, 2)).reshape(per_node * rank_size, width_cols)
    return (core_rows, next_rows)


def solution(mesh):
    placed = (P("node", "samp"), P("samp", None))
    return jax.shard_map(
        body,
        mesh=mesh,
        in_specs=placed,
        out_specs=(P(("node", "samp"), None), P("node", "samp")),
        check_vma=False,
    )
```

profile of v0, /device:TPU:3, one launch (start us, length us, event | category | flops | bytes accessed | tf_op | source)
XLA Modules:
  0.0 345.6 jit_solution(7007703798533776354)
XLA Ops:
  7.2 0.9 copy-done
  8.1 8.6 %fusion.16 = f32[8192,160]{0,1:T(8,128)} fusion(bf16[8192,512]{1,0:T(8,128)(2,1)} %param.2, bf16[512,160]{0,1:T(8,128)(2,1)S(1)} %copy-done), kind=kOutput, calls=%fused_computation.43 | convolution fusion | flops 1342177280 | bytes 13795328 | tf_op jit(solution)/shard_map/dot_general | solution.py:26
  16.8 103.1 %all-reduce.6.cloned.1.call-done = f32[8192,160]{0,1:T(8,128)} async-done(((f32[8192,160]{0,1:T(8,128)}), f32[8192,160]{0,1:T(8,128)}) %all-reduce.6.cloned.1.call-update) | async-done | bytes 5242896 | tf_op jit(solution)/shard_map/psum | solution.py:27
  119.9 9.0 %fusion.17 = f32[160,160]{0,1:T(8,128)} fusion(f32[8192,160]{0,1:T(8,128)} %all-reduce.6.cloned.1.call-done), kind=kOutput, calls=%fused_computation.44 | convolution fusion | flops 2516582400 | bytes 5345280 | tf_op jit(solution)/shard_map/dot_general | solution.py:28
  129.2 68.4 %all-reduce.8.cloned.1.call-done = f32[160,160]{0,1:T(8,128)} async-done(((f32[160,160]{0,1:T(8,128)}), f32[160,160]{0,1:T(8,128)}) %all-reduce.8.cloned.1.call-update) | async-done | bytes 102416 | tf_op jit(solution)/shard_map/psum | solution.py:31
  197.7 0.9 broadcast_multiply_fusion
  198.7 0.9 fusion.6
  199.6 11.7 %cholesky.51 = f32[128,128]{1,0:T(8,128)S(1)} custom-call(f32[128,128]{1,0:T(8,128)S(1)} %cholesky.124), custom_call_target="Cholesky" | custom-call | tf_op jit(solution)/shard_map/jit(cholesky)/cholesky | solution.py:14
  211.4 9.8 %custom-call.14 = f32[1,128,128]{1,2,0:T(8,128)S(1)} custom-call(f32[1,128,128]{2,1,0:T(8,128)S(1)} %get-tuple-element.23), custom_call_target="InvertDiagBlocksLowerTriangular" | custom-call | tf_op jit(solution)/shard_map/jit(cholesky)/cholesky | solution.py:14
  221.6 2.9 cholesky.110
  224.5 0.6 compare_reduce_fusion
  225.2 0.6 compare_reduce_fusion.1
  227.2 19.9 %custom-call.15 = f32[2,128,128]{1,2,0:T(8,128)S(1)} custom-call(f32[2,128,128]{2,1,0:T(8,128)S(1)} %pad_maximum_fusion), custom_call_target="InvertDiagBlocksLowerTriangular" | custom-call | tf_op jit(solution)/shard_map/triangular_solve | solution.py:16
  247.1 0.3 fusion.7
  247.7 0.3 fusion.13
  248.0 7.0 %fusion.2 = f32[8192,160]{0,1:T(8,128)S(1)} fusion(f32[8192,160]{0,1:T(8,128)} %all-reduce.6.cloned.1.call-done, f32[32,160]{0,1:T(8,128)S(1)} %fusion.13, f32[128,160]{0,1:T(8,128)S(1)} %fusion.7), kind=kOutput, calls=%fused_computation.5 | convolution fusion | flops 2516608000 | bytes 10588160 | tf_op jit(solution)/shard_map/dot_general | solution.py:33
  255.0 8.7 %fusion = f32[160,512]{0,1:T(8,128)S(1)} fusion(bf16[8192,512]{1,0:T(8,128)(2,1)} %param.2, f32[8192,160]{0,1:T(8,128)S(1)} %fusion.2), kind=kOutput, calls=%fused_computation | convolution fusion | flops 1343488000 | bytes 13959168 | tf_op jit(solution)/shard_map/nr,nc->rc/dot_general | solution.py:38
  263.8 0.3 copy.25
  264.1 12.1 %all_to_all.18 = f32[160,16,32]{0,1,2:T(8,128)S(1)} all-to-all(f32[160,16,32]{0,1,2:T(8,128)S(1)} %copy.25), channel_id=1, replica_groups=mesh['node'=8,'samp'=4] {'samp'}, dimensions={2} | all-to-all | bytes 655360 | tf_op jit(solution)/shard_map/all_to_all | solution.py:43
  276.2 1.1 copy.27
  277.4 2.5 constant_dynamic-slice_fusion
  279.9 57.6 %reduce-scatter.2.cloned.1.call-done = f32[160,8,8]{0,2,1:T(8,128)} async-done(((f32[160,64,8]{0,2,1:T(8,128)}), f32[160,8,8]{0,2,1:T(8,128)}) %reduce-scatter.2.cloned.1.call-update) | async-done | bytes 40976 | tf_op jit(solution)/shard_map/reduce_scatter | solution.py:44
  337.4 0.8 multiply_bitcast_fusion
  338.3 0.7 reshape.31
  (25 shorter events, 1.3 us)
Async XLA Ops:
  7.2 0.9 copy-start
  7.2 112.7 %all-reduce.6.cloned.1.call-start = ((), (), s32[]{:S(2)}) async-start(), calls=%async_computation.2 | async-start | bytes 10485760 | tf_op jit(solution)/shard_map/psum | solution.py:27
  16.7 180.9 %all-reduce.8.cloned.1.call-start = ((), (), s32[]{:S(2)}) async-start(), calls=%async_computation.3 | async-start | bytes 327680 | tf_op jit(solution)/shard_map/psum | solution.py:31
  129.0 208.5 %reduce-scatter.2.cloned.1.call-start = ((), (), s32[]{:S(2)}) async-start(), calls=%async_computation.4 | async-start | bytes 589824 | tf_op jit(solution)/shard_map/reduce_scatter | solution.py:44
  255.0 8.8 %copy-start.1 = (f32[8192,160]{0,1:T(8,128)}, f32[8192,160]{0,1:T(8,128)S(1)}, u32[]{:S(2)}) copy-start(f32[8192,160]{0,1:T(8,128)S(1)} %fusion.2) | copy-start | bytes 15728644
Sparse Core Ops, SparseCore 0:
  16.8 102.9 all-reduce.5
  129.1 68.5 all-reduce.7
  277.5 59.9 reduce-scatter.1
where the time goes:
time: 349 us; the launch traced here: 346 us
  waiting for transfers between devices  229 us (66%)
  other arithmetic  48.6 us (14%)
  matrix products  34.5 us (10%)
  between operations  15.2 us (4%)
  blocking collectives  12.1 us (3%)
  local copies, waits for them, and re-layouts  5.65 us (2%)
    psum x1, waiting for transfers between devices, body(): sketched = lax.psum(partial_value, 'samp')  103 us
    psum x1, waiting for transfers between devices, body(): gram_matrix = lax.psum(local_gram, 'node') / node_total  68.4 us
    reduce_scatter x1, waiting for transfers between devices, body(): lax.psum_scatter(regrouped, 'node', scatter_dimension=1, tiled=True)  57.6 us
    another operation x7, other arithmetic, triangle_inverse(): factor_lower = jnp.linalg.cholesky(gram_matrix)  25.8 us
    another operation x6, other arithmetic, triangle_inverse(): lax.linalg.triangular_solve(factor_lower, identity, left_side=True, lower...  20 us
    all_to_all x1, blocking collectives, body(): lax.all_to_all(coeff_cube, 'samp', split_axis=2, concat_axis=1, tiled=True)  12.1 us
    dot_general x1, matrix products, body(): jnp.dot(sketched.T, sketched, precision=highest_precision, preferred_elem...  9.05 us
    dot_general x1, matrix products, body(): jnp.einsum('nr,nc->rc', basis_all, snapshots, preferred_element_type=jnp....  8.74 us
  transfers between devices with their start and end apart: 3, of which 3 were waited for; matrix products, arithmetic and copies ran while one was open for 1% of the time, Pallas kernels for 0%

commit v1 on v0

v1 whole, which is shorter than its diff:
```python
import functools
import jax
import jax.numpy as jnp
from jax import lax
from jax.experimental import pallas as pl
from jax.experimental.pallas import tpu as pltpu
from jax.sharding import PartitionSpec as P

P1 = 64
P2 = 32
BAND = 32
F32 = jnp.float32
BF16 = jnp.bfloat16
HI = lax.Precision.HIGHEST
VMEM_LIMIT = 48 * 1024 * 1024


def iota(shape, dim):
    return lax.broadcasted_iota(jnp.int32, shape, dim)


def dot(a, b, dims, precision=None):
    return lax.dot_general(a, b, (dims, ((), ())), precision=precision, preferred_element_type=F32)


def params():
    return pltpu.CompilerParams(vmem_limit_bytes=VMEM_LIMIT)


def cost(flops, moved):
    return pl.CostEstimate(flops=int(flops), bytes_accessed=int(moved), transcendentals=0)


def sketch_kernel(ids_ref, x_ref, w_ref, o_ref):
    o_ref[...] = dot(w_ref[...], x_ref[...], ((1,), (1,)))


def sketch(ids, x, w_t, rows):
    rank, depth = w_t.shape
    steps = ids.shape[0]
    return pl.pallas_call(
        sketch_kernel,
        grid_spec=pltpu.PrefetchScalarGridSpec(
            num_scalar_prefetch=1,
            grid=(steps,),
            in_specs=[
                pl.BlockSpec((rows, depth), lambda i, ids: (ids[i], 0)),
                pl.BlockSpec((rank, depth), lambda i, ids: (0, 0)),
            ],
            out_specs=pl.BlockSpec((rank, rows), lambda i, ids: (0, i)),
        ),
        out_shape=jax.ShapeDtypeStruct((rank, steps * rows), F32),
        compiler_params=params(),
        cost_estimate=cost(2 * rank * depth * rows * steps, steps * rows * (depth * 2 + rank * 4)),
        name="sketch",
    )(ids, x, w_t)


def packing(rank):
    bands = rank // BAND
    pairs = [(i, j) for i in range(bands) for j in range(i, bands)]
    wide = 128 // BAND
    groups = -(-len(pairs) // wide)
    groups += groups % 2
    return pairs, wide, groups


def pack_gram(gram):
    pairs, wide, groups = packing(gram.shape[0])
    out = []
    for g in range(groups):
        chosen = pairs[g * wide:(g + 1) * wide]
        parts = [gram[i * BAND:(i + 1) * BAND, j * BAND:(j + 1) * BAND] for i, j in chosen]
        parts += [jnp.zeros((BAND, BAND), F32)] * (wide - len(chosen))
        out.append(jnp.concatenate(parts, axis=1))
    return jnp.concatenate(out, axis=0)


def gram_kernel(scale, a_ref, b_ref, s_ref, g_ref):
    s = a_ref[...] + b_ref[...]
    s_ref[...] = s
    g_ref[...] = pack_gram(dot(s, s, ((1,), (1,)), HI) * scale)


def own_gram(a, b, scale):
    rank, rows = a.shape
    groups = packing(rank)[2]
    return pl.pallas_call(
        functools.partial(gram_kernel, scale),
        out_shape=(
            jax.ShapeDtypeStruct((rank, rows), F32),
            jax.ShapeDtypeStruct((groups * BAND, 128), F32),
        ),
        compiler_params=params(),
        cost_estimate=cost(12 * rank * rank * rows, 16 * rank * rows),
        name="gram",
    )(a, b)


def wide_lanes(x, n):
    reps = -(-n // 128)
    return jnp.concatenate([x] * reps, axis=1)[:, :n] if reps > 1 else x[:, :n]


def band_rows(block, b):
    n = block.shape[1]
    count = BAND // 8
    part = [block[8 * i:8 * i + 8, :] for i in range(count)]
    sub = iota((8, n), 0)
    lane = iota((8, n), 1)
    for m in range(count):
        c0 = b * BAND + 8 * m
        live = count - m
        col = [
            [jnp.broadcast_to(part[m + i][:, c0 + k:c0 + k + 1], (8, 128)) for i in range(live)]
            for k in range(8)
        ]
        here = (lane >= c0) & (lane < c0 + 8)
        part[m] = jnp.where(here, jnp.where(lane - c0 == sub, 1.0, 0.0), part[m])
        for i in range(1, live):
            part[m + i] = jnp.where(here, 0.0, part[m + i])
        for j in range(8):
            inv_root = lax.rsqrt(jnp.broadcast_to(col[j][0][j:j + 1, :], (8, 128)))
            low = [x * inv_root for x in col[j]]
            for k in range(j + 1, 8):
                t = jnp.broadcast_to(low[0][k:k + 1, :], (8, 128))
                for i in range(live):
                    col[k][i] = col[k][i] - low[i] * t
            row = jnp.broadcast_to(part[m][j:j + 1, :], (8, n)) * wide_lanes(inv_root, n)
            for i in range(live):
                new = part[m + i] - wide_lanes(low[i], n) * row
                if i == 0:
                    new = jnp.where(sub > j, new, jnp.where(sub == j, row, part[m]))
                part[m + i] = new
    return jnp.concatenate(part, axis=0)


def factor_kernel(rank, g_ref, o_ref):
    pairs, wide, _ = packing(rank)
    o_ref[...] = jnp.zeros((rank, rank), F32)
    for at, (i, j) in enumerate(pairs):
        g, k = at // wide, at % wide
        o_ref[i * BAND:(i + 1) * BAND, j * BAND:(j + 1) * BAND] = g_ref[
            g * BAND:(g + 1) * BAND, k * BAND:(k + 1) * BAND]
    for b in range(rank // BAND):
        lo, hi = b * BAND, (b + 1) * BAND
        r = band_rows(o_ref[lo:hi, :], b)
        rows, cols = iota(r.shape, 0), iota(r.shape, 1)
        r = jnp.where((cols >= lo) & (cols < hi) & (cols - lo > rows), 0.0, r)
        o_ref[lo:hi, :] = jnp.where(cols < hi, r, 0.0)
        if hi < rank:
            left = jnp.where(cols >= hi, r, 0.0)
            update = dot(left, r, ((0,), (0,)), HI)
            kept = jnp.where(iota((rank - hi, rank), 1) // BAND == b, 0.0, o_ref[hi:, :])
            o_ref[hi:, :] = kept - update[hi:, :]


def factor_inverse(packed, rank):
    return pl.pallas_call(
        functools.partial(factor_kernel, rank),
        out_shape=jax.ShapeDtypeStruct((rank, rank), F32),
        compiler_params=params(),
        cost_estimate=cost(8e9, 4 * rank * rank),
        name="factor",
    )(packed)


def project_kernel(count, ids_ref, *refs):
    s_refs, x_refs = refs[:count], refs[count:2 * count]
    o_ref = refs[-1]
    rank = o_ref.shape[0]

    @pl.when(pl.program_id(0) == 0)
    def _():
        o_ref[...] = refs[2 * count][...] if len(refs) > 2 * count + 1 else jnp.zeros_like(o_ref)

    for s_ref, x_ref in zip(s_refs, x_refs):
        s = s_ref[...]
        high = s.astype(BF16)
        low = (s - high.astype(F32)).astype(BF16)
        both = dot(jnp.concatenate([high, low], axis=0), x_ref[...], ((1,), (0,)))
        o_ref[...] += both[:rank] + both[rank:]


def project(ids, parts, x, base, rows):
    count = len(parts)
    rank, span = parts[0].shape
    depth = x.shape[1]
    steps = span // rows
    bases = [] if base is None else [base]
    return pl.pallas_call(
        functools.partial(project_kernel, count),
        grid_spec=pltpu.PrefetchScalarGridSpec(
            num_scalar_prefetch=1,
            grid=(steps,),
            in_specs=[pl.BlockSpec((rank, rows), lambda i, ids: (0, i))] * count
            + [
                pl.BlockSpec((rows, depth), lambda i, ids, k=k: (ids[k] * steps + i, 0))
                for k in range(count)
            ]
            + [pl.BlockSpec((rank, depth), lambda i, ids: (0, 0))] * len(bases),
            out_specs=pl.BlockSpec((rank, depth), lambda i, ids: (0, 0)),
        ),
        out_shape=jax.ShapeDtypeStruct((rank, depth), F32),
        compiler_params=params(),
        cost_estimate=cost(4 * rank * depth * span * count, span * count * (depth * 2 + rank * 4)),
        name="project",
    )(ids, *parts, *([x] * count), *bases)


def folding(rank, width):
    best = 1
    for f in range(1, rank + 1):
        if rank % f == 0 and (rank // f) % 8 == 0 and f * width <= 128:
            best = f
    return best


def regroup_kernel(pieces, samp, per_node, width_cols, me_ref, t_ref, *refs):
    outs, hold = refs[:pieces], refs[pieces]
    rank, depth = t_ref.shape
    width = per_node * width_cols
    fold = folding(rank, width)
    tall = rank // fold
    dst = iota((depth, depth), 1)
    src = iota((depth, depth), 0)
    a, rest = dst // (samp * width), dst % (samp * width)
    s, rest = rest // width, rest % width
    want = (a * per_node + rest // width_cols) * (samp * width_cols) + s * width_cols + rest % width_cols
    move = jnp.where(src == want, 1.0, 0.0).astype(BF16)
    t = t_ref[...]
    high = t.astype(BF16)
    mid = (t - high.astype(F32)).astype(BF16)
    low = (t - high.astype(F32) - mid.astype(F32)).astype(BF16)
    moved = dot(jnp.concatenate([high, mid, low], axis=0), move, ((1,), (0,)))
    moved = moved[:rank] + moved[rank:2 * rank] + moved[2 * rank:]
    for i in range(pieces):
        piece = moved[:, i * width:(i + 1) * width]
        hold[i] = jnp.concatenate([piece[f * tall:(f + 1) * tall] for f in range(fold)], axis=1)
    me = me_ref[0]
    for k, out in enumerate(outs):
        out[...] = hold[me ^ k]


def regroup(me, t, samp, node, per_node, width_cols):
    rank, depth = t.shape
    width = per_node * width_cols
    fold = folding(rank, width)
    shape = (rank // fold, fold * width)
    return pl.pallas_call(
        functools.partial(regroup_kernel, node, samp, per_node, width_cols),
        in_specs=[pl.BlockSpec(memory_space=pltpu.SMEM), pl.BlockSpec(memory_space=pltpu.VMEM)],
        out_shape=[jax.ShapeDtypeStruct(shape, F32)] * node,
        scratch_shapes=[pltpu.VMEM((node,) + shape, F32)],
        compiler_params=params(),
        cost_estimate=cost(6 * rank * depth * depth, 8 * rank * depth),
        name="regroup",
    )(me, t)


def core_kernel(inv_ref, s_ref, o_ref):
    o_ref[...] = dot(inv_ref[...], s_ref[...], ((1,), (0,)), HI)


def core_product(inverse, s):
    rank, rows = s.shape
    return pl.pallas_call(
        core_kernel,
        out_shape=jax.ShapeDtypeStruct((rank, rows), F32),
        compiler_params=params(),
        cost_estimate=cost(12 * rank * rank * rows, 8 * rank * rows),
        name="core",
    )(inverse, s)


def coefficient_kernel(scale, per_node, width_cols, inv_ref, *refs):
    pieces, o_ref = refs[:-1], refs[-1]
    rank = inv_ref.shape[0]
    total = pieces[0][...]
    for p in pieces[1:]:
        total = total + p[...]
    width = per_node * width_cols
    fold = total.shape[1] // width
    total = jnp.concatenate([total[:, f * width:(f + 1) * width] for f in range(fold)], axis=0)
    out = dot(total, inv_ref[...], ((0,), (1,)), HI) * scale
    o_ref[...] = jnp.concatenate(
        [out[p * width_cols:(p + 1) * width_cols, :] for p in range(per_node)], axis=1)


def coefficients(inverse, pieces, scale, per_node, width_cols):
    rank = inverse.shape[0]
    return pl.pallas_call(
        functools.partial(coefficient_kernel, scale, per_node, width_cols),
        out_shape=jax.ShapeDtypeStruct((width_cols, per_node * rank), F32),
        compiler_params=params(),
        cost_estimate=cost(12 * rank * rank * per_node * width_cols, 4 * rank * rank),
        name="coefficient",
    )(inverse, *pieces)


def swap(value, axis, size, bit):
    return lax.ppermute(value, axis, [(i, i ^ bit) for i in range(size)])


def body(snapshots, sketch_matrix):
    rows_all = snapshots.shape[0]
    rank = sketch_matrix.shape[1]
    samp = lax.axis_size("samp")
    node = lax.axis_size("node")
    total = rows_all * node
    quarter = rows_all // samp
    rows = min(quarter, 1024)
    steps = quarter // rows
    me_s = lax.axis_index("samp").astype(jnp.int32)
    me_n = lax.axis_index("node").astype(jnp.int32)
    w_t = sketch_matrix.T

    def block_ids(d):
        return jnp.stack([(me_s ^ d) * steps + i for i in range(steps)])

    order = sorted(range(samp), key=lambda d: (-(d // 2), -(d % 2)))
    part = {d: sketch(block_ids(d), snapshots, w_t, rows) for d in order}

    held = dict(part)
    bit = 1
    while bit * 2 < samp:
        got = {d ^ bit: swap(held.pop(d), "samp", samp, bit) for d in order if d in held and d & bit}
        for d in got:
            held[d] = held[d] + got[d]
        bit *= 2
    last = bit
    ours, theirs = held[0], held[last]
    arrived = swap(theirs, "samp", samp, last)
    short = swap(ours.astype(BF16), "samp", samp, last)
    own, gram = own_gram(ours, arrived, 1.0 / total)

    full = {0: own, last: theirs + short.astype(F32)}
    bit = last // 2
    while bit:
        full.update({d ^ bit: swap(full[d], "samp", samp, bit) for d in list(full)})
        bit //= 2

    upper = (me_s & 1) == 1
    halves = jnp.split(gram, 2, axis=0)
    mine = jnp.where(upper, halves[1], halves[0])
    mine = mine + swap(jnp.where(upper, halves[0], halves[1]), "samp", samp, 1)
    bit = 2
    while bit < samp:
        mine = mine + swap(mine, "samp", samp, bit)
        bit *= 2
    bit = 1
    while bit < node:
        mine = mine + swap(mine, "node", node, bit)
        bit *= 2
    other = swap(mine, "samp", samp, 1)
    packed = jnp.concatenate([jnp.where(upper, other, mine), jnp.where(upper, mine, other)], axis=0)
    inverse = factor_inverse(packed, rank)

    def ids(ds):
        return jnp.stack([me_s ^ d for d in ds])

    t = project(ids([0]), [full[0]], snapshots, None, rows)
    t = project(ids([last]), [full[last]], snapshots, t, rows)
    rest = [d for d in full if d not in (0, last)]
    if rest:
        t = project(ids(rest), [full[d] for d in rest], snapshots, t, rows)

    per_node = P1 // node
    width_cols = P2 // samp
    spread = node // samp
    pieces = regroup(me_n[None], t, samp, node, per_node, width_cols)
    landed = []
    for k in range(node):
        pairs = []
        for n in range(node):
            a, s_to = (n ^ k) // samp, (n ^ k) % samp
            for s_from in range(samp):
                pairs.append((n * samp + s_from, (s_from * spread + a) * samp + s_to))
        landed.append(lax.ppermute(pieces[k], ("node", "samp"), pairs))
    core = core_product(inverse, own)
    coef = coefficients(inverse, landed, 1.0 / total, per_node, width_cols)
    return (core.T, coef.T)


def solution(mesh):
    placed = (P("node", "samp"), P("samp", None))
    return jax.shard_map(
        body,
        mesh=mesh,
        in_specs=placed,
        out_specs=(P(("node", "samp"), None), P("node", "samp")),
        check_vma=False,
    )
```

time: 349 us -> 129 us (0.37)
  the two profiles are of different devices: /device:TPU:3 before, /device:TPU:0 now
where the time goes in v1:
time: 129 us
  waiting for transfers between devices  54.7 us (42%)
  starting transfers between devices  35.9 us (28%)
  Pallas kernels  32 us (25%)
  other arithmetic  4.61 us (4%)
    ppermute x12, waiting for transfers between devices, swap(): return lax.ppermute(value, axis, [(i, i ^ bit) for i in range(size)])  50.2 us
    ppermute x8, starting transfers between devices, body(): landed.append(lax.ppermute(pieces[k], ('node', 'samp'), pairs))  23 us
    ppermute x12, starting transfers between devices, swap(): return lax.ppermute(value, axis, [(i, i ^ bit) for i in range(size)])  12.9 us
    pallas_call x4, Pallas kernels, sketch(): pl.pallas_call(sketch_kernel, grid_spec=pltpu.PrefetchScalarGridSpec(num_...  12.2 us
    pallas_call x3, Pallas kernels, project(): pl.pallas_call(functools.partial(project_kernel, count), grid_spec=pltpu....  9.01 us
    pallas_call x1, Pallas kernels, factor_inverse(): pl.pallas_call(functools.partial(factor_kernel, rank), out_shape=jax.Shap...  5.48 us
    ppermute x8, waiting for transfers between devices, body(): landed.append(lax.ppermute(pieces[k], ('node', 'samp'), pairs))  4.42 us
    add x1, other arithmetic, body(): full = {0: own, last: theirs + short.astype(F32)}  2.67 us
  transfers between devices with their start and end apart: 20, of which 8 were waited for; matrix products, arithmetic and copies ran while one was open for 1% of the time, Pallas kernels for 18%

profile of v1, /device:TPU:0, one launch (start us, length us, event | category | flops | bytes accessed | tf_op | source)
XLA Modules:
  0.0 129.0 jit_solution(4416043473587958329)
XLA Ops:
  1.6 2.9 %sketch.5 = f32[160,2048]{1,0:T(8,128)S(1)} custom-call(s32[2]{0:T(128)S(1)} %pad_add_fusion.1.ids_ref, bf16[8192,512]{1,0:T(8,128)(2,1)} %refs_3_.1, bf16[160,512]{1,0:T(8,128)(2,1)S(1)} %bitcast.16), custom_call_target="tpu_custom_call" | custom-call | flops 335544320 | bytes 3407872 | tf_op jit(solution)/shard_map/sketch/pallas_call | solution.py:41
  5.1 3.6 %sketch.7 = f32[160,2048]{1,0:T(8,128)} custom-call(s32[2]{0:T(128)S(1)} %pad_add_fusion.3.ids_ref, bf16[8192,512]{1,0:T(8,128)(2,1)} %refs_3_.1, bf16[160,512]{1,0:T(8,128)(2,1)S(1)} %bitcast.17), custom_call_target="tpu_custom_call" | custom-call | flops 335544320 | bytes 3407872 | tf_op jit(solution)/shard_map/sketch/pallas_call | solution.py:41
  8.8 2.9 %sketch.4 = f32[160,2048]{1,0:T(8,128)S(1)} custom-call(s32[2]{0:T(128)S(1)} %pad_add_fusion.ids_ref, bf16[8192,512]{1,0:T(8,128)(2,1)} %refs_3_.1, bf16[160,512]{1,0:T(8,128)(2,1)S(1)} %bitcast.18), custom_call_target="tpu_custom_call" | custom-call | flops 335544320 | bytes 3407872 | tf_op jit(solution)/shard_map/sketch/pallas_call | solution.py:41
  13.2 3.0 %collective-permute-start.10 = (bf16[160,2048]{1,0:T(8,128)(2,1)S(1)}, bf16[160,2048]{1,0:T(8,128)(2,1)S(1)}, u32[]{:S(2)}, u32[]{:S(2)}) collective-permute-start(bf16[160,2048]{1,0:T(8,128)(2,1)S(1)} %get-tuple-element.24), channel_id=1, source_target_pairs={{0,2},{1,3},{2,0},{3,1},{4,6},{5,7},{6,4},{7,5},{8,10},{9,11},{10,... | collective-permute-start | bytes 1966088 | tf_op jit(solution)/shard_map/ppermute | solution.py:302
  16.3 2.9 %sketch.6 = f32[160,2048]{1,0:T(8,128)S(1)} custom-call(s32[2]{0:T(128)S(1)} %pad_add_fusion.2.ids_ref, bf16[8192,512]{1,0:T(8,128)(2,1)} %refs_3_.1, bf16[160,512]{1,0:T(8,128)(2,1)S(1)} %bitcast.19), custom_call_target="tpu_custom_call" | custom-call | flops 335544320 | bytes 3407872 | tf_op jit(solution)/shard_map/sketch/pallas_call | solution.py:41
  19.2 12.0 %collective-permute-done.10 = bf16[160,2048]{1,0:T(8,128)(2,1)S(1)} collective-permute-done((bf16[160,2048]{1,0:T(8,128)(2,1)S(1)}, bf16[160,2048]{1,0:T(8,128)(2,1)S(1)}, u32[]{:S(2)}, u32[]{:S(2)}) %collective-permute-start.10) | collective-permute-done | bytes 655392 | tf_op jit(solution)/shard_map/ppermute | solution.py:302
  31.2 2.7 %convert_add_fusion = (f32[160,2048]{1,0:T(8,128)}, f32[160,2048]{1,0:T(8,128)S(1)}) fusion(bf16[160,2048]{1,0:T(8,128)(2,1)S(1)} %collective-permute-done.10, f32[160,2048]{1,0:T(8,128)S(1)} %sketch.6, f32[160,2048]{1,0:T(8,128)} %collective-permute-done.1), kind=kLoop, calls=%fused_computation | loop fusion | flops 983040 | bytes 5898240 | tf_op jit(solution)/shard_map/add | solution.py:337
  35.6 28.4 %collective-permute-done.2.b_ref = f32[160,2048]{1,0:T(8,128)S(1)} collective-permute-done((f32[160,2048]{1,0:T(8,128)S(1)}, f32[160,2048]{1,0:T(8,128)S(1)}, u32[]{:S(2)}, u32[]{:S(2)}) %collective-permute-start.2) | collective-permute-done | bytes 1310752 | tf_op jit(solution)/shard_map/ppermute | solution.py:302
  65.9 2.6 %collective-permute-done.3 = f32[64,128]{1,0:T(8,128)S(1)} collective-permute-done((f32[64,128]{1,0:T(8,128)S(1)}, f32[64,128]{1,0:T(8,128)S(1)}, u32[]{:S(2)}, u32[]{:S(2)}) %collective-permute-start.3) | collective-permute-done | bytes 32800 | tf_op jit(solution)/shard_map/ppermute | solution.py:302
  69.9 2.5 %collective-permute-done.4 = f32[64,128]{1,0:T(8,128)S(1)} collective-permute-done((f32[64,128]{1,0:T(8,128)S(1)}, f32[64,128]{1,0:T(8,128)S(1)}, u32[]{:S(2)}, u32[]{:S(2)}) %collective-permute-start.4) | collective-permute-done | bytes 32800 | tf_op jit(solution)/shard_map/ppermute | solution.py:302
  73.9 2.5 %collective-permute-done.5 = f32[64,128]{1,0:T(8,128)S(1)} collective-permute-done((f32[64,128]{1,0:T(8,128)S(1)}, f32[64,128]{1,0:T(8,128)S(1)}, u32[]{:S(2)}, u32[]{:S(2)}) %collective-permute-start.5) | collective-permute-done | bytes 32800 | tf_op jit(solution)/shard_map/ppermute | solution.py:302
  77.9 2.3 %collective-permute-done.6 = f32[64,128]{1,0:T(8,128)S(1)} collective-permute-done((f32[64,128]{1,0:T(8,128)S(1)}, f32[64,128]{1,0:T(8,128)S(1)}, u32[]{:S(2)}, u32[]{:S(2)}) %collective-permute-start.6) | collective-permute-done | bytes 32800 | tf_op jit(solution)/shard_map/ppermute | solution.py:302
  80.3 2.5 %collective-permute-start.7 = (f32[64,128]{1,0:T(8,128)S(1)}, f32[64,128]{1,0:T(8,128)S(1)}, u32[]{:S(2)}, u32[]{:S(2)}) collective-permute-start(f32[64,128]{1,0:T(8,128)S(1)} %add.45), channel_id=1, source_target_pairs={{0,16},{4,20},{8,24},{12,28},{16,0},{20,4},{24,8},{28,12},{1,17},{... | collective-permute-start | bytes 98312 | tf_op jit(solution)/shard_map/ppermute | solution.py:302
  82.8 2.3 %project.3.refs_2_ = f32[160,512]{1,0:T(8,128)S(1)} custom-call(s32[1]{0:T(128)} %bitcast.14.ids_ref, f32[160,2048]{1,0:T(8,128)S(1)} %get-tuple-element.13.s_ref.refs_0_, bf16[8192,512]{1,0:T(8,128)(2,1)} %refs_3_.1), custom_call_target="tpu_custom_call" | custom-call | flops 671088640 | bytes 3407872 | tf_op jit(solution)/shard_map/project/pallas_call | solution.py:191
  85.3 2.5 %project.4.refs_4_ = f32[160,512]{1,0:T(8,128)S(1)} custom-call(s32[1]{0:T(128)} %bitcast.13.ids_ref, f32[160,2048]{1,0:T(8,128)} %get-tuple-element.22.refs_0_, bf16[8192,512]{1,0:T(8,128)(2,1)} %refs_3_.1, f32[160,512]{1,0:T(8,128)S(1)} %project.3.refs_2_), custom_call_target="tpu_custom_call" | custom-call | flops 671088640 | bytes 3407872 | tf_op jit(solution)/shard_map/project/pallas_call | solution.py:191
  87.9 4.1 %project.5.t_ref = f32[160,512]{1,0:T(8,128)S(1)} custom-call(s32[2]{0:T(128)S(1)} %pad_add_fusion.4.ids_ref, f32[160,2048]{1,0:T(8,128)S(1)} %collective-permute-done.9.refs_0_, f32[160,2048]{1,0:T(8,128)} %collective-permute-done.11.refs_1_, bf16[8192,512]{1,0:T(8,128)(2,1)} %refs_3_.1, bf16[8192,512]{1,0:T(8,128)(2,1)} %refs_3_.1, ...), custom_call_target="tpu_custom_call" | custom-call | flops 1342177280 | bytes 6815744 | tf_op jit(solution)/shard_map/project/pallas_call | solution.py:191
  93.3 3.0 %collective-permute-start.13 = (f32[80,128]{1,0:T(8,128)S(1)}, f32[80,128]{1,0:T(8,128)S(1)}, u32[]{:S(2)}, u32[]{:S(2)}) collective-permute-start(f32[80,128]{1,0:T(8,128)S(1)} %get-tuple-element.15), channel_id=1, source_target_pairs={{0,1},{1,9},{2,17},{3,25},{4,0},{5,8},{6,16},{7,24},{8,3},{9,11},{... | collective-permute-start | bytes 122888 | tf_op jit(solution)/shard_map/ppermute | solution.py:379
  96.3 3.5 %collective-permute-start.14 = (f32[80,128]{1,0:T(8,128)S(1)}, f32[80,128]{1,0:T(8,128)S(1)}, u32[]{:S(2)}, u32[]{:S(2)}) collective-permute-start(f32[80,128]{1,0:T(8,128)S(1)} %get-tuple-element.16), channel_id=1, source_target_pairs={{0,2},{1,10},{2,18},{3,26},{4,3},{5,11},{6,19},{7,27},{8,0},{9,8},... | collective-permute-start | bytes 122888 | tf_op jit(solution)/shard_map/ppermute | solution.py:379
  99.8 5.5 %factor.1.inv_ref = f32[160,160]{1,0:T(8,128)S(1)} custom-call(f32[128,128]{1,0:T(8,128)S(1)} %pad_maximum_fusion.g_ref), custom_call_target="tpu_custom_call" | custom-call | flops 8000000000 | bytes 102400 | tf_op jit(solution)/shard_map/factor/pallas_call | solution.py:159
  105.2 4.3 %collective-permute-start.15 = (f32[80,128]{1,0:T(8,128)S(1)}, f32[80,128]{1,0:T(8,128)S(1)}, u32[]{:S(2)}, u32[]{:S(2)}) collective-permute-start(f32[80,128]{1,0:T(8,128)S(1)} %get-tuple-element.17), channel_id=1, source_target_pairs={{0,3},{1,11},{2,19},{3,27},{4,2},{5,10},{6,18},{7,26},{8,1},{9,9},... | collective-permute-start | bytes 122888 | tf_op jit(solution)/shard_map/ppermute | solution.py:379
  110.2 1.9 %collective-permute-start.17 = (f32[80,128]{1,0:T(8,128)S(1)}, f32[80,128]{1,0:T(8,128)S(1)}, u32[]{:S(2)}, u32[]{:S(2)}) collective-permute-start(f32[80,128]{1,0:T(8,128)S(1)} %get-tuple-element.19), channel_id=1, source_target_pairs={{0,5},{1,13},{2,21},{3,29},{4,4},{5,12},{6,20},{7,28},{8,7},{9,15}... | collective-permute-start | bytes 122888 | tf_op jit(solution)/shard_map/ppermute | solution.py:379
  112.2 8.9 %collective-permute-start.18 = (f32[80,128]{1,0:T(8,128)S(1)}, f32[80,128]{1,0:T(8,128)S(1)}, u32[]{:S(2)}, u32[]{:S(2)}) collective-permute-start(f32[80,128]{1,0:T(8,128)S(1)} %get-tuple-element.20), channel_id=1, source_target_pairs={{0,6},{1,14},{2,22},{3,30},{4,7},{5,15},{6,23},{7,31},{8,4},{9,12}... | collective-permute-start | bytes 122888 | tf_op jit(solution)/shard_map/ppermute | solution.py:379
  121.2 2.3 %core.1 = f32[160,2048]{1,0:T(8,128)} custom-call(f32[160,160]{1,0:T(8,128)S(1)} %factor.1.inv_ref, f32[160,2048]{1,0:T(8,128)S(1)} %get-tuple-element.13.s_ref.refs_0_), custom_call_target="tpu_custom_call" | custom-call | flops 629145600 | bytes 2621440 | tf_op jit(solution)/shard_map/core/pallas_call | solution.py:267
  123.7 4.2 %collective-permute-done.19.refs_7_ = f32[80,128]{1,0:T(8,128)S(1)} collective-permute-done((f32[80,128]{1,0:T(8,128)S(1)}, f32[80,128]{1,0:T(8,128)S(1)}, u32[]{:S(2)}, u32[]{:S(2)}) %collective-permute-start.19) | collective-permute-done | bytes 40992 | tf_op jit(solution)/shard_map/ppermute | solution.py:379
  (47 shorter events, 14.9 us)
Async XLA Ops:
  0.7 0.9 copy-start
  1.6 3.5 %copy-start.1 = (bf16[512,160]{0,1:T(8,128)(2,1)S(1)}, bf16[512,160]{0,1:T(8,128)(2,1)}, u32[]{:S(2)}) copy-start(bf16[512,160]{0,1:T(8,128)(2,1)} %param.3) | copy-start | bytes 491524
  4.5 7.2 %collective-permute-start = (f32[160,2048]{1,0:T(8,128)S(1)}, f32[160,2048]{1,0:T(8,128)}, u32[]{:S(2)}, u32[]{:S(2)}) collective-permute-start(f32[160,2048]{1,0:T(8,128)S(1)} %sketch.5), channel_id=1, source_target_pairs={{0,1},{1,0},{2,3},{3,2},{4,5},{5,4},{6,7},{7,6},{8,9},{9,8},{10,11... | collective-permute-start | bytes 3932168 | tf_op jit(solution)/shard_map/ppermute | solution.py:302
  8.7 10.5 %collective-permute-start.1 = (f32[160,2048]{1,0:T(8,128)}, f32[160,2048]{1,0:T(8,128)}, u32[]{:S(2)}, u32[]{:S(2)}) collective-permute-start(f32[160,2048]{1,0:T(8,128)} %sketch.7), channel_id=1, source_target_pairs={{0,1},{1,0},{2,3},{3,2},{4,5},{5,4},{6,7},{7,6},{8,9},{9,8},{10,11... | collective-permute-start | bytes 3932168 | tf_op jit(solution)/shard_map/ppermute | solution.py:302
  13.2 17.9 %collective-permute-start.10 = (bf16[160,2048]{1,0:T(8,128)(2,1)S(1)}, bf16[160,2048]{1,0:T(8,128)(2,1)S(1)}, u32[]{:S(2)}, u32[]{:S(2)}) collective-permute-start(bf16[160,2048]{1,0:T(8,128)(2,1)S(1)} %get-tuple-element.24), channel_id=1, source_target_pairs={{0,2},{1,3},{2,0},{3,1},{4,6},{5,7},{6,4},{7,5},{8,10},{9,11},{10,... | collective-permute-start | bytes 1966088 | tf_op jit(solution)/shard_map/ppermute | solution.py:302
  33.8 30.2 %collective-permute-start.2 = (f32[160,2048]{1,0:T(8,128)S(1)}, f32[160,2048]{1,0:T(8,128)S(1)}, u32[]{:S(2)}, u32[]{:S(2)}) collective-permute-start(f32[160,2048]{1,0:T(8,128)S(1)} %get-tuple-element.23), channel_id=1, source_target_pairs={{0,2},{1,3},{2,0},{3,1},{4,6},{5,7},{6,4},{7,5},{8,10},{9,11},{10,... | collective-permute-start | bytes 3932168 | tf_op jit(solution)/shard_map/ppermute | solution.py:302
  35.6 52.3 %collective-permute-start.11 = (f32[160,2048]{1,0:T(8,128)}, f32[160,2048]{1,0:T(8,128)}, u32[]{:S(2)}, u32[]{:S(2)}) collective-permute-start(f32[160,2048]{1,0:T(8,128)} %get-tuple-element.22.refs_0_), channel_id=1, source_target_pairs={{0,1},{1,0},{2,3},{3,2},{4,5},{5,4},{6,7},{7,6},{8,9},{9,8},{10,11... | collective-permute-start | bytes 3932168 | tf_op jit(solution)/shard_map/ppermute | solution.py:302
  65.4 22.5 %collective-permute-start.9 = (f32[160,2048]{1,0:T(8,128)S(1)}, f32[160,2048]{1,0:T(8,128)S(1)}, u32[]{:S(2)}, u32[]{:S(2)}) collective-permute-start(f32[160,2048]{1,0:T(8,128)S(1)} %get-tuple-element.13.s_ref.refs_0_), channel_id=1, source_target_pairs={{0,1},{1,0},{2,3},{3,2},{4,5},{5,4},{6,7},{7,6},{8,9},{9,8},{10,11... | collective-permute-start | bytes 3932168 | tf_op jit(solution)/shard_map/ppermute | solution.py:302
  65.5 3.0 %collective-permute-start.3 = (f32[64,128]{1,0:T(8,128)S(1)}, f32[64,128]{1,0:T(8,128)S(1)}, u32[]{:S(2)}, u32[]{:S(2)}) collective-permute-start(f32[64,128]{1,0:T(8,128)S(1)} %slice_select_fusion), channel_id=1, source_target_pairs={{0,1},{1,0},{2,3},{3,2},{4,5},{5,4},{6,7},{7,6},{8,9},{9,8},{10,11... | collective-permute-start | bytes 98312 | tf_op jit(solution)/shard_map/ppermute | solution.py:302
  68.5 3.9 %collective-permute-start.4 = (f32[64,128]{1,0:T(8,128)S(1)}, f32[64,128]{1,0:T(8,128)S(1)}, u32[]{:S(2)}, u32[]{:S(2)}) collective-permute-start(f32[64,128]{1,0:T(8,128)S(1)} %select_add_fusion), channel_id=1, source_target_pairs={{0,2},{1,3},{2,0},{3,1},{4,6},{5,7},{6,4},{7,5},{8,10},{9,11},{10,... | collective-permute-start | bytes 98312 | tf_op jit(solution)/shard_map/ppermute | solution.py:302
  72.4 3.9 %collective-permute-start.5 = (f32[64,128]{1,0:T(8,128)S(1)}, f32[64,128]{1,0:T(8,128)S(1)}, u32[]{:S(2)}, u32[]{:S(2)}) collective-permute-start(f32[64,128]{1,0:T(8,128)S(1)} %add.43), channel_id=1, source_target_pairs={{0,4},{4,0},{8,12},{12,8},{16,20},{20,16},{24,28},{28,24},{1,5},{5... | collective-permute-start | bytes 98312 | tf_op jit(solution)/shard_map/ppermute | solution.py:302
  76.4 3.9 %collective-permute-start.6 = (f32[64,128]{1,0:T(8,128)S(1)}, f32[64,128]{1,0:T(8,128)S(1)}, u32[]{:S(2)}, u32[]{:S(2)}) collective-permute-start(f32[64,128]{1,0:T(8,128)S(1)} %add.44), channel_id=1, source_target_pairs={{0,8},{4,12},{8,0},{12,4},{16,24},{20,28},{24,16},{28,20},{1,9},{5... | collective-permute-start | bytes 98312 | tf_op jit(solution)/shard_map/ppermute | solution.py:302
  80.3 4.9 %collective-permute-start.7 = (f32[64,128]{1,0:T(8,128)S(1)}, f32[64,128]{1,0:T(8,128)S(1)}, u32[]{:S(2)}, u32[]{:S(2)}) collective-permute-start(f32[64,128]{1,0:T(8,128)S(1)} %add.45), channel_id=1, source_target_pairs={{0,16},{4,20},{8,24},{12,28},{16,0},{20,4},{24,8},{28,12},{1,17},{... | collective-permute-start | bytes 98312 | tf_op jit(solution)/shard_map/ppermute | solution.py:302
  85.2 2.6 %collective-permute-start.8 = (f32[64,128]{1,0:T(8,128)S(1)}, f32[64,128]{1,0:T(8,128)S(1)}, u32[]{:S(2)}, u32[]{:S(2)}) collective-permute-start(f32[64,128]{1,0:T(8,128)S(1)} %add.46), channel_id=1, source_target_pairs={{0,1},{1,0},{2,3},{3,2},{4,5},{5,4},{6,7},{7,6},{8,9},{9,8},{10,11... | collective-permute-start | bytes 98312 | tf_op jit(solution)/shard_map/ppermute | solution.py:302
  92.6 17.6 %collective-permute-start.12 = (f32[80,128]{1,0:T(8,128)S(1)}, f32[80,128]{1,0:T(8,128)S(1)}, u32[]{:S(2)}, u32[]{:S(2)}) collective-permute-start(f32[80,128]{1,0:T(8,128)S(1)} %get-tuple-element.14), channel_id=1, source_target_pairs={{0,0},{1,8},{2,16},{3,24},{4,1},{5,9},{6,17},{7,25},{8,2},{9,10},{... | collective-permute-start | bytes 122888 | tf_op jit(solution)/shard_map/ppermute | solution.py:379
  93.3 18.9 %collective-permute-start.13 = (f32[80,128]{1,0:T(8,128)S(1)}, f32[80,128]{1,0:T(8,128)S(1)}, u32[]{:S(2)}, u32[]{:S(2)}) collective-permute-start(f32[80,128]{1,0:T(8,128)S(1)} %get-tuple-element.15), channel_id=1, source_target_pairs={{0,1},{1,9},{2,17},{3,25},{4,0},{5,8},{6,16},{7,24},{8,3},{9,11},{... | collective-permute-start | bytes 122888 | tf_op jit(solution)/shard_map/ppermute | solution.py:379
  96.3 24.9 %collective-permute-start.14 = (f32[80,128]{1,0:T(8,128)S(1)}, f32[80,128]{1,0:T(8,128)S(1)}, u32[]{:S(2)}, u32[]{:S(2)}) collective-permute-start(f32[80,128]{1,0:T(8,128)S(1)} %get-tuple-element.16), channel_id=1, source_target_pairs={{0,2},{1,10},{2,18},{3,26},{4,3},{5,11},{6,19},{7,27},{8,0},{9,8},... | collective-permute-start | bytes 122888 | tf_op jit(solution)/shard_map/ppermute | solution.py:379
  105.2 18.2 %collective-permute-start.15 = (f32[80,128]{1,0:T(8,128)S(1)}, f32[80,128]{1,0:T(8,128)S(1)}, u32[]{:S(2)}, u32[]{:S(2)}) collective-permute-start(f32[80,128]{1,0:T(8,128)S(1)} %get-tuple-element.17), channel_id=1, source_target_pairs={{0,3},{1,11},{2,19},{3,27},{4,2},{5,10},{6,18},{7,26},{8,1},{9,9},... | collective-permute-start | bytes 122888 | tf_op jit(solution)/shard_map/ppermute | solution.py:379
  109.6 13.9 %collective-permute-start.16 = (f32[80,128]{1,0:T(8,128)S(1)}, f32[80,128]{1,0:T(8,128)S(1)}, u32[]{:S(2)}, u32[]{:S(2)}) collective-permute-start(f32[80,128]{1,0:T(8,128)S(1)} %get-tuple-element.18), channel_id=1, source_target_pairs={{0,4},{1,12},{2,20},{3,28},{4,5},{5,13},{6,21},{7,29},{8,6},{9,14}... | collective-permute-start | bytes 122888 | tf_op jit(solution)/shard_map/ppermute | solution.py:379
  110.2 13.2 %collective-permute-start.17 = (f32[80,128]{1,0:T(8,128)S(1)}, f32[80,128]{1,0:T(8,128)S(1)}, u32[]{:S(2)}, u32[]{:S(2)}) collective-permute-start(f32[80,128]{1,0:T(8,128)S(1)} %get-tuple-element.19), channel_id=1, source_target_pairs={{0,5},{1,13},{2,21},{3,29},{4,4},{5,12},{6,20},{7,28},{8,7},{9,15}... | collective-permute-start | bytes 122888 | tf_op jit(solution)/shard_map/ppermute | solution.py:379
  112.2 11.6 %collective-permute-start.18 = (f32[80,128]{1,0:T(8,128)S(1)}, f32[80,128]{1,0:T(8,128)S(1)}, u32[]{:S(2)}, u32[]{:S(2)}) collective-permute-start(f32[80,128]{1,0:T(8,128)S(1)} %get-tuple-element.20), channel_id=1, source_target_pairs={{0,6},{1,14},{2,22},{3,30},{4,7},{5,15},{6,23},{7,31},{8,4},{9,12}... | collective-permute-start | bytes 122888 | tf_op jit(solution)/shard_map/ppermute | solution.py:379
  121.1 6.8 %collective-permute-start.19 = (f32[80,128]{1,0:T(8,128)S(1)}, f32[80,128]{1,0:T(8,128)S(1)}, u32[]{:S(2)}, u32[]{:S(2)}) collective-permute-start(f32[80,128]{1,0:T(8,128)S(1)} %get-tuple-element.21), channel_id=1, source_target_pairs={{0,7},{1,15},{2,23},{3,31},{4,6},{5,14},{6,22},{7,30},{8,5},{9,13}... | collective-permute-start | bytes 122888 | tf_op jit(solution)/shard_map/ppermute | solution.py:379

commit v2 on v1

--- a/solution.py
+++ b/solution.py
@@ -9,6 +9,7 @@
 P1 = 64
 P2 = 32
 BAND = 32
+CHUNKS = 2
 F32 = jnp.float32
 BF16 = jnp.bfloat16
 HI = lax.Precision.HIGHEST
@@ -76,25 +77,79 @@
     return jnp.concatenate(out, axis=0)
 
 
-def gram_kernel(scale, a_ref, b_ref, s_ref, g_ref):
+def split_kernel(a_ref, b_ref, both_ref, high_ref):
+    rank = a_ref.shape[0]
     s = a_ref[...] + b_ref[...]
-    s_ref[...] = s
-    g_ref[...] = pack_gram(dot(s, s, ((1,), (1,)), HI) * scale)
-
-
-def own_gram(a, b, scale):
+    high = s.astype(BF16)
+    high_ref[...] = high
+    both_ref[:rank, :] = high
+    both_ref[rank:, :] = (s - high.astype(F32)).astype(BF16)
+
+
+def split_sum(a, b):
     rank, rows = a.shape
+    return pl.pallas_call(
+        split_kernel,
+        out_shape=(
+            jax.ShapeDtypeStruct((2 * rank, rows), BF16),
+            jax.ShapeDtypeStruct((rank, rows), BF16),
+        ),
+        compiler_params=params(),
+        cost_estimate=cost(4 * rank * rows, 14 * rank * rows),
+        name="split",
+    )(a, b)
+
+
+def fold_square(x, rank):
+    return (x[:rank, :rank] + x[rank:, rank:]) + (x[:rank, rank:] + x[rank:, :rank])
+
+
+def gram_kernel(*refs):
+    o_ref = refs[-1]
+    rank = o_ref.shape[0]
+    total = None
+    for ref in refs[:-1]:
+        both = ref[...]
+        term = dot(both, both, ((1,), (1,)))
+        total = term if total is None else total + term
+    o_ref[...] = fold_square(total, rank)
+
+
+def local_gram(pairs):
+    rank, rows = pairs[0].shape[0] // 2, pairs[0].shape[1]
+    return pl.pallas_call(
+        gram_kernel,
+        out_shape=jax.ShapeDtypeStruct((rank, rank), F32),
+        compiler_params=params(),
+        cost_estimate=cost(8 * rank * rank * rows * len(pairs), 4 * rank * rows * len(pairs)),
+        name="gram",
+    )(*pairs)
+
+
+def cross_kernel(scale, count, *refs):
+    own, got, far, near = (refs[k * count:(k + 1) * count] for k in range(4))
+    g_ref, o_ref = refs[4 * count], refs[4 * count + 1]
+    rank = g_ref.shape[0]
+    total = None
+    for own_ref, got_ref, far_ref, near_ref in zip(own, got, far, near):
+        term = dot(own_ref[...], got_ref[...], ((1,), (1,)))
+        term = term[:rank] + term[rank:]
+        term = term + dot(near_ref[...], far_ref[rank:, :], ((1,), (1,)))
+        total = term if total is None else total + term
+    o_ref[...] = pack_gram((g_ref[...] + (total + total.T)) * scale)
+
+
+def cross_gram(own, got, far, near, gram, scale):
+    rank = gram.shape[0]
+    rows = got[0].shape[1] * len(got)
     groups = packing(rank)[2]
     return pl.pallas_call(
-        functools.partial(gram_kernel, scale),
-        out_shape=(
-            jax.ShapeDtypeStruct((rank, rows), F32),
-            jax.ShapeDtypeStruct((groups * BAND, 128), F32),
-        ),
-        compiler_params=params(),
-        cost_estimate=cost(12 * rank * rank * rows, 16 * rank * rows),
-        name="gram",
-    )(a, b)
+        functools.partial(cross_kernel, scale, len(own)),
+        out_shape=jax.ShapeDtypeStruct((groups * BAND, 128), F32),
+        compiler_params=params(),
+        cost_estimate=cost(6 * rank * rank * rows, 12 * rank * rows),
+        name="cross",
+    )(*own, *got, *far, *near, gram)
 
 
 def wide_lanes(x, n):
@@ -165,45 +220,58 @@
     )(packed)
 
 
-def project_kernel(count, ids_ref, *refs):
+def project_kernel(count, has_base, finish, ids_ref, *refs):
     s_refs, x_refs = refs[:count], refs[count:2 * count]
-    o_ref = refs[-1]
-    rank = o_ref.shape[0]
+    rest = refs[2 * count + has_base:]
+    t_ref = rest[-1]
+    rank = t_ref.shape[0]
 
     @pl.when(pl.program_id(0) == 0)
     def _():
-        o_ref[...] = refs[2 * count][...] if len(refs) > 2 * count + 1 else jnp.zeros_like(o_ref)
-
+        t_ref[...] = refs[2 * count][...] if has_base else jnp.zeros_like(t_ref)
+
+    total = None
     for s_ref, x_ref in zip(s_refs, x_refs):
-        s = s_ref[...]
-        high = s.astype(BF16)
-        low = (s - high.astype(F32)).astype(BF16)
-        both = dot(jnp.concatenate([high, low], axis=0), x_ref[...], ((1,), (0,)))
-        o_ref[...] += both[:rank] + both[rank:]
-
-
-def project(ids, parts, x, base, rows):
+        term = dot(s_ref[...], x_ref[...], ((1,), (0,)))
+        total = term if total is None else total + term
+    t_ref[...] += total if total.shape[0] == rank else total[:rank] + total[rank:]
+    if finish is not None:
+        @pl.when(pl.program_id(0) == pl.num_programs(0) - 1)
+        def _():
+            finish(t_ref[...], ids_ref[count], *rest[:-1])
+
+
+def project(ids, parts, x, rank, base, rows, finish=None, outs=(), scratch=()):
     count = len(parts)
-    rank, span = parts[0].shape
+    height, span = parts[0].shape
     depth = x.shape[1]
     steps = span // rows
     bases = [] if base is None else [base]
-    return pl.pallas_call(
-        functools.partial(project_kernel, count),
+    whole = pl.BlockSpec((rank, depth), lambda i, ids: (0, 0))
+    t_shape = jax.ShapeDtypeStruct((rank, depth), F32)
+    if finish is None:
+        out_specs, out_shape, scratch_shapes = whole, t_shape, []
+    else:
+        out_specs = [pl.BlockSpec(o.shape, lambda i, ids: (0, 0, 0)) for o in outs]
+        out_shape = list(outs)
+        scratch_shapes = list(scratch) + [pltpu.VMEM((rank, depth), F32)]
+    return pl.pallas_call(
+        functools.partial(project_kernel, count, len(bases), finish),
         grid_spec=pltpu.PrefetchScalarGridSpec(
             num_scalar_prefetch=1,
             grid=(steps,),
-            in_specs=[pl.BlockSpec((rank, rows), lambda i, ids: (0, i))] * count
+            in_specs=[pl.BlockSpec((height, rows), lambda i, ids: (0, i))] * count
             + [
                 pl.BlockSpec((rows, depth), lambda i, ids, k=k: (ids[k] * steps + i, 0))
                 for k in range(count)
             ]
-            + [pl.BlockSpec((rank, depth), lambda i, ids: (0, 0))] * len(bases),
-            out_specs=pl.BlockSpec((rank, depth), lambda i, ids: (0, 0)),
+            + [whole] * len(bases),
+            out_specs=out_specs,
+            scratch_shapes=scratch_shapes,
         ),
-        out_shape=jax.ShapeDtypeStruct((rank, depth), F32),
-        compiler_params=params(),
-        cost_estimate=cost(4 * rank * depth * span * count, span * count * (depth * 2 + rank * 4)),
+        out_shape=out_shape,
+        compiler_params=params(),
+        cost_estimate=cost(2 * height * depth * span * count, span * count * (depth + height) * 2),
         name="project",
     )(ids, *parts, *([x] * count), *bases)
 
@@ -216,9 +284,12 @@
     return best
 
 
-def regroup_kernel(pieces, samp, per_node, width_cols, me_ref, t_ref, *refs):
-    outs, hold = refs[:pieces], refs[pieces]
-    rank, depth = t_ref.shape
+def reverse_bits(p, count):
+    return sum(1 << (count - 1 - b) for b in range(count) if (p >> b) & 1)
+
+
+def regroup_tail(pieces, samp, per_node, width_cols, t, me, keep_ref, send_ref, hold):
+    rank, depth = t.shape
     width = per_node * width_cols
     fold = folding(rank, width)
     tall = rank // fold
@@ -228,7 +299,6 @@
     s, rest = rest // width, rest % width
     want = (a * per_node + rest // width_cols) * (samp * width_cols) + s * width_cols + rest % width_cols
     move = jnp.where(src == want, 1.0, 0.0).astype(BF16)
-    t = t_ref[...]
     high = t.astype(BF16)
     mid = (t - high.astype(F32)).astype(BF16)
     low = (t - high.astype(F32) - mid.astype(F32)).astype(BF16)
@@ -237,40 +307,33 @@
     for i in range(pieces):
         piece = moved[:, i * width:(i + 1) * width]
         hold[i] = jnp.concatenate([piece[f * tall:(f + 1) * tall] for f in range(fold)], axis=1)
-    me = me_ref[0]
-    for k, out in enumerate(outs):
-        out[...] = hold[me ^ k]
-
-
-def regroup(me, t, samp, node, per_node, width_cols):
-    rank, depth = t.shape
-    width = per_node * width_cols
-    fold = folding(rank, width)
-    shape = (rank // fold, fold * width)
-    return pl.pallas_call(
-        functools.partial(regroup_kernel, node, samp, per_node, width_cols),
-        in_specs=[pl.BlockSpec(memory_space=pltpu.SMEM), pl.BlockSpec(memory_space=pltpu.VMEM)],
-        out_shape=[jax.ShapeDtypeStruct(shape, F32)] * node,
-        scratch_shapes=[pltpu.VMEM((node,) + shape, F32)],
-        compiler_params=params(),
-        cost_estimate=cost(6 * rank * depth * depth, 8 * rank * depth),
-        name="regroup",
-    )(me, t)
-
-
-def core_kernel(inv_ref, s_ref, o_ref):
-    o_ref[...] = dot(inv_ref[...], s_ref[...], ((1,), (0,)), HI)
-
-
-def core_product(inverse, s):
-    rank, rows = s.shape
-    return pl.pallas_call(
-        core_kernel,
-        out_shape=jax.ShapeDtypeStruct((rank, rows), F32),
-        compiler_params=params(),
-        cost_estimate=cost(12 * rank * rank * rows, 8 * rank * rows),
+    bits = pieces.bit_length() - 1
+    for p in range(pieces):
+        out = send_ref if p >= pieces // 2 else keep_ref
+        out[p % (pieces // 2)] = hold[me ^ reverse_bits(p, bits)]
+
+
+def core_kernel(count, inv_ref, *refs):
+    both, high, low = (refs[k * count:(k + 1) * count] for k in range(3))
+    o_ref = refs[-1]
+    rank = inv_ref.shape[0]
+    for c in range(count):
+        s = both[c][:rank, :].astype(F32) + both[c][rank:, :].astype(F32)
+        s = s + (high[c][...].astype(F32) + low[c][...].astype(F32))
+        rows = s.shape[1]
+        o_ref[:, c * rows:(c + 1) * rows] = dot(inv_ref[...], s, ((1,), (0,)), HI)
+
+
+def core_product(inverse, both, high, low):
+    rank, rows = high[0].shape
+    count = len(both)
+    return pl.pallas_call(
+        functools.partial(core_kernel, count),
+        out_shape=jax.ShapeDtypeStruct((rank, rows * count), F32),
+        compiler_params=params(),
+        cost_estimate=cost(12 * rank * rank * rows * count, 12 * rank * rows * count),
         name="core",
-    )(inverse, s)
+    )(inverse, *both, *high, *low)
 
 
 def coefficient_kernel(scale, per_node, width_cols, inv_ref, *refs):
@@ -309,39 +372,63 @@
     node = lax.axis_size("node")
     total = rows_all * node
     quarter = rows_all // samp
-    rows = min(quarter, 1024)
-    steps = quarter // rows
+    chunks = CHUNKS
+    span = quarter // chunks
+    every = range(chunks)
     me_s = lax.axis_index("samp").astype(jnp.int32)
     me_n = lax.axis_index("node").astype(jnp.int32)
     w_t = sketch_matrix.T
-
-    def block_ids(d):
-        return jnp.stack([(me_s ^ d) * steps + i for i in range(steps)])
-
-    order = sorted(range(samp), key=lambda d: (-(d // 2), -(d % 2)))
-    part = {d: sketch(block_ids(d), snapshots, w_t, rows) for d in order}
-
-    held = dict(part)
-    bit = 1
-    while bit * 2 < samp:
-        got = {d ^ bit: swap(held.pop(d), "samp", samp, bit) for d in order if d in held and d & bit}
-        for d in got:
-            held[d] = held[d] + got[d]
-        bit *= 2
-    last = bit
-    ours, theirs = held[0], held[last]
-    arrived = swap(theirs, "samp", samp, last)
-    short = swap(ours.astype(BF16), "samp", samp, last)
-    own, gram = own_gram(ours, arrived, 1.0 / total)
-
-    full = {0: own, last: theirs + short.astype(F32)}
-    bit = last // 2
-    while bit:
-        full.update({d ^ bit: swap(full[d], "samp", samp, bit) for d in list(full)})
-        bit //= 2
-
+    last = samp // 2
+
+    def chip_sum(base, c):
+        ds = [base ^ d for d in range(last)]
+        held = {}
+        for d in sorted(ds, reverse=True):
+            ids = ((me_s ^ d) * chunks + c)[None]
+            held[d] = sketch(ids, snapshots, w_t, span)
+        bit = 1
+        while bit < last:
+            for d in [d for d in held if d & bit]:
+                got = swap(held.pop(d), "samp", samp, bit)
+                if bit * 2 < last:
+                    held[d ^ bit] = held[d ^ bit] + got
+                else:
+                    return split_sum(held[d ^ bit], got)
+            bit *= 2
+
+    far, far_high, own, own_high = [], [], [], []
+    got_high, near_high = [], []
+    for c in every:
+        both, high = chip_sum(last, c)
+        far.append(both)
+        got_high.append(swap(high, "samp", samp, last))
+    for c in every:
+        both, high = chip_sum(0, c)
+        own.append(both)
+        near_high.append(swap(high, "samp", samp, last))
+    got_low = []
+    for c in every:
+        low, _ = lax.optimization_barrier((far[c][rank:], got_high[c]))
+        got_low.append(swap(low, "samp", samp, last))
+    gram = local_gram(own + far)
+
+    def spread_over(table):
+        bit = last // 2
+        while bit:
+            table.update({d ^ bit: [swap(v, "samp", samp, bit) for v in table[d]] for d in list(table)})
+            bit //= 2
+        return table
+
+    def ids_of(ds):
+        return [(me_s ^ d) * chunks + c for d in ds for c in every]
+
+    rows = min(span, 256)
+    pairs = spread_over({0: own, last: far})
+    t = project(jnp.stack(ids_of(pairs)), [v for d in pairs for v in pairs[d]], snapshots, rank, None, rows)
+
+    packed = cross_gram(own, got_high, far, near_high, gram, 1.0 / total)
     upper = (me_s & 1) == 1
-    halves = jnp.split(gram, 2, axis=0)
+    halves = jnp.split(packed, 2, axis=0)
     mine = jnp.where(upper, halves[1], halves[0])
     mine = mine + swap(jnp.where(upper, halves[0], halves[1]), "samp", samp, 1)
     bit = 2
@@ -356,28 +443,37 @@
     packed = jnp.concatenate([jnp.where(upper, other, mine), jnp.where(upper, mine, other)], axis=0)
     inverse = factor_inverse(packed, rank)
 
-    def ids(ds):
-        return jnp.stack([me_s ^ d for d in ds])
-
-    t = project(ids([0]), [full[0]], snapshots, None, rows)
-    t = project(ids([last]), [full[last]], snapshots, t, rows)
-    rest = [d for d in full if d not in (0, last)]
-    if rest:
-        t = project(ids(rest), [full[d] for d in rest], snapshots, t, rows)
-
+    highs = spread_over({0: got_high, last: near_high})
+    first = [0, last]
+    t = project(jnp.stack(ids_of(first)), [v for d in first for v in highs[d]], snapshots, rank, t, rows)
+    then = [d for d in highs if d not in first]
     per_node = P1 // node
     width_cols = P2 // samp
+    width = per_node * width_cols
+    fold = folding(rank, width)
+    piece = (rank // fold, fold * width)
+    keep, send = project(
+        jnp.stack(ids_of(then) + [me_n]), [v for d in then for v in highs[d]], snapshots, rank, t, rows,
+        functools.partial(regroup_tail, node, samp, per_node, width_cols),
+        [jax.ShapeDtypeStruct((node // 2,) + piece, F32)] * 2,
+        [pltpu.VMEM((node,) + piece, F32)])
+
+    bit = 1
+    while keep.shape[0] > 1:
+        got = swap(send, "node", node, bit)
+        half = keep.shape[0] // 2
+        keep, send = keep[:half] + got[:half], keep[half:] + got[half:]
+        bit *= 2
     spread = node // samp
-    pieces = regroup(me_n[None], t, samp, node, per_node, width_cols)
     landed = []
-    for k in range(node):
-        pairs = []
+    for k, value in ((0, keep), (bit, send)):
+        route = []
         for n in range(node):
             a, s_to = (n ^ k) // samp, (n ^ k) % samp
             for s_from in range(samp):
-                pairs.append((n * samp + s_from, (s_from * spread + a) * samp + s_to))
-        landed.append(lax.ppermute(pieces[k], ("node", "samp"), pairs))
-    core = core_product(inverse, own)
+                route.append((n * samp + s_from, (s_from * spread + a) * samp + s_to))
+        landed.append(lax.ppermute(value[0], ("node", "samp"), route))
+    core = core_product(inverse, own, got_high, got_low)
     coef = coefficients(inverse, landed, 1.0 / total, per_node, width_cols)
     return (core.T, coef.T)
 

time: 129 us -> 120 us (0.930)
  the two profiles are of different devices: /device:TPU:0 before, /device:TPU:3 now
where the time goes in v2:
time: 120 us; the launch traced here: 119 us
  Pallas kernels  51.2 us (43%)
  starting transfers between devices  34.8 us (29%)
  waiting for transfers between devices  25.2 us (21%)
  local copies, waits for them, and re-layouts  6.93 us (6%)
    ppermute x26, starting transfers between devices, swap(): return lax.ppermute(value, axis, [(i, i ^ bit) for i in range(size)])  27.4 us
    ppermute x26, waiting for transfers between devices, swap(): return lax.ppermute(value, axis, [(i, i ^ bit) for i in range(size)])  22.8 us
    pallas_call x3, Pallas kernels, project(): pl.pallas_call(functools.partial(project_kernel, count, len(bases), finis...  16.7 us
    pallas_call x8, Pallas kernels, sketch(): pl.pallas_call(sketch_kernel, grid_spec=pltpu.PrefetchScalarGridSpec(num_...  15.4 us
    ppermute x2, starting transfers between devices, body(): landed.append(lax.ppermute(value[0], ('node', 'samp'), route))  7.37 us
    unnamed x16, local copies, waits for them, and re-layouts  6.72 us
    pallas_call x4, Pallas kernels, split_sum(): pl.pallas_call(split_kernel, out_shape=(jax.ShapeDtypeStruct((2 * rank, r...  6.51 us
    pallas_call x1, Pallas kernels, factor_inverse(): pl.pallas_call(functools.partial(factor_kernel, rank), out_shape=jax.Shap...  5.48 us
  transfers between devices with their start and end apart: 28, of which 10 were waited for; matrix products, arithmetic and copies ran while one was open for 0% of the time, Pallas kernels for 41%

profile of v2, /device:TPU:3, one launch (start us, length us, event | category | flops | bytes accessed | tf_op | source)
XLA Modules:
  0.0 119.2 jit_solution(1497404666236495080)
XLA Ops:
  1.6 1.7 %sketch.15 = f32[160,1024]{1,0:T(8,128)S(1)} custom-call(s32[1]{0:T(128)} %bitcast.8.ids_ref, bf16[8192,512]{1,0:T(8,128)(2,1)} %refs_7_.3, bf16[160,512]{1,0:T(8,128)(2,1)S(1)} %bitcast.16), custom_call_target="tpu_custom_call" | custom-call | flops 167772160 | bytes 1703936 | tf_op jit(solution)/shard_map/sketch/pallas_call | solution.py:42
  5.9 2.6 %sketch.11 = f32[160,1024]{1,0:T(8,128)} custom-call(s32[1]{0:T(128)} %bitcast.4.ids_ref, bf16[8192,512]{1,0:T(8,128)(2,1)} %refs_7_.3, bf16[160,512]{1,0:T(8,128)(2,1)S(1)} %bitcast.18), custom_call_target="tpu_custom_call" | custom-call | flops 167772160 | bytes 1703936 | tf_op jit(solution)/shard_map/sketch/pallas_call | solution.py:42
  8.9 2.6 %sketch.9 = f32[160,1024]{1,0:T(8,128)} custom-call(s32[1]{0:T(128)} %bitcast.2.ids_ref, bf16[8192,512]{1,0:T(8,128)(2,1)} %refs_7_.3, bf16[160,512]{1,0:T(8,128)(2,1)S(1)} %bitcast.19), custom_call_target="tpu_custom_call" | custom-call | flops 167772160 | bytes 1703936 | tf_op jit(solution)/shard_map/sketch/pallas_call | solution.py:42
  15.7 1.9 %split.20 = (bf16[320,1024]{1,0:T(8,128)(2,1)S(1)}, bf16[160,1024]{1,0:T(8,128)(2,1)}) custom-call(f32[160,1024]{1,0:T(8,128)S(1)} %sketch.12.a_ref, f32[160,1024]{1,0:T(8,128)} %collective-permute-done.2.b_ref), custom_call_target="tpu_custom_call" | custom-call | flops 655360 | bytes 2293760 | tf_op jit(solution)/shard_map/split/pallas_call | solution.py:91
  22.5 1.9 %split.19 = (bf16[320,1024]{1,0:T(8,128)(2,1)S(1)}, bf16[160,1024]{1,0:T(8,128)(2,1)}) custom-call(f32[160,1024]{1,0:T(8,128)S(1)} %sketch.10.a_ref, f32[160,1024]{1,0:T(8,128)} %collective-permute-done.1.b_ref), custom_call_target="tpu_custom_call" | custom-call | flops 655360 | bytes 2293760 | tf_op jit(solution)/shard_map/split/pallas_call | solution.py:91
  24.5 1.9 %split.18 = (bf16[320,1024]{1,0:T(8,128)(2,1)S(1)}, bf16[160,1024]{1,0:T(8,128)(2,1)}) custom-call(f32[160,1024]{1,0:T(8,128)S(1)} %sketch.8.a_ref, f32[160,1024]{1,0:T(8,128)} %collective-permute-done.b_ref), custom_call_target="tpu_custom_call" | custom-call | flops 655360 | bytes 2293760 | tf_op jit(solution)/shard_map/split/pallas_call | solution.py:91
  29.4 2.3 %collective-permute-done.3.refs_2_.refs_0_ = bf16[160,1024]{1,0:T(8,128)(2,1)S(1)} collective-permute-done((bf16[160,1024]{1,0:T(8,128)(2,1)}, bf16[160,1024]{1,0:T(8,128)(2,1)S(1)}, u32[]{:S(2)}, u32[]{:S(2)}) %collective-permute-start.3) | collective-permute-done | bytes 327712 | tf_op jit(solution)/shard_map/ppermute | solution.py:365
  31.8 2.3 %collective-permute-start.22 = (bf16[320,1024]{1,0:T(8,128)(2,1)S(1)}, bf16[320,1024]{1,0:T(8,128)(2,1)S(1)}, u32[]{:S(2)}, u32[]{:S(2)}) collective-permute-start(bf16[320,1024]{1,0:T(8,128)(2,1)S(1)} %get-tuple-element.18.refs_2_.refs_4_), channel_id=1, source_target_pairs={{0,1},{1,0},{2,3},{3,2},{4,5},{5,4},{6,7},{7,6},{8,9},{9,8},{10,11... | collective-permute-start | bytes 1966088 | tf_op jit(solution)/shard_map/ppermute | solution.py:365
  35.7 3.2 %collective-permute-done.7.refs_7_.refs_3_ = bf16[160,1024]{1,0:T(8,128)(2,1)} collective-permute-done((bf16[160,1024]{1,0:T(8,128)(2,1)}, bf16[160,1024]{1,0:T(8,128)(2,1)}, u32[]{:S(2)}, u32[]{:S(2)}) %collective-permute-start.7) | collective-permute-done | bytes 327712 | tf_op jit(solution)/shard_map/ppermute | solution.py:365
  38.9 2.3 %collective-permute-start.20 = (bf16[320,1024]{1,0:T(8,128)(2,1)S(1)}, bf16[320,1024]{1,0:T(8,128)(2,1)}, u32[]{:S(2)}, u32[]{:S(2)}) collective-permute-start(bf16[320,1024]{1,0:T(8,128)(2,1)S(1)} %get-tuple-element.14.refs_0_), channel_id=1, source_target_pairs={{0,1},{1,0},{2,3},{3,2},{4,5},{5,4},{6,7},{7,6},{8,9},{9,8},{10,11... | collective-permute-start | bytes 1966088 | tf_op jit(solution)/shard_map/ppermute | solution.py:365
  41.1 4.8 %collective-permute-done.6.refs_6_.refs_2_ = bf16[160,1024]{1,0:T(8,128)(2,1)} collective-permute-done((bf16[160,1024]{1,0:T(8,128)(2,1)}, bf16[160,1024]{1,0:T(8,128)(2,1)}, u32[]{:S(2)}, u32[]{:S(2)}) %collective-permute-start.6) | collective-permute-done | bytes 327712 | tf_op jit(solution)/shard_map/ppermute | solution.py:365
  45.9 1.9 %cross.1 = f32[128,128]{1,0:T(8,128)S(1)} custom-call(bf16[320,1024]{1,0:T(8,128)(2,1)S(1)} %get-tuple-element.14.refs_0_, bf16[320,1024]{1,0:T(8,128)(2,1)S(1)} %get-tuple-element.15.refs_1_, bf16[160,1024]{1,0:T(8,128)(2,1)S(1)} %collective-permute-done.3.refs_2_.refs_0_, bf16[160,1024]{1,0:T(8,128)(2,1)S(1)} %collective-permute-done.5.refs_3_.refs_1_, ...), custom_call_target="tpu_custom_call" | custom-call | flops 314572800 | bytes 3932160 | tf_op jit(solution)/shard_map/cross/pallas_call | solution.py:146
  50.1 2.8 %collective-permute-done.9 = f32[64,128]{1,0:T(8,128)S(1)} collective-permute-done((f32[64,128]{1,0:T(8,128)S(1)}, f32[64,128]{1,0:T(8,128)S(1)}, u32[]{:S(2)}, u32[]{:S(2)}) %collective-permute-start.9) | collective-permute-done | bytes 32800 | tf_op jit(solution)/shard_map/ppermute | solution.py:365
  58.4 2.3 %collective-permute-start.12 = (f32[64,128]{1,0:T(8,128)S(1)}, f32[64,128]{1,0:T(8,128)S(1)}, u32[]{:S(2)}, u32[]{:S(2)}) collective-permute-start(f32[64,128]{1,0:T(8,128)S(1)} %add.54), channel_id=1, source_target_pairs={{0,16},{4,20},{8,24},{12,28},{16,0},{20,4},{24,8},{28,12},{1,17},{... | collective-permute-start | bytes 98312 | tf_op jit(solution)/shard_map/ppermute | solution.py:365
  62.1 4.9 %collective-permute-start.17 = (bf16[160,1024]{1,0:T(8,128)(2,1)S(1)}, bf16[160,1024]{1,0:T(8,128)(2,1)}, u32[]{:S(2)}, u32[]{:S(2)}) collective-permute-start(bf16[160,1024]{1,0:T(8,128)(2,1)S(1)} %collective-permute-done.5.refs_3_.refs_1_), channel_id=1, source_target_pairs={{0,1},{1,0},{2,3},{3,2},{4,5},{5,4},{6,7},{7,6},{8,9},{9,8},{10,11... | collective-permute-start | bytes 983048 | tf_op jit(solution)/shard_map/ppermute | solution.py:365
  73.8 7.1 %project.3.refs_8_ = f32[160,512]{1,0:T(8,128)S(1)} custom-call(s32[8]{0:T(128)S(1)} %stack.11.ids_ref, bf16[320,1024]{1,0:T(8,128)(2,1)S(1)} %get-tuple-element.14.refs_0_, bf16[320,1024]{1,0:T(8,128)(2,1)S(1)} %get-tuple-element.15.refs_1_, bf16[320,1024]{1,0:T(8,128)(2,1)S(1)} %get-tuple-element.18.refs_2_.refs_4_, ...), custom_call_target="tpu_custom_call" | custom-call | flops 2684354560 | bytes 13631488 | tf_op jit(solution)/shard_map/project/pallas_call | solution.py:258
  80.9 4.5 %project.4.refs_8_ = f32[160,512]{1,0:T(8,128)S(1)} custom-call(s32[4]{0:T(128)S(1)} %pad_add_fusion.ids_ref, bf16[160,1024]{1,0:T(8,128)(2,1)S(1)} %collective-permute-done.3.refs_2_.refs_0_, bf16[160,1024]{1,0:T(8,128)(2,1)S(1)} %collective-permute-done.5.refs_3_.refs_1_, bf16[160,1024]{1,0:T(8,128)(2,1)} %collective-permute-done.6.refs_6_.refs_2_, ...), custom_call_target="tpu_custom_call" | custom-call | flops 671088640 | bytes 5505024 | tf_op jit(solution)/shard_map/project/pallas_call | solution.py:258
  88.0 5.1 %project.5 = (f32[4,80,128]{2,1,0:T(8,128)S(1)}, f32[4,80,128]{2,1,0:T(8,128)S(1)}) custom-call(s32[5]{0:T(128)S(1)} %stack.9.ids_ref, bf16[160,1024]{1,0:T(8,128)(2,1)} %collective-permute-done.16.refs_0_, bf16[160,1024]{1,0:T(8,128)(2,1)} %collective-permute-done.17.refs_1_, bf16[160,1024]{1,0:T(8,128)(2,1)} %collective-permute-done.18.refs_2_, ...), custom_call_target="tpu_custom_call" | custom-call | flops 671088640 | bytes 5505024 | tf_op jit(solution)/shard_map/project/pallas_call | solution.py:258
  94.5 4.5 %collective-permute-done.24 = f32[4,80,128]{2,1,0:T(8,128)S(1)} collective-permute-done((f32[4,80,128]{2,1,0:T(8,128)S(1)}, f32[4,80,128]{2,1,0:T(8,128)S(1)}, u32[]{:S(2)}, u32[]{:S(2)}) %collective-permute-start.24) | collective-permute-done | bytes 163872 | tf_op jit(solution)/shard_map/ppermute | solution.py:365
  100.4 5.5 %factor.1.inv_ref = f32[160,160]{1,0:T(8,128)S(1)} custom-call(f32[128,128]{1,0:T(8,128)S(1)} %pad_maximum_fusion.g_ref), custom_call_target="tpu_custom_call" | custom-call | flops 8000000000 | bytes 102400 | tf_op jit(solution)/shard_map/factor/pallas_call | solution.py:214
  105.9 5.1 %collective-permute-start.26 = (f32[80,128]{1,0:T(8,128)S(1)}, f32[80,128]{1,0:T(8,128)S(1)}, u32[]{:S(2)}, u32[]{:S(2)}) collective-permute-start(f32[80,128]{1,0:T(8,128)S(1)} %get-tuple-element.29), channel_id=1, source_target_pairs={{0,0},{1,8},{2,16},{3,24},{4,1},{5,9},{6,17},{7,25},{8,2},{9,10},{... | collective-permute-start | bytes 122888 | tf_op jit(solution)/shard_map/ppermute | solution.py:475
  111.0 2.3 %collective-permute-start.27 = (f32[80,128]{1,0:T(8,128)S(1)}, f32[80,128]{1,0:T(8,128)S(1)}, u32[]{:S(2)}, u32[]{:S(2)}) collective-permute-start(f32[80,128]{1,0:T(8,128)S(1)} %get-tuple-element.28), channel_id=1, source_target_pairs={{0,4},{1,12},{2,20},{3,28},{4,5},{5,13},{6,21},{7,29},{8,6},{9,14}... | collective-permute-start | bytes 122888 | tf_op jit(solution)/shard_map/ppermute | solution.py:475
  113.3 2.4 %core.1 = f32[160,2048]{1,0:T(8,128)} custom-call(f32[160,160]{1,0:T(8,128)S(1)} %factor.1.inv_ref, bf16[320,1024]{1,0:T(8,128)(2,1)S(1)} %get-tuple-element.14.refs_0_, bf16[320,1024]{1,0:T(8,128)(2,1)S(1)} %get-tuple-element.15.refs_1_, bf16[160,1024]{1,0:T(8,128)(2,1)S(1)} %collective-permute-done.3.refs_2_.refs_0_, ...), custom_call_target="tpu_custom_call" | custom-call | flops 629145600 | bytes 3932160 | tf_op jit(solution)/shard_map/core/pallas_call | solution.py:330
  115.7 2.4 %collective-permute-done.27.refs_1_ = f32[80,128]{1,0:T(8,128)S(1)} collective-permute-done((f32[80,128]{1,0:T(8,128)S(1)}, f32[80,128]{1,0:T(8,128)S(1)}, u32[]{:S(2)}, u32[]{:S(2)}) %collective-permute-start.27) | collective-permute-done | bytes 40992 | tf_op jit(solution)/shard_map/ppermute | solution.py:475
  (83 shorter events, 40.1 us)
Async XLA Ops:
  3.3 11.6 %collective-permute-start.4 = (f32[160,1024]{1,0:T(8,128)S(1)}, f32[160,1024]{1,0:T(8,128)S(1)}, u32[]{:S(2)}, u32[]{:S(2)}) collective-permute-start(f32[160,1024]{1,0:T(8,128)S(1)} %sketch.15), channel_id=1, source_target_pairs={{0,1},{1,0},{2,3},{3,2},{4,5},{5,4},{6,7},{7,6},{8,9},{9,8},{10,11... | collective-permute-start | bytes 1966088 | tf_op jit(solution)/shard_map/ppermute | solution.py:365
  5.8 10.0 %collective-permute-start.2 = (f32[160,1024]{1,0:T(8,128)S(1)}, f32[160,1024]{1,0:T(8,128)}, u32[]{:S(2)}, u32[]{:S(2)}) collective-permute-start(f32[160,1024]{1,0:T(8,128)S(1)} %sketch.13), channel_id=1, source_target_pairs={{0,1},{1,0},{2,3},{3,2},{4,5},{5,4},{6,7},{7,6},{8,9},{9,8},{10,11... | collective-permute-start | bytes 1966088 | tf_op jit(solution)/shard_map/ppermute | solution.py:365
  8.4 14.1 %collective-permute-start.1 = (f32[160,1024]{1,0:T(8,128)}, f32[160,1024]{1,0:T(8,128)}, u32[]{:S(2)}, u32[]{:S(2)}) collective-permute-start(f32[160,1024]{1,0:T(8,128)} %sketch.11), channel_id=1, source_target_pairs={{0,1},{1,0},{2,3},{3,2},{4,5},{5,4},{6,7},{7,6},{8,9},{9,8},{10,11... | collective-permute-start | bytes 1966088 | tf_op jit(solution)/shard_map/ppermute | solution.py:365
  11.5 13.0 %collective-permute-start = (f32[160,1024]{1,0:T(8,128)}, f32[160,1024]{1,0:T(8,128)}, u32[]{:S(2)}, u32[]{:S(2)}) collective-permute-start(f32[160,1024]{1,0:T(8,128)} %sketch.9), channel_id=1, source_target_pairs={{0,1},{1,0},{2,3},{3,2},{4,5},{5,4},{6,7},{7,6},{8,9},{9,8},{10,11... | collective-permute-start | bytes 1966088 | tf_op jit(solution)/shard_map/ppermute | solution.py:365
  15.7 13.7 %collective-permute-start.5 = (bf16[160,1024]{1,0:T(8,128)(2,1)}, bf16[160,1024]{1,0:T(8,128)(2,1)S(1)}, u32[]{:S(2)}, u32[]{:S(2)}) collective-permute-start(bf16[160,1024]{1,0:T(8,128)(2,1)} %get-tuple-element.17), channel_id=1, source_target_pairs={{0,2},{1,3},{2,0},{3,1},{4,6},{5,7},{6,4},{7,5},{8,10},{9,11},{10,... | collective-permute-start | bytes 983048 | tf_op jit(solution)/shard_map/ppermute | solution.py:365
  17.6 14.1 %collective-permute-start.3 = (bf16[160,1024]{1,0:T(8,128)(2,1)}, bf16[160,1024]{1,0:T(8,128)(2,1)S(1)}, u32[]{:S(2)}, u32[]{:S(2)}) collective-permute-start(bf16[160,1024]{1,0:T(8,128)(2,1)} %get-tuple-element.16), channel_id=1, source_target_pairs={{0,2},{1,3},{2,0},{3,1},{4,6},{5,7},{6,4},{7,5},{8,10},{9,11},{10,... | collective-permute-start | bytes 983048 | tf_op jit(solution)/shard_map/ppermute | solution.py:365
  24.5 14.4 %collective-permute-start.7 = (bf16[160,1024]{1,0:T(8,128)(2,1)}, bf16[160,1024]{1,0:T(8,128)(2,1)}, u32[]{:S(2)}, u32[]{:S(2)}) collective-permute-start(bf16[160,1024]{1,0:T(8,128)(2,1)} %get-tuple-element.21), channel_id=1, source_target_pairs={{0,2},{1,3},{2,0},{3,1},{4,6},{5,7},{6,4},{7,5},{8,10},{9,11},{10,... | collective-permute-start | bytes 983048 | tf_op jit(solution)/shard_map/ppermute | solution.py:365
  26.4 19.6 %collective-permute-start.6 = (bf16[160,1024]{1,0:T(8,128)(2,1)}, bf16[160,1024]{1,0:T(8,128)(2,1)}, u32[]{:S(2)}, u32[]{:S(2)}) collective-permute-start(bf16[160,1024]{1,0:T(8,128)(2,1)} %get-tuple-element.20), channel_id=1, source_target_pairs={{0,2},{1,3},{2,0},{3,1},{4,6},{5,7},{6,4},{7,5},{8,10},{9,11},{10,... | collective-permute-start | bytes 983048 | tf_op jit(solution)/shard_map/ppermute | solution.py:365
  27.8 39.2 %collective-permute-start.23 = (bf16[320,1024]{1,0:T(8,128)(2,1)S(1)}, bf16[320,1024]{1,0:T(8,128)(2,1)S(1)}, u32[]{:S(2)}, u32[]{:S(2)}) collective-permute-start(bf16[320,1024]{1,0:T(8,128)(2,1)S(1)} %get-tuple-element.19.refs_3_.refs_5_), channel_id=1, source_target_pairs={{0,1},{1,0},{2,3},{3,2},{4,5},{5,4},{6,7},{7,6},{8,9},{9,8},{10,11... | collective-permute-start | bytes 1966088 | tf_op jit(solution)/shard_map/ppermute | solution.py:365
  29.4 38.5 %collective-permute-start.21 = (bf16[320,1024]{1,0:T(8,128)(2,1)S(1)}, bf16[320,1024]{1,0:T(8,128)(2,1)S(1)}, u32[]{:S(2)}, u32[]{:S(2)}) collective-permute-start(bf16[320,1024]{1,0:T(8,128)(2,1)S(1)} %get-tuple-element.15.refs_1_), channel_id=1, source_target_pairs={{0,1},{1,0},{2,3},{3,2},{4,5},{5,4},{6,7},{7,6},{8,9},{9,8},{10,11... | collective-permute-start | bytes 1966088 | tf_op jit(solution)/shard_map/ppermute | solution.py:365
  31.8 37.5 %collective-permute-start.22 = (bf16[320,1024]{1,0:T(8,128)(2,1)S(1)}, bf16[320,1024]{1,0:T(8,128)(2,1)S(1)}, u32[]{:S(2)}, u32[]{:S(2)}) collective-permute-start(bf16[320,1024]{1,0:T(8,128)(2,1)S(1)} %get-tuple-element.18.refs_2_.refs_4_), channel_id=1, source_target_pairs={{0,1},{1,0},{2,3},{3,2},{4,5},{5,4},{6,7},{7,6},{8,9},{9,8},{10,11... | collective-permute-start | bytes 1966088 | tf_op jit(solution)/shard_map/ppermute | solution.py:365
  38.9 31.6 %collective-permute-start.20 = (bf16[320,1024]{1,0:T(8,128)(2,1)S(1)}, bf16[320,1024]{1,0:T(8,128)(2,1)}, u32[]{:S(2)}, u32[]{:S(2)}) collective-permute-start(bf16[320,1024]{1,0:T(8,128)(2,1)S(1)} %get-tuple-element.14.refs_0_), channel_id=1, source_target_pairs={{0,1},{1,0},{2,3},{3,2},{4,5},{5,4},{6,7},{7,6},{8,9},{9,8},{10,11... | collective-permute-start | bytes 1966088 | tf_op jit(solution)/shard_map/ppermute | solution.py:365
  58.4 3.7 %collective-permute-start.12 = (f32[64,128]{1,0:T(8,128)S(1)}, f32[64,128]{1,0:T(8,128)S(1)}, u32[]{:S(2)}, u32[]{:S(2)}) collective-permute-start(f32[64,128]{1,0:T(8,128)S(1)} %add.54), channel_id=1, source_target_pairs={{0,16},{4,20},{8,24},{12,28},{16,0},{20,4},{24,8},{28,12},{1,17},{... | collective-permute-start | bytes 98312 | tf_op jit(solution)/shard_map/ppermute | solution.py:365
  62.1 23.3 %collective-permute-start.17 = (bf16[160,1024]{1,0:T(8,128)(2,1)S(1)}, bf16[160,1024]{1,0:T(8,128)(2,1)}, u32[]{:S(2)}, u32[]{:S(2)}) collective-permute-start(bf16[160,1024]{1,0:T(8,128)(2,1)S(1)} %collective-permute-done.5.refs_3_.refs_1_), channel_id=1, source_target_pairs={{0,1},{1,0},{2,3},{3,2},{4,5},{5,4},{6,7},{7,6},{8,9},{9,8},{10,11... | collective-permute-start | bytes 983048 | tf_op jit(solution)/shard_map/ppermute | solution.py:365
  67.9 19.0 %collective-permute-start.16 = (bf16[160,1024]{1,0:T(8,128)(2,1)S(1)}, bf16[160,1024]{1,0:T(8,128)(2,1)}, u32[]{:S(2)}, u32[]{:S(2)}) collective-permute-start(bf16[160,1024]{1,0:T(8,128)(2,1)S(1)} %collective-permute-done.3.refs_2_.refs_0_), channel_id=1, source_target_pairs={{0,1},{1,0},{2,3},{3,2},{4,5},{5,4},{6,7},{7,6},{8,9},{9,8},{10,11... | collective-permute-start | bytes 983048 | tf_op jit(solution)/shard_map/ppermute | solution.py:365
  68.8 19.2 %collective-permute-start.19 = (bf16[160,1024]{1,0:T(8,128)(2,1)}, bf16[160,1024]{1,0:T(8,128)(2,1)}, u32[]{:S(2)}, u32[]{:S(2)}) collective-permute-start(bf16[160,1024]{1,0:T(8,128)(2,1)} %collective-permute-done.7.refs_7_.refs_3_), channel_id=1, source_target_pairs={{0,1},{1,0},{2,3},{3,2},{4,5},{5,4},{6,7},{7,6},{8,9},{9,8},{10,11... | collective-permute-start | bytes 983048 | tf_op jit(solution)/shard_map/ppermute | solution.py:365
  70.1 17.9 %collective-permute-start.18 = (bf16[160,1024]{1,0:T(8,128)(2,1)}, bf16[160,1024]{1,0:T(8,128)(2,1)}, u32[]{:S(2)}, u32[]{:S(2)}) collective-permute-start(bf16[160,1024]{1,0:T(8,128)(2,1)} %collective-permute-done.6.refs_6_.refs_2_), channel_id=1, source_target_pairs={{0,1},{1,0},{2,3},{3,2},{4,5},{5,4},{6,7},{7,6},{8,9},{9,8},{10,11... | collective-permute-start | bytes 983048 | tf_op jit(solution)/shard_map/ppermute | solution.py:365
  70.5 42.9 %collective-permute-start.15 = (bf16[160,1024]{1,0:T(8,128)(2,1)S(1)}, bf16[160,1024]{1,0:T(8,128)(2,1)S(1)}, u32[]{:S(2)}, u32[]{:S(2)}) collective-permute-start(bf16[160,1024]{1,0:T(8,128)(2,1)S(1)} %slice.31), channel_id=1, source_target_pairs={{0,2},{1,3},{2,0},{3,1},{4,6},{5,7},{6,4},{7,5},{8,10},{9,11},{10,... | collective-permute-start | bytes 983048 | tf_op jit(solution)/shard_map/ppermute | solution.py:365
  85.4 27.9 %collective-permute-start.14 = (bf16[160,1024]{1,0:T(8,128)(2,1)S(1)}, bf16[160,1024]{1,0:T(8,128)(2,1)S(1)}, u32[]{:S(2)}, u32[]{:S(2)}) collective-permute-start(bf16[160,1024]{1,0:T(8,128)(2,1)S(1)} %slice.30), channel_id=1, source_target_pairs={{0,2},{1,3},{2,0},{3,1},{4,6},{5,7},{6,4},{7,5},{8,10},{9,11},{10,... | collective-permute-start | bytes 983048 | tf_op jit(solution)/shard_map/ppermute | solution.py:365
  87.0 7.5 %collective-permute-start.13 = (f32[64,128]{1,0:T(8,128)S(1)}, f32[64,128]{1,0:T(8,128)S(1)}, u32[]{:S(2)}, u32[]{:S(2)}) collective-permute-start(f32[64,128]{1,0:T(8,128)S(1)} %add.55), channel_id=1, source_target_pairs={{0,1},{1,0},{2,3},{3,2},{4,5},{5,4},{6,7},{7,6},{8,9},{9,8},{10,11... | collective-permute-start | bytes 98312 | tf_op jit(solution)/shard_map/ppermute | solution.py:365
  93.2 5.9 %collective-permute-start.24 = (f32[4,80,128]{2,1,0:T(8,128)S(1)}, f32[4,80,128]{2,1,0:T(8,128)S(1)}, u32[]{:S(2)}, u32[]{:S(2)}) collective-permute-start(f32[4,80,128]{2,1,0:T(8,128)S(1)} %get-tuple-element.25), channel_id=1, source_target_pairs={{0,4},{4,0},{8,12},{12,8},{16,20},{20,16},{24,28},{28,24},{1,5},{5... | collective-permute-start | bytes 491528 | tf_op jit(solution)/shard_map/ppermute | solution.py:365
  99.1 6.8 %collective-permute-start.25 = (f32[2,80,128]{2,1,0:T(8,128)S(1)}, f32[2,80,128]{2,1,0:T(8,128)S(1)}, u32[]{:S(2)}, u32[]{:S(2)}) collective-permute-start(f32[2,80,128]{2,1,0:T(8,128)S(1)} %get-tuple-element.27), channel_id=1, source_target_pairs={{0,8},{4,12},{8,0},{12,4},{16,24},{20,28},{24,16},{28,20},{1,9},{5... | collective-permute-start | bytes 245768 | tf_op jit(solution)/shard_map/ppermute | solution.py:365
  105.9 9.8 %collective-permute-start.26 = (f32[80,128]{1,0:T(8,128)S(1)}, f32[80,128]{1,0:T(8,128)S(1)}, u32[]{:S(2)}, u32[]{:S(2)}) collective-permute-start(f32[80,128]{1,0:T(8,128)S(1)} %get-tuple-element.29), channel_id=1, source_target_pairs={{0,0},{1,8},{2,16},{3,24},{4,1},{5,9},{6,17},{7,25},{8,2},{9,10},{... | collective-permute-start | bytes 122888 | tf_op jit(solution)/shard_map/ppermute | solution.py:475
  111.0 7.1 %collective-permute-start.27 = (f32[80,128]{1,0:T(8,128)S(1)}, f32[80,128]{1,0:T(8,128)S(1)}, u32[]{:S(2)}, u32[]{:S(2)}) collective-permute-start(f32[80,128]{1,0:T(8,128)S(1)} %get-tuple-element.28), channel_id=1, source_target_pairs={{0,4},{1,12},{2,20},{3,28},{4,5},{5,13},{6,21},{7,29},{8,6},{9,14}... | collective-permute-start | bytes 122888 | tf_op jit(solution)/shard_map/ppermute | solution.py:475
  (12 other events, 21.6 us)

commit v3 on v2

--- a/solution.py
+++ b/solution.py
@@ -10,10 +10,13 @@
 P2 = 32
 BAND = 32
 CHUNKS = 2
+COST_CUT = 1
 F32 = jnp.float32
 BF16 = jnp.bfloat16
 HI = lax.Precision.HIGHEST
-VMEM_LIMIT = 48 * 1024 * 1024
+UNREAD = pl.BlockSpec(memory_space=pl.ANY)
+HELD = pl.BlockSpec(memory_space=pltpu.VMEM)
+VMEM_LIMIT = 56 * 1024 * 1024
 
 
 def iota(shape, dim):
@@ -29,32 +32,48 @@
 
 
 def cost(flops, moved):
-    return pl.CostEstimate(flops=int(flops), bytes_accessed=int(moved), transcendentals=0)
-
-
-def sketch_kernel(ids_ref, x_ref, w_ref, o_ref):
-    o_ref[...] = dot(w_ref[...], x_ref[...], ((1,), (1,)))
-
-
-def sketch(ids, x, w_t, rows):
-    rank, depth = w_t.shape
-    steps = ids.shape[0]
-    return pl.pallas_call(
-        sketch_kernel,
+    return pl.CostEstimate(flops=int(flops) // COST_CUT, bytes_accessed=int(moved) // COST_CUT, transcendentals=0)
+
+
+def sketch_kernel(count, ids_ref, x_ref, *refs):
+    w_refs, x_refs = refs[:count], (x_ref,) + refs[count:2 * count - 1]
+    both_ref, high_ref = refs[-2:]
+    rank = high_ref.shape[0]
+    s = None
+    for w_ref, ref in zip(w_refs, x_refs):
+        term = dot(w_ref[...], ref[...], ((1,), (1,)))
+        s = term if s is None else s + term
+    high = s.astype(BF16)
+    high_ref[...] = high
+    both_ref[:rank, :] = high
+    both_ref[rank:, :] = (s - high.astype(F32)).astype(BF16)
+
+
+def sketch(ids, x, ws, extra, rows, after=()):
+    rank, depth = ws[0].shape
+    count = len(ws)
+    return pl.pallas_call(
+        functools.partial(sketch_kernel, count),
         grid_spec=pltpu.PrefetchScalarGridSpec(
             num_scalar_prefetch=1,
-            grid=(steps,),
-            in_specs=[
-                pl.BlockSpec((rows, depth), lambda i, ids: (ids[i], 0)),
-                pl.BlockSpec((rank, depth), lambda i, ids: (0, 0)),
+            grid=(1,),
+            in_specs=[pl.BlockSpec((rows, depth), lambda i, ids: (ids[i], 0))]
+            + [pl.BlockSpec((rank, depth), lambda i, ids: (0, 0))] * count
+            + [pl.BlockSpec((rows, depth), lambda i, ids: (0, 0))] * (count - 1)
+            + [UNREAD] * len(after),
+            out_specs=[
+                pl.BlockSpec((2 * rank, rows), lambda i, ids: (0, 0)),
+                pl.BlockSpec((rank, rows), lambda i, ids: (0, 0)),
             ],
-            out_specs=pl.BlockSpec((rank, rows), lambda i, ids: (0, i)),
         ),
-        out_shape=jax.ShapeDtypeStruct((rank, steps * rows), F32),
-        compiler_params=params(),
-        cost_estimate=cost(2 * rank * depth * rows * steps, steps * rows * (depth * 2 + rank * 4)),
+        out_shape=(
+            jax.ShapeDtypeStruct((2 * rank, rows), BF16),
+            jax.ShapeDtypeStruct((rank, rows), BF16),
+        ),
+        compiler_params=params(),
+        cost_estimate=cost(2 * rank * depth * rows * count, rows * (depth * 2 * count + rank * 6)),
         name="sketch",
-    )(ids, x, w_t)
+    )(ids, x, *ws, *extra, *after)
 
 
 def packing(rank):
@@ -77,29 +96,6 @@
     return jnp.concatenate(out, axis=0)
 
 
-def split_kernel(a_ref, b_ref, both_ref, high_ref):
-    rank = a_ref.shape[0]
-    s = a_ref[...] + b_ref[...]
-    high = s.astype(BF16)
-    high_ref[...] = high
-    both_ref[:rank, :] = high
-    both_ref[rank:, :] = (s - high.astype(F32)).astype(BF16)
-
-
-def split_sum(a, b):
-    rank, rows = a.shape
-    return pl.pallas_call(
-        split_kernel,
-        out_shape=(
-            jax.ShapeDtypeStruct((2 * rank, rows), BF16),
-            jax.ShapeDtypeStruct((rank, rows), BF16),
-        ),
-        compiler_params=params(),
-        cost_estimate=cost(4 * rank * rows, 14 * rank * rows),
-        name="split",
-    )(a, b)
-
-
 def fold_square(x, rank):
     return (x[:rank, :rank] + x[rank:, rank:]) + (x[:rank, rank:] + x[rank:, :rank])
 
@@ -128,7 +124,7 @@
 
 def cross_kernel(scale, count, *refs):
     own, got, far, near = (refs[k * count:(k + 1) * count] for k in range(4))
-    g_ref, o_ref = refs[4 * count], refs[4 * count + 1]
+    g_ref, o_ref = refs[4 * count], refs[-1]
     rank = g_ref.shape[0]
     total = None
     for own_ref, got_ref, far_ref, near_ref in zip(own, got, far, near):
@@ -139,17 +135,18 @@
     o_ref[...] = pack_gram((g_ref[...] + (total + total.T)) * scale)
 
 
-def cross_gram(own, got, far, near, gram, scale):
+def cross_gram(own, got, far, near, gram, scale, after=()):
     rank = gram.shape[0]
     rows = got[0].shape[1] * len(got)
     groups = packing(rank)[2]
     return pl.pallas_call(
         functools.partial(cross_kernel, scale, len(own)),
+        in_specs=[HELD] * (4 * len(own) + 1) + [UNREAD] * len(after),
         out_shape=jax.ShapeDtypeStruct((groups * BAND, 128), F32),
         compiler_params=params(),
         cost_estimate=cost(6 * rank * rank * rows, 12 * rank * rows),
         name="cross",
-    )(*own, *got, *far, *near, gram)
+    )(*own, *got, *far, *near, gram, *after)
 
 
 def wide_lanes(x, n):
@@ -190,7 +187,8 @@
     return jnp.concatenate(part, axis=0)
 
 
-def factor_kernel(rank, g_ref, o_ref):
+def factor_kernel(rank, g_ref, *refs):
+    o_ref = refs[-1]
     pairs, wide, _ = packing(rank)
     o_ref[...] = jnp.zeros((rank, rank), F32)
     for at, (i, j) in enumerate(pairs):
@@ -210,53 +208,57 @@
             o_ref[hi:, :] = kept - update[hi:, :]
 
 
-def factor_inverse(packed, rank):
+def factor_inverse(packed, rank, after=()):
     return pl.pallas_call(
         functools.partial(factor_kernel, rank),
+        in_specs=[HELD] + [UNREAD] * len(after),
         out_shape=jax.ShapeDtypeStruct((rank, rank), F32),
         compiler_params=params(),
         cost_estimate=cost(8e9, 4 * rank * rank),
         name="factor",
-    )(packed)
-
-
-def project_kernel(count, has_base, finish, ids_ref, *refs):
-    s_refs, x_refs = refs[:count], refs[count:2 * count]
-    rest = refs[2 * count + has_base:]
+    )(packed, *after)
+
+
+def project_kernel(count, wide, has_base, unread, finish, ids_ref, *refs):
+    s_refs, x_refs = refs[:count], refs[count:count * (1 + wide)]
+    at = count * (1 + wide)
+    rest = refs[at + has_base + unread:]
     t_ref = rest[-1]
-    rank = t_ref.shape[0]
+    rank = t_ref.shape[1]
 
     @pl.when(pl.program_id(0) == 0)
     def _():
-        t_ref[...] = refs[2 * count][...] if has_base else jnp.zeros_like(t_ref)
-
-    total = None
-    for s_ref, x_ref in zip(s_refs, x_refs):
-        term = dot(s_ref[...], x_ref[...], ((1,), (0,)))
-        total = term if total is None else total + term
-    t_ref[...] += total if total.shape[0] == rank else total[:rank] + total[rank:]
+        t_ref[...] = refs[at][...] if has_base else jnp.zeros_like(t_ref)
+
+    for w in range(wide):
+        total = None
+        for k in range(count):
+            term = dot(s_refs[k][...], x_refs[w * count + k][...], ((1,), (0,)))
+            total = term if total is None else total + term
+        t_ref[w] += total if total.shape[0] == rank else total[:rank] + total[rank:]
     if finish is not None:
         @pl.when(pl.program_id(0) == pl.num_programs(0) - 1)
         def _():
-            finish(t_ref[...], ids_ref[count], *rest[:-1])
-
-
-def project(ids, parts, x, rank, base, rows, finish=None, outs=(), scratch=()):
+            finish(t_ref, ids_ref[count], *rest[:-1])
+
+
+def project(ids, parts, x, extra, rank, base, rows, after=(), finish=None, outs=(), scratch=()):
     count = len(parts)
+    wide = 1 + len(extra)
     height, span = parts[0].shape
     depth = x.shape[1]
     steps = span // rows
     bases = [] if base is None else [base]
-    whole = pl.BlockSpec((rank, depth), lambda i, ids: (0, 0))
-    t_shape = jax.ShapeDtypeStruct((rank, depth), F32)
+    whole = pl.BlockSpec((wide, rank, depth), lambda i, ids: (0, 0, 0))
+    t_shape = jax.ShapeDtypeStruct((wide, rank, depth), F32)
     if finish is None:
         out_specs, out_shape, scratch_shapes = whole, t_shape, []
     else:
         out_specs = [pl.BlockSpec(o.shape, lambda i, ids: (0, 0, 0)) for o in outs]
         out_shape = list(outs)
-        scratch_shapes = list(scratch) + [pltpu.VMEM((rank, depth), F32)]
-    return pl.pallas_call(
-        functools.partial(project_kernel, count, len(bases), finish),
+        scratch_shapes = list(scratch) + [pltpu.VMEM((wide, rank, depth), F32)]
+    return pl.pallas_call(
+        functools.partial(project_kernel, count, wide, len(bases), len(after), finish),
         grid_spec=pltpu.PrefetchScalarGridSpec(
             num_scalar_prefetch=1,
             grid=(steps,),
@@ -265,15 +267,17 @@
                 pl.BlockSpec((rows, depth), lambda i, ids, k=k: (ids[k] * steps + i, 0))
                 for k in range(count)
             ]
-            + [whole] * len(bases),
+            + [pl.BlockSpec((rows, depth), lambda i, ids: (i, 0))] * (count * (wide - 1))
+            + [whole] * len(bases) + [UNREAD] * len(after),
             out_specs=out_specs,
             scratch_shapes=scratch_shapes,
         ),
         out_shape=out_shape,
         compiler_params=params(),
-        cost_estimate=cost(2 * height * depth * span * count, span * count * (depth + height) * 2),
+        cost_estimate=cost(
+            2 * height * depth * span * count * wide, span * count * (depth * wide + height) * 2),
         name="project",
-    )(ids, *parts, *([x] * count), *bases)
+    )(ids, *parts, *([x] * count), *[v for values in extra for v in values], *bases, *after)
 
 
 def folding(rank, width):
@@ -288,8 +292,9 @@
     return sum(1 << (count - 1 - b) for b in range(count) if (p >> b) & 1)
 
 
-def regroup_tail(pieces, samp, per_node, width_cols, t, me, keep_ref, send_ref, hold):
-    rank, depth = t.shape
+def regroup_tail(pieces, samp, per_node, width_cols, t_ref, me, *refs):
+    outs, hold = refs[:-1], refs[-1]
+    wide, rank, depth = t_ref.shape
     width = per_node * width_cols
     fold = folding(rank, width)
     tall = rank // fold
@@ -299,18 +304,19 @@
     s, rest = rest // width, rest % width
     want = (a * per_node + rest // width_cols) * (samp * width_cols) + s * width_cols + rest % width_cols
     move = jnp.where(src == want, 1.0, 0.0).astype(BF16)
-    high = t.astype(BF16)
-    mid = (t - high.astype(F32)).astype(BF16)
-    low = (t - high.astype(F32) - mid.astype(F32)).astype(BF16)
-    moved = dot(jnp.concatenate([high, mid, low], axis=0), move, ((1,), (0,)))
-    moved = moved[:rank] + moved[rank:2 * rank] + moved[2 * rank:]
-    for i in range(pieces):
-        piece = moved[:, i * width:(i + 1) * width]
-        hold[i] = jnp.concatenate([piece[f * tall:(f + 1) * tall] for f in range(fold)], axis=1)
     bits = pieces.bit_length() - 1
-    for p in range(pieces):
-        out = send_ref if p >= pieces // 2 else keep_ref
-        out[p % (pieces // 2)] = hold[me ^ reverse_bits(p, bits)]
+    for w in range(wide):
+        t = t_ref[w]
+        high = t.astype(BF16)
+        mid = (t - high.astype(F32)).astype(BF16)
+        low = (t - high.astype(F32) - mid.astype(F32)).astype(BF16)
+        moved = dot(jnp.concatenate([high, mid, low], axis=0), move, ((1,), (0,)))
+        moved = moved[:rank] + moved[rank:2 * rank] + moved[2 * rank:]
+        for i in range(pieces):
+            piece = moved[:, i * width:(i + 1) * width]
+            hold[i] = jnp.concatenate([piece[f * tall:(f + 1) * tall] for f in range(fold)], axis=1)
+        for p in range(pieces):
+            outs[w][p] = hold[me ^ reverse_bits(p, bits)]
 
 
 def core_kernel(count, inv_ref, *refs):
@@ -380,53 +386,33 @@
     w_t = sketch_matrix.T
     last = samp // 2
 
-    def chip_sum(base, c):
-        ds = [base ^ d for d in range(last)]
-        held = {}
-        for d in sorted(ds, reverse=True):
-            ids = ((me_s ^ d) * chunks + c)[None]
-            held[d] = sketch(ids, snapshots, w_t, span)
-        bit = 1
-        while bit < last:
-            for d in [d for d in held if d & bit]:
-                got = swap(held.pop(d), "samp", samp, bit)
-                if bit * 2 < last:
-                    held[d ^ bit] = held[d ^ bit] + got
-                else:
-                    return split_sum(held[d ^ bit], got)
-            bit *= 2
-
-    far, far_high, own, own_high = [], [], [], []
-    got_high, near_high = [], []
-    for c in every:
-        both, high = chip_sum(last, c)
-        far.append(both)
-        got_high.append(swap(high, "samp", samp, last))
-    for c in every:
-        both, high = chip_sum(0, c)
-        own.append(both)
-        near_high.append(swap(high, "samp", samp, last))
-    got_low = []
-    for c in every:
-        low, _ = lax.optimization_barrier((far[c][rank:], got_high[c]))
-        got_low.append(swap(low, "samp", samp, last))
-    gram = local_gram(own + far)
-
-    def spread_over(table):
-        bit = last // 2
-        while bit:
-            table.update({d ^ bit: [swap(v, "samp", samp, bit) for v in table[d]] for d in list(table)})
-            bit //= 2
-        return table
-
-    def ids_of(ds):
-        return [(me_s ^ d) * chunks + c for d in ds for c in every]
-
-    rows = min(span, 256)
-    pairs = spread_over({0: own, last: far})
-    t = project(jnp.stack(ids_of(pairs)), [v for d in pairs for v in pairs[d]], snapshots, rank, None, rows)
-
-    packed = cross_gram(own, got_high, far, near_high, gram, 1.0 / total)
+    def quarter_of(d, c):
+        return (me_s ^ d) * chunks + c
+
+    def take(d, c):
+        return lax.dynamic_slice_in_dim(snapshots, quarter_of(d, c) * span, span, 0)
+
+    near = range(1, last)
+    ws = [w_t] + [swap(w_t, "samp", samp, d) for d in near]
+    blocks = [(base, c) for base in (last, 0) for c in every]
+    borrowed = {
+        (base, c): [swap(take(base ^ d, c), "samp", samp, d) for d in near] for base, c in blocks
+    }
+    pairs, arrived, done = {}, {}, ()
+    for base, c in blocks:
+        both, high = sketch(quarter_of(base, c)[None], snapshots, ws, borrowed[base, c], span, done)
+        done = (high,)
+        pairs[base, c] = both
+        arrived[base ^ last, c] = swap(high, "samp", samp, last)
+    gram = local_gram([pairs[b] for b in blocks])
+    ids = jnp.stack([quarter_of(*b) for b in blocks] + [me_n])
+    extra = [[borrowed[b][d - 1] for b in blocks] for d in near]
+    rows = min(span, 512)
+    t = project(ids, [pairs[b] for b in blocks], snapshots, extra, rank, None, rows)
+
+    own, far = ([pairs[b, c] for c in every] for b in (0, last))
+    got_high, near_high = ([arrived[b, c] for c in every] for b in (0, last))
+    packed = cross_gram(own, got_high, far, near_high, gram, 1.0 / total, after=(t,))
     upper = (me_s & 1) == 1
     halves = jnp.split(packed, 2, axis=0)
     mine = jnp.where(upper, halves[1], halves[0])
@@ -435,44 +421,50 @@
     while bit < samp:
         mine = mine + swap(mine, "samp", samp, bit)
         bit *= 2
+    begun = mine
     bit = 1
     while bit < node:
         mine = mine + swap(mine, "node", node, bit)
         bit *= 2
     other = swap(mine, "samp", samp, 1)
     packed = jnp.concatenate([jnp.where(upper, other, mine), jnp.where(upper, mine, other)], axis=0)
-    inverse = factor_inverse(packed, rank)
-
-    highs = spread_over({0: got_high, last: near_high})
-    first = [0, last]
-    t = project(jnp.stack(ids_of(first)), [v for d in first for v in highs[d]], snapshots, rank, t, rows)
-    then = [d for d in highs if d not in first]
+
+    got_low = []
+    for c in every:
+        low, _ = lax.optimization_barrier((far[c][rank:], begun))
+        got_low.append(swap(low, "samp", samp, last))
+
     per_node = P1 // node
     width_cols = P2 // samp
     width = per_node * width_cols
     fold = folding(rank, width)
     piece = (rank // fold, fold * width)
-    keep, send = project(
-        jnp.stack(ids_of(then) + [me_n]), [v for d in then for v in highs[d]], snapshots, rank, t, rows,
+    stacks = project(
+        ids, [arrived[b] for b in blocks], snapshots, extra, rank, t, rows, (),
         functools.partial(regroup_tail, node, samp, per_node, width_cols),
-        [jax.ShapeDtypeStruct((node // 2,) + piece, F32)] * 2,
+        [jax.ShapeDtypeStruct((node,) + piece, F32)] * last,
         [pltpu.VMEM((node,) + piece, F32)])
-
+    inverse = factor_inverse(packed, rank, after=(stacks[0],))
+
+    held = stacks[0]
+    for d in near:
+        held = held + swap(stacks[d], "samp", samp, d)
     bit = 1
-    while keep.shape[0] > 1:
-        got = swap(send, "node", node, bit)
-        half = keep.shape[0] // 2
-        keep, send = keep[:half] + got[:half], keep[half:] + got[half:]
+    while True:
+        half = held.shape[0] // 2
+        if half == 1:
+            break
+        held = held[:half] + swap(held[half:], "node", node, bit)
         bit *= 2
     spread = node // samp
     landed = []
-    for k, value in ((0, keep), (bit, send)):
+    for k, value in ((0, held[0]), (bit, held[1])):
         route = []
         for n in range(node):
             a, s_to = (n ^ k) // samp, (n ^ k) % samp
             for s_from in range(samp):
                 route.append((n * samp + s_from, (s_from * spread + a) * samp + s_to))
-        landed.append(lax.ppermute(value[0], ("node", "samp"), route))
+        landed.append(lax.ppermute(value, ("node", "samp"), route))
     core = core_product(inverse, own, got_high, got_low)
     coef = coefficients(inverse, landed, 1.0 / total, per_node, width_cols)
     return (core.T, coef.T)

time: 120 us -> 109 us (0.908)
  waiting for transfers between devices: 25.2 us -> 15.3 us
  starting transfers between devices: 34.8 us -> 27.5 us
  local copies, waits for them, and re-layouts: 6.93 us -> 12.9 us
  other arithmetic: 0.16 us -> 2.49 us
  Pallas kernels: 51.2 us -> 49.3 us
    ppermute x26 -> x20, waiting for transfers between devices: 22.8 us -> 15.3 us  [swap(): return lax.ppermute(value, axis, [(i, i ^ bit) for i in range(size)])]
    ppermute x26 -> x20, starting transfers between devices: 27.4 us -> 20.2 us  [swap(): return lax.ppermute(value, axis, [(i, i ^ bit) for i in range(size)])]
    pallas_call x17 -> x8, Pallas kernels: 46.1 us -> 39.2 us  [the longest x2 14.6 us: project(): pl.pallas_call(functools.partial(project_kernel, count, wide, len(bases),...]
    dynamic_slice x0 -> x1, local copies, waits for them, and re-layouts: none -> 4.3 us  [take(): return lax.dynamic_slice_in_dim(snapshots, quarter_of(d, c) * span, span, 0)]
    ppermute x2, waiting for transfers between devices: 2.4 us -> 0.01 us  [body(): landed.append(lax.ppermute(value, ('node', 'samp'), route))]
    pallas_call x1, Pallas kernels: 1.68 us -> 4.04 us  [local_gram(): pl.pallas_call(gram_kernel, out_shape=jax.ShapeDtypeStruct((rank, rank),...]
    pallas_call x1, Pallas kernels: 2.37 us -> 4.06 us  [core_product(): pl.pallas_call(functools.partial(core_kernel, count), out_shape=jax.Shape...]
    unnamed x16 -> x32, local copies, waits for them, and re-layouts: 6.72 us -> 7.97 us
  transfers between devices with their start and end apart: 28 -> 22, of which waited for: 10 -> 7; matrix products, arithmetic and copies ran while one was open for 0% -> 2% of each run, Pallas kernels for 41% -> 40%
where the time goes in v3:
time: 109 us; the launch traced here: 108 us
  Pallas kernels  49.3 us (45%)
  starting transfers between devices  27.5 us (25%)
  waiting for transfers between devices  15.3 us (14%)
  local copies, waits for them, and re-layouts  12.9 us (12%)
  other arithmetic  2.49 us (2%)
    ppermute x20, starting transfers between devices, swap(): return lax.ppermute(value, axis, [(i, i ^ bit) for i in range(size)])  20.2 us
    ppermute x20, waiting for transfers between devices, swap(): return lax.ppermute(value, axis, [(i, i ^ bit) for i in range(size)])  15.3 us
    pallas_call x2, Pallas kernels, project(): pl.pallas_call(functools.partial(project_kernel, count, wide, len(bases),...  14.6 us
    pallas_call x4, Pallas kernels, sketch(): pl.pallas_call(functools.partial(sketch_kernel, count), grid_spec=pltpu.P...  13.9 us
    unnamed x32, local copies, waits for them, and re-layouts  7.97 us
    ppermute x2, starting transfers between devices, body(): landed.append(lax.ppermute(value, ('node', 'samp'), route))  7.37 us
    pallas_call x1, Pallas kernels, factor_inverse(): pl.pallas_call(functools.partial(factor_kernel, rank), in_specs=[HELD] +...  7.02 us
    dynamic_slice x1, local copies, waits for them, and re-layouts, take(): return lax.dynamic_slice_in_dim(snapshots, quarter_of(d, c) * span, span, 0)  4.3 us
  transfers between devices with their start and end apart: 22, of which 7 were waited for; matrix products, arithmetic and copies ran while one was open for 2% of the time, Pallas kernels for 40%

profile of v3, /device:TPU:3, one launch (start us, length us, event | category | flops | bytes accessed | tf_op | source)
XLA Modules:
  0.0 108.4 jit_solution(15096157473125435254)
XLA Ops:
  0.7 4.3 %constant_dynamic-slice_fusion = (bf16[1024,512]{1,0:T(8,128)(2,1)}, bf16[1024,512]{1,0:T(8,128)(2,1)}, bf16[1024,512]{1,0:T(8,128)(2,1)}, bf16[1024,512]{1,0:T(8,128)(2,1)}) fusion(bf16[8192,512]{1,0:T(8,128)(2,1)} %refs_7_.3, s32[]{:T(128)S(6)} %select_n.36, s32[]{:T(128)S(6)} %select_n.35, s32[]{:T(128)S(6)} %select_n.34, s32[]{:T(128)S(6)} %select_n.33), kind=kLoop, calls=%fused_computation.9 | loop fusion | bytes 8388624 | tf_op jit(solution)/shard_map/dynamic_slice | solution.py:393
  10.3 3.5 %sketch.4 = (bf16[320,1024]{1,0:T(8,128)(2,1)}, bf16[160,1024]{1,0:T(8,128)(2,1)}) custom-call(s32[1]{0:T(128)} %bitcast.3.ids_ref, bf16[8192,512]{1,0:T(8,128)(2,1)} %refs_7_.3, bf16[160,512]{1,0:T(8,128)(2,1)} %bitcast.12, bf16[160,512]{1,0:T(8,128)(2,1)} %copy-done.8, bf16[1024,512]{1,0:T(8,128)(2,1)} %copy-done), custom_call_target="tpu_custom_call" | custom-call | flops 335544320 | bytes 3080192 | tf_op jit(solution)/shard_map/sketch/pallas_call | solution.py:55
  14.7 3.5 %sketch.5 = (bf16[320,1024]{1,0:T(8,128)(2,1)}, bf16[160,1024]{1,0:T(8,128)(2,1)}) custom-call(s32[1]{0:T(128)} %bitcast.2.ids_ref, bf16[8192,512]{1,0:T(8,128)(2,1)} %refs_7_.3, bf16[160,512]{1,0:T(8,128)(2,1)} %bitcast.13, bf16[160,512]{1,0:T(8,128)(2,1)} %copy-done.8, bf16[1024,512]{1,0:T(8,128)(2,1)} %copy-done.1, ...), custom_call_target="tpu_custom_call" | custom-call | flops 335544320 | bytes 3080192 | tf_op jit(solution)/shard_map/sketch/pallas_call | solution.py:55
  18.2 1.5 %collective-permute-start.6 = (bf16[160,1024]{1,0:T(8,128)(2,1)}, bf16[160,1024]{1,0:T(8,128)(2,1)S(1)}, u32[]{:S(2)}, u32[]{:S(2)}) collective-permute-start(bf16[160,1024]{1,0:T(8,128)(2,1)} %get-tuple-element.15.refs_3_), channel_id=1, source_target_pairs={{0,2},{1,3},{2,0},{3,1},{4,6},{5,7},{6,4},{7,5},{8,10},{9,11},{10,... | collective-permute-start | bytes 983048 | tf_op jit(solution)/shard_map/ppermute | solution.py:371
  20.6 3.5 %sketch.6 = (bf16[320,1024]{1,0:T(8,128)(2,1)}, bf16[160,1024]{1,0:T(8,128)(2,1)}) custom-call(s32[1]{0:T(128)} %bitcast.ids_ref, bf16[8192,512]{1,0:T(8,128)(2,1)} %refs_7_.3, bf16[160,512]{1,0:T(8,128)(2,1)} %bitcast.14, bf16[160,512]{1,0:T(8,128)(2,1)} %copy-done.8, bf16[1024,512]{1,0:T(8,128)(2,1)} %copy-done.2, bf16[160,1024]{1,0:T(8,128)(2,1)} %get-tuple-element.15.refs_3_), custom_call_target="tpu_custom_call" | custom-call | flops 335544320 | bytes 3080192 | tf_op jit(solution)/shard_map/sketch/pallas_call | solution.py:55
  24.2 3.5 %sketch.7 = (bf16[320,1024]{1,0:T(8,128)(2,1)}, bf16[160,1024]{1,0:T(8,128)(2,1)}) custom-call(s32[1]{0:T(128)} %bitcast.4.ids_ref, bf16[8192,512]{1,0:T(8,128)(2,1)} %refs_7_.3, bf16[160,512]{1,0:T(8,128)(2,1)} %bitcast.15, bf16[160,512]{1,0:T(8,128)(2,1)} %copy-done.8, bf16[1024,512]{1,0:T(8,128)(2,1)} %collective-permute-done.4.refs_2_.refs_11_, ...), custom_call_target="tpu_custom_call" | custom-call | flops 335544320 | bytes 3080192 | tf_op jit(solution)/shard_map/sketch/pallas_call | solution.py:55
  27.7 1.5 %collective-permute-start.8 = (bf16[160,1024]{1,0:T(8,128)(2,1)}, bf16[160,1024]{1,0:T(8,128)(2,1)S(1)}, u32[]{:S(2)}, u32[]{:S(2)}) collective-permute-start(bf16[160,1024]{1,0:T(8,128)(2,1)} %get-tuple-element.21), channel_id=1, source_target_pairs={{0,2},{1,3},{2,0},{3,1},{4,6},{5,7},{6,4},{7,5},{8,10},{9,11},{10,... | collective-permute-start | bytes 983048 | tf_op jit(solution)/shard_map/ppermute | solution.py:371
  29.1 4.0 %gram.1.refs_8_ = f32[160,160]{1,0:T(8,128)} custom-call(bf16[320,1024]{1,0:T(8,128)(2,1)} %get-tuple-element.19.refs_0_.refs_4_, bf16[320,1024]{1,0:T(8,128)(2,1)} %get-tuple-element.20.refs_1_.refs_5_, bf16[320,1024]{1,0:T(8,128)(2,1)} %get-tuple-element.16.refs_2_.refs_0_, bf16[320,1024]{1,0:T(8,128)(2,1)} %get-tuple-element.18.refs_3_.refs_1_), custom_call_target="tpu_custom_call" | custom-call | flops 838860800 | bytes 2621440 | tf_op jit(solution)/shard_map/gram/pallas_call | solution.py:116
  33.2 7.2 %project.2.refs_9_.refs_12_ = f32[2,160,512]{2,1,0:T(8,128)} custom-call(s32[5]{0:T(128)} %stack.5.ids_ref, bf16[320,1024]{1,0:T(8,128)(2,1)} %get-tuple-element.19.refs_0_.refs_4_, bf16[320,1024]{1,0:T(8,128)(2,1)} %get-tuple-element.20.refs_1_.refs_5_, bf16[320,1024]{1,0:T(8,128)(2,1)} %get-tuple-element.16.refs_2_.refs_0_, ...), custom_call_target="tpu_custom_call" | custom-call | flops 2684354560 | bytes 11010048 | tf_op jit(solution)/shard_map/project/pallas_call | solution.py:260
  40.4 3.6 %collective-permute-done.8.refs_7_.refs_1_ = bf16[160,1024]{1,0:T(8,128)(2,1)S(1)} collective-permute-done((bf16[160,1024]{1,0:T(8,128)(2,1)}, bf16[160,1024]{1,0:T(8,128)(2,1)S(1)}, u32[]{:S(2)}, u32[]{:S(2)}) %collective-permute-start.8) | collective-permute-done | bytes 327712 | tf_op jit(solution)/shard_map/ppermute | solution.py:371
  45.7 3.6 %cross.1 = f32[128,128]{1,0:T(8,128)} custom-call(bf16[320,1024]{1,0:T(8,128)(2,1)} %get-tuple-element.16.refs_2_.refs_0_, bf16[320,1024]{1,0:T(8,128)(2,1)} %get-tuple-element.18.refs_3_.refs_1_, bf16[160,1024]{1,0:T(8,128)(2,1)} %copy-done.5, bf16[160,1024]{1,0:T(8,128)(2,1)} %copy-done.6, bf16[320,1024]{1,0:T(8,128)(2,1)} %get-tuple-element.19.refs_0_.refs_4_, ...), custom_call_target="tpu_custom_call" | custom-call | flops 314572800 | bytes 3932160 | tf_op jit(solution)/shard_map/cross/pallas_call | solution.py:142
  51.3 7.4 %project.3 = (f32[8,80,128]{2,1,0:T(8,128)}, f32[8,80,128]{2,1,0:T(8,128)}) custom-call(s32[5]{0:T(128)} %stack.5.ids_ref, bf16[160,1024]{1,0:T(8,128)(2,1)} %copy-done.9, bf16[160,1024]{1,0:T(8,128)(2,1)} %copy-done.10, bf16[160,1024]{1,0:T(8,128)(2,1)} %copy-done.5, bf16[160,1024]{1,0:T(8,128)(2,1)} %copy-done.6, bf16[8192,512]{1,0:T(8,128)(2,1)} %refs_7_.3, ...), custom_call_target="tpu_custom_call" | custom-call | flops 1342177280 | bytes 9699328 | tf_op jit(solution)/shard_map/project/pallas_call | solution.py:260
  59.0 2.8 %collective-permute-done.10 = f32[64,128]{1,0:T(8,128)S(1)} collective-permute-done((f32[64,128]{1,0:T(8,128)S(1)}, f32[64,128]{1,0:T(8,128)S(1)}, u32[]{:S(2)}, u32[]{:S(2)}) %collective-permute-start.10) | collective-permute-done | bytes 32800 | tf_op jit(solution)/shard_map/ppermute | solution.py:371
  63.0 1.5 %collective-permute-done.11 = f32[64,128]{1,0:T(8,128)S(1)} collective-permute-done((f32[64,128]{1,0:T(8,128)S(1)}, f32[64,128]{1,0:T(8,128)S(1)}, u32[]{:S(2)}, u32[]{:S(2)}) %collective-permute-start.11) | collective-permute-done | bytes 32800 | tf_op jit(solution)/shard_map/ppermute | solution.py:371
  65.9 1.5 %collective-permute-done.12 = f32[64,128]{1,0:T(8,128)S(1)} collective-permute-done((f32[64,128]{1,0:T(8,128)S(1)}, f32[64,128]{1,0:T(8,128)S(1)}, u32[]{:S(2)}, u32[]{:S(2)}) %collective-permute-start.12) | collective-permute-done | bytes 32800 | tf_op jit(solution)/shard_map/ppermute | solution.py:371
  67.3 2.3 %collective-permute-start.13 = (f32[64,128]{1,0:T(8,128)S(1)}, f32[64,128]{1,0:T(8,128)S(1)}, u32[]{:S(2)}, u32[]{:S(2)}) collective-permute-start(f32[64,128]{1,0:T(8,128)S(1)} %add.61), channel_id=1, source_target_pairs={{0,16},{4,20},{8,24},{12,28},{16,0},{20,4},{24,8},{28,12},{1,17},{... | collective-permute-start | bytes 98312 | tf_op jit(solution)/shard_map/ppermute | solution.py:371
  71.0 4.9 %collective-permute-start.14 = (f32[64,128]{1,0:T(8,128)S(1)}, f32[64,128]{1,0:T(8,128)S(1)}, u32[]{:S(2)}, u32[]{:S(2)}) collective-permute-start(f32[64,128]{1,0:T(8,128)S(1)} %add.62), channel_id=1, source_target_pairs={{0,1},{1,0},{2,3},{3,2},{4,5},{5,4},{6,7},{7,6},{8,9},{9,8},{10,11... | collective-permute-start | bytes 98312 | tf_op jit(solution)/shard_map/ppermute | solution.py:371
  76.1 1.5 %collective-permute-start.15 = (bf16[160,1024]{1,0:T(8,128)(2,1)S(1)}, bf16[160,1024]{1,0:T(8,128)(2,1)S(1)}, u32[]{:S(2)}, u32[]{:S(2)}) collective-permute-start(bf16[160,1024]{1,0:T(8,128)(2,1)S(1)} %slice.24), channel_id=1, source_target_pairs={{0,2},{1,3},{2,0},{3,1},{4,6},{5,7},{6,4},{7,5},{8,10},{9,11},{10,... | collective-permute-start | bytes 983048 | tf_op jit(solution)/shard_map/ppermute | solution.py:371
  80.6 3.3 %collective-permute-done.18 = f32[4,80,128]{2,1,0:T(8,128)S(1)} collective-permute-done((f32[4,80,128]{2,1,0:T(8,128)S(1)}, f32[4,80,128]{2,1,0:T(8,128)S(1)}, u32[]{:S(2)}, u32[]{:S(2)}) %collective-permute-start.18) | collective-permute-done | bytes 163872 | tf_op jit(solution)/shard_map/ppermute | solution.py:371
  85.2 7.0 %factor.1.inv_ref = f32[160,160]{1,0:T(8,128)} custom-call(f32[128,128]{1,0:T(8,128)} %pad_maximum_fusion.g_ref, f32[8,80,128]{2,1,0:T(8,128)} %get-tuple-element.22.refs_0_), custom_call_target="tpu_custom_call" | custom-call | flops 8000000000 | bytes 102400 | tf_op jit(solution)/shard_map/factor/pallas_call | solution.py:212
  92.3 5.7 %collective-permute-start.20 = (f32[80,128]{1,0:T(8,128)S(1)}, f32[80,128]{1,0:T(8,128)S(1)}, u32[]{:S(2)}, u32[]{:S(2)}) collective-permute-start(f32[80,128]{1,0:T(8,128)S(1)} %get-tuple-element.31), channel_id=1, source_target_pairs={{0,0},{1,8},{2,16},{3,24},{4,1},{5,9},{6,17},{7,25},{8,2},{9,10},{... | collective-permute-start | bytes 122888 | tf_op jit(solution)/shard_map/ppermute | solution.py:467
  98.0 1.7 %collective-permute-start.21 = (f32[80,128]{1,0:T(8,128)S(1)}, f32[80,128]{1,0:T(8,128)S(1)}, u32[]{:S(2)}, u32[]{:S(2)}) collective-permute-start(f32[80,128]{1,0:T(8,128)S(1)} %get-tuple-element.30), channel_id=1, source_target_pairs={{0,4},{1,12},{2,20},{3,28},{4,5},{5,13},{6,21},{7,29},{8,6},{9,14}... | collective-permute-start | bytes 122888 | tf_op jit(solution)/shard_map/ppermute | solution.py:467
  101.1 4.1 %core.1 = f32[160,2048]{1,0:T(8,128)} custom-call(f32[160,160]{1,0:T(8,128)} %factor.1.inv_ref, bf16[320,1024]{1,0:T(8,128)(2,1)} %get-tuple-element.16.refs_2_.refs_0_, bf16[320,1024]{1,0:T(8,128)(2,1)} %get-tuple-element.18.refs_3_.refs_1_, bf16[160,1024]{1,0:T(8,128)(2,1)} %copy-done.5, bf16[160,1024]{1,0:T(8,128)(2,1)} %copy-done.6, ...), custom_call_target="tpu_custom_call" | custom-call | flops 629145600 | bytes 3932160 | tf_op jit(solution)/shard_map/core/pallas_call | solution.py:336
  106.4 2.0 %coefficient.1 = f32[8,1280]{1,0:T(8,128)} custom-call(f32[160,160]{1,0:T(8,128)} %factor.1.inv_ref, f32[80,128]{1,0:T(8,128)} %copy-done.14, f32[80,128]{1,0:T(8,128)} %copy-done.15), custom_call_target="tpu_custom_call" | custom-call | flops 19660800 | bytes 102400 | tf_op jit(solution)/shard_map/coefficient/pallas_call | solution.py:361
  (81 shorter events, 22.4 us)
Async XLA Ops:
  5.0 3.7 %collective-permute-start.3 = (bf16[1024,512]{1,0:T(8,128)(2,1)}, bf16[1024,512]{1,0:T(8,128)(2,1)S(1)}, u32[]{:S(2)}, u32[]{:S(2)}) collective-permute-start(bf16[1024,512]{1,0:T(8,128)(2,1)} %get-tuple-element.27), channel_id=1, source_target_pairs={{0,1},{1,0},{2,3},{3,2},{4,5},{5,4},{6,7},{7,6},{8,9},{9,8},{10,11... | collective-permute-start | bytes 3145736 | tf_op jit(solution)/shard_map/ppermute | solution.py:371
  5.6 8.1 %collective-permute-start.2 = (bf16[1024,512]{1,0:T(8,128)(2,1)}, bf16[1024,512]{1,0:T(8,128)(2,1)S(1)}, u32[]{:S(2)}, u32[]{:S(2)}) collective-permute-start(bf16[1024,512]{1,0:T(8,128)(2,1)} %get-tuple-element.28), channel_id=1, source_target_pairs={{0,1},{1,0},{2,3},{3,2},{4,5},{5,4},{6,7},{7,6},{8,9},{9,8},{10,11... | collective-permute-start | bytes 3145736 | tf_op jit(solution)/shard_map/ppermute | solution.py:371
  5.6 14.0 %collective-permute-start.1 = (bf16[1024,512]{1,0:T(8,128)(2,1)}, bf16[1024,512]{1,0:T(8,128)(2,1)S(1)}, u32[]{:S(2)}, u32[]{:S(2)}) collective-permute-start(bf16[1024,512]{1,0:T(8,128)(2,1)} %get-tuple-element.29), channel_id=1, source_target_pairs={{0,1},{1,0},{2,3},{3,2},{4,5},{5,4},{6,7},{7,6},{8,9},{9,8},{10,11... | collective-permute-start | bytes 3145736 | tf_op jit(solution)/shard_map/ppermute | solution.py:371
  6.2 18.0 %collective-permute-start.4 = (bf16[1024,512]{1,0:T(8,128)(2,1)}, bf16[1024,512]{1,0:T(8,128)(2,1)}, u32[]{:S(2)}, u32[]{:S(2)}) collective-permute-start(bf16[1024,512]{1,0:T(8,128)(2,1)} %get-tuple-element.26), channel_id=1, source_target_pairs={{0,1},{1,0},{2,3},{3,2},{4,5},{5,4},{6,7},{7,6},{8,9},{9,8},{10,11... | collective-permute-start | bytes 3145736 | tf_op jit(solution)/shard_map/ppermute | solution.py:371
  6.2 2.5 %collective-permute-start = (bf16[160,512]{1,0:T(8,128)(2,1)S(1)}, bf16[160,512]{1,0:T(8,128)(2,1)S(1)}, u32[]{:S(2)}, u32[]{:S(2)}) collective-permute-start(bf16[160,512]{1,0:T(8,128)(2,1)S(1)} %bitcast.16), channel_id=1, source_target_pairs={{0,1},{1,0},{2,3},{3,2},{4,5},{5,4},{6,7},{7,6},{8,9},{9,8},{10,11... | collective-permute-start | bytes 491528 | tf_op jit(solution)/shard_map/ppermute | solution.py:371
  13.8 30.2 %collective-permute-start.5 = (bf16[160,1024]{1,0:T(8,128)(2,1)}, bf16[160,1024]{1,0:T(8,128)(2,1)S(1)}, u32[]{:S(2)}, u32[]{:S(2)}) collective-permute-start(bf16[160,1024]{1,0:T(8,128)(2,1)} %get-tuple-element.14.refs_3_), channel_id=1, source_target_pairs={{0,2},{1,3},{2,0},{3,1},{4,6},{5,7},{6,4},{7,5},{8,10},{9,11},{10,... | collective-permute-start | bytes 983048 | tf_op jit(solution)/shard_map/ppermute | solution.py:371
  18.2 25.8 %collective-permute-start.6 = (bf16[160,1024]{1,0:T(8,128)(2,1)}, bf16[160,1024]{1,0:T(8,128)(2,1)S(1)}, u32[]{:S(2)}, u32[]{:S(2)}) collective-permute-start(bf16[160,1024]{1,0:T(8,128)(2,1)} %get-tuple-element.15.refs_3_), channel_id=1, source_target_pairs={{0,2},{1,3},{2,0},{3,1},{4,6},{5,7},{6,4},{7,5},{8,10},{9,11},{10,... | collective-permute-start | bytes 983048 | tf_op jit(solution)/shard_map/ppermute | solution.py:371
  24.1 19.8 %collective-permute-start.7 = (bf16[160,1024]{1,0:T(8,128)(2,1)}, bf16[160,1024]{1,0:T(8,128)(2,1)S(1)}, u32[]{:S(2)}, u32[]{:S(2)}) collective-permute-start(bf16[160,1024]{1,0:T(8,128)(2,1)} %get-tuple-element.17.refs_3_), channel_id=1, source_target_pairs={{0,2},{1,3},{2,0},{3,1},{4,6},{5,7},{6,4},{7,5},{8,10},{9,11},{10,... | collective-permute-start | bytes 983048 | tf_op jit(solution)/shard_map/ppermute | solution.py:371
  27.7 16.3 %collective-permute-start.8 = (bf16[160,1024]{1,0:T(8,128)(2,1)}, bf16[160,1024]{1,0:T(8,128)(2,1)S(1)}, u32[]{:S(2)}, u32[]{:S(2)}) collective-permute-start(bf16[160,1024]{1,0:T(8,128)(2,1)} %get-tuple-element.21), channel_id=1, source_target_pairs={{0,2},{1,3},{2,0},{3,1},{4,6},{5,7},{6,4},{7,5},{8,10},{9,11},{10,... | collective-permute-start | bytes 983048 | tf_op jit(solution)/shard_map/ppermute | solution.py:371
  50.1 25.9 %copy-start.4 = (bf16[320,1024]{1,0:T(8,128)(2,1)S(1)}, bf16[320,1024]{1,0:T(8,128)(2,1)}, u32[]{:S(2)}) copy-start(bf16[320,1024]{1,0:T(8,128)(2,1)} %get-tuple-element.20.refs_1_.refs_5_) | copy-start | bytes 1966084
  50.1 25.9 %copy-start.3 = (bf16[320,1024]{1,0:T(8,128)(2,1)S(1)}, bf16[320,1024]{1,0:T(8,128)(2,1)}, u32[]{:S(2)}) copy-start(bf16[320,1024]{1,0:T(8,128)(2,1)} %get-tuple-element.19.refs_0_.refs_4_) | copy-start | bytes 1966084
  50.1 8.9 %collective-permute-start.9 = (f32[64,128]{1,0:T(8,128)S(1)}, f32[64,128]{1,0:T(8,128)S(1)}, u32[]{:S(2)}, u32[]{:S(2)}) collective-permute-start(f32[64,128]{1,0:T(8,128)S(1)} %slice_select_fusion), channel_id=1, source_target_pairs={{0,1},{1,0},{2,3},{3,2},{4,5},{5,4},{6,7},{7,6},{8,9},{9,8},{10,11... | collective-permute-start | bytes 98312 | tf_op jit(solution)/shard_map/ppermute | solution.py:371
  58.7 18.8 %collective-permute-start.17 = (f32[8,80,128]{2,1,0:T(8,128)}, f32[8,80,128]{2,1,0:T(8,128)S(1)}, u32[]{:S(2)}, u32[]{:S(2)}) collective-permute-start(f32[8,80,128]{2,1,0:T(8,128)} %get-tuple-element.25), channel_id=1, source_target_pairs={{0,1},{1,0},{2,3},{3,2},{4,5},{5,4},{6,7},{7,6},{8,9},{9,8},{10,11... | collective-permute-start | bytes 983048 | tf_op jit(solution)/shard_map/ppermute | solution.py:371
  59.0 2.8 %collective-permute-start.10 = (f32[64,128]{1,0:T(8,128)S(1)}, f32[64,128]{1,0:T(8,128)S(1)}, u32[]{:S(2)}, u32[]{:S(2)}) collective-permute-start(f32[64,128]{1,0:T(8,128)S(1)} %select_add_fusion), channel_id=1, source_target_pairs={{0,2},{1,3},{2,0},{3,1},{4,6},{5,7},{6,4},{7,5},{8,10},{9,11},{10,... | collective-permute-start | bytes 98312 | tf_op jit(solution)/shard_map/ppermute | solution.py:371
  61.8 2.8 %collective-permute-start.11 = (f32[64,128]{1,0:T(8,128)S(1)}, f32[64,128]{1,0:T(8,128)S(1)}, u32[]{:S(2)}, u32[]{:S(2)}) collective-permute-start(f32[64,128]{1,0:T(8,128)S(1)} %add.59), channel_id=1, source_target_pairs={{0,4},{4,0},{8,12},{12,8},{16,20},{20,16},{24,28},{28,24},{1,5},{5... | collective-permute-start | bytes 98312 | tf_op jit(solution)/shard_map/ppermute | solution.py:371
  64.6 2.8 %collective-permute-start.12 = (f32[64,128]{1,0:T(8,128)S(1)}, f32[64,128]{1,0:T(8,128)S(1)}, u32[]{:S(2)}, u32[]{:S(2)}) collective-permute-start(f32[64,128]{1,0:T(8,128)S(1)} %add.60), channel_id=1, source_target_pairs={{0,8},{4,12},{8,0},{12,4},{16,24},{20,28},{24,16},{28,20},{1,9},{5... | collective-permute-start | bytes 98312 | tf_op jit(solution)/shard_map/ppermute | solution.py:371
  67.3 3.7 %collective-permute-start.13 = (f32[64,128]{1,0:T(8,128)S(1)}, f32[64,128]{1,0:T(8,128)S(1)}, u32[]{:S(2)}, u32[]{:S(2)}) collective-permute-start(f32[64,128]{1,0:T(8,128)S(1)} %add.61), channel_id=1, source_target_pairs={{0,16},{4,20},{8,24},{12,28},{16,0},{20,4},{24,8},{28,12},{1,17},{... | collective-permute-start | bytes 98312 | tf_op jit(solution)/shard_map/ppermute | solution.py:371
  71.0 8.9 %collective-permute-start.14 = (f32[64,128]{1,0:T(8,128)S(1)}, f32[64,128]{1,0:T(8,128)S(1)}, u32[]{:S(2)}, u32[]{:S(2)}) collective-permute-start(f32[64,128]{1,0:T(8,128)S(1)} %add.62), channel_id=1, source_target_pairs={{0,1},{1,0},{2,3},{3,2},{4,5},{5,4},{6,7},{7,6},{8,9},{9,8},{10,11... | collective-permute-start | bytes 98312 | tf_op jit(solution)/shard_map/ppermute | solution.py:371
  76.0 23.6 %collective-permute-start.16 = (bf16[160,1024]{1,0:T(8,128)(2,1)S(1)}, bf16[160,1024]{1,0:T(8,128)(2,1)S(1)}, u32[]{:S(2)}, u32[]{:S(2)}) collective-permute-start(bf16[160,1024]{1,0:T(8,128)(2,1)S(1)} %slice.25), channel_id=1, source_target_pairs={{0,2},{1,3},{2,0},{3,1},{4,6},{5,7},{6,4},{7,5},{8,10},{9,11},{10,... | collective-permute-start | bytes 983048 | tf_op jit(solution)/shard_map/ppermute | solution.py:371
  76.1 23.6 %collective-permute-start.15 = (bf16[160,1024]{1,0:T(8,128)(2,1)S(1)}, bf16[160,1024]{1,0:T(8,128)(2,1)S(1)}, u32[]{:S(2)}, u32[]{:S(2)}) collective-permute-start(bf16[160,1024]{1,0:T(8,128)(2,1)S(1)} %slice.24), channel_id=1, source_target_pairs={{0,2},{1,3},{2,0},{3,1},{4,6},{5,7},{6,4},{7,5},{8,10},{9,11},{10,... | collective-permute-start | bytes 983048 | tf_op jit(solution)/shard_map/ppermute | solution.py:371
  78.6 5.2 %collective-permute-start.18 = (f32[4,80,128]{2,1,0:T(8,128)S(1)}, f32[4,80,128]{2,1,0:T(8,128)S(1)}, u32[]{:S(2)}, u32[]{:S(2)}) collective-permute-start(f32[4,80,128]{2,1,0:T(8,128)S(1)} %slice.33), channel_id=1, source_target_pairs={{0,4},{4,0},{8,12},{12,8},{16,20},{20,16},{24,28},{28,24},{1,5},{5... | collective-permute-start | bytes 491528 | tf_op jit(solution)/shard_map/ppermute | solution.py:371
  83.9 8.4 %collective-permute-start.19 = (f32[2,80,128]{2,1,0:T(8,128)S(1)}, f32[2,80,128]{2,1,0:T(8,128)S(1)}, u32[]{:S(2)}, u32[]{:S(2)}) collective-permute-start(f32[2,80,128]{2,1,0:T(8,128)S(1)} %slice.35), channel_id=1, source_target_pairs={{0,8},{4,12},{8,0},{12,4},{16,24},{20,28},{24,16},{28,20},{1,9},{5... | collective-permute-start | bytes 245768 | tf_op jit(solution)/shard_map/ppermute | solution.py:371
  92.3 12.9 %collective-permute-start.20 = (f32[80,128]{1,0:T(8,128)S(1)}, f32[80,128]{1,0:T(8,128)S(1)}, u32[]{:S(2)}, u32[]{:S(2)}) collective-permute-start(f32[80,128]{1,0:T(8,128)S(1)} %get-tuple-element.31), channel_id=1, source_target_pairs={{0,0},{1,8},{2,16},{3,24},{4,1},{5,9},{6,17},{7,25},{8,2},{9,10},{... | collective-permute-start | bytes 122888 | tf_op jit(solution)/shard_map/ppermute | solution.py:467
  98.0 7.2 %collective-permute-start.21 = (f32[80,128]{1,0:T(8,128)S(1)}, f32[80,128]{1,0:T(8,128)S(1)}, u32[]{:S(2)}, u32[]{:S(2)}) collective-permute-start(f32[80,128]{1,0:T(8,128)S(1)} %get-tuple-element.30), channel_id=1, source_target_pairs={{0,4},{1,12},{2,20},{3,28},{4,5},{5,13},{6,21},{7,29},{8,6},{9,14}... | collective-permute-start | bytes 122888 | tf_op jit(solution)/shard_map/ppermute | solution.py:467
  (14 other events, 24.1 us)

commit v4 on v3

v4 whole, which is shorter than its diff:
```python
import functools
import jax
import jax.numpy as jnp
from jax import lax
from jax.experimental import pallas as pl
from jax.experimental.pallas import tpu as pltpu
from jax.sharding import PartitionSpec as P

P1 = 64
P2 = 32
BAND = 32
UNIT = 1024
SKETCH_ROWS = 1024
COST_CUT = 1
F32 = jnp.float32
BF16 = jnp.bfloat16
HI = lax.Precision.HIGHEST
UNREAD = pl.BlockSpec(memory_space=pl.ANY)
HELD = pl.BlockSpec(memory_space=pltpu.VMEM)
VMEM_LIMIT = 48 * 1024 * 1024


def iota(shape, dim):
    return lax.broadcasted_iota(jnp.int32, shape, dim)


def dot(a, b, dims, precision=None):
    return lax.dot_general(a, b, (dims, ((), ())), precision=precision, preferred_element_type=F32)


def params():
    return pltpu.CompilerParams(vmem_limit_bytes=VMEM_LIMIT)


def cost(flops, moved):
    return pl.CostEstimate(flops=int(flops) // COST_CUT, bytes_accessed=int(moved) // COST_CUT, transcendentals=0)


def sketch_kernel(count, ids_ref, x_ref, *refs):
    w_refs, x_refs = refs[:count], (x_ref,) + refs[count:2 * count - 1]
    both_ref, high_ref = refs[-2:]
    rank = high_ref.shape[0]
    s = None
    for w_ref, ref in zip(w_refs, x_refs):
        term = dot(w_ref[...], ref[...], ((1,), (1,)))
        s = term if s is None else s + term
    high = s.astype(BF16)
    high_ref[...] = high
    both_ref[:rank, :] = high
    both_ref[rank:, :] = (s - high.astype(F32)).astype(BF16)


def sketch(ids, x, ws, extra, size, after=()):
    rank, depth = ws[0].shape
    count = len(ws)
    rows = min(size, SKETCH_ROWS)
    return pl.pallas_call(
        functools.partial(sketch_kernel, count),
        grid_spec=pltpu.PrefetchScalarGridSpec(
            num_scalar_prefetch=1,
            grid=(size // rows,),
            in_specs=[pl.BlockSpec((rows, depth), lambda i, ids: (ids[0] + i, 0))]
            + [pl.BlockSpec((rank, depth), lambda i, ids: (0, 0))] * count
            + [pl.BlockSpec((rows, depth), lambda i, ids: (i, 0))] * (count - 1)
            + [UNREAD] * len(after),
            out_specs=[
                pl.BlockSpec((2 * rank, rows), lambda i, ids: (0, i)),
                pl.BlockSpec((rank, rows), lambda i, ids: (0, i)),
            ],
        ),
        out_shape=(
            jax.ShapeDtypeStruct((2 * rank, size), BF16),
            jax.ShapeDtypeStruct((rank, size), BF16),
        ),
        compiler_params=params(),
        cost_estimate=cost(2 * rank * depth * size * count, size * (depth * 2 * count + rank * 6)),
        name="sketch",
    )(ids, x, *ws, *extra, *after)


def packing(rank):
    bands = rank // BAND
    pairs = [(i, j) for i in range(bands) for j in range(i, bands)]
    wide = 128 // BAND
    groups = -(-len(pairs) // wide)
    groups += groups % 2
    return pairs, wide, groups


def pack_gram(gram):
    pairs, wide, groups = packing(gram.shape[0])
    out = []
    for g in range(groups):
        chosen = pairs[g * wide:(g + 1) * wide]
        parts = [gram[i * BAND:(i + 1) * BAND, j * BAND:(j + 1) * BAND] for i, j in chosen]
        parts += [jnp.zeros((BAND, BAND), F32)] * (wide - len(chosen))
        out.append(jnp.concatenate(parts, axis=1))
    return jnp.concatenate(out, axis=0)


def fold_square(x, rank):
    return (x[:rank, :rank] + x[rank:, rank:]) + (x[:rank, rank:] + x[rank:, :rank])


def gram_kernel(*refs):
    o_ref = refs[-1]
    rank = o_ref.shape[0]
    total = None
    for ref in refs[:-1]:
        both = ref[...]
        term = dot(both, both, ((1,), (1,)))
        total = term if total is None else total + term
    o_ref[...] = fold_square(total, rank)


def local_gram(pairs):
    rank = pairs[0].shape[0] // 2
    rows = sum(v.shape[1] for v in pairs)
    return pl.pallas_call(
        gram_kernel,
        out_shape=jax.ShapeDtypeStruct((rank, rank), F32),
        compiler_params=params(),
        cost_estimate=cost(8 * rank * rank * rows, 4 * rank * rows),
        name="gram",
    )(*pairs)


def cross_terms(own, got, far, near):
    rank = (got + near)[0].shape[0]
    total = None
    for own_ref, got_ref in zip(own, got):
        term = dot(own_ref[...], got_ref[...], ((1,), (1,)))
        term = term[:rank] + term[rank:]
        total = term if total is None else total + term
    for far_ref, near_ref in zip(far, near):
        term = dot(near_ref[...], far_ref[rank:, :], ((1,), (1,)))
        total = term if total is None else total + term
    return total + total.T


def cross_kernel(counts, *refs):
    a, b = counts
    groups = refs[:a], refs[a:2 * a], refs[2 * a:2 * a + b], refs[2 * a + b:2 * a + 2 * b]
    refs[-1][...] = refs[2 * a + 2 * b][...] + cross_terms(*groups)


def cross_gram(own, got, far, near, gram, after=()):
    rank = gram.shape[0]
    rows = sum(v.shape[1] for v in got + near)
    counts = (len(own), len(far))
    return pl.pallas_call(
        functools.partial(cross_kernel, counts),
        in_specs=[HELD] * (2 * sum(counts) + 1) + [UNREAD] * len(after),
        out_shape=jax.ShapeDtypeStruct((rank, rank), F32),
        compiler_params=params(),
        cost_estimate=cost(4 * rank * rank * rows, 6 * rank * rows),
        name="cross",
    )(*own, *got, *far, *near, gram, *after)


def wide_lanes(x, n):
    reps = -(-n // 128)
    return jnp.concatenate([x] * reps, axis=1)[:, :n] if reps > 1 else x[:, :n]


def band_rows(block, b):
    n = block.shape[1]
    count = BAND // 8
    part = [block[8 * i:8 * i + 8, :] for i in range(count)]
    sub = iota((8, n), 0)
    lane = iota((8, n), 1)
    for m in range(count):
        c0 = b * BAND + 8 * m
        live = count - m
        col = [
            [jnp.broadcast_to(part[m + i][:, c0 + k:c0 + k + 1], (8, 128)) for i in range(live)]
            for k in range(8)
        ]
        here = (lane >= c0) & (lane < c0 + 8)
        part[m] = jnp.where(here, jnp.where(lane - c0 == sub, 1.0, 0.0), part[m])
        for i in range(1, live):
            part[m + i] = jnp.where(here, 0.0, part[m + i])
        for j in range(8):
            inv_root = lax.rsqrt(jnp.broadcast_to(col[j][0][j:j + 1, :], (8, 128)))
            low = [x * inv_root for x in col[j]]
            for k in range(j + 1, 8):
                t = jnp.broadcast_to(low[0][k:k + 1, :], (8, 128))
                for i in range(live):
                    col[k][i] = col[k][i] - low[i] * t
            row = jnp.broadcast_to(part[m][j:j + 1, :], (8, n)) * wide_lanes(inv_root, n)
            for i in range(live):
                new = part[m + i] - wide_lanes(low[i], n) * row
                if i == 0:
                    new = jnp.where(sub > j, new, jnp.where(sub == j, row, part[m]))
                part[m + i] = new
    return jnp.concatenate(part, axis=0)


def factor_kernel(rank, me_ref, mine_ref, other_ref, *refs):
    o_ref, g_ref = refs[-2:]
    pairs, wide, groups = packing(rank)
    half = groups * BAND // 2
    mine_at = pl.multiple_of((me_ref[0] & 1) * half, half)
    g_ref[pl.ds(mine_at, half), :] = mine_ref[...]
    g_ref[pl.ds(pl.multiple_of(half - mine_at, half), half), :] = other_ref[...]
    o_ref[...] = jnp.zeros((rank, rank), F32)
    for at, (i, j) in enumerate(pairs):
        g, k = at // wide, at % wide
        o_ref[i * BAND:(i + 1) * BAND, j * BAND:(j + 1) * BAND] = g_ref[
            g * BAND:(g + 1) * BAND, k * BAND:(k + 1) * BAND]
    for b in range(rank // BAND):
        lo, hi = b * BAND, (b + 1) * BAND
        r = band_rows(o_ref[lo:hi, :], b)
        rows, cols = iota(r.shape, 0), iota(r.shape, 1)
        r = jnp.where((cols >= lo) & (cols < hi) & (cols - lo > rows), 0.0, r)
        o_ref[lo:hi, :] = jnp.where(cols < hi, r, 0.0)
        if hi < rank:
            left = jnp.where(cols >= hi, r, 0.0)
            update = dot(left, r, ((0,), (0,)), HI)
            kept = jnp.where(iota((rank - hi, rank), 1) // BAND == b, 0.0, o_ref[hi:, :])
            o_ref[hi:, :] = kept - update[hi:, :]


def factor_inverse(me, mine, other, rank, after=()):
    return pl.pallas_call(
        functools.partial(factor_kernel, rank),
        in_specs=[pl.BlockSpec(memory_space=pltpu.SMEM)] + [HELD] * 2 + [UNREAD] * len(after),
        out_shape=jax.ShapeDtypeStruct((rank, rank), F32),
        scratch_shapes=[pltpu.VMEM((2 * mine.shape[0], 128), F32)],
        compiler_params=params(),
        cost_estimate=cost(8e9, 4 * rank * rank),
        name="factor",
    )(me, mine, other, *after)


def project_kernel(count, wide, has_base, aside, finish, ids_ref, *refs):
    s_refs, x_refs = refs[:count], refs[count:count * (1 + wide)]
    at = count * (1 + wide)
    beside = refs[at + has_base:at + has_base + aside]
    rest = refs[at + has_base + aside:]
    t_ref = rest[-1]
    rank = t_ref.shape[1]

    @pl.when(pl.program_id(0) == 0)
    def _():
        t_ref[...] = refs[at][...] if has_base else jnp.zeros_like(t_ref)

    for w in range(wide):
        total = None
        for k in range(count):
            term = dot(s_refs[k][...], x_refs[w * count + k][...], ((1,), (0,)))
            total = term if total is None else total + term
        t_ref[w] += total if total.shape[0] == rank else total[:rank] + total[rank:]
    if finish is not None:
        @pl.when(pl.program_id(0) == pl.num_programs(0) - 1)
        def _():
            finish(t_ref, ids_ref, beside, *rest[:-1])


def project(ids, work, x, rank, base, rows, beside=(), finish=None, outs=(), scratch=(), after=()):
    wide = 1 + len(work[0][2])
    height = work[0][0].shape[0]
    depth = x.shape[1]
    unit = UNIT
    steps = unit // rows
    parts, s_specs, own_specs, more, more_specs = [], [], [], [[] for _ in range(wide - 1)], []
    for array, slot, lent in work:
        for u in range(array.shape[1] // unit):
            parts.append(array)
            s_specs.append(pl.BlockSpec((height, rows), lambda i, ids, u=u: (0, u * steps + i)))
            own_specs.append(pl.BlockSpec(
                (rows, depth), lambda i, ids, u=u, slot=slot: ((ids[slot] + u) * steps + i, 0)))
            more_specs.append(pl.BlockSpec((rows, depth), lambda i, ids, u=u: (u * steps + i, 0)))
            for w in range(wide - 1):
                more[w].append(lent[w])
    count = len(parts)
    bases = [] if base is None else [base]
    whole = pl.BlockSpec((wide, rank, depth), lambda i, ids: (0, 0, 0))
    t_shape = jax.ShapeDtypeStruct((wide, rank, depth), F32)
    if finish is None:
        out_specs, out_shape, scratch_shapes = whole, t_shape, []
    else:
        out_specs = [pl.BlockSpec(o.shape, lambda i, ids: (0, 0)) for o in outs]
        out_shape = list(outs)
        scratch_shapes = list(scratch) + [pltpu.VMEM((wide, rank, depth), F32)]
    return pl.pallas_call(
        functools.partial(
            project_kernel, count, wide, len(bases), len(beside) + len(after), finish),
        grid_spec=pltpu.PrefetchScalarGridSpec(
            num_scalar_prefetch=1,
            grid=(steps,),
            in_specs=s_specs + own_specs + more_specs * (wide - 1) + [whole] * len(bases)
            + [pl.BlockSpec(v.shape, lambda i, ids: (0, 0)) for v in beside] + [UNREAD] * len(after),
            out_specs=out_specs,
            scratch_shapes=scratch_shapes,
        ),
        out_shape=out_shape,
        compiler_params=params(),
        cost_estimate=cost(
            2 * height * depth * unit * count * wide, unit * count * (depth * wide + height) * 2),
        name="project",
    )(ids, *parts, *([x] * count), *[v for values in more for v in values], *bases, *beside, *after)


def folding(rank, width):
    best = 1
    for f in range(1, rank + 1):
        if rank % f == 0 and (rank // f) % 8 == 0 and f * width <= 128:
            best = f
    return best


def reverse_bits(p, count):
    return sum(1 << (count - 1 - b) for b in range(count) if (p >> b) & 1)


def tail(pieces, samp, per_node, width_cols, scale, counts, t_ref, ids_ref, beside, *refs):
    outs, hold, packed_ref = refs[:-2], refs[-2], refs[-1]
    wide, rank, depth = t_ref.shape
    width = per_node * width_cols
    fold = folding(rank, width)
    tall = rank // fold
    me_node, me_samp = ids_ref[ids_ref.shape[0] - 2], ids_ref[ids_ref.shape[0] - 1]
    a, b = counts
    groups = beside[:a], beside[a:2 * a], beside[2 * a:2 * a + b], beside[2 * a + b:2 * a + 2 * b]
    packed_ref[...] = pack_gram((beside[2 * a + 2 * b][...] + cross_terms(*groups)) * scale)
    half = packed_ref.shape[0] // 2
    mine_at = pl.multiple_of((me_samp & 1) * half, half)
    outs[0][pieces * tall:, :] = packed_ref[pl.ds(mine_at, half), :]
    outs[1][pieces * tall:, :] = packed_ref[pl.ds(pl.multiple_of(half - mine_at, half), half), :]
    for out in outs[2:]:
        out[pieces * tall:, :] = jnp.zeros((half, 128), F32)
    dst = iota((depth, depth), 1)
    src = iota((depth, depth), 0)
    a, rest = dst // (samp * width), dst % (samp * width)
    s, rest = rest // width, rest % width
    want = (a * per_node + rest // width_cols) * (samp * width_cols) + s * width_cols + rest % width_cols
    move = jnp.where(src == want, 1.0, 0.0).astype(BF16)
    bits = pieces.bit_length() - 1
    for w in range(wide):
        t = t_ref[w]
        high = t.astype(BF16)
        mid = (t - high.astype(F32)).astype(BF16)
        low = (t - high.astype(F32) - mid.astype(F32)).astype(BF16)
        moved = dot(jnp.concatenate([high, mid, low], axis=0), move, ((1,), (0,)))
        moved = moved[:rank] + moved[rank:2 * rank] + moved[2 * rank:]
        for i in range(pieces):
            piece = moved[:, i * width:(i + 1) * width]
            parts = [piece[f * tall:(f + 1) * tall] for f in range(fold)]
            if fold * width < 128:
                parts.append(jnp.zeros((tall, 128 - fold * width), F32))
            hold[i] = jnp.concatenate(parts, axis=1)
        for p in range(pieces):
            outs[w][p * tall:(p + 1) * tall, :] = hold[me_node ^ reverse_bits(p, bits)]


def finish_kernel(scale, per_node, width_cols, count, inv_ref, piece_ref, *refs):
    both, high, low = (refs[k * count:(k + 1) * count] for k in range(3))
    core_ref, coef_ref = refs[-2:]
    rank = inv_ref.shape[0]
    inverse = inv_ref[...]
    at = 0
    for c in range(count):
        s = both[c][:rank, :].astype(F32) + both[c][rank:, :].astype(F32)
        s = s + (high[c][...].astype(F32) + low[c][...].astype(F32))
        rows = s.shape[1]
        core_ref[:, at:at + rows] = dot(inverse, s, ((1,), (0,)), HI)
        at += rows
    width = per_node * width_cols
    fold = folding(rank, width)
    total = piece_ref[...]
    total = jnp.concatenate([total[:, f * width:(f + 1) * width] for f in range(fold)], axis=0)
    out = dot(total, inverse, ((0,), (1,)), HI) * scale
    coef_ref[...] = jnp.concatenate(
        [out[p * width_cols:(p + 1) * width_cols, :] for p in range(per_node)], axis=1)


def finish(inverse, piece, both, high, low, scale, per_node, width_cols):
    rank = inverse.shape[0]
    count = len(both)
    rows = sum(v.shape[1] for v in high)
    return pl.pallas_call(
        functools.partial(finish_kernel, scale, per_node, width_cols, count),
        out_shape=(
            jax.ShapeDtypeStruct((rank, rows), F32),
            jax.ShapeDtypeStruct((width_cols, per_node * rank), F32),
        ),
        compiler_params=params(),
        cost_estimate=cost(12 * rank * rank * rows, 12 * rank * rows),
        name="finish",
    )(inverse, piece, *both, *high, *low)


def swap(value, axis, size, bit):
    return lax.ppermute(value, axis, [(i, i ^ bit) for i in range(size)])


def body(snapshots, sketch_matrix):
    rows_all = snapshots.shape[0]
    rank = sketch_matrix.shape[1]
    samp = lax.axis_size("samp")
    node = lax.axis_size("node")
    total = rows_all * node
    quarter = rows_all // samp
    me_s = lax.axis_index("samp").astype(jnp.int32)
    me_n = lax.axis_index("node").astype(jnp.int32)
    w_t = sketch_matrix.T
    last = samp // 2
    near = range(1, last)
    starts, sizes = (0, UNIT), (UNIT, quarter - UNIT)
    blocks = [(last, 0), (last, 1), (0, 0), (0, 1)]

    ws = [w_t] + [swap(w_t, "samp", samp, d) for d in near]
    borrowed, made = {}, None
    for base, c in blocks:
        lent = []
        for d in near:
            at = (me_s ^ base ^ d) * quarter + starts[c]
            if made is not None:
                at, _ = lax.optimization_barrier((at, made))
            made = lax.dynamic_slice_in_dim(snapshots, at, sizes[c], 0)
            lent.append(swap(made, "samp", samp, d))
        borrowed[base, c] = lent

    def first_unit(base, c):
        return (me_s ^ base) * (quarter // UNIT) + starts[c] // UNIT

    pairs, arrived, done = {}, {}, ()
    for base, c in blocks:
        both, high = sketch(
            first_unit(base, c)[None], snapshots, ws, borrowed[base, c], sizes[c], done)
        done = (high,)
        pairs[base, c] = both
        arrived[base ^ last, c] = swap(high, "samp", samp, last)
    gram = local_gram([pairs[b] for b in blocks])
    ids = jnp.stack([first_unit(*b) for b in blocks] + [me_n, me_s])
    slot = {b: k for k, b in enumerate(blocks)}
    rows = min(UNIT, 512)
    t = project(ids, [(pairs[b], slot[b], borrowed[b]) for b in blocks], snapshots, rank, None, rows)

    order = [(base ^ last, c) for base, c in blocks]
    early, late = order[:-1], order[-1:]

    def groups(chosen):
        own = [b for b in chosen if b[0] == 0]
        far = [b for b in chosen if b[0] == last]
        return [pairs[b] for b in own], [arrived[b] for b in own], [pairs[b] for b in far], [arrived[b] for b in far]

    gram = cross_gram(*groups(early), gram, after=(t,))
    t = project(
        ids, [(arrived[b], slot[b], borrowed[b]) for b in early], snapshots, rank, t, rows, after=(gram,))
    per_node = P1 // node
    width_cols = P2 // samp
    tall = rank // folding(rank, per_node * width_cols)
    packed_rows = packing(rank)[2] * BAND
    ends = groups(late)
    beside = [v for group in ends for v in group] + [gram]
    message = jax.ShapeDtypeStruct((node * tall + packed_rows // 2, 128), F32)
    messages = project(
        ids, [(arrived[b], slot[b], borrowed[b]) for b in late], snapshots, rank, t, rows, beside,
        functools.partial(
            tail, node, samp, per_node, width_cols, 1.0 / total, (len(ends[0]), len(ends[2]))),
        [message] * last,
        [pltpu.VMEM((node, tall, 128), F32), pltpu.VMEM((packed_rows, 128), F32)])

    held = messages[0]
    for d in near:
        held = held + swap(messages[d], "samp", samp, d)
    edge = node * tall
    pieces, half = held[:edge], held[edge:]
    bit = 2
    while bit < samp:
        half = half + swap(half, "samp", samp, bit)
        bit *= 2
    crossed = half
    bit = 1
    while bit < node:
        edge //= 2
        got = swap(jnp.concatenate([pieces[edge:], half], axis=0), "node", node, bit)
        pieces, half = pieces[:edge] + got[:edge], half + got[edge:]
        bit *= 2
    other = swap(half, "samp", samp, 1)
    spread = node // samp
    route = [
        (n * samp + s, (s * spread + n // samp) * samp + n % samp) for n in range(node) for s in range(samp)
    ]
    piece = lax.ppermute(pieces, ("node", "samp"), route)

    got_low = []
    for c in range(2):
        low, _ = lax.optimization_barrier((pairs[last, c][rank:], crossed))
        got_low.append(swap(low, "samp", samp, last))

    inverse = factor_inverse(me_s[None], half, other, rank)
    core, coef = finish(
        inverse, piece, [pairs[0, c] for c in range(2)], [arrived[0, c] for c in range(2)], got_low,
        1.0 / total, per_node, width_cols)
    return (core.T, coef.T)


def solution(mesh):
    placed = (P("node", "samp"), P("samp", None))
    return jax.shard_map(
        body,
        mesh=mesh,
        in_specs=placed,
        out_specs=(P(("node", "samp"), None), P("node", "samp")),
        check_vma=False,
    )
```

time: 109 us -> 87.2 us (0.80)
  Pallas kernels: 49.3 us -> 32.2 us
  waiting for transfers between devices: 15.3 us -> 20.1 us
  starting transfers between devices: 27.5 us -> 23.6 us
  local copies, waits for them, and re-layouts: 12.9 us -> 9.8 us
  other arithmetic: 2.49 us -> 0.13 us
    pallas_call x4 -> x3, Pallas kernels: 16.7 us -> 8.69 us  [the longest x1 5.5 us: factor_inverse(): pl.pallas_call(functools.partial(factor_kernel, rank), in_specs=[pl.Block...]
    unnamed x32 -> x6, local copies, waits for them, and re-layouts: 7.97 us -> 0.01 us
    dynamic_slice x1 -> x4, local copies, waits for them, and re-layouts: 4.3 us -> 9.63 us  [body(): made = lax.dynamic_slice_in_dim(snapshots, at, sizes[c], 0)]
    pallas_call x4, Pallas kernels: 13.9 us -> 8.91 us  [sketch(): pl.pallas_call(functools.partial(sketch_kernel, count), grid_spec=pltpu.P...]
    ppermute x20 -> x17, waiting for transfers between devices: 15.3 us -> 20.1 us  [swap(): return lax.ppermute(value, axis, [(i, i ^ bit) for i in range(size)])]
    ppermute x20 -> x17, starting transfers between devices: 20.2 us -> 17.7 us  [swap(): return lax.ppermute(value, axis, [(i, i ^ bit) for i in range(size)])]
    pallas_call x1, Pallas kernels: 4.04 us -> 1.69 us  [local_gram(): pl.pallas_call(gram_kernel, out_shape=jax.ShapeDtypeStruct((rank, rank),...]
    pallas_call x2 -> x3, Pallas kernels: 14.6 us -> 12.9 us  [project(): pl.pallas_call(functools.partial(project_kernel, count, wide, len(bases),...]
  transfers between devices with their start and end apart: 22 -> 18, of which waited for: 7 -> 8; matrix products, arithmetic and copies ran while one was open for 2% -> 9% of each run, Pallas kernels for 40% -> 30%
where the time goes in v4:
time: 87.2 us; the launch traced here: 86.8 us
  Pallas kernels  32.2 us (37%)
  starting transfers between devices  23.6 us (27%)
  waiting for transfers between devices  20.1 us (23%)
  local copies, waits for them, and re-layouts  9.8 us (11%)
  between operations  0.93 us (1%)
    ppermute x17, waiting for transfers between devices, swap(): return lax.ppermute(value, axis, [(i, i ^ bit) for i in range(size)])  20.1 us
    ppermute x17, starting transfers between devices, swap(): return lax.ppermute(value, axis, [(i, i ^ bit) for i in range(size)])  17.7 us
    pallas_call x3, Pallas kernels, project(): pl.pallas_call(functools.partial(project_kernel, count, wide, len(bases),...  12.9 us
    dynamic_slice x4, local copies, waits for them, and re-layouts, body(): made = lax.dynamic_slice_in_dim(snapshots, at, sizes[c], 0)  9.63 us
    pallas_call x4, Pallas kernels, sketch(): pl.pallas_call(functools.partial(sketch_kernel, count), grid_spec=pltpu.P...  8.91 us
    ppermute x1, starting transfers between devices, body(): piece = lax.ppermute(pieces, ('node', 'samp'), route)  5.89 us
    pallas_call x1, Pallas kernels, factor_inverse(): pl.pallas_call(functools.partial(factor_kernel, rank), in_specs=[pl.Block...  5.5 us
    pallas_call x1, Pallas kernels, finish(): pl.pallas_call(functools.partial(finish_kernel, scale, per_node, width_co...  2.5 us
  transfers between devices with their start and end apart: 18, of which 8 were waited for; matrix products, arithmetic and copies ran while one was open for 9% of the time, Pallas kernels for 30%

profile of v4, /device:TPU:3, one launch (start us, length us, event | category | flops | bytes accessed | tf_op | source)
XLA Modules:
  0.0 86.8 jit_solution(1877537063881529359)
XLA Ops:
  0.7 2.3 %constant_dynamic-slice_fusion.3 = bf16[1024,512]{1,0:T(8,128)(2,1)} fusion(bf16[8192,512]{1,0:T(8,128)(2,1)} %refs_1_.1, s32[]{:T(128)S(6)} %select_n.12), kind=kLoop, calls=%fused_computation.12 | loop fusion | bytes 2097156 | tf_op jit(solution)/shard_map/dynamic_slice | solution.py:421
  3.6 2.5 %constant_dynamic-slice_fusion.2 = bf16[1024,512]{1,0:T(8,128)(2,1)} fusion(bf16[8192,512]{1,0:T(8,128)(2,1)} %refs_1_.1, s32[]{:T(128)S(6)} %select_n.13), kind=kLoop, calls=%fused_computation.11 | loop fusion | bytes 2097156 | tf_op jit(solution)/shard_map/dynamic_slice | solution.py:421
  6.1 2.4 %constant_dynamic-slice_fusion.1 = bf16[1024,512]{1,0:T(8,128)(2,1)} fusion(bf16[8192,512]{1,0:T(8,128)(2,1)} %refs_1_.1, s32[]{:T(128)S(6)} %select_n.14), kind=kLoop, calls=%fused_computation.10 | loop fusion | bytes 2097156 | tf_op jit(solution)/shard_map/dynamic_slice | solution.py:421
  9.0 2.4 %constant_dynamic-slice_fusion = bf16[1024,512]{1,0:T(8,128)(2,1)} fusion(bf16[8192,512]{1,0:T(8,128)(2,1)} %refs_1_.1, s32[]{:T(128)S(6)} %select_n.15), kind=kLoop, calls=%fused_computation.9 | loop fusion | bytes 2097156 | tf_op jit(solution)/shard_map/dynamic_slice | solution.py:421
  12.1 1.9 %collective-permute-done.refs_1_ = bf16[160,512]{1,0:T(8,128)(2,1)S(1)} collective-permute-done((bf16[160,512]{1,0:T(8,128)(2,1)S(1)}, bf16[160,512]{1,0:T(8,128)(2,1)S(1)}, u32[]{:S(2)}, u32[]{:S(2)}) %collective-permute-start) | collective-permute-done | bytes 163872 | tf_op jit(solution)/shard_map/ppermute | solution.py:395
  14.0 2.0 %sketch.4 = (bf16[320,1024]{1,0:T(8,128)(2,1)S(1)}, bf16[160,1024]{1,0:T(8,128)(2,1)S(1)}) custom-call(s32[1]{0:T(128)} %bitcast.1.ids_ref, bf16[8192,512]{1,0:T(8,128)(2,1)} %refs_1_.1, bf16[160,512]{1,0:T(8,128)(2,1)S(1)} %bitcast.10, bf16[160,512]{1,0:T(8,128)(2,1)S(1)} %collective-permute-done.refs_1_, ...), custom_call_target="tpu_custom_call" | custom-call | flops 335544320 | bytes 3080192 | tf_op jit(solution)/shard_map/sketch/pallas_call | solution.py:57
  16.1 2.1 %sketch.5 = (bf16[320,1024]{1,0:T(8,128)(2,1)S(1)}, bf16[160,1024]{1,0:T(8,128)(2,1)S(1)}) custom-call(s32[1]{0:T(128)} %bitcast.2.ids_ref, bf16[8192,512]{1,0:T(8,128)(2,1)} %refs_1_.1, bf16[160,512]{1,0:T(8,128)(2,1)S(1)} %bitcast.11, bf16[160,512]{1,0:T(8,128)(2,1)S(1)} %collective-permute-done.refs_1_, ...), custom_call_target="tpu_custom_call" | custom-call | flops 335544320 | bytes 3080192 | tf_op jit(solution)/shard_map/sketch/pallas_call | solution.py:57
  19.7 2.4 %sketch.6 = (bf16[320,1024]{1,0:T(8,128)(2,1)S(1)}, bf16[160,1024]{1,0:T(8,128)(2,1)S(1)}) custom-call(s32[1]{0:T(128)} %bitcast.3.ids_ref, bf16[8192,512]{1,0:T(8,128)(2,1)} %refs_1_.1, bf16[160,512]{1,0:T(8,128)(2,1)S(1)} %bitcast.12, bf16[160,512]{1,0:T(8,128)(2,1)S(1)} %collective-permute-done.refs_1_, ...), custom_call_target="tpu_custom_call" | custom-call | flops 335544320 | bytes 3080192 | tf_op jit(solution)/shard_map/sketch/pallas_call | solution.py:57
  22.3 2.4 %sketch.7 = (bf16[320,1024]{1,0:T(8,128)(2,1)S(1)}, bf16[160,1024]{1,0:T(8,128)(2,1)S(1)}) custom-call(s32[1]{0:T(128)} %bitcast.4.ids_ref, bf16[8192,512]{1,0:T(8,128)(2,1)} %refs_1_.1, bf16[160,512]{1,0:T(8,128)(2,1)S(1)} %bitcast.13, bf16[160,512]{1,0:T(8,128)(2,1)S(1)} %collective-permute-done.refs_1_, ...), custom_call_target="tpu_custom_call" | custom-call | flops 335544320 | bytes 3080192 | tf_op jit(solution)/shard_map/sketch/pallas_call | solution.py:57
  24.6 1.5 %collective-permute-start.5 = (bf16[160,1024]{1,0:T(8,128)(2,1)S(1)}, bf16[160,1024]{1,0:T(8,128)(2,1)S(1)}, u32[]{:S(2)}, u32[]{:S(2)}) collective-permute-start(bf16[160,1024]{1,0:T(8,128)(2,1)S(1)} %get-tuple-element.25), channel_id=1, source_target_pairs={{0,2},{1,3},{2,0},{3,1},{4,6},{5,7},{6,4},{7,5},{8,10},{9,11},{10,... | collective-permute-start | bytes 983048 | tf_op jit(solution)/shard_map/ppermute | solution.py:395
  26.1 1.7 %gram.1.refs_6_ = f32[160,160]{1,0:T(8,128)S(1)} custom-call(bf16[320,1024]{1,0:T(8,128)(2,1)S(1)} %get-tuple-element.26.refs_0_.refs_4_, bf16[320,1024]{1,0:T(8,128)(2,1)S(1)} %get-tuple-element.27.refs_1_.refs_4_, bf16[320,1024]{1,0:T(8,128)(2,1)S(1)} %get-tuple-element.28.refs_2_.refs_0_, bf16[320,1024]{1,0:T(8,128)(2,1)S(1)} %get-tuple-element.29.refs_3_.refs_1_), custom_call_target="tpu_custom_call" | custom-call | flops 838860800 | bytes 2621440 | tf_op jit(solution)/shard_map/gram/pallas_call | solution.py:119
  27.8 6.0 %project.3.refs_7_.refs_9_ = f32[2,160,512]{2,1,0:T(8,128)S(1)} custom-call(s32[6]{0:T(128)S(1)} %stack.24.ids_ref, bf16[320,1024]{1,0:T(8,128)(2,1)S(1)} %get-tuple-element.26.refs_0_.refs_4_, bf16[320,1024]{1,0:T(8,128)(2,1)S(1)} %get-tuple-element.27.refs_1_.refs_4_, bf16[320,1024]{1,0:T(8,128)(2,1)S(1)} %get-tuple-element.28.refs_2_.refs_0_, ...), custom_call_target="tpu_custom_call" | custom-call | flops 2684354560 | bytes 11010048 | tf_op jit(solution)/shard_map/project/pallas_call | solution.py:286
  33.8 5.2 %collective-permute-done.8.refs_5_.refs_2_ = bf16[160,1024]{1,0:T(8,128)(2,1)S(1)} collective-permute-done((bf16[160,1024]{1,0:T(8,128)(2,1)S(1)}, bf16[160,1024]{1,0:T(8,128)(2,1)S(1)}, u32[]{:S(2)}, u32[]{:S(2)}) %collective-permute-start.8) | collective-permute-done | bytes 327712 | tf_op jit(solution)/shard_map/ppermute | solution.py:395
  39.8 3.6 %project.4.refs_3_ = f32[2,160,512]{2,1,0:T(8,128)S(1)} custom-call(s32[6]{0:T(128)S(1)} %stack.24.ids_ref, bf16[160,1024]{1,0:T(8,128)(2,1)S(1)} %collective-permute-done.6.refs_2_.refs_0_, bf16[160,1024]{1,0:T(8,128)(2,1)S(1)} %collective-permute-done.7.refs_3_.refs_1_, bf16[160,1024]{1,0:T(8,128)(2,1)S(1)} %collective-permute-done.8.refs_5_.refs_2_, ...), custom_call_target="tpu_custom_call" | custom-call | flops 1006632960 | bytes 7274496 | tf_op jit(solution)/shard_map/project/pallas_call | solution.py:286
  43.4 2.7 %collective-permute-done.5.refs_0_.refs_5_ = bf16[160,1024]{1,0:T(8,128)(2,1)S(1)} collective-permute-done((bf16[160,1024]{1,0:T(8,128)(2,1)S(1)}, bf16[160,1024]{1,0:T(8,128)(2,1)S(1)}, u32[]{:S(2)}, u32[]{:S(2)}) %collective-permute-start.5) | collective-permute-done | bytes 327712 | tf_op jit(solution)/shard_map/ppermute | solution.py:395
  46.1 3.3 %project.5 = (f32[704,128]{1,0:T(8,128)S(1)}, f32[704,128]{1,0:T(8,128)S(1)}) custom-call(s32[6]{0:T(128)S(1)} %stack.24.ids_ref, bf16[160,1024]{1,0:T(8,128)(2,1)S(1)} %collective-permute-done.5.refs_0_.refs_5_, bf16[8192,512]{1,0:T(8,128)(2,1)} %refs_1_.1, bf16[1024,512]{1,0:T(8,128)(2,1)S(1)} %collective-permute-done.3.refs_2_.refs_9_, ...), custom_call_target="tpu_custom_call" | custom-call | flops 335544320 | bytes 2424832 | tf_op jit(solution)/shard_map/project/pallas_call | solution.py:286
  52.2 2.7 %collective-permute-done.10 = f32[64,128]{1,0:T(8,128)S(1)} collective-permute-done((f32[64,128]{1,0:T(8,128)S(1)}, f32[64,128]{1,0:T(8,128)S(1)}, u32[]{:S(2)}, u32[]{:S(2)}) %collective-permute-start.10) | collective-permute-done | bytes 32800 | tf_op jit(solution)/shard_map/ppermute | solution.py:395
  56.2 3.6 %collective-permute-done.11 = f32[384,128]{1,0:T(8,128)S(1)} collective-permute-done((f32[384,128]{1,0:T(8,128)S(1)}, f32[384,128]{1,0:T(8,128)S(1)}, u32[]{:S(2)}, u32[]{:S(2)}) %collective-permute-start.11) | collective-permute-done | bytes 196640 | tf_op jit(solution)/shard_map/ppermute | solution.py:395
  61.3 2.3 %collective-permute-done.12 = f32[224,128]{1,0:T(8,128)S(1)} collective-permute-done((f32[224,128]{1,0:T(8,128)S(1)}, f32[224,128]{1,0:T(8,128)S(1)}, u32[]{:S(2)}, u32[]{:S(2)}) %collective-permute-start.12) | collective-permute-done | bytes 114720 | tf_op jit(solution)/shard_map/ppermute | solution.py:395
  63.7 2.4 %collective-permute-start.13 = (f32[144,128]{1,0:T(8,128)S(1)}, f32[144,128]{1,0:T(8,128)S(1)}, u32[]{:S(2)}, u32[]{:S(2)}) collective-permute-start(f32[144,128]{1,0:T(8,128)S(1)} %pad_maximum_fusion.2), channel_id=1, source_target_pairs={{0,16},{4,20},{8,24},{12,28},{16,0},{20,4},{24,8},{28,12},{1,17},{... | collective-permute-start | bytes 221192 | tf_op jit(solution)/shard_map/ppermute | solution.py:395
  67.9 4.9 %collective-permute-start.14 = (f32[64,128]{1,0:T(8,128)S(1)}, f32[64,128]{1,0:T(8,128)S(1)}, u32[]{:S(2)}, u32[]{:S(2)}) collective-permute-start(f32[64,128]{1,0:T(8,128)S(1)} %slice_add_fusion.3.mine_ref), channel_id=1, source_target_pairs={{0,1},{1,0},{2,3},{3,2},{4,5},{5,4},{6,7},{7,6},{8,9},{9,8},{10,11... | collective-permute-start | bytes 98312 | tf_op jit(solution)/shard_map/ppermute | solution.py:395
  72.8 5.9 %collective-permute-start.15 = (f32[80,128]{1,0:T(8,128)S(1)}, f32[80,128]{1,0:T(8,128)S(1)}, u32[]{:S(2)}, u32[]{:S(2)}) collective-permute-start(f32[80,128]{1,0:T(8,128)S(1)} %slice_add_fusion.2), channel_id=1, source_target_pairs={{0,0},{1,8},{2,16},{3,24},{4,1},{5,9},{6,17},{7,25},{8,2},{9,10},{... | collective-permute-start | bytes 122888 | tf_op jit(solution)/shard_map/ppermute | solution.py:487
  78.7 5.5 %factor.1.inv_ref = f32[160,160]{1,0:T(8,128)S(1)} custom-call(s32[1]{0:T(128)} %bitcast.me_ref, f32[64,128]{1,0:T(8,128)S(1)} %slice_add_fusion.3.mine_ref, f32[64,128]{1,0:T(8,128)S(1)} %collective-permute-done.14.other_ref), custom_call_target="tpu_custom_call" | custom-call | flops 8000000000 | bytes 102400 | tf_op jit(solution)/shard_map/factor/pallas_call | solution.py:225
  84.2 2.5 %finish.1 = (f32[160,2048]{1,0:T(8,128)}, f32[8,1280]{1,0:T(8,128)}) custom-call(f32[160,160]{1,0:T(8,128)S(1)} %factor.1.inv_ref, f32[80,128]{1,0:T(8,128)S(1)} %collective-permute-done.15.piece_ref, bf16[320,1024]{1,0:T(8,128)(2,1)S(1)} %get-tuple-element.28.refs_2_.refs_0_, bf16[320,1024]{1,0:T(8,128)(2,1)S(1)} %get-tuple-element.29.refs_3_.refs_1_, ...), custom_call_target="tpu_custom_call" | custom-call | flops 629145600 | bytes 3932160 | tf_op jit(solution)/shard_map/finish/pallas_call | solution.py:382
  (51 shorter events, 11.4 us)
Async XLA Ops:
  0.6 10.8 %copy-start.2 = (bf16[512,160]{0,1:T(8,128)(2,1)S(1)}, bf16[512,160]{0,1:T(8,128)(2,1)}, u32[]{:S(2)}) copy-start(bf16[512,160]{0,1:T(8,128)(2,1)} %param.3) | copy-start | bytes 491524
  2.9 11.0 %collective-permute-start.4 = (bf16[1024,512]{1,0:T(8,128)(2,1)}, bf16[1024,512]{1,0:T(8,128)(2,1)S(1)}, u32[]{:S(2)}, u32[]{:S(2)}) collective-permute-start(bf16[1024,512]{1,0:T(8,128)(2,1)} %constant_dynamic-slice_fusion.3), channel_id=1, source_target_pairs={{0,1},{1,0},{2,3},{3,2},{4,5},{5,4},{6,7},{7,6},{8,9},{9,8},{10,11... | collective-permute-start | bytes 3145736 | tf_op jit(solution)/shard_map/ppermute | solution.py:395
  6.1 10.1 %collective-permute-start.3 = (bf16[1024,512]{1,0:T(8,128)(2,1)}, bf16[1024,512]{1,0:T(8,128)(2,1)S(1)}, u32[]{:S(2)}, u32[]{:S(2)}) collective-permute-start(bf16[1024,512]{1,0:T(8,128)(2,1)} %constant_dynamic-slice_fusion.2), channel_id=1, source_target_pairs={{0,1},{1,0},{2,3},{3,2},{4,5},{5,4},{6,7},{7,6},{8,9},{9,8},{10,11... | collective-permute-start | bytes 3145736 | tf_op jit(solution)/shard_map/ppermute | solution.py:395
  8.5 11.2 %collective-permute-start.2 = (bf16[1024,512]{1,0:T(8,128)(2,1)}, bf16[1024,512]{1,0:T(8,128)(2,1)S(1)}, u32[]{:S(2)}, u32[]{:S(2)}) collective-permute-start(bf16[1024,512]{1,0:T(8,128)(2,1)} %constant_dynamic-slice_fusion.1), channel_id=1, source_target_pairs={{0,1},{1,0},{2,3},{3,2},{4,5},{5,4},{6,7},{7,6},{8,9},{9,8},{10,11... | collective-permute-start | bytes 3145736 | tf_op jit(solution)/shard_map/ppermute | solution.py:395
  11.5 10.8 %collective-permute-start.1 = (bf16[1024,512]{1,0:T(8,128)(2,1)}, bf16[1024,512]{1,0:T(8,128)(2,1)}, u32[]{:S(2)}, u32[]{:S(2)}) collective-permute-start(bf16[1024,512]{1,0:T(8,128)(2,1)} %constant_dynamic-slice_fusion), channel_id=1, source_target_pairs={{0,1},{1,0},{2,3},{3,2},{4,5},{5,4},{6,7},{7,6},{8,9},{9,8},{10,11... | collective-permute-start | bytes 3145736 | tf_op jit(solution)/shard_map/ppermute | solution.py:395
  11.5 2.5 %collective-permute-start = (bf16[160,512]{1,0:T(8,128)(2,1)S(1)}, bf16[160,512]{1,0:T(8,128)(2,1)S(1)}, u32[]{:S(2)}, u32[]{:S(2)}) collective-permute-start(bf16[160,512]{1,0:T(8,128)(2,1)S(1)} %bitcast.9), channel_id=1, source_target_pairs={{0,1},{1,0},{2,3},{3,2},{4,5},{5,4},{6,7},{7,6},{8,9},{9,8},{10,11... | collective-permute-start | bytes 491528 | tf_op jit(solution)/shard_map/ppermute | solution.py:395
  16.1 17.8 %collective-permute-start.6 = (bf16[160,1024]{1,0:T(8,128)(2,1)S(1)}, bf16[160,1024]{1,0:T(8,128)(2,1)S(1)}, u32[]{:S(2)}, u32[]{:S(2)}) collective-permute-start(bf16[160,1024]{1,0:T(8,128)(2,1)S(1)} %get-tuple-element.22.refs_3_), channel_id=1, source_target_pairs={{0,2},{1,3},{2,0},{3,1},{4,6},{5,7},{6,4},{7,5},{8,10},{9,11},{10,... | collective-permute-start | bytes 983048 | tf_op jit(solution)/shard_map/ppermute | solution.py:395
  18.2 15.6 %collective-permute-start.7 = (bf16[160,1024]{1,0:T(8,128)(2,1)S(1)}, bf16[160,1024]{1,0:T(8,128)(2,1)S(1)}, u32[]{:S(2)}, u32[]{:S(2)}) collective-permute-start(bf16[160,1024]{1,0:T(8,128)(2,1)S(1)} %get-tuple-element.23.refs_3_), channel_id=1, source_target_pairs={{0,2},{1,3},{2,0},{3,1},{4,6},{5,7},{6,4},{7,5},{8,10},{9,11},{10,... | collective-permute-start | bytes 983048 | tf_op jit(solution)/shard_map/ppermute | solution.py:395
  19.7 4.9 %copy-start = (bf16[1024,512]{1,0:T(8,128)(2,1)}, bf16[1024,512]{1,0:T(8,128)(2,1)S(1)}, u32[]{:S(2)}) copy-start(bf16[1024,512]{1,0:T(8,128)(2,1)S(1)} %collective-permute-done.2.refs_2_.refs_10_.refs_6_) | copy-start | bytes 3145732
  22.2 16.9 %collective-permute-start.8 = (bf16[160,1024]{1,0:T(8,128)(2,1)S(1)}, bf16[160,1024]{1,0:T(8,128)(2,1)S(1)}, u32[]{:S(2)}, u32[]{:S(2)}) collective-permute-start(bf16[160,1024]{1,0:T(8,128)(2,1)S(1)} %get-tuple-element.24.refs_3_), channel_id=1, source_target_pairs={{0,2},{1,3},{2,0},{3,1},{4,6},{5,7},{6,4},{7,5},{8,10},{9,11},{10,... | collective-permute-start | bytes 983048 | tf_op jit(solution)/shard_map/ppermute | solution.py:395
  24.6 21.5 %collective-permute-start.5 = (bf16[160,1024]{1,0:T(8,128)(2,1)S(1)}, bf16[160,1024]{1,0:T(8,128)(2,1)S(1)}, u32[]{:S(2)}, u32[]{:S(2)}) collective-permute-start(bf16[160,1024]{1,0:T(8,128)(2,1)S(1)} %get-tuple-element.25), channel_id=1, source_target_pairs={{0,2},{1,3},{2,0},{3,1},{4,6},{5,7},{6,4},{7,5},{8,10},{9,11},{10,... | collective-permute-start | bytes 983048 | tf_op jit(solution)/shard_map/ppermute | solution.py:395
  27.8 11.9 %copy-start.1 = (bf16[1024,512]{1,0:T(8,128)(2,1)S(1)}, bf16[1024,512]{1,0:T(8,128)(2,1)}, u32[]{:S(2)}) copy-start(bf16[1024,512]{1,0:T(8,128)(2,1)} %copy-done) | copy-start | bytes 3145732
  49.4 2.6 %collective-permute-start.9 = (f32[704,128]{1,0:T(8,128)S(1)}, f32[704,128]{1,0:T(8,128)S(1)}, u32[]{:S(2)}, u32[]{:S(2)}) collective-permute-start(f32[704,128]{1,0:T(8,128)S(1)} %get-tuple-element.31), channel_id=1, source_target_pairs={{0,1},{1,0},{2,3},{3,2},{4,5},{5,4},{6,7},{7,6},{8,9},{9,8},{10,11... | collective-permute-start | bytes 1081352 | tf_op jit(solution)/shard_map/ppermute | solution.py:395
  52.1 2.8 %collective-permute-start.10 = (f32[64,128]{1,0:T(8,128)S(1)}, f32[64,128]{1,0:T(8,128)S(1)}, u32[]{:S(2)}, u32[]{:S(2)}) collective-permute-start(f32[64,128]{1,0:T(8,128)S(1)} %slice.63), channel_id=1, source_target_pairs={{0,2},{1,3},{2,0},{3,1},{4,6},{5,7},{6,4},{7,5},{8,10},{9,11},{10,... | collective-permute-start | bytes 98312 | tf_op jit(solution)/shard_map/ppermute | solution.py:395
  54.9 4.9 %collective-permute-start.11 = (f32[384,128]{1,0:T(8,128)S(1)}, f32[384,128]{1,0:T(8,128)S(1)}, u32[]{:S(2)}, u32[]{:S(2)}) collective-permute-start(f32[384,128]{1,0:T(8,128)S(1)} %pad_maximum_fusion), channel_id=1, source_target_pairs={{0,4},{4,0},{8,12},{12,8},{16,20},{20,16},{24,28},{28,24},{1,5},{5... | collective-permute-start | bytes 589832 | tf_op jit(solution)/shard_map/ppermute | solution.py:395
  59.9 3.7 %collective-permute-start.12 = (f32[224,128]{1,0:T(8,128)S(1)}, f32[224,128]{1,0:T(8,128)S(1)}, u32[]{:S(2)}, u32[]{:S(2)}) collective-permute-start(f32[224,128]{1,0:T(8,128)S(1)} %pad_maximum_fusion.1), channel_id=1, source_target_pairs={{0,8},{4,12},{8,0},{12,4},{16,24},{20,28},{24,16},{28,20},{1,9},{5... | collective-permute-start | bytes 344072 | tf_op jit(solution)/shard_map/ppermute | solution.py:395
  63.7 4.2 %collective-permute-start.13 = (f32[144,128]{1,0:T(8,128)S(1)}, f32[144,128]{1,0:T(8,128)S(1)}, u32[]{:S(2)}, u32[]{:S(2)}) collective-permute-start(f32[144,128]{1,0:T(8,128)S(1)} %pad_maximum_fusion.2), channel_id=1, source_target_pairs={{0,16},{4,20},{8,24},{12,28},{16,0},{20,4},{24,8},{28,12},{1,17},{... | collective-permute-start | bytes 221192 | tf_op jit(solution)/shard_map/ppermute | solution.py:395
  66.1 18.1 %collective-permute-start.16 = (bf16[160,1024]{1,0:T(8,128)(2,1)S(1)}, bf16[160,1024]{1,0:T(8,128)(2,1)S(1)}, u32[]{:S(2)}, u32[]{:S(2)}) collective-permute-start(bf16[160,1024]{1,0:T(8,128)(2,1)S(1)} %slice.61), channel_id=1, source_target_pairs={{0,2},{1,3},{2,0},{3,1},{4,6},{5,7},{6,4},{7,5},{8,10},{9,11},{10,... | collective-permute-start | bytes 983048 | tf_op jit(solution)/shard_map/ppermute | solution.py:395
  66.4 17.8 %collective-permute-start.17 = (bf16[160,1024]{1,0:T(8,128)(2,1)S(1)}, bf16[160,1024]{1,0:T(8,128)(2,1)S(1)}, u32[]{:S(2)}, u32[]{:S(2)}) collective-permute-start(bf16[160,1024]{1,0:T(8,128)(2,1)S(1)} %slice.62), channel_id=1, source_target_pairs={{0,2},{1,3},{2,0},{3,1},{4,6},{5,7},{6,4},{7,5},{8,10},{9,11},{10,... | collective-permute-start | bytes 983048 | tf_op jit(solution)/shard_map/ppermute | solution.py:395
  67.9 10.8 %collective-permute-start.14 = (f32[64,128]{1,0:T(8,128)S(1)}, f32[64,128]{1,0:T(8,128)S(1)}, u32[]{:S(2)}, u32[]{:S(2)}) collective-permute-start(f32[64,128]{1,0:T(8,128)S(1)} %slice_add_fusion.3.mine_ref), channel_id=1, source_target_pairs={{0,1},{1,0},{2,3},{3,2},{4,5},{5,4},{6,7},{7,6},{8,9},{9,8},{10,11... | collective-permute-start | bytes 98312 | tf_op jit(solution)/shard_map/ppermute | solution.py:395
  72.8 11.4 %collective-permute-start.15 = (f32[80,128]{1,0:T(8,128)S(1)}, f32[80,128]{1,0:T(8,128)S(1)}, u32[]{:S(2)}, u32[]{:S(2)}) collective-permute-start(f32[80,128]{1,0:T(8,128)S(1)} %slice_add_fusion.2), channel_id=1, source_target_pairs={{0,0},{1,8},{2,16},{3,24},{4,1},{5,9},{6,17},{7,25},{8,2},{9,10},{... | collective-permute-start | bytes 122888 | tf_op jit(solution)/shard_map/ppermute | solution.py:487

commit v5 on v4

--- a/solution.py
+++ b/solution.py
@@ -11,6 +11,7 @@
 BAND = 32
 UNIT = 1024
 SKETCH_ROWS = 1024
+EARLY_STAGE, LATE_STAGE = 1, 4
 COST_CUT = 1
 F32 = jnp.float32
 BF16 = jnp.bfloat16
@@ -34,6 +35,49 @@
 
 def cost(flops, moved):
     return pl.CostEstimate(flops=int(flops) // COST_CUT, bytes_accessed=int(moved) // COST_CUT, transcendentals=0)
+
+
+def lend_kernel(size, stride, at, ids_ref, x_ref, *refs):
+    count = ids_ref.shape[0]
+    extra = 1 if at is not None else 0
+    outs, sems = refs[-1 - count:-1], refs[-1]
+    copies = []
+    for k in range(count):
+        first = pl.multiple_of(ids_ref[k] * size, size)
+        for part in range(size // stride):
+            copies.append(pltpu.make_async_copy(
+                x_ref.at[pl.ds(first + part * stride, stride)],
+                outs[k].at[pl.ds(part * stride, stride)],
+                sems.at[len(copies)]))
+    if extra:
+        copies.append(pltpu.make_async_copy(
+            refs[0], outs[0].at[pl.ds(at, refs[0].shape[0])], sems.at[len(copies)]))
+    for copy in copies:
+        copy.start()
+    for copy in copies:
+        copy.wait()
+
+
+def lend(ids, x, size, w=None, after=()):
+    count = ids.shape[0]
+    depth = x.shape[1]
+    stride = size // 2
+    at, height = None, size
+    if w is not None:
+        rank = w.shape[0]
+        at = -(-size // rank) * rank
+        height = at + rank
+    more = [] if w is None else [w]
+    return pl.pallas_call(
+        functools.partial(lend_kernel, size, stride, at),
+        in_specs=[pl.BlockSpec(memory_space=pltpu.SMEM)] + [UNREAD] * (1 + len(more) + len(after)),
+        out_specs=[pl.BlockSpec(memory_space=pl.ANY)] * count,
+        out_shape=[jax.ShapeDtypeStruct((height, depth), BF16)] * count,
+        scratch_shapes=[pltpu.SemaphoreType.DMA((2 * count + len(more),))],
+        compiler_params=params(),
+        cost_estimate=cost(0, 4 * count * height * depth),
+        name="lend",
+    )(ids, x, *more, *after)
 
 
 def sketch_kernel(count, ids_ref, x_ref, *refs):
@@ -50,7 +94,7 @@
     both_ref[rank:, :] = (s - high.astype(F32)).astype(BF16)
 
 
-def sketch(ids, x, ws, extra, size, after=()):
+def sketch(ids, x, ws, extra, size, w_at, after=()):
     rank, depth = ws[0].shape
     count = len(ws)
     rows = min(size, SKETCH_ROWS)
@@ -60,7 +104,8 @@
             num_scalar_prefetch=1,
             grid=(size // rows,),
             in_specs=[pl.BlockSpec((rows, depth), lambda i, ids: (ids[0] + i, 0))]
-            + [pl.BlockSpec((rank, depth), lambda i, ids: (0, 0))] * count
+            + [pl.BlockSpec((rank, depth), lambda i, ids: (0, 0))]
+            + [pl.BlockSpec((rank, depth), lambda i, ids: (w_at // rank, 0))] * (count - 1)
             + [pl.BlockSpec((rows, depth), lambda i, ids: (i, 0))] * (count - 1)
             + [UNREAD] * len(after),
             out_specs=[
@@ -102,60 +147,30 @@
     return (x[:rank, :rank] + x[rank:, rank:]) + (x[:rank, rank:] + x[rank:, :rank])
 
 
-def gram_kernel(*refs):
+def gram_kernel(scale, count, *refs):
     o_ref = refs[-1]
-    rank = o_ref.shape[0]
+    rank = refs[count].shape[0]
     total = None
-    for ref in refs[:-1]:
-        both = ref[...]
+    for own_ref, got_ref in zip(refs[:count], refs[count:2 * count]):
+        s = own_ref[:rank, :].astype(F32) + own_ref[rank:, :].astype(F32) + got_ref[...].astype(F32)
+        high = s.astype(BF16)
+        both = jnp.concatenate([high, (s - high.astype(F32)).astype(BF16)], axis=0)
         term = dot(both, both, ((1,), (1,)))
         total = term if total is None else total + term
-    o_ref[...] = fold_square(total, rank)
-
-
-def local_gram(pairs):
-    rank = pairs[0].shape[0] // 2
-    rows = sum(v.shape[1] for v in pairs)
-    return pl.pallas_call(
-        gram_kernel,
-        out_shape=jax.ShapeDtypeStruct((rank, rank), F32),
-        compiler_params=params(),
-        cost_estimate=cost(8 * rank * rank * rows, 4 * rank * rows),
+    o_ref[...] = pack_gram(fold_square(total, rank) * scale)
+
+
+def own_gram(own, got, scale, after=()):
+    rank = got[0].shape[0]
+    rows = sum(v.shape[1] for v in got)
+    return pl.pallas_call(
+        functools.partial(gram_kernel, scale, len(own)),
+        in_specs=[HELD] * (2 * len(own)) + [UNREAD] * len(after),
+        out_shape=jax.ShapeDtypeStruct((packing(rank)[2] * BAND, 128), F32),
+        compiler_params=params(),
+        cost_estimate=cost(8 * rank * rank * rows, 6 * rank * rows),
         name="gram",
-    )(*pairs)
-
-
-def cross_terms(own, got, far, near):
-    rank = (got + near)[0].shape[0]
-    total = None
-    for own_ref, got_ref in zip(own, got):
-        term = dot(own_ref[...], got_ref[...], ((1,), (1,)))
-        term = term[:rank] + term[rank:]
-        total = term if total is None else total + term
-    for far_ref, near_ref in zip(far, near):
-        term = dot(near_ref[...], far_ref[rank:, :], ((1,), (1,)))
-        total = term if total is None else total + term
-    return total + total.T
-
-
-def cross_kernel(counts, *refs):
-    a, b = counts
-    groups = refs[:a], refs[a:2 * a], refs[2 * a:2 * a + b], refs[2 * a + b:2 * a + 2 * b]
-    refs[-1][...] = refs[2 * a + 2 * b][...] + cross_terms(*groups)
-
-
-def cross_gram(own, got, far, near, gram, after=()):
-    rank = gram.shape[0]
-    rows = sum(v.shape[1] for v in got + near)
-    counts = (len(own), len(far))
-    return pl.pallas_call(
-        functools.partial(cross_kernel, counts),
-        in_specs=[HELD] * (2 * sum(counts) + 1) + [UNREAD] * len(after),
-        out_shape=jax.ShapeDtypeStruct((rank, rank), F32),
-        compiler_params=params(),
-        cost_estimate=cost(4 * rank * rank * rows, 6 * rank * rows),
-        name="cross",
-    )(*own, *got, *far, *near, gram, *after)
+    )(*own, *got, *after)
 
 
 def wide_lanes(x, n):
@@ -314,22 +329,13 @@
     return sum(1 << (count - 1 - b) for b in range(count) if (p >> b) & 1)
 
 
-def tail(pieces, samp, per_node, width_cols, scale, counts, t_ref, ids_ref, beside, *refs):
-    outs, hold, packed_ref = refs[:-2], refs[-2], refs[-1]
+def tail(pieces, samp, per_node, width_cols, t_ref, ids_ref, beside, *refs):
+    outs, hold = refs[:-1], refs[-1]
     wide, rank, depth = t_ref.shape
     width = per_node * width_cols
     fold = folding(rank, width)
     tall = rank // fold
-    me_node, me_samp = ids_ref[ids_ref.shape[0] - 2], ids_ref[ids_ref.shape[0] - 1]
-    a, b = counts
-    groups = beside[:a], beside[a:2 * a], beside[2 * a:2 * a + b], beside[2 * a + b:2 * a + 2 * b]
-    packed_ref[...] = pack_gram((beside[2 * a + 2 * b][...] + cross_terms(*groups)) * scale)
-    half = packed_ref.shape[0] // 2
-    mine_at = pl.multiple_of((me_samp & 1) * half, half)
-    outs[0][pieces * tall:, :] = packed_ref[pl.ds(mine_at, half), :]
-    outs[1][pieces * tall:, :] = packed_ref[pl.ds(pl.multiple_of(half - mine_at, half), half), :]
-    for out in outs[2:]:
-        out[pieces * tall:, :] = jnp.zeros((half, 128), F32)
+    me_node = ids_ref[ids_ref.shape[0] - 1]
     dst = iota((depth, depth), 1)
     src = iota((depth, depth), 0)
     a, rest = dst // (samp * width), dst % (samp * width)
@@ -354,41 +360,52 @@
             outs[w][p * tall:(p + 1) * tall, :] = hold[me_node ^ reverse_bits(p, bits)]
 
 
-def finish_kernel(scale, per_node, width_cols, count, inv_ref, piece_ref, *refs):
+def core_kernel(count, inv_ref, *refs):
     both, high, low = (refs[k * count:(k + 1) * count] for k in range(3))
-    core_ref, coef_ref = refs[-2:]
+    core_ref = refs[-1]
     rank = inv_ref.shape[0]
-    inverse = inv_ref[...]
     at = 0
     for c in range(count):
         s = both[c][:rank, :].astype(F32) + both[c][rank:, :].astype(F32)
         s = s + (high[c][...].astype(F32) + low[c][...].astype(F32))
         rows = s.shape[1]
-        core_ref[:, at:at + rows] = dot(inverse, s, ((1,), (0,)), HI)
+        core_ref[:, at:at + rows] = dot(inv_ref[...], s, ((1,), (0,)), HI)
         at += rows
+
+
+def core_product(inverse, both, high, low):
+    rank = inverse.shape[0]
+    count = len(both)
+    rows = sum(v.shape[1] for v in high)
+    return pl.pallas_call(
+        functools.partial(core_kernel, count),
+        out_shape=jax.ShapeDtypeStruct((rank, rows), F32),
+        compiler_params=params(),
+        cost_estimate=cost(12 * rank * rank * rows, 12 * rank * rows),
+        name="core",
+    )(inverse, *both, *high, *low)
+
+
+def coefficient_kernel(scale, per_node, width_cols, inv_ref, piece_ref, o_ref):
+    rank = inv_ref.shape[0]
     width = per_node * width_cols
     fold = folding(rank, width)
     total = piece_ref[...]
     total = jnp.concatenate([total[:, f * width:(f + 1) * width] for f in range(fold)], axis=0)
-    out = dot(total, inverse, ((0,), (1,)), HI) * scale
-    coef_ref[...] = jnp.concatenate(
+    out = dot(total, inv_ref[...], ((0,), (1,)), HI) * scale
+    o_ref[...] = jnp.concatenate(
         [out[p * width_cols:(p + 1) * width_cols, :] for p in range(per_node)], axis=1)
 
 
-def finish(inverse, piece, both, high, low, scale, per_node, width_cols):
+def coefficients(inverse, piece, scale, per_node, width_cols):
     rank = inverse.shape[0]
-    count = len(both)
-    rows = sum(v.shape[1] for v in high)
-    return pl.pallas_call(
-        functools.partial(finish_kernel, scale, per_node, width_cols, count),
-        out_shape=(
-            jax.ShapeDtypeStruct((rank, rows), F32),
-            jax.ShapeDtypeStruct((width_cols, per_node * rank), F32),
-        ),
-        compiler_params=params(),
-        cost_estimate=cost(12 * rank * rank * rows, 12 * rank * rows),
-        name="finish",
-    )(inverse, piece, *both, *high, *low)
+    return pl.pallas_call(
+        functools.partial(coefficient_kernel, scale, per_node, width_cols),
+        out_shape=jax.ShapeDtypeStruct((width_cols, per_node * rank), F32),
+        compiler_params=params(),
+        cost_estimate=cost(12 * rank * rank * per_node * width_cols, 4 * rank * rank),
+        name="coefficient",
+    )(inverse, piece)
 
 
 def swap(value, axis, size, bit):
@@ -410,91 +427,88 @@
     starts, sizes = (0, UNIT), (UNIT, quarter - UNIT)
     blocks = [(last, 0), (last, 1), (0, 0), (0, 1)]
 
-    ws = [w_t] + [swap(w_t, "samp", samp, d) for d in near]
-    borrowed, made = {}, None
-    for base, c in blocks:
-        lent = []
-        for d in near:
-            at = (me_s ^ base ^ d) * quarter + starts[c]
-            if made is not None:
-                at, _ = lax.optimization_barrier((at, made))
-            made = lax.dynamic_slice_in_dim(snapshots, at, sizes[c], 0)
-            lent.append(swap(made, "samp", samp, d))
-        borrowed[base, c] = lent
-
-    def first_unit(base, c):
+    def block_of(base, c):
         return (me_s ^ base) * (quarter // UNIT) + starts[c] // UNIT
+
+    borrowed = {b: [] for b in blocks}
+    ws, w_at = [w_t], 0
+    for d in near:
+        out = lend(jnp.stack([block_of(blocks[0][0] ^ d, blocks[0][1])]), snapshots, UNIT, w_t)
+        w_at = out[0].shape[0] - rank
+        out += lend(jnp.stack([block_of(base ^ d, c) for base, c in blocks[1:]]), snapshots, UNIT, after=out)
+        for b, v in zip(blocks, out):
+            borrowed[b].append(swap(v, "samp", samp, d))
+        ws.append(borrowed[blocks[0]][-1])
 
     pairs, arrived, done = {}, {}, ()
     for base, c in blocks:
         both, high = sketch(
-            first_unit(base, c)[None], snapshots, ws, borrowed[base, c], sizes[c], done)
+            block_of(base, c)[None], snapshots, ws, borrowed[base, c], UNIT, w_at, done)
         done = (high,)
         pairs[base, c] = both
         arrived[base ^ last, c] = swap(high, "samp", samp, last)
-    gram = local_gram([pairs[b] for b in blocks])
-    ids = jnp.stack([first_unit(*b) for b in blocks] + [me_n, me_s])
+    own = [pairs[0, c] for c in range(2)]
+    got_high = [arrived[0, c] for c in range(2)]
+
+    ids = jnp.stack([block_of(*b) for b in blocks] + [me_n])
     slot = {b: k for k, b in enumerate(blocks)}
     rows = min(UNIT, 512)
     t = project(ids, [(pairs[b], slot[b], borrowed[b]) for b in blocks], snapshots, rank, None, rows)
 
+    packed = own_gram(own, got_high, 1.0 / total, (t,))
+    upper = (me_s & 1) == 1
+    halves = jnp.split(packed, 2, axis=0)
+    half = jnp.where(upper, halves[1], halves[0])
+    stages = []
+    half = half + swap(jnp.where(upper, halves[0], halves[1]), "samp", samp, 1)
+    stages.append(half)
+    bit = 2
+    while bit < samp:
+        half = half + swap(half, "samp", samp, bit)
+        stages.append(half)
+        bit *= 2
+    bit = 1
+    while bit < node:
+        half = half + swap(half, "node", node, bit)
+        stages.append(half)
+        bit *= 2
+    other = swap(half, "samp", samp, 1)
+
     order = [(base ^ last, c) for base, c in blocks]
     early, late = order[:-1], order[-1:]
-
-    def groups(chosen):
-        own = [b for b in chosen if b[0] == 0]
-        far = [b for b in chosen if b[0] == last]
-        return [pairs[b] for b in own], [arrived[b] for b in own], [pairs[b] for b in far], [arrived[b] for b in far]
-
-    gram = cross_gram(*groups(early), gram, after=(t,))
     t = project(
-        ids, [(arrived[b], slot[b], borrowed[b]) for b in early], snapshots, rank, t, rows, after=(gram,))
+        ids, [(arrived[b], slot[b], borrowed[b]) for b in early], snapshots, rank, t, rows,
+        after=(stages[EARLY_STAGE],))
     per_node = P1 // node
     width_cols = P2 // samp
     tall = rank // folding(rank, per_node * width_cols)
-    packed_rows = packing(rank)[2] * BAND
-    ends = groups(late)
-    beside = [v for group in ends for v in group] + [gram]
-    message = jax.ShapeDtypeStruct((node * tall + packed_rows // 2, 128), F32)
     messages = project(
-        ids, [(arrived[b], slot[b], borrowed[b]) for b in late], snapshots, rank, t, rows, beside,
-        functools.partial(
-            tail, node, samp, per_node, width_cols, 1.0 / total, (len(ends[0]), len(ends[2]))),
-        [message] * last,
-        [pltpu.VMEM((node, tall, 128), F32), pltpu.VMEM((packed_rows, 128), F32)])
-
-    held = messages[0]
+        ids, [(arrived[b], slot[b], borrowed[b]) for b in late], snapshots, rank, t, rows, (),
+        functools.partial(tail, node, samp, per_node, width_cols),
+        [jax.ShapeDtypeStruct((node * tall, 128), F32)] * last,
+        [pltpu.VMEM((node, tall, 128), F32)], (stages[LATE_STAGE],))
+    inverse = factor_inverse(me_s[None], half, other, rank, (messages[0],))
+
+    got_low = []
+    for c in range(2):
+        low, _ = lax.optimization_barrier((pairs[last, c][rank:], arrived[late[0]]))
+        got_low.append(swap(low, "samp", samp, last))
+
+    pieces = messages[0]
     for d in near:
-        held = held + swap(messages[d], "samp", samp, d)
-    edge = node * tall
-    pieces, half = held[:edge], held[edge:]
-    bit = 2
-    while bit < samp:
-        half = half + swap(half, "samp", samp, bit)
-        bit *= 2
-    crossed = half
+        pieces = pieces + swap(messages[d], "samp", samp, d)
     bit = 1
     while bit < node:
-        edge //= 2
-        got = swap(jnp.concatenate([pieces[edge:], half], axis=0), "node", node, bit)
-        pieces, half = pieces[:edge] + got[:edge], half + got[edge:]
+        edge = pieces.shape[0] // 2
+        pieces = pieces[:edge] + swap(pieces[edge:], "node", node, bit)
         bit *= 2
-    other = swap(half, "samp", samp, 1)
     spread = node // samp
     route = [
         (n * samp + s, (s * spread + n // samp) * samp + n % samp) for n in range(node) for s in range(samp)
     ]
     piece = lax.ppermute(pieces, ("node", "samp"), route)
-
-    got_low = []
-    for c in range(2):
-        low, _ = lax.optimization_barrier((pairs[last, c][rank:], crossed))
-        got_low.append(swap(low, "samp", samp, last))
-
-    inverse = factor_inverse(me_s[None], half, other, rank)
-    core, coef = finish(
-        inverse, piece, [pairs[0, c] for c in range(2)], [arrived[0, c] for c in range(2)], got_low,
-        1.0 / total, per_node, width_cols)
+    core = core_product(inverse, own, got_high, got_low)
+    coef = coefficients(inverse, piece, 1.0 / total, per_node, width_cols)
     return (core.T, coef.T)
 
 

time: 87.2 us -> 224 us (2.57); the launches traced: 86.8 us -> 221 us
  Pallas kernels: 32.2 us -> 166 us
  local copies, waits for them, and re-layouts: 9.8 us -> 3.93 us
  waiting for transfers between devices: 20.1 us -> 23.9 us
  starting transfers between devices: 23.6 us -> 26 us
    pallas_call x3 -> x5, Pallas kernels: 4.87 us -> 137 us  [the longest x2 130 us: lend(): pl.pallas_call(functools.partial(lend_kernel, size, stride, at), in_specs...]
    dynamic_slice x4 -> x0, local copies, waits for them, and re-layouts: 9.63 us -> none  [body(): made = lax.dynamic_slice_in_dim(snapshots, at, sizes[c], 0)]
    ppermute x17 -> x20, waiting for transfers between devices: 20.1 us -> 23.9 us  [swap(): return lax.ppermute(value, axis, [(i, i ^ bit) for i in range(size)])]
    unnamed x6 -> x22, local copies, waits for them, and re-layouts: 0.01 us -> 3.77 us
    ppermute x17 -> x20, starting transfers between devices: 17.7 us -> 21.1 us  [swap(): return lax.ppermute(value, axis, [(i, i ^ bit) for i in range(size)])]
  transfers between devices with their start and end apart: 18 -> 21, of which waited for: 8 -> 5; matrix products, arithmetic and copies ran while one was open for 9% -> 0% of each run, Pallas kernels for 30% -> 57%
where the time goes in v5:
time: 224 us; the launch traced here: 221 us
  Pallas kernels  166 us (74%)
  starting transfers between devices  26 us (12%)
  waiting for transfers between devices  23.9 us (11%)
  local copies, waits for them, and re-layouts  3.93 us (2%)
    pallas_call x2, Pallas kernels, lend(): pl.pallas_call(functools.partial(lend_kernel, size, stride, at), in_specs...  130 us
    ppermute x20, waiting for transfers between devices, swap(): return lax.ppermute(value, axis, [(i, i ^ bit) for i in range(size)])  23.9 us
    ppermute x20, starting transfers between devices, swap(): return lax.ppermute(value, axis, [(i, i ^ bit) for i in range(size)])  21.1 us
    pallas_call x3, Pallas kernels, project(): pl.pallas_call(functools.partial(project_kernel, count, wide, len(bases),...  13 us
    pallas_call x4, Pallas kernels, sketch(): pl.pallas_call(functools.partial(sketch_kernel, count), grid_spec=pltpu.P...  10.6 us
    pallas_call x1, Pallas kernels, factor_inverse(): pl.pallas_call(functools.partial(factor_kernel, rank), in_specs=[pl.Block...  5.5 us
    ppermute x1, starting transfers between devices, body(): piece = lax.ppermute(pieces, ('node', 'samp'), route)  4.92 us
  transfers between devices with their start and end apart: 21, of which 5 were waited for; matrix products, arithmetic and copies ran while one was open for 0% of the time, Pallas kernels for 57%

profile of v5, /device:TPU:3, one launch (start us, length us, event | category | flops | bytes accessed | tf_op | source)
XLA Modules:
  0.0 220.7 jit_solution(7523165763999130065)
XLA Ops:
  1.6 32.9 %lend.2.refs_0_ = bf16[1280,512]{1,0:T(8,128)(2,1)} custom-call(s32[1]{0:T(128)} %bitcast.3.ids_ref, bf16[8192,512]{1,0:T(8,128)(2,1)} %refs_1_.1, bf16[160,512]{1,0:T(8,128)(2,1)S(1)} %bitcast.13), custom_call_target="tpu_custom_call" | custom-call | bytes 2621440 | tf_op jit(solution)/shard_map/lend/pallas_call | solution.py:71
  35.3 97.0 %lend.3 = (bf16[1024,512]{1,0:T(8,128)(2,1)}, bf16[1024,512]{1,0:T(8,128)(2,1)}, bf16[1024,512]{1,0:T(8,128)(2,1)}) custom-call(s32[3]{0:T(128)S(1)} %pad_add_fusion.ids_ref, bf16[8192,512]{1,0:T(8,128)(2,1)} %refs_1_.1, bf16[1280,512]{1,0:T(8,128)(2,1)} %lend.2.refs_0_), custom_call_target="tpu_custom_call" | custom-call | bytes 6291456 | tf_op jit(solution)/shard_map/lend/pallas_call | solution.py:71
  134.0 2.8 %sketch.4 = (bf16[320,1024]{1,0:T(8,128)(2,1)S(1)}, bf16[160,1024]{1,0:T(8,128)(2,1)}) custom-call(s32[1]{0:T(128)} %bitcast.8.ids_ref, bf16[8192,512]{1,0:T(8,128)(2,1)} %refs_1_.1, bf16[160,512]{1,0:T(8,128)(2,1)S(1)} %bitcast.14, bf16[1280,512]{1,0:T(8,128)(2,1)S(1)} %collective-permute-done.refs_1_.refs_2_.refs_8_, ...), custom_call_target="tpu_custom_call" | custom-call | flops 335544320 | bytes 3080192 | tf_op jit(solution)/shard_map/sketch/pallas_call | solution.py:101
  136.8 3.3 %sketch.5 = (bf16[320,1024]{1,0:T(8,128)(2,1)S(1)}, bf16[160,1024]{1,0:T(8,128)(2,1)}) custom-call(s32[1]{0:T(128)} %bitcast.7.ids_ref, bf16[8192,512]{1,0:T(8,128)(2,1)} %refs_1_.1, bf16[160,512]{1,0:T(8,128)(2,1)S(1)} %bitcast.15, bf16[1280,512]{1,0:T(8,128)(2,1)S(1)} %collective-permute-done.refs_1_.refs_2_.refs_8_, ...), custom_call_target="tpu_custom_call" | custom-call | flops 335544320 | bytes 3080192 | tf_op jit(solution)/shard_map/sketch/pallas_call | solution.py:101
  143.2 2.0 sketch.6
  145.3 2.5 %sketch.7 = (bf16[320,1024]{1,0:T(8,128)(2,1)S(1)}, bf16[160,1024]{1,0:T(8,128)(2,1)S(1)}) custom-call(s32[1]{0:T(128)} %bitcast.9.ids_ref, bf16[8192,512]{1,0:T(8,128)(2,1)} %refs_1_.1, bf16[160,512]{1,0:T(8,128)(2,1)S(1)} %bitcast.17, bf16[1280,512]{1,0:T(8,128)(2,1)S(1)} %collective-permute-done.refs_1_.refs_2_.refs_8_, ...), custom_call_target="tpu_custom_call" | custom-call | flops 335544320 | bytes 3080192 | tf_op jit(solution)/shard_map/sketch/pallas_call | solution.py:101
  147.8 5.9 %project.3.refs_4_.refs_9_ = f32[2,160,512]{2,1,0:T(8,128)S(1)} custom-call(s32[5]{0:T(128)S(1)} %stack.31.ids_ref, bf16[320,1024]{1,0:T(8,128)(2,1)S(1)} %copy-done.8, bf16[320,1024]{1,0:T(8,128)(2,1)S(1)} %copy-done.10, bf16[320,1024]{1,0:T(8,128)(2,1)S(1)} %get-tuple-element.21.refs_2_.refs_0_, bf16[320,1024]{1,0:T(8,128)(2,1)S(1)} %get-tuple-element.24.refs_3_.refs_1_, ...), custom_call_target="tpu_custom_call" | custom-call | flops 2684354560 | bytes 11010048 | tf_op jit(solution)/shard_map/project/pallas_call | solution.py:301
  153.7 2.3 %gram.1 = f32[128,128]{1,0:T(8,128)S(1)} custom-call(bf16[320,1024]{1,0:T(8,128)(2,1)S(1)} %get-tuple-element.21.refs_2_.refs_0_, bf16[320,1024]{1,0:T(8,128)(2,1)S(1)} %get-tuple-element.24.refs_3_.refs_1_, bf16[160,1024]{1,0:T(8,128)(2,1)} %collective-permute-done.4.refs_2_.refs_0_, bf16[160,1024]{1,0:T(8,128)(2,1)} %collective-permute-done.5.refs_3_.refs_1_, ...), custom_call_target="tpu_custom_call" | custom-call | flops 419430400 | bytes 1966080 | tf_op jit(solution)/shard_map/gram/pallas_call | solution.py:166
  157.1 1.5 collective-permute-start.12
  158.6 15.4 %collective-permute-done.7 = f32[64,128]{1,0:T(8,128)S(1)} collective-permute-done((f32[64,128]{1,0:T(8,128)S(1)}, f32[64,128]{1,0:T(8,128)S(1)}, u32[]{:S(2)}, u32[]{:S(2)}) %collective-permute-start.7) | collective-permute-done | bytes 32800 | tf_op jit(solution)/shard_map/ppermute | solution.py:412
  175.3 1.5 collective-permute-done.8
  176.9 1.3 collective-permute-start.9
  178.2 1.5 collective-permute-done.9
  179.6 2.3 %collective-permute-start.10 = (f32[64,128]{1,0:T(8,128)S(1)}, f32[64,128]{1,0:T(8,128)S(1)}, u32[]{:S(2)}, u32[]{:S(2)}) collective-permute-start(f32[64,128]{1,0:T(8,128)S(1)} %add.48), channel_id=1, source_target_pairs={{0,16},{4,20},{8,24},{12,28},{16,0},{20,4},{24,8},{28,12},{1,17},{... | collective-permute-start | bytes 98312 | tf_op jit(solution)/shard_map/ppermute | solution.py:412
  182.0 3.6 %project.4.refs_3_ = f32[2,160,512]{2,1,0:T(8,128)S(1)} custom-call(s32[5]{0:T(128)S(1)} %stack.31.ids_ref, bf16[160,1024]{1,0:T(8,128)(2,1)} %collective-permute-done.4.refs_2_.refs_0_, bf16[160,1024]{1,0:T(8,128)(2,1)} %collective-permute-done.5.refs_3_.refs_1_, bf16[160,1024]{1,0:T(8,128)(2,1)S(1)} %collective-permute-done.13.refs_2_, ...), custom_call_target="tpu_custom_call" | custom-call | flops 1006632960 | bytes 7274496 | tf_op jit(solution)/shard_map/project/pallas_call | solution.py:301
  185.6 3.5 %project.5 = (f32[640,128]{1,0:T(8,128)S(1)}, f32[640,128]{1,0:T(8,128)S(1)}) custom-call(s32[5]{0:T(128)S(1)} %stack.31.ids_ref, bf16[160,1024]{1,0:T(8,128)(2,1)S(1)} %collective-permute-done.12.refs_0_, bf16[8192,512]{1,0:T(8,128)(2,1)} %refs_1_.1, bf16[1024,512]{1,0:T(8,128)(2,1)} %collective-permute-done.2.refs_2_.refs_9_, ...), custom_call_target="tpu_custom_call" | custom-call | flops 335544320 | bytes 2424832 | tf_op jit(solution)/shard_map/project/pallas_call | solution.py:301
  189.1 3.7 %collective-permute-start.16 = (f32[640,128]{1,0:T(8,128)S(1)}, f32[640,128]{1,0:T(8,128)S(1)}, u32[]{:S(2)}, u32[]{:S(2)}) collective-permute-start(f32[640,128]{1,0:T(8,128)S(1)} %get-tuple-element.31), channel_id=1, source_target_pairs={{0,1},{1,0},{2,3},{3,2},{4,5},{5,4},{6,7},{7,6},{8,9},{9,8},{10,11... | collective-permute-start | bytes 983048 | tf_op jit(solution)/shard_map/ppermute | solution.py:412
  194.1 1.3 collective-permute-start.17
  195.4 4.2 %collective-permute-done.17 = f32[320,128]{1,0:T(8,128)S(1)} collective-permute-done((f32[320,128]{1,0:T(8,128)S(1)}, f32[320,128]{1,0:T(8,128)S(1)}, u32[]{:S(2)}, u32[]{:S(2)}) %collective-permute-start.17) | collective-permute-done | bytes 163872 | tf_op jit(solution)/shard_map/ppermute | solution.py:412
  202.4 2.0 collective-permute-start.11
  204.4 1.3 collective-permute-start.19
  205.7 5.5 %factor.1.inv_ref = f32[160,160]{1,0:T(8,128)S(1)} custom-call(s32[1]{0:T(128)} %bitcast.me_ref, f32[64,128]{1,0:T(8,128)S(1)} %add.49.refs_4_.mine_ref, f32[64,128]{1,0:T(8,128)S(1)} %collective-permute-done.11.other_ref, f32[640,128]{1,0:T(8,128)S(1)} %get-tuple-element.28.refs_0_), custom_call_target="tpu_custom_call" | custom-call | flops 8000000000 | bytes 102400 | tf_op jit(solution)/shard_map/factor/pallas_call | solution.py:240
  211.3 4.9 %collective-permute-start.20 = (f32[80,128]{1,0:T(8,128)S(1)}, f32[80,128]{1,0:T(8,128)S(1)}, u32[]{:S(2)}, u32[]{:S(2)}) collective-permute-start(f32[80,128]{1,0:T(8,128)S(1)} %slice_add_fusion.2), channel_id=1, source_target_pairs={{0,0},{1,8},{2,16},{3,24},{4,1},{5,9},{6,17},{7,25},{8,2},{9,10},{... | collective-permute-start | bytes 122888 | tf_op jit(solution)/shard_map/ppermute | solution.py:509
  216.2 3.5 %core.1 = f32[160,2048]{1,0:T(8,128)} custom-call(f32[160,160]{1,0:T(8,128)S(1)} %factor.1.inv_ref, bf16[320,1024]{1,0:T(8,128)(2,1)S(1)} %get-tuple-element.21.refs_2_.refs_0_, bf16[320,1024]{1,0:T(8,128)(2,1)S(1)} %get-tuple-element.24.refs_3_.refs_1_, bf16[160,1024]{1,0:T(8,128)(2,1)} %collective-permute-done.4.refs_2_.refs_0_, ...), custom_call_target="tpu_custom_call" | custom-call | flops 629145600 | bytes 3932160 | tf_op jit(solution)/shard_map/core/pallas_call | solution.py:380
  (70 shorter events, 14.2 us)
Async XLA Ops:
  34.5 98.5 %collective-permute-start = (bf16[1280,512]{1,0:T(8,128)(2,1)}, bf16[1280,512]{1,0:T(8,128)(2,1)S(1)}, u32[]{:S(2)}, u32[]{:S(2)}) collective-permute-start(bf16[1280,512]{1,0:T(8,128)(2,1)} %lend.2.refs_0_), channel_id=1, source_target_pairs={{0,1},{1,0},{2,3},{3,2},{4,5},{5,4},{6,7},{7,6},{8,9},{9,8},{10,11... | collective-permute-start | bytes 3932168 | tf_op jit(solution)/shard_map/ppermute | solution.py:412
  132.3 4.5 %collective-permute-start.2 = (bf16[1024,512]{1,0:T(8,128)(2,1)}, bf16[1024,512]{1,0:T(8,128)(2,1)}, u32[]{:S(2)}, u32[]{:S(2)}) collective-permute-start(bf16[1024,512]{1,0:T(8,128)(2,1)} %get-tuple-element.18), channel_id=1, source_target_pairs={{0,1},{1,0},{2,3},{3,2},{4,5},{5,4},{6,7},{7,6},{8,9},{9,8},{10,11... | collective-permute-start | bytes 3145736 | tf_op jit(solution)/shard_map/ppermute | solution.py:412
  132.4 9.9 %collective-permute-start.1 = (bf16[1024,512]{1,0:T(8,128)(2,1)}, bf16[1024,512]{1,0:T(8,128)(2,1)S(1)}, u32[]{:S(2)}, u32[]{:S(2)}) collective-permute-start(bf16[1024,512]{1,0:T(8,128)(2,1)} %get-tuple-element.17), channel_id=1, source_target_pairs={{0,1},{1,0},{2,3},{3,2},{4,5},{5,4},{6,7},{7,6},{8,9},{9,8},{10,11... | collective-permute-start | bytes 3145736 | tf_op jit(solution)/shard_map/ppermute | solution.py:412
  132.8 12.4 %collective-permute-start.3 = (bf16[1024,512]{1,0:T(8,128)(2,1)}, bf16[1024,512]{1,0:T(8,128)(2,1)S(1)}, u32[]{:S(2)}, u32[]{:S(2)}) collective-permute-start(bf16[1024,512]{1,0:T(8,128)(2,1)} %get-tuple-element.22), channel_id=1, source_target_pairs={{0,1},{1,0},{2,3},{3,2},{4,5},{5,4},{6,7},{7,6},{8,9},{9,8},{10,11... | collective-permute-start | bytes 3145736 | tf_op jit(solution)/shard_map/ppermute | solution.py:412
  132.9 12.3 %copy-start = (bf16[1280,512]{1,0:T(8,128)(2,1)}, bf16[1280,512]{1,0:T(8,128)(2,1)S(1)}, u32[]{:S(2)}) copy-start(bf16[1280,512]{1,0:T(8,128)(2,1)S(1)} %collective-permute-done.refs_1_.refs_2_.refs_8_) | copy-start | bytes 3932164
  136.8 16.9 %collective-permute-start.4 = (bf16[160,1024]{1,0:T(8,128)(2,1)}, bf16[160,1024]{1,0:T(8,128)(2,1)}, u32[]{:S(2)}, u32[]{:S(2)}) collective-permute-start(bf16[160,1024]{1,0:T(8,128)(2,1)} %get-tuple-element.19.refs_3_), channel_id=1, source_target_pairs={{0,2},{1,3},{2,0},{3,1},{4,6},{5,7},{6,4},{7,5},{8,10},{9,11},{10,... | collective-permute-start | bytes 983048 | tf_op jit(solution)/shard_map/ppermute | solution.py:412
  141.0 12.7 %collective-permute-start.5 = (bf16[160,1024]{1,0:T(8,128)(2,1)}, bf16[160,1024]{1,0:T(8,128)(2,1)}, u32[]{:S(2)}, u32[]{:S(2)}) collective-permute-start(bf16[160,1024]{1,0:T(8,128)(2,1)} %get-tuple-element.20.refs_3_), channel_id=1, source_target_pairs={{0,2},{1,3},{2,0},{3,1},{4,6},{5,7},{6,4},{7,5},{8,10},{9,11},{10,... | collective-permute-start | bytes 983048 | tf_op jit(solution)/shard_map/ppermute | solution.py:412
  153.7 28.3 %copy-start.1 = (bf16[1280,512]{1,0:T(8,128)(2,1)S(1)}, bf16[1280,512]{1,0:T(8,128)(2,1)}, u32[]{:S(2)}) copy-start(bf16[1280,512]{1,0:T(8,128)(2,1)} %copy-done) | copy-start | bytes 3932164
  153.7 28.3 %copy-start.3 = (bf16[1024,512]{1,0:T(8,128)(2,1)S(1)}, bf16[1024,512]{1,0:T(8,128)(2,1)}, u32[]{:S(2)}) copy-start(bf16[1024,512]{1,0:T(8,128)(2,1)} %copy-done.2) | copy-start | bytes 3145732
  156.0 2.5 %collective-permute-start.6 = (f32[64,128]{1,0:T(8,128)S(1)}, f32[64,128]{1,0:T(8,128)S(1)}, u32[]{:S(2)}, u32[]{:S(2)}) collective-permute-start(f32[64,128]{1,0:T(8,128)S(1)} %slice_select_fusion), channel_id=1, source_target_pairs={{0,1},{1,0},{2,3},{3,2},{4,5},{5,4},{6,7},{7,6},{8,9},{9,8},{10,11... | collective-permute-start | bytes 98312 | tf_op jit(solution)/shard_map/ppermute | solution.py:412
  157.1 24.9 %collective-permute-start.13 = (bf16[160,1024]{1,0:T(8,128)(2,1)S(1)}, bf16[160,1024]{1,0:T(8,128)(2,1)S(1)}, u32[]{:S(2)}, u32[]{:S(2)}) collective-permute-start(bf16[160,1024]{1,0:T(8,128)(2,1)S(1)} %get-tuple-element.23.refs_3_), channel_id=1, source_target_pairs={{0,2},{1,3},{2,0},{3,1},{4,6},{5,7},{6,4},{7,5},{8,10},{9,11},{10,... | collective-permute-start | bytes 983048 | tf_op jit(solution)/shard_map/ppermute | solution.py:412
  157.1 28.6 %collective-permute-start.12 = (bf16[160,1024]{1,0:T(8,128)(2,1)S(1)}, bf16[160,1024]{1,0:T(8,128)(2,1)S(1)}, u32[]{:S(2)}, u32[]{:S(2)}) collective-permute-start(bf16[160,1024]{1,0:T(8,128)(2,1)S(1)} %get-tuple-element.27), channel_id=1, source_target_pairs={{0,2},{1,3},{2,0},{3,1},{4,6},{5,7},{6,4},{7,5},{8,10},{9,11},{10,... | collective-permute-start | bytes 983048 | tf_op jit(solution)/shard_map/ppermute | solution.py:412
  158.6 15.5 %collective-permute-start.7 = (f32[64,128]{1,0:T(8,128)S(1)}, f32[64,128]{1,0:T(8,128)S(1)}, u32[]{:S(2)}, u32[]{:S(2)}) collective-permute-start(f32[64,128]{1,0:T(8,128)S(1)} %select_add_fusion), channel_id=1, source_target_pairs={{0,2},{1,3},{2,0},{3,1},{4,6},{5,7},{6,4},{7,5},{8,10},{9,11},{10,... | collective-permute-start | bytes 98312 | tf_op jit(solution)/shard_map/ppermute | solution.py:412
  174.1 2.8 %collective-permute-start.8 = (f32[64,128]{1,0:T(8,128)S(1)}, f32[64,128]{1,0:T(8,128)S(1)}, u32[]{:S(2)}, u32[]{:S(2)}) collective-permute-start(f32[64,128]{1,0:T(8,128)S(1)} %add.46.refs_10_), channel_id=1, source_target_pairs={{0,4},{4,0},{8,12},{12,8},{16,20},{20,16},{24,28},{28,24},{1,5},{5... | collective-permute-start | bytes 98312 | tf_op jit(solution)/shard_map/ppermute | solution.py:412
  176.9 2.8 %collective-permute-start.9 = (f32[64,128]{1,0:T(8,128)S(1)}, f32[64,128]{1,0:T(8,128)S(1)}, u32[]{:S(2)}, u32[]{:S(2)}) collective-permute-start(f32[64,128]{1,0:T(8,128)S(1)} %add.47), channel_id=1, source_target_pairs={{0,8},{4,12},{8,0},{12,4},{16,24},{20,28},{24,16},{28,20},{1,9},{5... | collective-permute-start | bytes 98312 | tf_op jit(solution)/shard_map/ppermute | solution.py:412
  179.6 6.0 %collective-permute-start.10 = (f32[64,128]{1,0:T(8,128)S(1)}, f32[64,128]{1,0:T(8,128)S(1)}, u32[]{:S(2)}, u32[]{:S(2)}) collective-permute-start(f32[64,128]{1,0:T(8,128)S(1)} %add.48), channel_id=1, source_target_pairs={{0,16},{4,20},{8,24},{12,28},{16,0},{20,4},{24,8},{28,12},{1,17},{... | collective-permute-start | bytes 98312 | tf_op jit(solution)/shard_map/ppermute | solution.py:412
  189.1 4.9 %collective-permute-start.16 = (f32[640,128]{1,0:T(8,128)S(1)}, f32[640,128]{1,0:T(8,128)S(1)}, u32[]{:S(2)}, u32[]{:S(2)}) collective-permute-start(f32[640,128]{1,0:T(8,128)S(1)} %get-tuple-element.31), channel_id=1, source_target_pairs={{0,1},{1,0},{2,3},{3,2},{4,5},{5,4},{6,7},{7,6},{8,9},{9,8},{10,11... | collective-permute-start | bytes 983048 | tf_op jit(solution)/shard_map/ppermute | solution.py:412
  194.1 5.5 %collective-permute-start.17 = (f32[320,128]{1,0:T(8,128)S(1)}, f32[320,128]{1,0:T(8,128)S(1)}, u32[]{:S(2)}, u32[]{:S(2)}) collective-permute-start(f32[320,128]{1,0:T(8,128)S(1)} %slice.33), channel_id=1, source_target_pairs={{0,4},{4,0},{8,12},{12,8},{16,20},{20,16},{24,28},{28,24},{1,5},{5... | collective-permute-start | bytes 491528 | tf_op jit(solution)/shard_map/ppermute | solution.py:412
  199.6 4.8 %collective-permute-start.18 = (f32[160,128]{1,0:T(8,128)S(1)}, f32[160,128]{1,0:T(8,128)S(1)}, u32[]{:S(2)}, u32[]{:S(2)}) collective-permute-start(f32[160,128]{1,0:T(8,128)S(1)} %slice.35), channel_id=1, source_target_pairs={{0,8},{4,12},{8,0},{12,4},{16,24},{20,28},{24,16},{28,20},{1,9},{5... | collective-permute-start | bytes 245768 | tf_op jit(solution)/shard_map/ppermute | solution.py:412
  200.8 15.3 %collective-permute-start.14 = (bf16[160,1024]{1,0:T(8,128)(2,1)S(1)}, bf16[160,1024]{1,0:T(8,128)(2,1)S(1)}, u32[]{:S(2)}, u32[]{:S(2)}) collective-permute-start(bf16[160,1024]{1,0:T(8,128)(2,1)S(1)} %slice.24), channel_id=1, source_target_pairs={{0,2},{1,3},{2,0},{3,1},{4,6},{5,7},{6,4},{7,5},{8,10},{9,11},{10,... | collective-permute-start | bytes 983048 | tf_op jit(solution)/shard_map/ppermute | solution.py:412
  201.2 15.0 %collective-permute-start.15 = (bf16[160,1024]{1,0:T(8,128)(2,1)S(1)}, bf16[160,1024]{1,0:T(8,128)(2,1)S(1)}, u32[]{:S(2)}, u32[]{:S(2)}) collective-permute-start(bf16[160,1024]{1,0:T(8,128)(2,1)S(1)} %slice.25), channel_id=1, source_target_pairs={{0,2},{1,3},{2,0},{3,1},{4,6},{5,7},{6,4},{7,5},{8,10},{9,11},{10,... | collective-permute-start | bytes 983048 | tf_op jit(solution)/shard_map/ppermute | solution.py:412
  202.4 3.4 %collective-permute-start.11 = (f32[64,128]{1,0:T(8,128)S(1)}, f32[64,128]{1,0:T(8,128)S(1)}, u32[]{:S(2)}, u32[]{:S(2)}) collective-permute-start(f32[64,128]{1,0:T(8,128)S(1)} %add.49.refs_4_.mine_ref), channel_id=1, source_target_pairs={{0,1},{1,0},{2,3},{3,2},{4,5},{5,4},{6,7},{7,6},{8,9},{9,8},{10,11... | collective-permute-start | bytes 98312 | tf_op jit(solution)/shard_map/ppermute | solution.py:412
  204.4 6.8 %collective-permute-start.19 = (f32[80,128]{1,0:T(8,128)S(1)}, f32[80,128]{1,0:T(8,128)S(1)}, u32[]{:S(2)}, u32[]{:S(2)}) collective-permute-start(f32[80,128]{1,0:T(8,128)S(1)} %slice.37), channel_id=1, source_target_pairs={{0,16},{4,20},{8,24},{12,28},{16,0},{20,4},{24,8},{28,12},{1,17},{... | collective-permute-start | bytes 122888 | tf_op jit(solution)/shard_map/ppermute | solution.py:412
  211.3 8.4 %collective-permute-start.20 = (f32[80,128]{1,0:T(8,128)S(1)}, f32[80,128]{1,0:T(8,128)S(1)}, u32[]{:S(2)}, u32[]{:S(2)}) collective-permute-start(f32[80,128]{1,0:T(8,128)S(1)} %slice_add_fusion.2), channel_id=1, source_target_pairs={{0,0},{1,8},{2,16},{3,24},{4,1},{5,9},{6,17},{7,25},{8,2},{9,10},{... | collective-permute-start | bytes 122888 | tf_op jit(solution)/shard_map/ppermute | solution.py:509
  (8 other events, 14.6 us)

commit v6 on v5

--- a/solution.py
+++ b/solution.py
@@ -11,7 +11,9 @@
 BAND = 32
 UNIT = 1024
 SKETCH_ROWS = 1024
-EARLY_STAGE, LATE_STAGE = 1, 4
+LEND_PARTS = 4
+FACTOR_FIRST = True
+FACTOR_COST = 8e5
 COST_CUT = 1
 F32 = jnp.float32
 BF16 = jnp.bfloat16
@@ -61,7 +63,7 @@
 def lend(ids, x, size, w=None, after=()):
     count = ids.shape[0]
     depth = x.shape[1]
-    stride = size // 2
+    stride = size // LEND_PARTS
     at, height = None, size
     if w is not None:
         rank = w.shape[0]
@@ -71,9 +73,9 @@
     return pl.pallas_call(
         functools.partial(lend_kernel, size, stride, at),
         in_specs=[pl.BlockSpec(memory_space=pltpu.SMEM)] + [UNREAD] * (1 + len(more) + len(after)),
-        out_specs=[pl.BlockSpec(memory_space=pl.ANY)] * count,
+        out_specs=[HELD] * count,
         out_shape=[jax.ShapeDtypeStruct((height, depth), BF16)] * count,
-        scratch_shapes=[pltpu.SemaphoreType.DMA((2 * count + len(more),))],
+        scratch_shapes=[pltpu.SemaphoreType.DMA((LEND_PARTS * count + len(more),))],
         compiler_params=params(),
         cost_estimate=cost(0, 4 * count * height * depth),
         name="lend",
@@ -147,30 +149,30 @@
     return (x[:rank, :rank] + x[rank:, rank:]) + (x[:rank, rank:] + x[rank:, :rank])
 
 
-def gram_kernel(scale, count, *refs):
+def gram_kernel(scale, has_base, own_ref, got_ref, *refs):
     o_ref = refs[-1]
-    rank = refs[count].shape[0]
-    total = None
-    for own_ref, got_ref in zip(refs[:count], refs[count:2 * count]):
-        s = own_ref[:rank, :].astype(F32) + own_ref[rank:, :].astype(F32) + got_ref[...].astype(F32)
-        high = s.astype(BF16)
-        both = jnp.concatenate([high, (s - high.astype(F32)).astype(BF16)], axis=0)
-        term = dot(both, both, ((1,), (1,)))
-        total = term if total is None else total + term
-    o_ref[...] = pack_gram(fold_square(total, rank) * scale)
-
-
-def own_gram(own, got, scale, after=()):
-    rank = got[0].shape[0]
-    rows = sum(v.shape[1] for v in got)
-    return pl.pallas_call(
-        functools.partial(gram_kernel, scale, len(own)),
-        in_specs=[HELD] * (2 * len(own)) + [UNREAD] * len(after),
-        out_shape=jax.ShapeDtypeStruct((packing(rank)[2] * BAND, 128), F32),
+    rank = got_ref.shape[0]
+    s = own_ref[:rank, :].astype(F32) + own_ref[rank:, :].astype(F32) + got_ref[...].astype(F32)
+    high = s.astype(BF16)
+    both = jnp.concatenate([high, (s - high.astype(F32)).astype(BF16)], axis=0)
+    total = fold_square(dot(both, both, ((1,), (1,))), rank)
+    if has_base:
+        total = total + refs[0][...]
+    o_ref[...] = total if scale is None else pack_gram(total * scale)
+
+
+def own_gram(own, got, base, scale, after=()):
+    rank, rows = got.shape
+    bases = [] if base is None else [base]
+    shape = (rank, rank) if scale is None else (packing(rank)[2] * BAND, 128)
+    return pl.pallas_call(
+        functools.partial(gram_kernel, scale, len(bases)),
+        in_specs=[HELD] * (2 + len(bases)) + [UNREAD] * len(after),
+        out_shape=jax.ShapeDtypeStruct(shape, F32),
         compiler_params=params(),
         cost_estimate=cost(8 * rank * rank * rows, 6 * rank * rows),
         name="gram",
-    )(*own, *got, *after)
+    )(own, got, *bases, *after)
 
 
 def wide_lanes(x, n):
@@ -211,13 +213,9 @@
     return jnp.concatenate(part, axis=0)
 
 
-def factor_kernel(rank, me_ref, mine_ref, other_ref, *refs):
-    o_ref, g_ref = refs[-2:]
-    pairs, wide, groups = packing(rank)
-    half = groups * BAND // 2
-    mine_at = pl.multiple_of((me_ref[0] & 1) * half, half)
-    g_ref[pl.ds(mine_at, half), :] = mine_ref[...]
-    g_ref[pl.ds(pl.multiple_of(half - mine_at, half), half), :] = other_ref[...]
+def factor_kernel(rank, g_ref, *refs):
+    o_ref = refs[-1]
+    pairs, wide, _ = packing(rank)
     o_ref[...] = jnp.zeros((rank, rank), F32)
     for at, (i, j) in enumerate(pairs):
         g, k = at // wide, at % wide
@@ -236,16 +234,15 @@
             o_ref[hi:, :] = kept - update[hi:, :]
 
 
-def factor_inverse(me, mine, other, rank, after=()):
+def factor_inverse(packed, rank, after=()):
     return pl.pallas_call(
         functools.partial(factor_kernel, rank),
-        in_specs=[pl.BlockSpec(memory_space=pltpu.SMEM)] + [HELD] * 2 + [UNREAD] * len(after),
+        in_specs=[HELD] + [UNREAD] * len(after),
         out_shape=jax.ShapeDtypeStruct((rank, rank), F32),
-        scratch_shapes=[pltpu.VMEM((2 * mine.shape[0], 128), F32)],
-        compiler_params=params(),
-        cost_estimate=cost(8e9, 4 * rank * rank),
+        compiler_params=params(),
+        cost_estimate=cost(FACTOR_COST, 4 * rank * rank),
         name="factor",
-    )(me, mine, other, *after)
+    )(packed, *after)
 
 
 def project_kernel(count, wide, has_base, aside, finish, ids_ref, *refs):
@@ -440,45 +437,47 @@
             borrowed[b].append(swap(v, "samp", samp, d))
         ws.append(borrowed[blocks[0]][-1])
 
-    pairs, arrived, done = {}, {}, ()
-    for base, c in blocks:
-        both, high = sketch(
-            block_of(base, c)[None], snapshots, ws, borrowed[base, c], UNIT, w_at, done)
-        done = (high,)
-        pairs[base, c] = both
-        arrived[base ^ last, c] = swap(high, "samp", samp, last)
-    own = [pairs[0, c] for c in range(2)]
-    got_high = [arrived[0, c] for c in range(2)]
+    pairs, highs, arrived, done = {}, {}, {}, ()
+
+    def cross(b):
+        arrived[b[0] ^ last, b[1]] = swap(highs[b], "samp", samp, last)
 
     ids = jnp.stack([block_of(*b) for b in blocks] + [me_n])
     slot = {b: k for k, b in enumerate(blocks)}
     rows = min(UNIT, 512)
+    for b in blocks:
+        pairs[b], highs[b] = sketch(block_of(*b)[None], snapshots, ws, borrowed[b], UNIT, w_at, done)
+        done = (highs[b],)
+        if b[0] == last:
+            cross(b)
+    own = [pairs[0, c] for c in range(2)]
+    got_high = [arrived[0, c] for c in range(2)]
     t = project(ids, [(pairs[b], slot[b], borrowed[b]) for b in blocks], snapshots, rank, None, rows)
 
-    packed = own_gram(own, got_high, 1.0 / total, (t,))
-    upper = (me_s & 1) == 1
-    halves = jnp.split(packed, 2, axis=0)
-    half = jnp.where(upper, halves[1], halves[0])
-    stages = []
-    half = half + swap(jnp.where(upper, halves[0], halves[1]), "samp", samp, 1)
-    stages.append(half)
-    bit = 2
-    while bit < samp:
-        half = half + swap(half, "samp", samp, bit)
-        stages.append(half)
-        bit *= 2
+    gram = own_gram(own[0], got_high[0], None, None, (t,))
+    gram = own_gram(own[1], got_high[1], gram, 1.0 / total)
+    gram = gram + swap(gram, "samp", samp, last)
+    for b in blocks:
+        if b[0] == 0:
+            highs[b], _ = lax.optimization_barrier((highs[b], gram))
+            cross(b)
+    bit = last // 2
+    while bit:
+        gram = gram + swap(gram, "samp", samp, bit)
+        bit //= 2
+    stages = [gram]
     bit = 1
     while bit < node:
-        half = half + swap(half, "node", node, bit)
-        stages.append(half)
+        gram = gram + swap(gram, "node", node, bit)
+        stages.append(gram)
         bit *= 2
-    other = swap(half, "samp", samp, 1)
+    inverse = factor_inverse(gram, rank)
 
     order = [(base ^ last, c) for base, c in blocks]
     early, late = order[:-1], order[-1:]
     t = project(
         ids, [(arrived[b], slot[b], borrowed[b]) for b in early], snapshots, rank, t, rows,
-        after=(stages[EARLY_STAGE],))
+        after=(stages[0],))
     per_node = P1 // node
     width_cols = P2 // samp
     tall = rank // folding(rank, per_node * width_cols)
@@ -486,8 +485,7 @@
         ids, [(arrived[b], slot[b], borrowed[b]) for b in late], snapshots, rank, t, rows, (),
         functools.partial(tail, node, samp, per_node, width_cols),
         [jax.ShapeDtypeStruct((node * tall, 128), F32)] * last,
-        [pltpu.VMEM((node, tall, 128), F32)], (stages[LATE_STAGE],))
-    inverse = factor_inverse(me_s[None], half, other, rank, (messages[0],))
+        [pltpu.VMEM((node, tall, 128), F32)], (inverse,) if FACTOR_FIRST else ())
 
     got_low = []
     for c in range(2):

time: 224 us -> 94.8 us (0.42)
  the two profiles are of different devices: /device:TPU:3 before, /device:TPU:0 now
where the time goes in v6:
time: 94.8 us; the launch traced here: 94.4 us
  Pallas kernels  39 us (41%)
  waiting for transfers between devices  29.3 us (31%)
  starting transfers between devices  22.9 us (24%)
  local copies, waits for them, and re-layouts  2 us (2%)
    ppermute x19, waiting for transfers between devices, swap(): return lax.ppermute(value, axis, [(i, i ^ bit) for i in range(size)])  29.3 us
    ppermute x19, starting transfers between devices, swap(): return lax.ppermute(value, axis, [(i, i ^ bit) for i in range(size)])  22.2 us
    pallas_call x3, Pallas kernels, project(): pl.pallas_call(functools.partial(project_kernel, count, wide, len(bases),...  12.8 us
    pallas_call x4, Pallas kernels, sketch(): pl.pallas_call(functools.partial(sketch_kernel, count), grid_spec=pltpu.P...  9.37 us
    pallas_call x2, Pallas kernels, lend(): pl.pallas_call(functools.partial(lend_kernel, size, stride, at), in_specs...  6.39 us
    pallas_call x1, Pallas kernels, factor_inverse(): pl.pallas_call(functools.partial(factor_kernel, rank), in_specs=[HELD] +...  5.49 us
    pallas_call x1, Pallas kernels, core_product(): pl.pallas_call(functools.partial(core_kernel, count), out_shape=jax.Shape...  2.39 us
  transfers between devices with their start and end apart: 20, of which 12 were waited for; matrix products, arithmetic and copies ran while one was open for 0% of the time, Pallas kernels for 33%

profile of v6, /device:TPU:0, one launch (start us, length us, event | category | flops | bytes accessed | tf_op | source)
XLA Modules:
  0.0 94.4 jit_solution(1706770375660593922)
XLA Ops:
  1.6 2.3 %lend.2.refs_0_ = bf16[1280,512]{1,0:T(8,128)(2,1)} custom-call(s32[1]{0:T(128)} %bitcast.2.ids_ref, bf16[8192,512]{1,0:T(8,128)(2,1)} %refs_1_.1, bf16[160,512]{1,0:T(8,128)(2,1)S(1)} %bitcast.12), custom_call_target="tpu_custom_call" | custom-call | bytes 2621440 | tf_op jit(solution)/shard_map/lend/pallas_call | solution.py:73
  4.4 4.1 %lend.3 = (bf16[1024,512]{1,0:T(8,128)(2,1)}, bf16[1024,512]{1,0:T(8,128)(2,1)}, bf16[1024,512]{1,0:T(8,128)(2,1)}) custom-call(s32[3]{0:T(128)S(1)} %pad_add_fusion.ids_ref, bf16[8192,512]{1,0:T(8,128)(2,1)} %refs_1_.1, bf16[1280,512]{1,0:T(8,128)(2,1)} %lend.2.refs_0_), custom_call_target="tpu_custom_call" | custom-call | bytes 6291456 | tf_op jit(solution)/shard_map/lend/pallas_call | solution.py:73
  10.2 2.5 %sketch.4 = (bf16[320,1024]{1,0:T(8,128)(2,1)S(1)}, bf16[160,1024]{1,0:T(8,128)(2,1)S(1)}) custom-call(s32[1]{0:T(128)} %bitcast.8.ids_ref, bf16[8192,512]{1,0:T(8,128)(2,1)} %refs_1_.1, bf16[160,512]{1,0:T(8,128)(2,1)S(1)} %bitcast.13, bf16[1280,512]{1,0:T(8,128)(2,1)S(1)} %collective-permute-done.refs_1_.refs_2_.refs_8_, ...), custom_call_target="tpu_custom_call" | custom-call | flops 335544320 | bytes 3080192 | tf_op jit(solution)/shard_map/sketch/pallas_call | solution.py:103
  12.8 3.0 %collective-permute-start.5 = (bf16[160,1024]{1,0:T(8,128)(2,1)S(1)}, bf16[160,1024]{1,0:T(8,128)(2,1)S(1)}, u32[]{:S(2)}, u32[]{:S(2)}) collective-permute-start(bf16[160,1024]{1,0:T(8,128)(2,1)S(1)} %get-tuple-element.22.refs_3_), channel_id=1, source_target_pairs={{0,2},{1,3},{2,0},{3,1},{4,6},{5,7},{6,4},{7,5},{8,10},{9,11},{10,... | collective-permute-start | bytes 983048 | tf_op jit(solution)/shard_map/ppermute | solution.py:409
  15.7 2.4 %sketch.5 = (bf16[320,1024]{1,0:T(8,128)(2,1)S(1)}, bf16[160,1024]{1,0:T(8,128)(2,1)S(1)}) custom-call(s32[1]{0:T(128)} %bitcast.7.ids_ref, bf16[8192,512]{1,0:T(8,128)(2,1)} %refs_1_.1, bf16[160,512]{1,0:T(8,128)(2,1)S(1)} %bitcast.14, bf16[1280,512]{1,0:T(8,128)(2,1)S(1)} %collective-permute-done.refs_1_.refs_2_.refs_8_, ...), custom_call_target="tpu_custom_call" | custom-call | flops 335544320 | bytes 3080192 | tf_op jit(solution)/shard_map/sketch/pallas_call | solution.py:103
  18.2 2.1 %sketch.6 = (bf16[320,1024]{1,0:T(8,128)(2,1)S(1)}, bf16[160,1024]{1,0:T(8,128)(2,1)S(1)}) custom-call(s32[1]{0:T(128)} %bitcast.6.ids_ref, bf16[8192,512]{1,0:T(8,128)(2,1)} %refs_1_.1, bf16[160,512]{1,0:T(8,128)(2,1)S(1)} %bitcast.15, bf16[1280,512]{1,0:T(8,128)(2,1)S(1)} %collective-permute-done.refs_1_.refs_2_.refs_8_, ...), custom_call_target="tpu_custom_call" | custom-call | flops 335544320 | bytes 3080192 | tf_op jit(solution)/shard_map/sketch/pallas_call | solution.py:103
  20.3 2.4 %sketch.7 = (bf16[320,1024]{1,0:T(8,128)(2,1)S(1)}, bf16[160,1024]{1,0:T(8,128)(2,1)S(1)}) custom-call(s32[1]{0:T(128)} %bitcast.ids_ref, bf16[8192,512]{1,0:T(8,128)(2,1)} %refs_1_.1, bf16[160,512]{1,0:T(8,128)(2,1)S(1)} %bitcast.16, bf16[1280,512]{1,0:T(8,128)(2,1)S(1)} %collective-permute-done.refs_1_.refs_2_.refs_8_, ...), custom_call_target="tpu_custom_call" | custom-call | flops 335544320 | bytes 3080192 | tf_op jit(solution)/shard_map/sketch/pallas_call | solution.py:103
  22.8 5.9 %project.3.refs_0_.refs_9_ = f32[2,160,512]{2,1,0:T(8,128)S(1)} custom-call(s32[5]{0:T(128)S(1)} %stack.31.ids_ref, bf16[320,1024]{1,0:T(8,128)(2,1)S(1)} %get-tuple-element.27.refs_0_, bf16[320,1024]{1,0:T(8,128)(2,1)S(1)} %get-tuple-element.28.refs_1_, bf16[320,1024]{1,0:T(8,128)(2,1)S(1)} %get-tuple-element.26.refs_2_.own_ref.refs_0_, ...), custom_call_target="tpu_custom_call" | custom-call | flops 2684354560 | bytes 11010048 | tf_op jit(solution)/shard_map/project/pallas_call | solution.py:298
  31.5 1.8 %collective-permute-start.6 = (f32[128,128]{1,0:T(8,128)S(1)}, f32[128,128]{1,0:T(8,128)S(1)}, u32[]{:S(2)}, u32[]{:S(2)}) collective-permute-start(f32[128,128]{1,0:T(8,128)S(1)} %gram.3), channel_id=1, source_target_pairs={{0,2},{1,3},{2,0},{3,1},{4,6},{5,7},{6,4},{7,5},{8,10},{9,11},{10,... | collective-permute-start | bytes 196616 | tf_op jit(solution)/shard_map/ppermute | solution.py:409
  33.3 2.5 %collective-permute-done.6 = f32[128,128]{1,0:T(8,128)S(1)} collective-permute-done((f32[128,128]{1,0:T(8,128)S(1)}, f32[128,128]{1,0:T(8,128)S(1)}, u32[]{:S(2)}, u32[]{:S(2)}) %collective-permute-start.6) | collective-permute-done | bytes 65568 | tf_op jit(solution)/shard_map/ppermute | solution.py:409
  35.8 1.8 %collective-permute-start.14 = (bf16[160,1024]{1,0:T(8,128)(2,1)S(1)}, bf16[160,1024]{1,0:T(8,128)(2,1)S(1)}, u32[]{:S(2)}, u32[]{:S(2)}) collective-permute-start(bf16[160,1024]{1,0:T(8,128)(2,1)S(1)} %get-tuple-element.33.refs_3_), channel_id=1, source_target_pairs={{0,2},{1,3},{2,0},{3,1},{4,6},{5,7},{6,4},{7,5},{8,10},{9,11},{10,... | collective-permute-start | bytes 983048 | tf_op jit(solution)/shard_map/ppermute | solution.py:409
  40.5 2.7 %collective-permute-done.8 = f32[128,128]{1,0:T(8,128)S(1)} collective-permute-done((f32[128,128]{1,0:T(8,128)S(1)}, f32[128,128]{1,0:T(8,128)S(1)}, u32[]{:S(2)}, u32[]{:S(2)}) %collective-permute-start.8) | collective-permute-done | bytes 65568 | tf_op jit(solution)/shard_map/ppermute | solution.py:409
  44.9 2.7 %collective-permute-done.9 = f32[128,128]{1,0:T(8,128)S(1)} collective-permute-done((f32[128,128]{1,0:T(8,128)S(1)}, f32[128,128]{1,0:T(8,128)S(1)}, u32[]{:S(2)}, u32[]{:S(2)}) %collective-permute-start.9) | collective-permute-done | bytes 65568 | tf_op jit(solution)/shard_map/ppermute | solution.py:409
  47.6 2.6 %collective-permute-start.10 = (f32[128,128]{1,0:T(8,128)S(1)}, f32[128,128]{1,0:T(8,128)S(1)}, u32[]{:S(2)}, u32[]{:S(2)}) collective-permute-start(f32[128,128]{1,0:T(8,128)S(1)} %add.48), channel_id=1, source_target_pairs={{0,16},{4,20},{8,24},{12,28},{16,0},{20,4},{24,8},{28,12},{1,17},{... | collective-permute-start | bytes 196616 | tf_op jit(solution)/shard_map/ppermute | solution.py:409
  50.3 2.6 %collective-permute-done.10 = f32[128,128]{1,0:T(8,128)S(1)} collective-permute-done((f32[128,128]{1,0:T(8,128)S(1)}, f32[128,128]{1,0:T(8,128)S(1)}, u32[]{:S(2)}, u32[]{:S(2)}) %collective-permute-start.10) | collective-permute-done | bytes 65568 | tf_op jit(solution)/shard_map/ppermute | solution.py:409
  52.8 5.5 %factor.1.inv_ref.refs_4_ = f32[160,160]{1,0:T(8,128)S(1)} custom-call(f32[128,128]{1,0:T(8,128)S(1)} %add.49.g_ref), custom_call_target="tpu_custom_call" | custom-call | flops 800000 | bytes 102400 | tf_op jit(solution)/shard_map/factor/pallas_call | solution.py:238
  58.4 3.5 %project.4.refs_3_ = f32[2,160,512]{2,1,0:T(8,128)S(1)} custom-call(s32[5]{0:T(128)S(1)} %stack.31.ids_ref, bf16[160,1024]{1,0:T(8,128)(2,1)S(1)} %collective-permute-done.5.got_ref.refs_2_.refs_0_, bf16[160,1024]{1,0:T(8,128)(2,1)S(1)} %collective-permute-done.4.got_ref.refs_3_.refs_1_, bf16[160,1024]{1,0:T(8,128)(2,1)S(1)} %collective-permute-done.14.refs_2_, ...), custom_call_target="tpu_custom_call" | custom-call | flops 1006632960 | bytes 7274496 | tf_op jit(solution)/shard_map/project/pallas_call | solution.py:298
  61.9 3.5 %project.5 = (f32[640,128]{1,0:T(8,128)S(1)}, f32[640,128]{1,0:T(8,128)S(1)}) custom-call(s32[5]{0:T(128)S(1)} %stack.31.ids_ref, bf16[160,1024]{1,0:T(8,128)(2,1)S(1)} %collective-permute-done.11.refs_0_, bf16[8192,512]{1,0:T(8,128)(2,1)} %refs_1_.1, bf16[1024,512]{1,0:T(8,128)(2,1)} %collective-permute-done.3.refs_2_.refs_9_, ...), custom_call_target="tpu_custom_call" | custom-call | flops 335544320 | bytes 2424832 | tf_op jit(solution)/shard_map/project/pallas_call | solution.py:298
  68.7 4.7 %collective-permute-done.16 = f32[320,128]{1,0:T(8,128)S(1)} collective-permute-done((f32[320,128]{1,0:T(8,128)S(1)}, f32[320,128]{1,0:T(8,128)S(1)}, u32[]{:S(2)}, u32[]{:S(2)}) %collective-permute-start.16) | collective-permute-done | bytes 163872 | tf_op jit(solution)/shard_map/ppermute | solution.py:409
  78.0 2.8 %collective-permute-start.18 = (f32[80,128]{1,0:T(8,128)S(1)}, f32[80,128]{1,0:T(8,128)S(1)}, u32[]{:S(2)}, u32[]{:S(2)}) collective-permute-start(f32[80,128]{1,0:T(8,128)S(1)} %slice.37), channel_id=1, source_target_pairs={{0,16},{4,20},{8,24},{12,28},{16,0},{20,4},{24,8},{28,12},{1,17},{... | collective-permute-start | bytes 122888 | tf_op jit(solution)/shard_map/ppermute | solution.py:409
  80.8 2.2 %collective-permute-done.18 = f32[80,128]{1,0:T(8,128)S(1)} collective-permute-done((f32[80,128]{1,0:T(8,128)S(1)}, f32[80,128]{1,0:T(8,128)S(1)}, u32[]{:S(2)}, u32[]{:S(2)}) %collective-permute-start.18) | collective-permute-done | bytes 40992 | tf_op jit(solution)/shard_map/ppermute | solution.py:409
  83.6 2.2 %collective-permute-done.13.refs_5_ = bf16[160,1024]{1,0:T(8,128)(2,1)S(1)} collective-permute-done((bf16[160,1024]{1,0:T(8,128)(2,1)S(1)}, bf16[160,1024]{1,0:T(8,128)(2,1)S(1)}, u32[]{:S(2)}, u32[]{:S(2)}) %collective-permute-start.13) | collective-permute-done | bytes 327712 | tf_op jit(solution)/shard_map/ppermute | solution.py:409
  85.9 5.0 %collective-permute-done.12.refs_4_ = bf16[160,1024]{1,0:T(8,128)(2,1)S(1)} collective-permute-done((bf16[160,1024]{1,0:T(8,128)(2,1)S(1)}, bf16[160,1024]{1,0:T(8,128)(2,1)S(1)}, u32[]{:S(2)}, u32[]{:S(2)}) %collective-permute-start.12) | collective-permute-done | bytes 327712 | tf_op jit(solution)/shard_map/ppermute | solution.py:409
  90.9 2.4 %core.1 = f32[160,2048]{1,0:T(8,128)} custom-call(f32[160,160]{1,0:T(8,128)S(1)} %factor.1.inv_ref.refs_4_, bf16[320,1024]{1,0:T(8,128)(2,1)S(1)} %get-tuple-element.26.refs_2_.own_ref.refs_0_, bf16[320,1024]{1,0:T(8,128)(2,1)S(1)} %get-tuple-element.25.refs_3_.own_ref.refs_1_, bf16[160,1024]{1,0:T(8,128)(2,1)S(1)} %collective-permute-done.5.got_ref.refs_2_.refs_0_, ...), custom_call_target="tpu_custom_call" | custom-call | flops 629145600 | bytes 3932160 | tf_op jit(solution)/shard_map/core/pallas_call | solution.py:377
  (58 shorter events, 20.2 us)
Async XLA Ops:
  3.8 5.5 %collective-permute-start = (bf16[1280,512]{1,0:T(8,128)(2,1)}, bf16[1280,512]{1,0:T(8,128)(2,1)S(1)}, u32[]{:S(2)}, u32[]{:S(2)}) collective-permute-start(bf16[1280,512]{1,0:T(8,128)(2,1)} %lend.2.refs_0_), channel_id=1, source_target_pairs={{0,1},{1,0},{2,3},{3,2},{4,5},{5,4},{6,7},{7,6},{8,9},{9,8},{10,11... | collective-permute-start | bytes 3932168 | tf_op jit(solution)/shard_map/ppermute | solution.py:409
  8.6 7.2 %collective-permute-start.3 = (bf16[1024,512]{1,0:T(8,128)(2,1)}, bf16[1024,512]{1,0:T(8,128)(2,1)}, u32[]{:S(2)}, u32[]{:S(2)}) collective-permute-start(bf16[1024,512]{1,0:T(8,128)(2,1)} %get-tuple-element.21), channel_id=1, source_target_pairs={{0,1},{1,0},{2,3},{3,2},{4,5},{5,4},{6,7},{7,6},{8,9},{9,8},{10,11... | collective-permute-start | bytes 3145736 | tf_op jit(solution)/shard_map/ppermute | solution.py:409
  8.7 9.5 %collective-permute-start.2 = (bf16[1024,512]{1,0:T(8,128)(2,1)}, bf16[1024,512]{1,0:T(8,128)(2,1)S(1)}, u32[]{:S(2)}, u32[]{:S(2)}) collective-permute-start(bf16[1024,512]{1,0:T(8,128)(2,1)} %get-tuple-element.20), channel_id=1, source_target_pairs={{0,1},{1,0},{2,3},{3,2},{4,5},{5,4},{6,7},{7,6},{8,9},{9,8},{10,11... | collective-permute-start | bytes 3145736 | tf_op jit(solution)/shard_map/ppermute | solution.py:409
  9.1 11.1 %collective-permute-start.1 = (bf16[1024,512]{1,0:T(8,128)(2,1)}, bf16[1024,512]{1,0:T(8,128)(2,1)S(1)}, u32[]{:S(2)}, u32[]{:S(2)}) collective-permute-start(bf16[1024,512]{1,0:T(8,128)(2,1)} %get-tuple-element.19), channel_id=1, source_target_pairs={{0,1},{1,0},{2,3},{3,2},{4,5},{5,4},{6,7},{7,6},{8,9},{9,8},{10,11... | collective-permute-start | bytes 3145736 | tf_op jit(solution)/shard_map/ppermute | solution.py:409
  10.2 10.1 %copy-start = (bf16[1280,512]{1,0:T(8,128)(2,1)}, bf16[1280,512]{1,0:T(8,128)(2,1)S(1)}, u32[]{:S(2)}) copy-start(bf16[1280,512]{1,0:T(8,128)(2,1)S(1)} %collective-permute-done.refs_1_.refs_2_.refs_8_) | copy-start | bytes 3932164
  12.8 15.9 %collective-permute-start.5 = (bf16[160,1024]{1,0:T(8,128)(2,1)S(1)}, bf16[160,1024]{1,0:T(8,128)(2,1)S(1)}, u32[]{:S(2)}, u32[]{:S(2)}) collective-permute-start(bf16[160,1024]{1,0:T(8,128)(2,1)S(1)} %get-tuple-element.22.refs_3_), channel_id=1, source_target_pairs={{0,2},{1,3},{2,0},{3,1},{4,6},{5,7},{6,4},{7,5},{8,10},{9,11},{10,... | collective-permute-start | bytes 983048 | tf_op jit(solution)/shard_map/ppermute | solution.py:409
  18.1 12.6 %collective-permute-start.4 = (bf16[160,1024]{1,0:T(8,128)(2,1)S(1)}, bf16[160,1024]{1,0:T(8,128)(2,1)S(1)}, u32[]{:S(2)}, u32[]{:S(2)}) collective-permute-start(bf16[160,1024]{1,0:T(8,128)(2,1)S(1)} %get-tuple-element.23.refs_3_), channel_id=1, source_target_pairs={{0,2},{1,3},{2,0},{3,1},{4,6},{5,7},{6,4},{7,5},{8,10},{9,11},{10,... | collective-permute-start | bytes 983048 | tf_op jit(solution)/shard_map/ppermute | solution.py:409
  20.3 2.5 %copy-start.2 = (bf16[1024,512]{1,0:T(8,128)(2,1)}, bf16[1024,512]{1,0:T(8,128)(2,1)S(1)}, u32[]{:S(2)}) copy-start(bf16[1024,512]{1,0:T(8,128)(2,1)S(1)} %collective-permute-done.1.refs_2_.refs_11_.refs_7_) | copy-start | bytes 3145732
  29.4 29.0 %copy-start.1 = (bf16[1280,512]{1,0:T(8,128)(2,1)S(1)}, bf16[1280,512]{1,0:T(8,128)(2,1)}, u32[]{:S(2)}) copy-start(bf16[1280,512]{1,0:T(8,128)(2,1)} %copy-done) | copy-start | bytes 3932164
  29.4 29.0 %copy-start.3 = (bf16[1024,512]{1,0:T(8,128)(2,1)S(1)}, bf16[1024,512]{1,0:T(8,128)(2,1)}, u32[]{:S(2)}) copy-start(bf16[1024,512]{1,0:T(8,128)(2,1)} %copy-done.2) | copy-start | bytes 3145732
  31.5 4.3 %collective-permute-start.6 = (f32[128,128]{1,0:T(8,128)S(1)}, f32[128,128]{1,0:T(8,128)S(1)}, u32[]{:S(2)}, u32[]{:S(2)}) collective-permute-start(f32[128,128]{1,0:T(8,128)S(1)} %gram.3), channel_id=1, source_target_pairs={{0,2},{1,3},{2,0},{3,1},{4,6},{5,7},{6,4},{7,5},{8,10},{9,11},{10,... | collective-permute-start | bytes 196616 | tf_op jit(solution)/shard_map/ppermute | solution.py:409
  35.8 22.5 %collective-permute-start.14 = (bf16[160,1024]{1,0:T(8,128)(2,1)S(1)}, bf16[160,1024]{1,0:T(8,128)(2,1)S(1)}, u32[]{:S(2)}, u32[]{:S(2)}) collective-permute-start(bf16[160,1024]{1,0:T(8,128)(2,1)S(1)} %get-tuple-element.33.refs_3_), channel_id=1, source_target_pairs={{0,2},{1,3},{2,0},{3,1},{4,6},{5,7},{6,4},{7,5},{8,10},{9,11},{10,... | collective-permute-start | bytes 983048 | tf_op jit(solution)/shard_map/ppermute | solution.py:409
  37.6 1.3 %collective-permute-start.7 = (f32[128,128]{1,0:T(8,128)S(1)}, f32[128,128]{1,0:T(8,128)S(1)}, u32[]{:S(2)}, u32[]{:S(2)}) collective-permute-start(f32[128,128]{1,0:T(8,128)S(1)} %add.45), channel_id=1, source_target_pairs={{0,1},{1,0},{2,3},{3,2},{4,5},{5,4},{6,7},{7,6},{8,9},{9,8},{10,11... | collective-permute-start | bytes 196616 | tf_op jit(solution)/shard_map/ppermute | solution.py:409
  37.6 24.2 %collective-permute-start.11 = (bf16[160,1024]{1,0:T(8,128)(2,1)S(1)}, bf16[160,1024]{1,0:T(8,128)(2,1)S(1)}, u32[]{:S(2)}, u32[]{:S(2)}) collective-permute-start(bf16[160,1024]{1,0:T(8,128)(2,1)S(1)} %get-tuple-element.30), channel_id=1, source_target_pairs={{0,2},{1,3},{2,0},{3,1},{4,6},{5,7},{6,4},{7,5},{8,10},{9,11},{10,... | collective-permute-start | bytes 983048 | tf_op jit(solution)/shard_map/ppermute | solution.py:409
  38.9 4.3 %collective-permute-start.8 = (f32[128,128]{1,0:T(8,128)S(1)}, f32[128,128]{1,0:T(8,128)S(1)}, u32[]{:S(2)}, u32[]{:S(2)}) collective-permute-start(f32[128,128]{1,0:T(8,128)S(1)} %add.46.refs_10_), channel_id=1, source_target_pairs={{0,4},{4,0},{8,12},{12,8},{16,20},{20,16},{24,28},{28,24},{1,5},{5... | collective-permute-start | bytes 196616 | tf_op jit(solution)/shard_map/ppermute | solution.py:409
  43.3 4.3 %collective-permute-start.9 = (f32[128,128]{1,0:T(8,128)S(1)}, f32[128,128]{1,0:T(8,128)S(1)}, u32[]{:S(2)}, u32[]{:S(2)}) collective-permute-start(f32[128,128]{1,0:T(8,128)S(1)} %add.47), channel_id=1, source_target_pairs={{0,8},{4,12},{8,0},{12,4},{16,24},{20,28},{24,16},{28,20},{1,9},{5... | collective-permute-start | bytes 196616 | tf_op jit(solution)/shard_map/ppermute | solution.py:409
  47.6 5.2 %collective-permute-start.10 = (f32[128,128]{1,0:T(8,128)S(1)}, f32[128,128]{1,0:T(8,128)S(1)}, u32[]{:S(2)}, u32[]{:S(2)}) collective-permute-start(f32[128,128]{1,0:T(8,128)S(1)} %add.48), channel_id=1, source_target_pairs={{0,16},{4,20},{8,24},{12,28},{16,0},{20,4},{24,8},{28,12},{1,17},{... | collective-permute-start | bytes 196616 | tf_op jit(solution)/shard_map/ppermute | solution.py:409
  65.4 1.7 %collective-permute-start.15 = (f32[640,128]{1,0:T(8,128)S(1)}, f32[640,128]{1,0:T(8,128)S(1)}, u32[]{:S(2)}, u32[]{:S(2)}) collective-permute-start(f32[640,128]{1,0:T(8,128)S(1)} %get-tuple-element.35), channel_id=1, source_target_pairs={{0,1},{1,0},{2,3},{3,2},{4,5},{5,4},{6,7},{7,6},{8,9},{9,8},{10,11... | collective-permute-start | bytes 983048 | tf_op jit(solution)/shard_map/ppermute | solution.py:409
  67.1 6.3 %collective-permute-start.16 = (f32[320,128]{1,0:T(8,128)S(1)}, f32[320,128]{1,0:T(8,128)S(1)}, u32[]{:S(2)}, u32[]{:S(2)}) collective-permute-start(f32[320,128]{1,0:T(8,128)S(1)} %slice.33), channel_id=1, source_target_pairs={{0,4},{4,0},{8,12},{12,8},{16,20},{20,16},{24,28},{28,24},{1,5},{5... | collective-permute-start | bytes 491528 | tf_op jit(solution)/shard_map/ppermute | solution.py:409
  73.5 4.5 %collective-permute-start.17 = (f32[160,128]{1,0:T(8,128)S(1)}, f32[160,128]{1,0:T(8,128)S(1)}, u32[]{:S(2)}, u32[]{:S(2)}) collective-permute-start(f32[160,128]{1,0:T(8,128)S(1)} %slice.35), channel_id=1, source_target_pairs={{0,8},{4,12},{8,0},{12,4},{16,24},{20,28},{24,16},{28,20},{1,9},{5... | collective-permute-start | bytes 245768 | tf_op jit(solution)/shard_map/ppermute | solution.py:409
  75.1 10.7 %collective-permute-start.13 = (bf16[160,1024]{1,0:T(8,128)(2,1)S(1)}, bf16[160,1024]{1,0:T(8,128)(2,1)S(1)}, u32[]{:S(2)}, u32[]{:S(2)}) collective-permute-start(bf16[160,1024]{1,0:T(8,128)(2,1)S(1)} %slice.25), channel_id=1, source_target_pairs={{0,2},{1,3},{2,0},{3,1},{4,6},{5,7},{6,4},{7,5},{8,10},{9,11},{10,... | collective-permute-start | bytes 983048 | tf_op jit(solution)/shard_map/ppermute | solution.py:409
  76.0 14.9 %collective-permute-start.12 = (bf16[160,1024]{1,0:T(8,128)(2,1)S(1)}, bf16[160,1024]{1,0:T(8,128)(2,1)S(1)}, u32[]{:S(2)}, u32[]{:S(2)}) collective-permute-start(bf16[160,1024]{1,0:T(8,128)(2,1)S(1)} %slice.24), channel_id=1, source_target_pairs={{0,2},{1,3},{2,0},{3,1},{4,6},{5,7},{6,4},{7,5},{8,10},{9,11},{10,... | collective-permute-start | bytes 983048 | tf_op jit(solution)/shard_map/ppermute | solution.py:409
  78.0 5.0 %collective-permute-start.18 = (f32[80,128]{1,0:T(8,128)S(1)}, f32[80,128]{1,0:T(8,128)S(1)}, u32[]{:S(2)}, u32[]{:S(2)}) collective-permute-start(f32[80,128]{1,0:T(8,128)S(1)} %slice.37), channel_id=1, source_target_pairs={{0,16},{4,20},{8,24},{12,28},{16,0},{20,4},{24,8},{28,12},{1,17},{... | collective-permute-start | bytes 122888 | tf_op jit(solution)/shard_map/ppermute | solution.py:409
  83.0 10.3 %collective-permute-start.19 = (f32[80,128]{1,0:T(8,128)S(1)}, f32[80,128]{1,0:T(8,128)S(1)}, u32[]{:S(2)}, u32[]{:S(2)}) collective-permute-start(f32[80,128]{1,0:T(8,128)S(1)} %slice_add_fusion.2), channel_id=1, source_target_pairs={{0,0},{1,8},{2,16},{3,24},{4,1},{5,9},{6,17},{7,25},{8,2},{9,10},{... | collective-permute-start | bytes 122888 | tf_op jit(solution)/shard_map/ppermute | solution.py:507
  (2 other events, 1.8 us)

commit v7 on v6

--- a/solution.py
+++ b/solution.py
@@ -10,10 +10,10 @@
 P2 = 32
 BAND = 32
 UNIT = 1024
-SKETCH_ROWS = 1024
 LEND_PARTS = 4
-FACTOR_FIRST = True
-FACTOR_COST = 8e5
+PLACE = (True, 2, True, 1, 2)
+PROJECT_ROWS = 512
+FACTOR_COST = 6e9
 COST_CUT = 1
 F32 = jnp.float32
 BF16 = jnp.bfloat16
@@ -82,10 +82,12 @@
     )(ids, x, *more, *after)
 
 
-def sketch_kernel(count, ids_ref, x_ref, *refs):
+def sketch_kernel(count, lent, ids_ref, x_ref, *refs):
     w_refs, x_refs = refs[:count], (x_ref,) + refs[count:2 * count - 1]
-    both_ref, high_ref = refs[-2:]
+    both_ref, high_ref = refs[len(refs) - lent - 2:len(refs) - lent]
     rank = high_ref.shape[0]
+    for k in range(lent):
+        refs[len(refs) - lent + k][...] = refs[2 * count - 1 + k][...]
     s = None
     for w_ref, ref in zip(w_refs, x_refs):
         term = dot(w_ref[...], ref[...], ((1,), (1,)))
@@ -99,30 +101,32 @@
 def sketch(ids, x, ws, extra, size, w_at, after=()):
     rank, depth = ws[0].shape
     count = len(ws)
-    rows = min(size, SKETCH_ROWS)
-    return pl.pallas_call(
-        functools.partial(sketch_kernel, count),
+    lent = ids.shape[0] - 1
+    return pl.pallas_call(
+        functools.partial(sketch_kernel, count, lent),
         grid_spec=pltpu.PrefetchScalarGridSpec(
             num_scalar_prefetch=1,
-            grid=(size // rows,),
-            in_specs=[pl.BlockSpec((rows, depth), lambda i, ids: (ids[0] + i, 0))]
+            grid=(1,),
+            in_specs=[pl.BlockSpec((size, depth), lambda i, ids: (ids[0], 0))]
             + [pl.BlockSpec((rank, depth), lambda i, ids: (0, 0))]
             + [pl.BlockSpec((rank, depth), lambda i, ids: (w_at // rank, 0))] * (count - 1)
-            + [pl.BlockSpec((rows, depth), lambda i, ids: (i, 0))] * (count - 1)
+            + [pl.BlockSpec((size, depth), lambda i, ids: (0, 0))] * (count - 1)
+            + [pl.BlockSpec((size, depth), lambda i, ids, k=k: (ids[1 + k], 0)) for k in range(lent)]
             + [UNREAD] * len(after),
             out_specs=[
-                pl.BlockSpec((2 * rank, rows), lambda i, ids: (0, i)),
-                pl.BlockSpec((rank, rows), lambda i, ids: (0, i)),
-            ],
+                pl.BlockSpec((2 * rank, size), lambda i, ids: (0, 0)),
+                pl.BlockSpec((rank, size), lambda i, ids: (0, 0)),
+            ] + [pl.BlockSpec((size, depth), lambda i, ids: (0, 0))] * lent,
         ),
-        out_shape=(
+        out_shape=[
             jax.ShapeDtypeStruct((2 * rank, size), BF16),
             jax.ShapeDtypeStruct((rank, size), BF16),
-        ),
-        compiler_params=params(),
-        cost_estimate=cost(2 * rank * depth * size * count, size * (depth * 2 * count + rank * 6)),
+        ] + [jax.ShapeDtypeStruct((size, depth), BF16)] * lent,
+        compiler_params=params(),
+        cost_estimate=cost(
+            2 * rank * depth * size * count, size * (depth * 2 * (count + 2 * lent) + rank * 6)),
         name="sketch",
-    )(ids, x, *ws, *extra, *after)
+    )(ids, x, *ws, *extra, *([x] * lent), *after)
 
 
 def packing(rank):
@@ -245,11 +249,10 @@
     )(packed, *after)
 
 
-def project_kernel(count, wide, has_base, aside, finish, ids_ref, *refs):
-    s_refs, x_refs = refs[:count], refs[count:count * (1 + wide)]
-    at = count * (1 + wide)
-    beside = refs[at + has_base:at + has_base + aside]
-    rest = refs[at + has_base + aside:]
+def project_kernel(count, wide, has_base, unread, finish, ids_ref, *refs):
+    pair_refs, high_refs, x_refs = refs[:count], refs[count:2 * count], refs[2 * count:count * (2 + wide)]
+    at = count * (2 + wide)
+    rest = refs[at + has_base + unread:]
     t_ref = rest[-1]
     rank = t_ref.shape[1]
 
@@ -257,35 +260,30 @@
     def _():
         t_ref[...] = refs[at][...] if has_base else jnp.zeros_like(t_ref)
 
+    sums = []
+    for pair_ref, high_ref in zip(pair_refs, high_refs):
+        s = pair_ref[:rank, :].astype(F32) + pair_ref[rank:, :].astype(F32) + high_ref[...].astype(F32)
+        high = s.astype(BF16)
+        sums.append(jnp.concatenate([high, (s - high.astype(F32)).astype(BF16)], axis=0))
     for w in range(wide):
         total = None
         for k in range(count):
-            term = dot(s_refs[k][...], x_refs[w * count + k][...], ((1,), (0,)))
+            term = dot(sums[k], x_refs[w * count + k][...], ((1,), (0,)))
             total = term if total is None else total + term
-        t_ref[w] += total if total.shape[0] == rank else total[:rank] + total[rank:]
+        t_ref[w] += total[:rank] + total[rank:]
     if finish is not None:
         @pl.when(pl.program_id(0) == pl.num_programs(0) - 1)
         def _():
-            finish(t_ref, ids_ref, beside, *rest[:-1])
-
-
-def project(ids, work, x, rank, base, rows, beside=(), finish=None, outs=(), scratch=(), after=()):
-    wide = 1 + len(work[0][2])
-    height = work[0][0].shape[0]
+            finish(t_ref, ids_ref, *rest[:-1])
+
+
+def project(ids, work, x, base, after=(), finish=None, outs=(), scratch=()):
+    count = len(work)
+    wide = 1 + len(work[0][3])
+    rank, span = work[0][1].shape
     depth = x.shape[1]
-    unit = UNIT
-    steps = unit // rows
-    parts, s_specs, own_specs, more, more_specs = [], [], [], [[] for _ in range(wide - 1)], []
-    for array, slot, lent in work:
-        for u in range(array.shape[1] // unit):
-            parts.append(array)
-            s_specs.append(pl.BlockSpec((height, rows), lambda i, ids, u=u: (0, u * steps + i)))
-            own_specs.append(pl.BlockSpec(
-                (rows, depth), lambda i, ids, u=u, slot=slot: ((ids[slot] + u) * steps + i, 0)))
-            more_specs.append(pl.BlockSpec((rows, depth), lambda i, ids, u=u: (u * steps + i, 0)))
-            for w in range(wide - 1):
-                more[w].append(lent[w])
-    count = len(parts)
+    rows = min(span, PROJECT_ROWS)
+    steps = span // rows
     bases = [] if base is None else [base]
     whole = pl.BlockSpec((wide, rank, depth), lambda i, ids: (0, 0, 0))
     t_shape = jax.ShapeDtypeStruct((wide, rank, depth), F32)
@@ -296,22 +294,29 @@
         out_shape = list(outs)
         scratch_shapes = list(scratch) + [pltpu.VMEM((wide, rank, depth), F32)]
     return pl.pallas_call(
-        functools.partial(
-            project_kernel, count, wide, len(bases), len(beside) + len(after), finish),
+        functools.partial(project_kernel, count, wide, len(bases), len(after), finish),
         grid_spec=pltpu.PrefetchScalarGridSpec(
             num_scalar_prefetch=1,
             grid=(steps,),
-            in_specs=s_specs + own_specs + more_specs * (wide - 1) + [whole] * len(bases)
-            + [pl.BlockSpec(v.shape, lambda i, ids: (0, 0)) for v in beside] + [UNREAD] * len(after),
+            in_specs=[pl.BlockSpec((2 * rank, rows), lambda i, ids: (0, i))] * count
+            + [pl.BlockSpec((rank, rows), lambda i, ids: (0, i))] * count
+            + [
+                pl.BlockSpec((rows, depth), lambda i, ids, slot=w[2]: (ids[slot] * steps + i, 0))
+                for w in work
+            ]
+            + [pl.BlockSpec((rows, depth), lambda i, ids: (i, 0))] * (count * (wide - 1))
+            + [whole] * len(bases) + [UNREAD] * len(after),
             out_specs=out_specs,
             scratch_shapes=scratch_shapes,
         ),
         out_shape=out_shape,
         compiler_params=params(),
         cost_estimate=cost(
-            2 * height * depth * unit * count * wide, unit * count * (depth * wide + height) * 2),
+            4 * rank * depth * span * count * wide, span * count * (depth * wide + 3 * rank) * 2),
         name="project",
-    )(ids, *parts, *([x] * count), *[v for values in more for v in values], *bases, *beside, *after)
+    )(
+        ids, *[w[0] for w in work], *[w[1] for w in work], *([x] * count),
+        *[w[3][d] for d in range(wide - 1) for w in work], *bases, *after)
 
 
 def folding(rank, width):
@@ -326,7 +331,7 @@
     return sum(1 << (count - 1 - b) for b in range(count) if (p >> b) & 1)
 
 
-def tail(pieces, samp, per_node, width_cols, t_ref, ids_ref, beside, *refs):
+def tail(pieces, samp, per_node, width_cols, t_ref, ids_ref, *refs):
     outs, hold = refs[:-1], refs[-1]
     wide, rank, depth = t_ref.shape
     width = per_node * width_cols
@@ -358,14 +363,14 @@
 
 
 def core_kernel(count, inv_ref, *refs):
-    both, high, low = (refs[k * count:(k + 1) * count] for k in range(3))
-    core_ref = refs[-1]
+    both, high = refs[:count], refs[count:2 * count]
+    low_ref, core_ref = refs[-2:]
     rank = inv_ref.shape[0]
     at = 0
     for c in range(count):
         s = both[c][:rank, :].astype(F32) + both[c][rank:, :].astype(F32)
-        s = s + (high[c][...].astype(F32) + low[c][...].astype(F32))
         rows = s.shape[1]
+        s = s + (high[c][...].astype(F32) + low_ref[:, at:at + rows].astype(F32))
         core_ref[:, at:at + rows] = dot(inv_ref[...], s, ((1,), (0,)), HI)
         at += rows
 
@@ -380,7 +385,7 @@
         compiler_params=params(),
         cost_estimate=cost(12 * rank * rank * rows, 12 * rank * rows),
         name="core",
-    )(inverse, *both, *high, *low)
+    )(inverse, *both, *high, low)
 
 
 def coefficient_kernel(scale, per_node, width_cols, inv_ref, piece_ref, o_ref):
@@ -429,13 +434,21 @@
 
     borrowed = {b: [] for b in blocks}
     ws, w_at = [w_t], 0
-    for d in near:
-        out = lend(jnp.stack([block_of(blocks[0][0] ^ d, blocks[0][1])]), snapshots, UNIT, w_t)
-        w_at = out[0].shape[0] - rank
-        out += lend(jnp.stack([block_of(base ^ d, c) for base, c in blocks[1:]]), snapshots, UNIT, after=out)
-        for b, v in zip(blocks, out):
-            borrowed[b].append(swap(v, "samp", samp, d))
-        ws.append(borrowed[blocks[0]][-1])
+
+    def borrow(chosen, after, w=None):
+        out = ()
+        for d in near:
+            out = lend(jnp.stack([block_of(b[0] ^ d, b[1]) for b in chosen]), snapshots, UNIT, w, after)
+            for b, v in zip(chosen, out):
+                borrowed[b].append(swap(v, "samp", samp, d))
+            after = tuple(out[:1])
+        return after
+
+    done = borrow(blocks[:1], (), w_t)
+    for v in borrowed[blocks[0]]:
+        w_at = v.shape[0] - rank
+        ws.append(v)
+    borrow(blocks[1:2], done)
 
     pairs, highs, arrived, done = {}, {}, {}, ()
 
@@ -444,18 +457,24 @@
 
     ids = jnp.stack([block_of(*b) for b in blocks] + [me_n])
     slot = {b: k for k, b in enumerate(blocks)}
-    rows = min(UNIT, 512)
-    for b in blocks:
-        pairs[b], highs[b] = sketch(block_of(*b)[None], snapshots, ws, borrowed[b], UNIT, w_at, done)
+    for k, b in enumerate(blocks):
+        later = blocks[k + 2:k + 3]
+        numbers = [block_of(*b)] + [block_of(o[0] ^ d, o[1]) for o in later for d in near]
+        out = sketch(jnp.stack(numbers), snapshots, ws, borrowed[b], UNIT, w_at, done)
+        pairs[b], highs[b] = out[:2]
         done = (highs[b],)
+        for o in later:
+            borrowed[o] = [swap(v, "samp", samp, d) for d, v in zip(near, out[2:])]
         if b[0] == last:
             cross(b)
     own = [pairs[0, c] for c in range(2)]
     got_high = [arrived[0, c] for c in range(2)]
-    t = project(ids, [(pairs[b], slot[b], borrowed[b]) for b in blocks], snapshots, rank, None, rows)
-
-    gram = own_gram(own[0], got_high[0], None, None, (t,))
-    gram = own_gram(own[1], got_high[1], gram, 1.0 / total)
+
+    def parts(chosen):
+        return [(pairs[b], arrived[b], slot[b], borrowed[b]) for b in chosen]
+
+    gram = own_gram(own[0], got_high[0], None, None)
+    gram = own_gram(own[1], got_high[1], gram, 1.0 / total, done)
     gram = gram + swap(gram, "samp", samp, last)
     for b in blocks:
         if b[0] == 0:
@@ -465,41 +484,43 @@
     while bit:
         gram = gram + swap(gram, "samp", samp, bit)
         bit //= 2
-    stages = [gram]
-    bit = 1
-    while bit < node:
-        gram = gram + swap(gram, "node", node, bit)
-        stages.append(gram)
-        bit *= 2
-    inverse = factor_inverse(gram, rank)
-
-    order = [(base ^ last, c) for base, c in blocks]
-    early, late = order[:-1], order[-1:]
-    t = project(
-        ids, [(arrived[b], slot[b], borrowed[b]) for b in early], snapshots, rank, t, rows,
-        after=(stages[0],))
+    begun = gram
+    t = project(ids, parts([(0, 0), (0, 1)]), snapshots, None, (gram,) if PLACE[0] else ())
+    rounds = node.bit_length() - 1
+    for k in range(rounds):
+        if k == rounds - PLACE[1]:
+            gram, t = lax.optimization_barrier((gram, t))
+        if k == rounds - 1:
+            t = project(ids, parts([(last, 0)]), snapshots, t, (gram,))
+            if PLACE[2]:
+                gram, t = lax.optimization_barrier((gram, t))
+        gram = gram + swap(gram, "node", node, 1 << k)
+    late = [(last, 1)]
+
     per_node = P1 // node
     width_cols = P2 // samp
     tall = rank // folding(rank, per_node * width_cols)
     messages = project(
-        ids, [(arrived[b], slot[b], borrowed[b]) for b in late], snapshots, rank, t, rows, (),
+        ids, parts(late), snapshots, t, (),
         functools.partial(tail, node, samp, per_node, width_cols),
         [jax.ShapeDtypeStruct((node * tall, 128), F32)] * last,
-        [pltpu.VMEM((node, tall, 128), F32)], (inverse,) if FACTOR_FIRST else ())
-
-    got_low = []
-    for c in range(2):
-        low, _ = lax.optimization_barrier((pairs[last, c][rank:], arrived[late[0]]))
-        got_low.append(swap(low, "samp", samp, last))
+        [pltpu.VMEM((node, tall, 128), F32)])
+
+    low = jnp.concatenate([pairs[last, c][rank:] for c in range(2)], axis=1)
+    low, _ = lax.optimization_barrier((low, begun))
+    got_low = swap(low, "samp", samp, last)
 
     pieces = messages[0]
     for d in near:
         pieces = pieces + swap(messages[d], "samp", samp, d)
-    bit = 1
-    while bit < node:
+    inverse = factor_inverse(gram, rank, (pieces,))
+    for k in range(rounds):
+        if k == min(PLACE[3], rounds - 1):
+            pieces, inverse = lax.optimization_barrier((pieces, inverse))
+        if k == min(PLACE[4], rounds - 1):
+            pieces, got_low = lax.optimization_barrier((pieces, got_low))
         edge = pieces.shape[0] // 2
-        pieces = pieces[:edge] + swap(pieces[edge:], "node", node, bit)
-        bit *= 2
+        pieces = pieces[:edge] + swap(pieces[edge:], "node", node, 1 << k)
     spread = node // samp
     route = [
         (n * samp + s, (s * spread + n // samp) * samp + n % samp) for n in range(node) for s in range(samp)

time: 94.8 us -> 94.7 us (level)
  the two profiles are of different devices: /device:TPU:0 before, /device:TPU:3 now
where the time goes in v7:
time: 94.7 us; the launch traced here: 93 us
  Pallas kernels  41 us (43%)
  waiting for transfers between devices  25.1 us (27%)
  starting transfers between devices  22.6 us (24%)
  local copies, waits for them, and re-layouts  3.15 us (3%)
    ppermute x18, waiting for transfers between devices, swap(): return lax.ppermute(value, axis, [(i, i ^ bit) for i in range(size)])  25.1 us
    ppermute x18, starting transfers between devices, swap(): return lax.ppermute(value, axis, [(i, i ^ bit) for i in range(size)])  17.1 us
    pallas_call x4, Pallas kernels, sketch(): pl.pallas_call(functools.partial(sketch_kernel, count, lent), grid_spec=p...  14.6 us
    pallas_call x3, Pallas kernels, project(): pl.pallas_call(functools.partial(project_kernel, count, wide, len(bases),...  10.6 us
    pallas_call x1, Pallas kernels, factor_inverse(): pl.pallas_call(functools.partial(factor_kernel, rank), in_specs=[HELD] +...  5.48 us
    ppermute x1, starting transfers between devices, body(): piece = lax.ppermute(pieces, ('node', 'samp'), route)  5.44 us
    pallas_call x2, Pallas kernels, lend(): pl.pallas_call(functools.partial(lend_kernel, size, stride, at), in_specs...  3.46 us
    pallas_call x1, Pallas kernels, core_product(): pl.pallas_call(functools.partial(core_kernel, count), out_shape=jax.Shape...  3.33 us
  transfers between devices with their start and end apart: 19, of which 10 were waited for; matrix products, arithmetic and copies ran while one was open for 0% of the time, Pallas kernels for 36%

profile of v7, /device:TPU:3, one launch (start us, length us, event | category | flops | bytes accessed | tf_op | source)
XLA Modules:
  0.0 93.0 jit_solution(2308859413804179956)
XLA Ops:
  3.5 2.2 %lend.3 = bf16[1024,512]{1,0:T(8,128)(2,1)} custom-call(s32[1]{0:T(128)} %bitcast.8.ids_ref, bf16[8192,512]{1,0:T(8,128)(2,1)} %refs_2_.3, bf16[1280,512]{1,0:T(8,128)(2,1)S(1)} %lend.2.refs_0_), custom_call_target="tpu_custom_call" | custom-call | bytes 2097152 | tf_op jit(solution)/shard_map/lend/pallas_call | solution.py:73
  6.2 4.0 %sketch.4 = (bf16[320,1024]{1,0:T(8,128)(2,1)S(1)}, bf16[160,1024]{1,0:T(8,128)(2,1)}, bf16[1024,512]{1,0:T(8,128)(2,1)}) custom-call(s32[2]{0:T(128)S(1)} %pad_add_fusion.1.ids_ref, bf16[8192,512]{1,0:T(8,128)(2,1)} %refs_2_.3, bf16[160,512]{1,0:T(8,128)(2,1)S(1)} %bitcast.13, bf16[1280,512]{1,0:T(8,128)(2,1)S(1)} %collective-permute-done.refs_1_.refs_2_.refs_3_, ...), custom_call_target="tpu_custom_call" | custom-call | flops 335544320 | bytes 5177344 | tf_op jit(solution)/shard_map/sketch/pallas_call | solution.py:105
  10.7 4.3 %sketch.5 = (bf16[320,1024]{1,0:T(8,128)(2,1)S(1)}, bf16[160,1024]{1,0:T(8,128)(2,1)}, bf16[1024,512]{1,0:T(8,128)(2,1)}) custom-call(s32[2]{0:T(128)S(1)} %pad_add_fusion.ids_ref, bf16[8192,512]{1,0:T(8,128)(2,1)} %refs_2_.3, bf16[160,512]{1,0:T(8,128)(2,1)S(1)} %bitcast.14, bf16[1280,512]{1,0:T(8,128)(2,1)S(1)} %collective-permute-done.refs_1_.refs_2_.refs_3_, ...), custom_call_target="tpu_custom_call" | custom-call | flops 335544320 | bytes 5177344 | tf_op jit(solution)/shard_map/sketch/pallas_call | solution.py:105
  17.4 3.2 %sketch.6 = (bf16[320,1024]{1,0:T(8,128)(2,1)S(1)}, bf16[160,1024]{1,0:T(8,128)(2,1)}) custom-call(s32[1]{0:T(128)} %bitcast.2.ids_ref, bf16[8192,512]{1,0:T(8,128)(2,1)} %refs_2_.3, bf16[160,512]{1,0:T(8,128)(2,1)S(1)} %bitcast.15, bf16[1280,512]{1,0:T(8,128)(2,1)S(1)} %collective-permute-done.refs_1_.refs_2_.refs_3_, ...), custom_call_target="tpu_custom_call" | custom-call | flops 335544320 | bytes 3080192 | tf_op jit(solution)/shard_map/sketch/pallas_call | solution.py:105
  20.6 4.5 %collective-permute-done.5.got_ref.refs_2_ = bf16[160,1024]{1,0:T(8,128)(2,1)S(1)} collective-permute-done((bf16[160,1024]{1,0:T(8,128)(2,1)}, bf16[160,1024]{1,0:T(8,128)(2,1)S(1)}, u32[]{:S(2)}, u32[]{:S(2)}) %collective-permute-start.5) | collective-permute-done | bytes 327712 | tf_op jit(solution)/shard_map/ppermute | solution.py:414
  25.8 3.1 %sketch.7 = (bf16[320,1024]{1,0:T(8,128)(2,1)S(1)}, bf16[160,1024]{1,0:T(8,128)(2,1)}) custom-call(s32[1]{0:T(128)} %bitcast.3.ids_ref, bf16[8192,512]{1,0:T(8,128)(2,1)} %refs_2_.3, bf16[160,512]{1,0:T(8,128)(2,1)S(1)} %bitcast.16, bf16[1280,512]{1,0:T(8,128)(2,1)S(1)} %collective-permute-done.refs_1_.refs_2_.refs_3_, ...), custom_call_target="tpu_custom_call" | custom-call | flops 335544320 | bytes 3080192 | tf_op jit(solution)/shard_map/sketch/pallas_call | solution.py:105
  28.9 3.3 %collective-permute-done.4.got_ref.refs_3_ = bf16[160,1024]{1,0:T(8,128)(2,1)} collective-permute-done((bf16[160,1024]{1,0:T(8,128)(2,1)}, bf16[160,1024]{1,0:T(8,128)(2,1)}, u32[]{:S(2)}, u32[]{:S(2)}) %collective-permute-start.4) | collective-permute-done | bytes 327712 | tf_op jit(solution)/shard_map/ppermute | solution.py:414
  32.2 1.7 %gram.3 = f32[128,128]{1,0:T(8,128)S(1)} custom-call(bf16[320,1024]{1,0:T(8,128)(2,1)S(1)} %get-tuple-element.32.own_ref.refs_1_, bf16[160,1024]{1,0:T(8,128)(2,1)} %collective-permute-done.4.got_ref.refs_3_, f32[160,160]{1,0:T(8,128)S(1)} %gram.2.refs_0_, bf16[160,1024]{1,0:T(8,128)(2,1)} %get-tuple-element.34.refs_1_), custom_call_target="tpu_custom_call" | custom-call | flops 209715200 | bytes 983040 | tf_op jit(solution)/shard_map/gram/pallas_call | solution.py:172
  34.3 2.8 %collective-permute-done.6 = f32[128,128]{1,0:T(8,128)S(1)} collective-permute-done((f32[128,128]{1,0:T(8,128)S(1)}, f32[128,128]{1,0:T(8,128)S(1)}, u32[]{:S(2)}, u32[]{:S(2)}) %collective-permute-start.6) | collective-permute-done | bytes 65568 | tf_op jit(solution)/shard_map/ppermute | solution.py:414
  38.7 2.9 %collective-permute-start.8 = (f32[128,128]{1,0:T(8,128)S(1)}, f32[128,128]{1,0:T(8,128)S(1)}, u32[]{:S(2)}, u32[]{:S(2)}) collective-permute-start(f32[128,128]{1,0:T(8,128)S(1)} %add.45), channel_id=1, source_target_pairs={{0,1},{1,0},{2,3},{3,2},{4,5},{5,4},{6,7},{7,6},{8,9},{9,8},{10,11... | collective-permute-start | bytes 196616 | tf_op jit(solution)/shard_map/ppermute | solution.py:414
  45.0 3.9 %project.3.refs_4_ = f32[2,160,512]{2,1,0:T(8,128)S(1)} custom-call(s32[5]{0:T(128)S(1)} %stack.45.ids_ref, bf16[320,1024]{1,0:T(8,128)(2,1)S(1)} %get-tuple-element.33.own_ref.refs_0_, bf16[320,1024]{1,0:T(8,128)(2,1)S(1)} %get-tuple-element.32.own_ref.refs_1_, bf16[160,1024]{1,0:T(8,128)(2,1)S(1)} %collective-permute-done.5.got_ref.refs_2_, ...), custom_call_target="tpu_custom_call" | custom-call | flops 1342177280 | bytes 6160384 | tf_op jit(solution)/shard_map/project/pallas_call | solution.py:296
  50.3 2.1 %collective-permute-done.10 = f32[128,128]{1,0:T(8,128)S(1)} collective-permute-done((f32[128,128]{1,0:T(8,128)S(1)}, f32[128,128]{1,0:T(8,128)S(1)}, u32[]{:S(2)}, u32[]{:S(2)}) %collective-permute-start.10) | collective-permute-done | bytes 65568 | tf_op jit(solution)/shard_map/ppermute | solution.py:414
  52.5 2.9 %project.4.refs_4_ = f32[2,160,512]{2,1,0:T(8,128)S(1)} custom-call(s32[5]{0:T(128)S(1)} %stack.45.ids_ref, bf16[320,1024]{1,0:T(8,128)(2,1)S(1)} %copy-done.5, bf16[160,1024]{1,0:T(8,128)(2,1)} %collective-permute-done.11.refs_1_, bf16[8192,512]{1,0:T(8,128)(2,1)} %refs_2_.3, bf16[1280,512]{1,0:T(8,128)(2,1)S(1)} %collective-permute-done.refs_1_.refs_2_.refs_3_, ...), custom_call_target="tpu_custom_call" | custom-call | flops 671088640 | bytes 3080192 | tf_op jit(solution)/shard_map/project/pallas_call | solution.py:296
  55.4 3.8 %project.5 = (f32[640,128]{1,0:T(8,128)S(1)}, f32[640,128]{1,0:T(8,128)S(1)}) custom-call(s32[5]{0:T(128)S(1)} %stack.45.ids_ref, bf16[320,1024]{1,0:T(8,128)(2,1)S(1)} %copy-done.7, bf16[160,1024]{1,0:T(8,128)(2,1)S(1)} %collective-permute-done.7.refs_1_, bf16[8192,512]{1,0:T(8,128)(2,1)} %refs_2_.3, ...), custom_call_target="tpu_custom_call" | custom-call | flops 671088640 | bytes 3080192 | tf_op jit(solution)/shard_map/project/pallas_call | solution.py:296
  59.2 1.6 %collective-permute-start.12 = (f32[640,128]{1,0:T(8,128)S(1)}, f32[640,128]{1,0:T(8,128)S(1)}, u32[]{:S(2)}, u32[]{:S(2)}) collective-permute-start(f32[640,128]{1,0:T(8,128)S(1)} %get-tuple-element.41), channel_id=1, source_target_pairs={{0,1},{1,0},{2,3},{3,2},{4,5},{5,4},{6,7},{7,6},{8,9},{9,8},{10,11... | collective-permute-start | bytes 983048 | tf_op jit(solution)/shard_map/ppermute | solution.py:414
  60.8 2.4 %collective-permute-start.14 = (f32[128,128]{1,0:T(8,128)S(1)}, f32[128,128]{1,0:T(8,128)S(1)}, u32[]{:S(2)}, u32[]{:S(2)}) collective-permute-start(f32[128,128]{1,0:T(8,128)S(1)} %add.48.refs_5_), channel_id=1, source_target_pairs={{0,16},{4,20},{8,24},{12,28},{16,0},{20,4},{24,8},{28,12},{1,17},{... | collective-permute-start | bytes 196616 | tf_op jit(solution)/shard_map/ppermute | solution.py:414
  63.6 1.9 %collective-permute-done.14 = f32[128,128]{1,0:T(8,128)S(1)} collective-permute-done((f32[128,128]{1,0:T(8,128)S(1)}, f32[128,128]{1,0:T(8,128)S(1)}, u32[]{:S(2)}, u32[]{:S(2)}) %collective-permute-start.14) | collective-permute-done | bytes 65568 | tf_op jit(solution)/shard_map/ppermute | solution.py:414
  65.9 5.5 %factor.1.inv_ref = f32[160,160]{1,0:T(8,128)S(1)} custom-call(f32[128,128]{1,0:T(8,128)S(1)} %add.51.g_ref, f32[640,128]{1,0:T(8,128)S(1)} %add.49.refs_0_), custom_call_target="tpu_custom_call" | custom-call | flops 6000000000 | bytes 102400 | tf_op jit(solution)/shard_map/factor/pallas_call | solution.py:242
  71.4 2.2 %collective-permute-start.15 = (f32[160,128]{1,0:T(8,128)S(1)}, f32[160,128]{1,0:T(8,128)S(1)}, u32[]{:S(2)}, u32[]{:S(2)}) collective-permute-start(f32[160,128]{1,0:T(8,128)S(1)} %slice.27), channel_id=1, source_target_pairs={{0,8},{4,12},{8,0},{12,4},{16,24},{20,28},{24,16},{28,20},{1,9},{5... | collective-permute-start | bytes 245768 | tf_op jit(solution)/shard_map/ppermute | solution.py:414
  73.6 2.1 %collective-permute-done.15 = f32[160,128]{1,0:T(8,128)S(1)} collective-permute-done((f32[160,128]{1,0:T(8,128)S(1)}, f32[160,128]{1,0:T(8,128)S(1)}, u32[]{:S(2)}, u32[]{:S(2)}) %collective-permute-start.15) | collective-permute-done | bytes 81952 | tf_op jit(solution)/shard_map/ppermute | solution.py:414
  75.8 3.6 %collective-permute-done.16.refs_4_ = bf16[160,2048]{1,0:T(8,128)(2,1)S(1)} collective-permute-done((bf16[160,2048]{1,0:T(8,128)(2,1)S(1)}, bf16[160,2048]{1,0:T(8,128)(2,1)S(1)}, u32[]{:S(2)}, u32[]{:S(2)}) %collective-permute-start.16) | collective-permute-done | bytes 655392 | tf_op jit(solution)/shard_map/ppermute | solution.py:414
  79.4 3.7 %collective-permute-done.17 = f32[80,128]{1,0:T(8,128)S(1)} collective-permute-done((f32[80,128]{1,0:T(8,128)S(1)}, f32[80,128]{1,0:T(8,128)S(1)}, u32[]{:S(2)}, u32[]{:S(2)}) %collective-permute-start.17) | collective-permute-done | bytes 40992 | tf_op jit(solution)/shard_map/ppermute | solution.py:414
  83.1 5.4 %collective-permute-start.18 = (f32[80,128]{1,0:T(8,128)S(1)}, f32[80,128]{1,0:T(8,128)S(1)}, u32[]{:S(2)}, u32[]{:S(2)}) collective-permute-start(f32[80,128]{1,0:T(8,128)S(1)} %slice_add_fusion.2), channel_id=1, source_target_pairs={{0,0},{1,8},{2,16},{3,24},{4,1},{5,9},{6,17},{7,25},{8,2},{9,10},{... | collective-permute-start | bytes 122888 | tf_op jit(solution)/shard_map/ppermute | solution.py:528
  88.6 3.3 %core.1 = f32[160,2048]{1,0:T(8,128)} custom-call(f32[160,160]{1,0:T(8,128)S(1)} %factor.1.inv_ref, bf16[320,1024]{1,0:T(8,128)(2,1)S(1)} %get-tuple-element.33.own_ref.refs_0_, bf16[320,1024]{1,0:T(8,128)(2,1)S(1)} %get-tuple-element.32.own_ref.refs_1_, bf16[160,1024]{1,0:T(8,128)(2,1)S(1)} %collective-permute-done.5.got_ref.refs_2_, ...), custom_call_target="tpu_custom_call" | custom-call | flops 629145600 | bytes 3932160 | tf_op jit(solution)/shard_map/core/pallas_call | solution.py:382
  (62 shorter events, 15.6 us)
Async XLA Ops:
  2.8 3.4 %collective-permute-start = (bf16[1280,512]{1,0:T(8,128)(2,1)S(1)}, bf16[1280,512]{1,0:T(8,128)(2,1)S(1)}, u32[]{:S(2)}, u32[]{:S(2)}) collective-permute-start(bf16[1280,512]{1,0:T(8,128)(2,1)S(1)} %lend.2.refs_0_), channel_id=1, source_target_pairs={{0,1},{1,0},{2,3},{3,2},{4,5},{5,4},{6,7},{7,6},{8,9},{9,8},{10,11... | collective-permute-start | bytes 3932168 | tf_op jit(solution)/shard_map/ppermute | solution.py:414
  3.5 2.7 %copy-start.3 = (bf16[512,160]{0,1:T(8,128)(2,1)S(1)}, bf16[512,160]{0,1:T(8,128)(2,1)}, u32[]{:S(2)}) copy-start(bf16[512,160]{0,1:T(8,128)(2,1)} %param.3) | copy-start | bytes 491524
  5.8 4.9 %collective-permute-start.1 = (bf16[1024,512]{1,0:T(8,128)(2,1)}, bf16[1024,512]{1,0:T(8,128)(2,1)}, u32[]{:S(2)}, u32[]{:S(2)}) collective-permute-start(bf16[1024,512]{1,0:T(8,128)(2,1)} %lend.3), channel_id=1, source_target_pairs={{0,1},{1,0},{2,3},{3,2},{4,5},{5,4},{6,7},{7,6},{8,9},{9,8},{10,11... | collective-permute-start | bytes 3145736 | tf_op jit(solution)/shard_map/ppermute | solution.py:414
  10.2 4.8 %copy-start.4 = (bf16[320,1024]{1,0:T(8,128)(2,1)}, bf16[320,1024]{1,0:T(8,128)(2,1)S(1)}, u32[]{:S(2)}) copy-start(bf16[320,1024]{1,0:T(8,128)(2,1)S(1)} %get-tuple-element.36.refs_0_) | copy-start | bytes 1966084
  10.2 7.2 %collective-permute-start.3 = (bf16[1024,512]{1,0:T(8,128)(2,1)}, bf16[1024,512]{1,0:T(8,128)(2,1)S(1)}, u32[]{:S(2)}, u32[]{:S(2)}) collective-permute-start(bf16[1024,512]{1,0:T(8,128)(2,1)} %get-tuple-element.28), channel_id=1, source_target_pairs={{0,1},{1,0},{2,3},{3,2},{4,5},{5,4},{6,7},{7,6},{8,9},{9,8},{10,11... | collective-permute-start | bytes 3145736 | tf_op jit(solution)/shard_map/ppermute | solution.py:414
  15.8 10.0 %collective-permute-start.2 = (bf16[1024,512]{1,0:T(8,128)(2,1)}, bf16[1024,512]{1,0:T(8,128)(2,1)}, u32[]{:S(2)}, u32[]{:S(2)}) collective-permute-start(bf16[1024,512]{1,0:T(8,128)(2,1)} %get-tuple-element.27), channel_id=1, source_target_pairs={{0,1},{1,0},{2,3},{3,2},{4,5},{5,4},{6,7},{7,6},{8,9},{9,8},{10,11... | collective-permute-start | bytes 3145736 | tf_op jit(solution)/shard_map/ppermute | solution.py:414
  15.9 9.1 %collective-permute-start.5 = (bf16[160,1024]{1,0:T(8,128)(2,1)}, bf16[160,1024]{1,0:T(8,128)(2,1)S(1)}, u32[]{:S(2)}, u32[]{:S(2)}) collective-permute-start(bf16[160,1024]{1,0:T(8,128)(2,1)} %get-tuple-element.25.refs_4_), channel_id=1, source_target_pairs={{0,2},{1,3},{2,0},{3,1},{4,6},{5,7},{6,4},{7,5},{8,10},{9,11},{10,... | collective-permute-start | bytes 983048 | tf_op jit(solution)/shard_map/ppermute | solution.py:414
  15.9 16.3 %collective-permute-start.4 = (bf16[160,1024]{1,0:T(8,128)(2,1)}, bf16[160,1024]{1,0:T(8,128)(2,1)}, u32[]{:S(2)}, u32[]{:S(2)}) collective-permute-start(bf16[160,1024]{1,0:T(8,128)(2,1)} %get-tuple-element.29.refs_3_), channel_id=1, source_target_pairs={{0,2},{1,3},{2,0},{3,1},{4,6},{5,7},{6,4},{7,5},{8,10},{9,11},{10,... | collective-permute-start | bytes 983048 | tf_op jit(solution)/shard_map/ppermute | solution.py:414
  17.4 3.2 %copy-start = (bf16[1024,512]{1,0:T(8,128)(2,1)}, bf16[1024,512]{1,0:T(8,128)(2,1)S(1)}, u32[]{:S(2)}) copy-start(bf16[1024,512]{1,0:T(8,128)(2,1)S(1)} %collective-permute-done.3.refs_2_.refs_6_) | copy-start | bytes 3145732
  33.9 3.2 %collective-permute-start.6 = (f32[128,128]{1,0:T(8,128)S(1)}, f32[128,128]{1,0:T(8,128)S(1)}, u32[]{:S(2)}, u32[]{:S(2)}) collective-permute-start(f32[128,128]{1,0:T(8,128)S(1)} %gram.3), channel_id=1, source_target_pairs={{0,2},{1,3},{2,0},{3,1},{4,6},{5,7},{6,4},{7,5},{8,10},{9,11},{10,... | collective-permute-start | bytes 196616 | tf_op jit(solution)/shard_map/ppermute | solution.py:414
  37.1 15.3 %collective-permute-start.11 = (bf16[160,1024]{1,0:T(8,128)(2,1)}, bf16[160,1024]{1,0:T(8,128)(2,1)}, u32[]{:S(2)}, u32[]{:S(2)}) collective-permute-start(bf16[160,1024]{1,0:T(8,128)(2,1)} %get-tuple-element.37.refs_3_), channel_id=1, source_target_pairs={{0,2},{1,3},{2,0},{3,1},{4,6},{5,7},{6,4},{7,5},{8,10},{9,11},{10,... | collective-permute-start | bytes 983048 | tf_op jit(solution)/shard_map/ppermute | solution.py:414
  37.5 17.8 %collective-permute-start.7 = (bf16[160,1024]{1,0:T(8,128)(2,1)}, bf16[160,1024]{1,0:T(8,128)(2,1)S(1)}, u32[]{:S(2)}, u32[]{:S(2)}) collective-permute-start(bf16[160,1024]{1,0:T(8,128)(2,1)} %get-tuple-element.34.refs_1_), channel_id=1, source_target_pairs={{0,2},{1,3},{2,0},{3,1},{4,6},{5,7},{6,4},{7,5},{8,10},{9,11},{10,... | collective-permute-start | bytes 983048 | tf_op jit(solution)/shard_map/ppermute | solution.py:414
  38.7 3.8 %collective-permute-start.8 = (f32[128,128]{1,0:T(8,128)S(1)}, f32[128,128]{1,0:T(8,128)S(1)}, u32[]{:S(2)}, u32[]{:S(2)}) collective-permute-start(f32[128,128]{1,0:T(8,128)S(1)} %add.45), channel_id=1, source_target_pairs={{0,1},{1,0},{2,3},{3,2},{4,5},{5,4},{6,7},{7,6},{8,9},{9,8},{10,11... | collective-permute-start | bytes 196616 | tf_op jit(solution)/shard_map/ppermute | solution.py:414
  42.5 6.4 %collective-permute-start.9 = (f32[128,128]{1,0:T(8,128)S(1)}, f32[128,128]{1,0:T(8,128)S(1)}, u32[]{:S(2)}, u32[]{:S(2)}) collective-permute-start(f32[128,128]{1,0:T(8,128)S(1)} %add.46.refs_8_), channel_id=1, source_target_pairs={{0,4},{4,0},{8,12},{12,8},{16,20},{20,16},{24,28},{28,24},{1,5},{5... | collective-permute-start | bytes 196616 | tf_op jit(solution)/shard_map/ppermute | solution.py:414
  45.0 7.4 %copy-start.5 = (bf16[320,1024]{1,0:T(8,128)(2,1)S(1)}, bf16[320,1024]{1,0:T(8,128)(2,1)}, u32[]{:S(2)}) copy-start(bf16[320,1024]{1,0:T(8,128)(2,1)} %copy-done.4) | copy-start | bytes 1966084
  49.0 3.5 %collective-permute-start.10 = (f32[128,128]{1,0:T(8,128)S(1)}, f32[128,128]{1,0:T(8,128)S(1)}, u32[]{:S(2)}, u32[]{:S(2)}) collective-permute-start(f32[128,128]{1,0:T(8,128)S(1)} %add.47), channel_id=1, source_target_pairs={{0,8},{4,12},{8,0},{12,4},{16,24},{20,28},{24,16},{28,20},{1,9},{5... | collective-permute-start | bytes 196616 | tf_op jit(solution)/shard_map/ppermute | solution.py:414
  52.5 2.9 %copy-start.7 = (bf16[320,1024]{1,0:T(8,128)(2,1)S(1)}, bf16[320,1024]{1,0:T(8,128)(2,1)}, u32[]{:S(2)}) copy-start(bf16[320,1024]{1,0:T(8,128)(2,1)} %copy-done.6) | copy-start | bytes 1966084
  59.2 6.3 %collective-permute-start.12 = (f32[640,128]{1,0:T(8,128)S(1)}, f32[640,128]{1,0:T(8,128)S(1)}, u32[]{:S(2)}, u32[]{:S(2)}) collective-permute-start(f32[640,128]{1,0:T(8,128)S(1)} %get-tuple-element.41), channel_id=1, source_target_pairs={{0,1},{1,0},{2,3},{3,2},{4,5},{5,4},{6,7},{7,6},{8,9},{9,8},{10,11... | collective-permute-start | bytes 983048 | tf_op jit(solution)/shard_map/ppermute | solution.py:414
  60.8 4.7 %collective-permute-start.14 = (f32[128,128]{1,0:T(8,128)S(1)}, f32[128,128]{1,0:T(8,128)S(1)}, u32[]{:S(2)}, u32[]{:S(2)}) collective-permute-start(f32[128,128]{1,0:T(8,128)S(1)} %add.48.refs_5_), channel_id=1, source_target_pairs={{0,16},{4,20},{8,24},{12,28},{16,0},{20,4},{24,8},{28,12},{1,17},{... | collective-permute-start | bytes 196616 | tf_op jit(solution)/shard_map/ppermute | solution.py:414
  63.3 16.1 %collective-permute-start.16 = (bf16[160,2048]{1,0:T(8,128)(2,1)S(1)}, bf16[160,2048]{1,0:T(8,128)(2,1)S(1)}, u32[]{:S(2)}, u32[]{:S(2)}) collective-permute-start(bf16[160,2048]{1,0:T(8,128)(2,1)S(1)} %pad_maximum_fusion), channel_id=1, source_target_pairs={{0,2},{1,3},{2,0},{3,1},{4,6},{5,7},{6,4},{7,5},{8,10},{9,11},{10,... | collective-permute-start | bytes 1966088 | tf_op jit(solution)/shard_map/ppermute | solution.py:414
  65.6 5.8 %collective-permute-start.13 = (f32[320,128]{1,0:T(8,128)S(1)}, f32[320,128]{1,0:T(8,128)S(1)}, u32[]{:S(2)}, u32[]{:S(2)}) collective-permute-start(f32[320,128]{1,0:T(8,128)S(1)} %slice.33), channel_id=1, source_target_pairs={{0,4},{4,0},{8,12},{12,8},{16,20},{20,16},{24,28},{28,24},{1,5},{5... | collective-permute-start | bytes 491528 | tf_op jit(solution)/shard_map/ppermute | solution.py:414
  71.4 4.4 %collective-permute-start.15 = (f32[160,128]{1,0:T(8,128)S(1)}, f32[160,128]{1,0:T(8,128)S(1)}, u32[]{:S(2)}, u32[]{:S(2)}) collective-permute-start(f32[160,128]{1,0:T(8,128)S(1)} %slice.27), channel_id=1, source_target_pairs={{0,8},{4,12},{8,0},{12,4},{16,24},{20,28},{24,16},{28,20},{1,9},{5... | collective-permute-start | bytes 245768 | tf_op jit(solution)/shard_map/ppermute | solution.py:414
  79.4 3.8 %collective-permute-start.17 = (f32[80,128]{1,0:T(8,128)S(1)}, f32[80,128]{1,0:T(8,128)S(1)}, u32[]{:S(2)}, u32[]{:S(2)}) collective-permute-start(f32[80,128]{1,0:T(8,128)S(1)} %slice.31), channel_id=1, source_target_pairs={{0,16},{4,20},{8,24},{12,28},{16,0},{20,4},{24,8},{28,12},{1,17},{... | collective-permute-start | bytes 122888 | tf_op jit(solution)/shard_map/ppermute | solution.py:414
  83.1 8.8 %collective-permute-start.18 = (f32[80,128]{1,0:T(8,128)S(1)}, f32[80,128]{1,0:T(8,128)S(1)}, u32[]{:S(2)}, u32[]{:S(2)}) collective-permute-start(f32[80,128]{1,0:T(8,128)S(1)} %slice_add_fusion.2), channel_id=1, source_target_pairs={{0,0},{1,8},{2,16},{3,24},{4,1},{5,9},{6,17},{7,25},{8,2},{9,10},{... | collective-permute-start | bytes 122888 | tf_op jit(solution)/shard_map/ppermute | solution.py:528
  (3 other events, 3.0 us)

commit v8 on v7

--- a/solution.py
+++ b/solution.py
@@ -11,8 +11,8 @@
 BAND = 32
 UNIT = 1024
 LEND_PARTS = 4
-PLACE = (True, 2, True, 1, 2)
 PROJECT_ROWS = 512
+SKETCH_STEPS = 1
 FACTOR_COST = 6e9
 COST_CUT = 1
 F32 = jnp.float32
@@ -102,21 +102,23 @@
     rank, depth = ws[0].shape
     count = len(ws)
     lent = ids.shape[0] - 1
+    steps = SKETCH_STEPS
+    rows = size // steps
     return pl.pallas_call(
         functools.partial(sketch_kernel, count, lent),
         grid_spec=pltpu.PrefetchScalarGridSpec(
             num_scalar_prefetch=1,
-            grid=(1,),
-            in_specs=[pl.BlockSpec((size, depth), lambda i, ids: (ids[0], 0))]
+            grid=(steps,),
+            in_specs=[pl.BlockSpec((rows, depth), lambda i, ids: (ids[0] * steps + i, 0))]
             + [pl.BlockSpec((rank, depth), lambda i, ids: (0, 0))]
             + [pl.BlockSpec((rank, depth), lambda i, ids: (w_at // rank, 0))] * (count - 1)
-            + [pl.BlockSpec((size, depth), lambda i, ids: (0, 0))] * (count - 1)
-            + [pl.BlockSpec((size, depth), lambda i, ids, k=k: (ids[1 + k], 0)) for k in range(lent)]
+            + [pl.BlockSpec((rows, depth), lambda i, ids: (i, 0))] * (count - 1)
+            + [pl.BlockSpec((rows, depth), lambda i, ids, k=k: (ids[1 + k] * steps + i, 0)) for k in range(lent)]
             + [UNREAD] * len(after),
             out_specs=[
-                pl.BlockSpec((2 * rank, size), lambda i, ids: (0, 0)),
-                pl.BlockSpec((rank, size), lambda i, ids: (0, 0)),
-            ] + [pl.BlockSpec((size, depth), lambda i, ids: (0, 0))] * lent,
+                pl.BlockSpec((2 * rank, rows), lambda i, ids: (0, i)),
+                pl.BlockSpec((rank, rows), lambda i, ids: (0, i)),
+            ] + [pl.BlockSpec((rows, depth), lambda i, ids: (i, 0))] * lent,
         ),
         out_shape=[
             jax.ShapeDtypeStruct((2 * rank, size), BF16),
@@ -249,10 +251,11 @@
     )(packed, *after)
 
 
-def project_kernel(count, wide, has_base, unread, finish, ids_ref, *refs):
+def project_kernel(count, wide, has_base, aside, finish, ids_ref, *refs):
     pair_refs, high_refs, x_refs = refs[:count], refs[count:2 * count], refs[2 * count:count * (2 + wide)]
     at = count * (2 + wide)
-    rest = refs[at + has_base + unread:]
+    beside = refs[at + has_base:at + has_base + aside]
+    rest = refs[at + has_base + aside:]
     t_ref = rest[-1]
     rank = t_ref.shape[1]
 
@@ -274,10 +277,10 @@
     if finish is not None:
         @pl.when(pl.program_id(0) == pl.num_programs(0) - 1)
         def _():
-            finish(t_ref, ids_ref, *rest[:-1])
-
-
-def project(ids, work, x, base, after=(), finish=None, outs=(), scratch=()):
+            finish(t_ref, ids_ref, beside, *rest[:-1])
+
+
+def project(ids, work, x, base, beside=(), finish=None, outs=(), scratch=()):
     count = len(work)
     wide = 1 + len(work[0][3])
     rank, span = work[0][1].shape
@@ -294,7 +297,7 @@
         out_shape = list(outs)
         scratch_shapes = list(scratch) + [pltpu.VMEM((wide, rank, depth), F32)]
     return pl.pallas_call(
-        functools.partial(project_kernel, count, wide, len(bases), len(after), finish),
+        functools.partial(project_kernel, count, wide, len(bases), len(beside), finish),
         grid_spec=pltpu.PrefetchScalarGridSpec(
             num_scalar_prefetch=1,
             grid=(steps,),
@@ -305,7 +308,7 @@
                 for w in work
             ]
             + [pl.BlockSpec((rows, depth), lambda i, ids: (i, 0))] * (count * (wide - 1))
-            + [whole] * len(bases) + [UNREAD] * len(after),
+            + [whole] * len(bases) + [pl.BlockSpec(v.shape, lambda i, ids: (0, 0)) for v in beside],
             out_specs=out_specs,
             scratch_shapes=scratch_shapes,
         ),
@@ -316,7 +319,7 @@
         name="project",
     )(
         ids, *[w[0] for w in work], *[w[1] for w in work], *([x] * count),
-        *[w[3][d] for d in range(wide - 1) for w in work], *bases, *after)
+        *[w[3][d] for d in range(wide - 1) for w in work], *bases, *beside)
 
 
 def folding(rank, width):
@@ -331,13 +334,18 @@
     return sum(1 << (count - 1 - b) for b in range(count) if (p >> b) & 1)
 
 
-def tail(pieces, samp, per_node, width_cols, t_ref, ids_ref, *refs):
+def tail(pieces, samp, per_node, width_cols, t_ref, ids_ref, beside, *refs):
     outs, hold = refs[:-1], refs[-1]
     wide, rank, depth = t_ref.shape
     width = per_node * width_cols
     fold = folding(rank, width)
     tall = rank // fold
     me_node = ids_ref[ids_ref.shape[0] - 1]
+    gram_ref = beside[0]
+    for out in outs[:2]:
+        out[pieces * tall:, :] = gram_ref[...]
+    for out in outs[2:]:
+        out[pieces * tall:, :] = jnp.zeros(gram_ref.shape, F32)
     dst = iota((depth, depth), 1)
     src = iota((depth, depth), 0)
     a, rest = dst // (samp * width), dst % (samp * width)
@@ -362,52 +370,41 @@
             outs[w][p * tall:(p + 1) * tall, :] = hold[me_node ^ reverse_bits(p, bits)]
 
 
-def core_kernel(count, inv_ref, *refs):
+def finish_kernel(scale, per_node, width_cols, count, inv_ref, piece_ref, *refs):
     both, high = refs[:count], refs[count:2 * count]
-    low_ref, core_ref = refs[-2:]
+    low_ref, core_ref, coef_ref = refs[-3:]
     rank = inv_ref.shape[0]
+    inverse = inv_ref[...]
     at = 0
     for c in range(count):
         s = both[c][:rank, :].astype(F32) + both[c][rank:, :].astype(F32)
         rows = s.shape[1]
         s = s + (high[c][...].astype(F32) + low_ref[:, at:at + rows].astype(F32))
-        core_ref[:, at:at + rows] = dot(inv_ref[...], s, ((1,), (0,)), HI)
+        core_ref[:, at:at + rows] = dot(inverse, s, ((1,), (0,)), HI)
         at += rows
-
-
-def core_product(inverse, both, high, low):
+    width = per_node * width_cols
+    fold = folding(rank, width)
+    total = piece_ref[...]
+    total = jnp.concatenate([total[:, f * width:(f + 1) * width] for f in range(fold)], axis=0)
+    out = dot(total, inverse, ((0,), (1,)), HI) * scale
+    coef_ref[...] = jnp.concatenate(
+        [out[p * width_cols:(p + 1) * width_cols, :] for p in range(per_node)], axis=1)
+
+
+def finish(inverse, piece, both, high, low, scale, per_node, width_cols):
     rank = inverse.shape[0]
     count = len(both)
     rows = sum(v.shape[1] for v in high)
     return pl.pallas_call(
-        functools.partial(core_kernel, count),
-        out_shape=jax.ShapeDtypeStruct((rank, rows), F32),
+        functools.partial(finish_kernel, scale, per_node, width_cols, count),
+        out_shape=(
+            jax.ShapeDtypeStruct((rank, rows), F32),
+            jax.ShapeDtypeStruct((width_cols, per_node * rank), F32),
+        ),
         compiler_params=params(),
         cost_estimate=cost(12 * rank * rank * rows, 12 * rank * rows),
-        name="core",
-    )(inverse, *both, *high, low)
-
-
-def coefficient_kernel(scale, per_node, width_cols, inv_ref, piece_ref, o_ref):
-    rank = inv_ref.shape[0]
-    width = per_node * width_cols
-    fold = folding(rank, width)
-    total = piece_ref[...]
-    total = jnp.concatenate([total[:, f * width:(f + 1) * width] for f in range(fold)], axis=0)
-    out = dot(total, inv_ref[...], ((0,), (1,)), HI) * scale
-    o_ref[...] = jnp.concatenate(
-        [out[p * width_cols:(p + 1) * width_cols, :] for p in range(per_node)], axis=1)
-
-
-def coefficients(inverse, piece, scale, per_node, width_cols):
-    rank = inverse.shape[0]
-    return pl.pallas_call(
-        functools.partial(coefficient_kernel, scale, per_node, width_cols),
-        out_shape=jax.ShapeDtypeStruct((width_cols, per_node * rank), F32),
-        compiler_params=params(),
-        cost_estimate=cost(12 * rank * rank * per_node * width_cols, 4 * rank * rank),
-        name="coefficient",
-    )(inverse, piece)
+        name="finish",
+    )(inverse, piece, *both, *high, low)
 
 
 def swap(value, axis, size, bit):
@@ -448,25 +445,20 @@
     for v in borrowed[blocks[0]]:
         w_at = v.shape[0] - rank
         ws.append(v)
-    borrow(blocks[1:2], done)
-
-    pairs, highs, arrived, done = {}, {}, {}, ()
-
-    def cross(b):
-        arrived[b[0] ^ last, b[1]] = swap(highs[b], "samp", samp, last)
-
+    borrow(blocks[1:], done)
+
+    pairs, arrived, done = {}, {}, ()
     ids = jnp.stack([block_of(*b) for b in blocks] + [me_n])
     slot = {b: k for k, b in enumerate(blocks)}
     for k, b in enumerate(blocks):
-        later = blocks[k + 2:k + 3]
+        later = ()
         numbers = [block_of(*b)] + [block_of(o[0] ^ d, o[1]) for o in later for d in near]
         out = sketch(jnp.stack(numbers), snapshots, ws, borrowed[b], UNIT, w_at, done)
-        pairs[b], highs[b] = out[:2]
-        done = (highs[b],)
+        pairs[b], high = out[:2]
+        done = (high,)
+        arrived[b[0] ^ last, b[1]] = swap(high, "samp", samp, last)
         for o in later:
             borrowed[o] = [swap(v, "samp", samp, d) for d, v in zip(near, out[2:])]
-        if b[0] == last:
-            cross(b)
     own = [pairs[0, c] for c in range(2)]
     got_high = [arrived[0, c] for c in range(2)]
 
@@ -476,58 +468,42 @@
     gram = own_gram(own[0], got_high[0], None, None)
     gram = own_gram(own[1], got_high[1], gram, 1.0 / total, done)
     gram = gram + swap(gram, "samp", samp, last)
-    for b in blocks:
-        if b[0] == 0:
-            highs[b], _ = lax.optimization_barrier((highs[b], gram))
-            cross(b)
-    bit = last // 2
-    while bit:
-        gram = gram + swap(gram, "samp", samp, bit)
-        bit //= 2
-    begun = gram
-    t = project(ids, parts([(0, 0), (0, 1)]), snapshots, None, (gram,) if PLACE[0] else ())
-    rounds = node.bit_length() - 1
-    for k in range(rounds):
-        if k == rounds - PLACE[1]:
-            gram, t = lax.optimization_barrier((gram, t))
-        if k == rounds - 1:
-            t = project(ids, parts([(last, 0)]), snapshots, t, (gram,))
-            if PLACE[2]:
-                gram, t = lax.optimization_barrier((gram, t))
-        gram = gram + swap(gram, "node", node, 1 << k)
+
+    t = project(ids, parts([(0, 0), (0, 1)]), snapshots, None)
+    t = project(ids, parts([(last, 0)]), snapshots, t)
     late = [(last, 1)]
-
     per_node = P1 // node
     width_cols = P2 // samp
     tall = rank // folding(rank, per_node * width_cols)
     messages = project(
-        ids, parts(late), snapshots, t, (),
+        ids, parts(late), snapshots, t, [gram],
         functools.partial(tail, node, samp, per_node, width_cols),
-        [jax.ShapeDtypeStruct((node * tall, 128), F32)] * last,
+        [jax.ShapeDtypeStruct((node * tall + gram.shape[0], 128), F32)] * last,
         [pltpu.VMEM((node, tall, 128), F32)])
 
     low = jnp.concatenate([pairs[last, c][rank:] for c in range(2)], axis=1)
-    low, _ = lax.optimization_barrier((low, begun))
+    low, _ = lax.optimization_barrier((low, gram))
     got_low = swap(low, "samp", samp, last)
 
-    pieces = messages[0]
+    held = messages[0]
     for d in near:
-        pieces = pieces + swap(messages[d], "samp", samp, d)
-    inverse = factor_inverse(gram, rank, (pieces,))
+        held = held + swap(messages[d], "samp", samp, d)
+    edge = node * tall
+    pieces, gram = held[:edge], held[edge:]
+    rounds = node.bit_length() - 1
     for k in range(rounds):
-        if k == min(PLACE[3], rounds - 1):
-            pieces, inverse = lax.optimization_barrier((pieces, inverse))
-        if k == min(PLACE[4], rounds - 1):
+        if k == rounds - 1:
             pieces, got_low = lax.optimization_barrier((pieces, got_low))
-        edge = pieces.shape[0] // 2
-        pieces = pieces[:edge] + swap(pieces[edge:], "node", node, 1 << k)
+        edge //= 2
+        got = swap(jnp.concatenate([pieces[edge:], gram], axis=0), "node", node, 1 << k)
+        pieces, gram = pieces[:edge] + got[:edge], gram + got[edge:]
     spread = node // samp
     route = [
         (n * samp + s, (s * spread + n // samp) * samp + n % samp) for n in range(node) for s in range(samp)
     ]
     piece = lax.ppermute(pieces, ("node", "samp"), route)
-    core = core_product(inverse, own, got_high, got_low)
-    coef = coefficients(inverse, piece, 1.0 / total, per_node, width_cols)
+    inverse = factor_inverse(gram, rank)
+    core, coef = finish(inverse, piece, own, got_high, got_low, 1.0 / total, per_node, width_cols)
     return (core.T, coef.T)
 
 

time: 94.7 us -> 88.4 us (0.933); the launches traced: 93 us -> 88 us
  starting transfers between devices: 22.6 us -> 19 us
  Pallas kernels: 41 us -> 37.8 us
  waiting for transfers between devices: 25.1 us -> 28.2 us
  local copies, waits for them, and re-layouts: 3.15 us -> 1.92 us
    ppermute x18 -> x14, starting transfers between devices: 17.1 us -> 11.1 us  [swap(): return lax.ppermute(value, axis, [(i, i ^ bit) for i in range(size)])]
    ppermute x18 -> x14, waiting for transfers between devices: 25.1 us -> 28.2 us  [swap(): return lax.ppermute(value, axis, [(i, i ^ bit) for i in range(size)])]
    ppermute x1, starting transfers between devices: 5.44 us -> 7.92 us  [body(): piece = lax.ppermute(pieces, ('node', 'samp'), route)]
    pallas_call x4, Pallas kernels: 14.6 us -> 12.3 us  [sketch(): pl.pallas_call(functools.partial(sketch_kernel, count, lent), grid_spec=p...]
    pallas_call x2 -> x1, Pallas kernels: 4.41 us -> 2.42 us  [finish(): pl.pallas_call(functools.partial(finish_kernel, scale, per_node, width_co...]
    pallas_call x2, Pallas kernels: 3.46 us -> 5.35 us  [lend(): pl.pallas_call(functools.partial(lend_kernel, size, stride, at), in_specs...]
    unnamed x16 -> x12, local copies, waits for them, and re-layouts: 2.99 us -> 1.76 us
    pallas_call x2, Pallas kernels: 2.45 us -> 1.48 us  [own_gram(): pl.pallas_call(functools.partial(gram_kernel, scale, len(bases)), in_spec...]
  transfers between devices with their start and end apart: 19 -> 15, of which waited for: 10 -> 8; matrix products, arithmetic and copies ran while one was open for 0% -> 0% of each run, Pallas kernels for 36% -> 34%
where the time goes in v8:
time: 88.4 us; the launch traced here: 88 us
  Pallas kernels  37.8 us (43%)
  waiting for transfers between devices  28.2 us (32%)
  starting transfers between devices  19 us (21%)
  local copies, waits for them, and re-layouts  1.92 us (2%)
    ppermute x14, waiting for transfers between devices, swap(): return lax.ppermute(value, axis, [(i, i ^ bit) for i in range(size)])  28.2 us
    pallas_call x4, Pallas kernels, sketch(): pl.pallas_call(functools.partial(sketch_kernel, count, lent), grid_spec=p...  12.3 us
    ppermute x14, starting transfers between devices, swap(): return lax.ppermute(value, axis, [(i, i ^ bit) for i in range(size)])  11.1 us
    pallas_call x3, Pallas kernels, project(): pl.pallas_call(functools.partial(project_kernel, count, wide, len(bases),...  10.7 us
    ppermute x1, starting transfers between devices, body(): piece = lax.ppermute(pieces, ('node', 'samp'), route)  7.92 us
    pallas_call x1, Pallas kernels, factor_inverse(): pl.pallas_call(functools.partial(factor_kernel, rank), in_specs=[HELD] +...  5.48 us
    pallas_call x2, Pallas kernels, lend(): pl.pallas_call(functools.partial(lend_kernel, size, stride, at), in_specs...  5.35 us
    pallas_call x1, Pallas kernels, finish(): pl.pallas_call(functools.partial(finish_kernel, scale, per_node, width_co...  2.42 us
  transfers between devices with their start and end apart: 15, of which 8 were waited for; matrix products, arithmetic and copies ran while one was open for 0% of the time, Pallas kernels for 34%

profile of v8, /device:TPU:3, one launch (start us, length us, event | category | flops | bytes accessed | tf_op | source)
XLA Modules:
  0.0 88.0 jit_solution(16533615104598175717)
XLA Ops:
  1.6 1.2 %lend.2.refs_0_ = bf16[1280,512]{1,0:T(8,128)(2,1)S(1)} custom-call(s32[1]{0:T(128)} %bitcast.6.ids_ref, bf16[8192,512]{1,0:T(8,128)(2,1)} %refs_2_.3, bf16[160,512]{1,0:T(8,128)(2,1)S(1)} %bitcast.12), custom_call_target="tpu_custom_call" | custom-call | bytes 2621440 | tf_op jit(solution)/shard_map/lend/pallas_call | solution.py:73
  3.6 4.1 %lend.3 = (bf16[1024,512]{1,0:T(8,128)(2,1)}, bf16[1024,512]{1,0:T(8,128)(2,1)}, bf16[1024,512]{1,0:T(8,128)(2,1)}) custom-call(s32[3]{0:T(128)S(1)} %pad_add_fusion.ids_ref, bf16[8192,512]{1,0:T(8,128)(2,1)} %refs_2_.3, bf16[1280,512]{1,0:T(8,128)(2,1)S(1)} %lend.2.refs_0_), custom_call_target="tpu_custom_call" | custom-call | bytes 6291456 | tf_op jit(solution)/shard_map/lend/pallas_call | solution.py:73
  8.4 2.8 %sketch.4 = (bf16[320,1024]{1,0:T(8,128)(2,1)S(1)}, bf16[160,1024]{1,0:T(8,128)(2,1)}) custom-call(s32[1]{0:T(128)} %bitcast.ids_ref, bf16[8192,512]{1,0:T(8,128)(2,1)} %refs_2_.3, bf16[160,512]{1,0:T(8,128)(2,1)S(1)} %bitcast.13, bf16[1280,512]{1,0:T(8,128)(2,1)S(1)} %collective-permute-done.refs_1_.refs_2_.refs_3_, ...), custom_call_target="tpu_custom_call" | custom-call | flops 335544320 | bytes 3080192 | tf_op jit(solution)/shard_map/sketch/pallas_call | solution.py:107
  11.2 3.3 %sketch.5 = (bf16[320,1024]{1,0:T(8,128)(2,1)S(1)}, bf16[160,1024]{1,0:T(8,128)(2,1)}) custom-call(s32[1]{0:T(128)} %bitcast.1.ids_ref, bf16[8192,512]{1,0:T(8,128)(2,1)} %refs_2_.3, bf16[160,512]{1,0:T(8,128)(2,1)S(1)} %bitcast.14, bf16[1280,512]{1,0:T(8,128)(2,1)S(1)} %collective-permute-done.refs_1_.refs_2_.refs_3_, ...), custom_call_target="tpu_custom_call" | custom-call | flops 335544320 | bytes 3080192 | tf_op jit(solution)/shard_map/sketch/pallas_call | solution.py:107
  16.6 3.1 %sketch.6 = (bf16[320,1024]{1,0:T(8,128)(2,1)S(1)}, bf16[160,1024]{1,0:T(8,128)(2,1)}) custom-call(s32[1]{0:T(128)} %bitcast.2.ids_ref, bf16[8192,512]{1,0:T(8,128)(2,1)} %refs_2_.3, bf16[160,512]{1,0:T(8,128)(2,1)S(1)} %bitcast.15, bf16[1280,512]{1,0:T(8,128)(2,1)S(1)} %collective-permute-done.refs_1_.refs_2_.refs_3_, ...), custom_call_target="tpu_custom_call" | custom-call | flops 335544320 | bytes 3080192 | tf_op jit(solution)/shard_map/sketch/pallas_call | solution.py:107
  20.0 3.1 %sketch.7 = (bf16[320,1024]{1,0:T(8,128)(2,1)S(1)}, bf16[160,1024]{1,0:T(8,128)(2,1)}) custom-call(s32[1]{0:T(128)} %bitcast.3.ids_ref, bf16[8192,512]{1,0:T(8,128)(2,1)} %refs_2_.3, bf16[160,512]{1,0:T(8,128)(2,1)S(1)} %bitcast.16, bf16[1280,512]{1,0:T(8,128)(2,1)S(1)} %collective-permute-done.refs_1_.refs_2_.refs_3_, ...), custom_call_target="tpu_custom_call" | custom-call | flops 335544320 | bytes 3080192 | tf_op jit(solution)/shard_map/sketch/pallas_call | solution.py:107
  25.1 2.2 %collective-permute-done.7.refs_3_.got_ref = bf16[160,1024]{1,0:T(8,128)(2,1)S(1)} collective-permute-done((bf16[160,1024]{1,0:T(8,128)(2,1)}, bf16[160,1024]{1,0:T(8,128)(2,1)S(1)}, u32[]{:S(2)}, u32[]{:S(2)}) %collective-permute-start.7) | collective-permute-done | bytes 327712 | tf_op jit(solution)/shard_map/ppermute | solution.py:411
  28.5 4.0 %project.3.refs_4_ = f32[2,160,512]{2,1,0:T(8,128)S(1)} custom-call(s32[5]{0:T(128)S(1)} %stack.42.ids_ref, bf16[320,1024]{1,0:T(8,128)(2,1)S(1)} %get-tuple-element.29.refs_0_.own_ref, bf16[320,1024]{1,0:T(8,128)(2,1)S(1)} %get-tuple-element.30.refs_1_.own_ref, bf16[160,1024]{1,0:T(8,128)(2,1)S(1)} %collective-permute-done.6.refs_2_.got_ref, ...), custom_call_target="tpu_custom_call" | custom-call | flops 1342177280 | bytes 6160384 | tf_op jit(solution)/shard_map/project/pallas_call | solution.py:299
  32.5 1.9 %collective-permute-done.5.refs_1_ = bf16[160,1024]{1,0:T(8,128)(2,1)} collective-permute-done((bf16[160,1024]{1,0:T(8,128)(2,1)}, bf16[160,1024]{1,0:T(8,128)(2,1)}, u32[]{:S(2)}, u32[]{:S(2)}) %collective-permute-start.5) | collective-permute-done | bytes 327712 | tf_op jit(solution)/shard_map/ppermute | solution.py:411
  34.4 2.9 %project.4.refs_4_ = f32[2,160,512]{2,1,0:T(8,128)S(1)} custom-call(s32[5]{0:T(128)S(1)} %stack.42.ids_ref, bf16[320,1024]{1,0:T(8,128)(2,1)S(1)} %copy-done.3, bf16[160,1024]{1,0:T(8,128)(2,1)} %collective-permute-done.5.refs_1_, bf16[8192,512]{1,0:T(8,128)(2,1)} %refs_2_.3, bf16[1280,512]{1,0:T(8,128)(2,1)S(1)} %collective-permute-done.refs_1_.refs_2_.refs_3_, ...), custom_call_target="tpu_custom_call" | custom-call | flops 671088640 | bytes 3080192 | tf_op jit(solution)/shard_map/project/pallas_call | solution.py:299
  37.3 5.6 %collective-permute-done.8 = f32[128,128]{1,0:T(8,128)S(1)} collective-permute-done((f32[128,128]{1,0:T(8,128)S(1)}, f32[128,128]{1,0:T(8,128)S(1)}, u32[]{:S(2)}, u32[]{:S(2)}) %collective-permute-start.8) | collective-permute-done | bytes 65568 | tf_op jit(solution)/shard_map/ppermute | solution.py:411
  42.9 3.9 %project.5 = (f32[768,128]{1,0:T(8,128)S(1)}, f32[768,128]{1,0:T(8,128)S(1)}) custom-call(s32[5]{0:T(128)S(1)} %stack.42.ids_ref, bf16[320,1024]{1,0:T(8,128)(2,1)S(1)} %copy-done.5, bf16[160,1024]{1,0:T(8,128)(2,1)} %collective-permute-done.4.refs_1_, bf16[8192,512]{1,0:T(8,128)(2,1)} %refs_2_.3, bf16[1024,512]{1,0:T(8,128)(2,1)} %collective-permute-done.1.refs_2_.refs_3_, ...), custom_call_target="tpu_custom_call" | custom-call | flops 671088640 | bytes 3080192 | tf_op jit(solution)/shard_map/project/pallas_call | solution.py:299
  46.8 1.2 %collective-permute-start.9 = (f32[768,128]{1,0:T(8,128)S(1)}, f32[768,128]{1,0:T(8,128)S(1)}, u32[]{:S(2)}, u32[]{:S(2)}) collective-permute-start(f32[768,128]{1,0:T(8,128)S(1)} %get-tuple-element.32), channel_id=1, source_target_pairs={{0,1},{1,0},{2,3},{3,2},{4,5},{5,4},{6,7},{7,6},{8,9},{9,8},{10,11... | collective-permute-start | bytes 1179656 | tf_op jit(solution)/shard_map/ppermute | solution.py:411
  48.0 1.3 %collective-permute-done.9 = f32[768,128]{1,0:T(8,128)S(1)} collective-permute-done((f32[768,128]{1,0:T(8,128)S(1)}, f32[768,128]{1,0:T(8,128)S(1)}, u32[]{:S(2)}, u32[]{:S(2)}) %collective-permute-start.9) | collective-permute-done | bytes 393248 | tf_op jit(solution)/shard_map/ppermute | solution.py:411
  49.4 1.3 %collective-permute-start.10 = (f32[448,128]{1,0:T(8,128)S(1)}, f32[448,128]{1,0:T(8,128)S(1)}, u32[]{:S(2)}, u32[]{:S(2)}) collective-permute-start(f32[448,128]{1,0:T(8,128)S(1)} %concatenate.16), channel_id=1, source_target_pairs={{0,4},{4,0},{8,12},{12,8},{16,20},{20,16},{24,28},{28,24},{1,5},{5... | collective-permute-start | bytes 688136 | tf_op jit(solution)/shard_map/ppermute | solution.py:411
  51.1 5.2 %collective-permute-done.10 = f32[448,128]{1,0:T(8,128)S(1)} collective-permute-done((f32[448,128]{1,0:T(8,128)S(1)}, f32[448,128]{1,0:T(8,128)S(1)}, u32[]{:S(2)}, u32[]{:S(2)}) %collective-permute-start.10) | collective-permute-done | bytes 229408 | tf_op jit(solution)/shard_map/ppermute | solution.py:411
  56.4 1.4 %collective-permute-start.11 = (f32[288,128]{1,0:T(8,128)S(1)}, f32[288,128]{1,0:T(8,128)S(1)}, u32[]{:S(2)}, u32[]{:S(2)}) collective-permute-start(f32[288,128]{1,0:T(8,128)S(1)} %pad_maximum_fusion.1), channel_id=1, source_target_pairs={{0,8},{4,12},{8,0},{12,4},{16,24},{20,28},{24,16},{28,20},{1,9},{5... | collective-permute-start | bytes 442376 | tf_op jit(solution)/shard_map/ppermute | solution.py:411
  57.7 3.0 %collective-permute-done.11 = f32[288,128]{1,0:T(8,128)S(1)} collective-permute-done((f32[288,128]{1,0:T(8,128)S(1)}, f32[288,128]{1,0:T(8,128)S(1)}, u32[]{:S(2)}, u32[]{:S(2)}) %collective-permute-start.11) | collective-permute-done | bytes 147488 | tf_op jit(solution)/shard_map/ppermute | solution.py:411
  60.7 5.7 %collective-permute-done.12.refs_4_ = bf16[160,2048]{1,0:T(8,128)(2,1)S(1)} collective-permute-done((bf16[160,2048]{1,0:T(8,128)(2,1)S(1)}, bf16[160,2048]{1,0:T(8,128)(2,1)S(1)}, u32[]{:S(2)}, u32[]{:S(2)}) %collective-permute-start.12) | collective-permute-done | bytes 655392 | tf_op jit(solution)/shard_map/ppermute | solution.py:411
  66.5 2.4 %collective-permute-start.13 = (f32[208,128]{1,0:T(8,128)S(1)}, f32[208,128]{1,0:T(8,128)S(1)}, u32[]{:S(2)}, u32[]{:S(2)}) collective-permute-start(f32[208,128]{1,0:T(8,128)S(1)} %pad_maximum_fusion.2), channel_id=1, source_target_pairs={{0,16},{4,20},{8,24},{12,28},{16,0},{20,4},{24,8},{28,12},{1,17},{... | collective-permute-start | bytes 319496 | tf_op jit(solution)/shard_map/ppermute | solution.py:411
  68.9 3.3 %collective-permute-done.13 = f32[208,128]{1,0:T(8,128)S(1)} collective-permute-done((f32[208,128]{1,0:T(8,128)S(1)}, f32[208,128]{1,0:T(8,128)S(1)}, u32[]{:S(2)}, u32[]{:S(2)}) %collective-permute-start.13) | collective-permute-done | bytes 106528 | tf_op jit(solution)/shard_map/ppermute | solution.py:411
  72.2 7.9 %collective-permute-start.14 = (f32[80,128]{1,0:T(8,128)S(1)}, f32[80,128]{1,0:T(8,128)S(1)}, u32[]{:S(2)}, u32[]{:S(2)}) collective-permute-start(f32[80,128]{1,0:T(8,128)S(1)} %slice_add_fusion.5), channel_id=1, source_target_pairs={{0,0},{1,8},{2,16},{3,24},{4,1},{5,9},{6,17},{7,25},{8,2},{9,10},{... | collective-permute-start | bytes 122888 | tf_op jit(solution)/shard_map/ppermute | solution.py:504
  80.1 5.5 %factor.1.inv_ref = f32[160,160]{1,0:T(8,128)S(1)} custom-call(f32[128,128]{1,0:T(8,128)S(1)} %slice_add_fusion.2.g_ref), custom_call_target="tpu_custom_call" | custom-call | flops 6000000000 | bytes 102400 | tf_op jit(solution)/shard_map/factor/pallas_call | solution.py:244
  85.6 2.4 %finish.1 = (f32[160,2048]{1,0:T(8,128)}, f32[8,1280]{1,0:T(8,128)}) custom-call(f32[160,160]{1,0:T(8,128)S(1)} %factor.1.inv_ref, f32[80,128]{1,0:T(8,128)S(1)} %collective-permute-done.14.piece_ref, bf16[320,1024]{1,0:T(8,128)(2,1)S(1)} %get-tuple-element.29.refs_0_.own_ref, bf16[320,1024]{1,0:T(8,128)(2,1)S(1)} %get-tuple-element.30.refs_1_.own_ref, ...), custom_call_target="tpu_custom_call" | custom-call | flops 629145600 | bytes 3932160 | tf_op jit(solution)/shard_map/finish/pallas_call | solution.py:398
  (49 shorter events, 8.5 us)
Async XLA Ops:
  0.6 0.9 %copy-start = (bf16[512,160]{0,1:T(8,128)(2,1)S(1)}, bf16[512,160]{0,1:T(8,128)(2,1)}, u32[]{:S(2)}) copy-start(bf16[512,160]{0,1:T(8,128)(2,1)} %param.3) | copy-start | bytes 491524
  2.8 5.6 %collective-permute-start = (bf16[1280,512]{1,0:T(8,128)(2,1)S(1)}, bf16[1280,512]{1,0:T(8,128)(2,1)S(1)}, u32[]{:S(2)}, u32[]{:S(2)}) collective-permute-start(bf16[1280,512]{1,0:T(8,128)(2,1)S(1)} %lend.2.refs_0_), channel_id=1, source_target_pairs={{0,1},{1,0},{2,3},{3,2},{4,5},{5,4},{6,7},{7,6},{8,9},{9,8},{10,11... | collective-permute-start | bytes 3932168 | tf_op jit(solution)/shard_map/ppermute | solution.py:411
  3.6 4.8 %copy-start.1 = (bf16[512,160]{0,1:T(8,128)(2,1)S(1)}, bf16[512,160]{0,1:T(8,128)(2,1)}, u32[]{:S(2)}) copy-start(bf16[512,160]{0,1:T(8,128)(2,1)} %param.3) | copy-start | bytes 491524
  7.7 3.5 %collective-permute-start.1 = (bf16[1024,512]{1,0:T(8,128)(2,1)}, bf16[1024,512]{1,0:T(8,128)(2,1)}, u32[]{:S(2)}, u32[]{:S(2)}) collective-permute-start(bf16[1024,512]{1,0:T(8,128)(2,1)} %get-tuple-element.20), channel_id=1, source_target_pairs={{0,1},{1,0},{2,3},{3,2},{4,5},{5,4},{6,7},{7,6},{8,9},{9,8},{10,11... | collective-permute-start | bytes 3145736 | tf_op jit(solution)/shard_map/ppermute | solution.py:411
  7.8 8.8 %collective-permute-start.3 = (bf16[1024,512]{1,0:T(8,128)(2,1)}, bf16[1024,512]{1,0:T(8,128)(2,1)}, u32[]{:S(2)}, u32[]{:S(2)}) collective-permute-start(bf16[1024,512]{1,0:T(8,128)(2,1)} %get-tuple-element.24), channel_id=1, source_target_pairs={{0,1},{1,0},{2,3},{3,2},{4,5},{5,4},{6,7},{7,6},{8,9},{9,8},{10,11... | collective-permute-start | bytes 3145736 | tf_op jit(solution)/shard_map/ppermute | solution.py:411
  8.3 11.6 %collective-permute-start.2 = (bf16[1024,512]{1,0:T(8,128)(2,1)}, bf16[1024,512]{1,0:T(8,128)(2,1)}, u32[]{:S(2)}, u32[]{:S(2)}) collective-permute-start(bf16[1024,512]{1,0:T(8,128)(2,1)} %get-tuple-element.23), channel_id=1, source_target_pairs={{0,1},{1,0},{2,3},{3,2},{4,5},{5,4},{6,7},{7,6},{8,9},{9,8},{10,11... | collective-permute-start | bytes 3145736 | tf_op jit(solution)/shard_map/ppermute | solution.py:411
  11.2 3.4 %copy-start.2 = (bf16[320,1024]{1,0:T(8,128)(2,1)}, bf16[320,1024]{1,0:T(8,128)(2,1)S(1)}, u32[]{:S(2)}) copy-start(bf16[320,1024]{1,0:T(8,128)(2,1)S(1)} %get-tuple-element.28.refs_0_) | copy-start | bytes 1966084
  11.2 13.2 %collective-permute-start.6 = (bf16[160,1024]{1,0:T(8,128)(2,1)}, bf16[160,1024]{1,0:T(8,128)(2,1)S(1)}, u32[]{:S(2)}, u32[]{:S(2)}) collective-permute-start(bf16[160,1024]{1,0:T(8,128)(2,1)} %get-tuple-element.21.refs_3_), channel_id=1, source_target_pairs={{0,2},{1,3},{2,0},{3,1},{4,6},{5,7},{6,4},{7,5},{8,10},{9,11},{10,... | collective-permute-start | bytes 983048 | tf_op jit(solution)/shard_map/ppermute | solution.py:411
  14.6 0.8 copy-start.4
  15.4 11.9 %collective-permute-start.7 = (bf16[160,1024]{1,0:T(8,128)(2,1)}, bf16[160,1024]{1,0:T(8,128)(2,1)S(1)}, u32[]{:S(2)}, u32[]{:S(2)}) collective-permute-start(bf16[160,1024]{1,0:T(8,128)(2,1)} %get-tuple-element.25.refs_3_), channel_id=1, source_target_pairs={{0,2},{1,3},{2,0},{3,1},{4,6},{5,7},{6,4},{7,5},{8,10},{9,11},{10,... | collective-permute-start | bytes 983048 | tf_op jit(solution)/shard_map/ppermute | solution.py:411
  19.7 14.7 %collective-permute-start.5 = (bf16[160,1024]{1,0:T(8,128)(2,1)}, bf16[160,1024]{1,0:T(8,128)(2,1)}, u32[]{:S(2)}, u32[]{:S(2)}) collective-permute-start(bf16[160,1024]{1,0:T(8,128)(2,1)} %get-tuple-element.26.refs_3_), channel_id=1, source_target_pairs={{0,2},{1,3},{2,0},{3,1},{4,6},{5,7},{6,4},{7,5},{8,10},{9,11},{10,... | collective-permute-start | bytes 983048 | tf_op jit(solution)/shard_map/ppermute | solution.py:411
  23.1 19.8 %collective-permute-start.4 = (bf16[160,1024]{1,0:T(8,128)(2,1)}, bf16[160,1024]{1,0:T(8,128)(2,1)}, u32[]{:S(2)}, u32[]{:S(2)}) collective-permute-start(bf16[160,1024]{1,0:T(8,128)(2,1)} %get-tuple-element.27.refs_1_), channel_id=1, source_target_pairs={{0,2},{1,3},{2,0},{3,1},{4,6},{5,7},{6,4},{7,5},{8,10},{9,11},{10,... | collective-permute-start | bytes 983048 | tf_op jit(solution)/shard_map/ppermute | solution.py:411
  28.1 6.4 %copy-start.3 = (bf16[320,1024]{1,0:T(8,128)(2,1)S(1)}, bf16[320,1024]{1,0:T(8,128)(2,1)}, u32[]{:S(2)}) copy-start(bf16[320,1024]{1,0:T(8,128)(2,1)} %copy-done.2) | copy-start | bytes 1966084
  28.1 14.8 %collective-permute-start.8 = (f32[128,128]{1,0:T(8,128)S(1)}, f32[128,128]{1,0:T(8,128)S(1)}, u32[]{:S(2)}, u32[]{:S(2)}) collective-permute-start(f32[128,128]{1,0:T(8,128)S(1)} %gram.3), channel_id=1, source_target_pairs={{0,2},{1,3},{2,0},{3,1},{4,6},{5,7},{6,4},{7,5},{8,10},{9,11},{10,... | collective-permute-start | bytes 196616 | tf_op jit(solution)/shard_map/ppermute | solution.py:411
  34.4 8.4 %copy-start.5 = (bf16[320,1024]{1,0:T(8,128)(2,1)S(1)}, bf16[320,1024]{1,0:T(8,128)(2,1)}, u32[]{:S(2)}) copy-start(bf16[320,1024]{1,0:T(8,128)(2,1)} %copy-done.4) | copy-start | bytes 1966084
  46.8 2.6 %collective-permute-start.9 = (f32[768,128]{1,0:T(8,128)S(1)}, f32[768,128]{1,0:T(8,128)S(1)}, u32[]{:S(2)}, u32[]{:S(2)}) collective-permute-start(f32[768,128]{1,0:T(8,128)S(1)} %get-tuple-element.32), channel_id=1, source_target_pairs={{0,1},{1,0},{2,3},{3,2},{4,5},{5,4},{6,7},{7,6},{8,9},{9,8},{10,11... | collective-permute-start | bytes 1179656 | tf_op jit(solution)/shard_map/ppermute | solution.py:411
  49.4 6.9 %collective-permute-start.10 = (f32[448,128]{1,0:T(8,128)S(1)}, f32[448,128]{1,0:T(8,128)S(1)}, u32[]{:S(2)}, u32[]{:S(2)}) collective-permute-start(f32[448,128]{1,0:T(8,128)S(1)} %concatenate.16), channel_id=1, source_target_pairs={{0,4},{4,0},{8,12},{12,8},{16,20},{20,16},{24,28},{28,24},{1,5},{5... | collective-permute-start | bytes 688136 | tf_op jit(solution)/shard_map/ppermute | solution.py:411
  50.8 15.7 %collective-permute-start.12 = (bf16[160,2048]{1,0:T(8,128)(2,1)S(1)}, bf16[160,2048]{1,0:T(8,128)(2,1)S(1)}, u32[]{:S(2)}, u32[]{:S(2)}) collective-permute-start(bf16[160,2048]{1,0:T(8,128)(2,1)S(1)} %pad_maximum_fusion), channel_id=1, source_target_pairs={{0,2},{1,3},{2,0},{3,1},{4,6},{5,7},{6,4},{7,5},{8,10},{9,11},{10,... | collective-permute-start | bytes 1966088 | tf_op jit(solution)/shard_map/ppermute | solution.py:411
  56.4 4.4 %collective-permute-start.11 = (f32[288,128]{1,0:T(8,128)S(1)}, f32[288,128]{1,0:T(8,128)S(1)}, u32[]{:S(2)}, u32[]{:S(2)}) collective-permute-start(f32[288,128]{1,0:T(8,128)S(1)} %pad_maximum_fusion.1), channel_id=1, source_target_pairs={{0,8},{4,12},{8,0},{12,4},{16,24},{20,28},{24,16},{28,20},{1,9},{5... | collective-permute-start | bytes 442376 | tf_op jit(solution)/shard_map/ppermute | solution.py:411
  66.5 5.7 %collective-permute-start.13 = (f32[208,128]{1,0:T(8,128)S(1)}, f32[208,128]{1,0:T(8,128)S(1)}, u32[]{:S(2)}, u32[]{:S(2)}) collective-permute-start(f32[208,128]{1,0:T(8,128)S(1)} %pad_maximum_fusion.2), channel_id=1, source_target_pairs={{0,16},{4,20},{8,24},{12,28},{16,0},{20,4},{24,8},{28,12},{1,17},{... | collective-permute-start | bytes 319496 | tf_op jit(solution)/shard_map/ppermute | solution.py:411
  72.2 13.4 %collective-permute-start.14 = (f32[80,128]{1,0:T(8,128)S(1)}, f32[80,128]{1,0:T(8,128)S(1)}, u32[]{:S(2)}, u32[]{:S(2)}) collective-permute-start(f32[80,128]{1,0:T(8,128)S(1)} %slice_add_fusion.5), channel_id=1, source_target_pairs={{0,0},{1,8},{2,16},{3,24},{4,1},{5,9},{6,17},{7,25},{8,2},{9,10},{... | collective-permute-start | bytes 122888 | tf_op jit(solution)/shard_map/ppermute | solution.py:504

commit v9 on v8

--- a/solution.py
+++ b/solution.py
@@ -12,6 +12,7 @@
 UNIT = 1024
 LEND_PARTS = 4
 PROJECT_ROWS = 512
+PLACE = (1, True, 1, 1, -1)
 SKETCH_STEPS = 1
 FACTOR_COST = 6e9
 COST_CUT = 1
@@ -341,11 +342,6 @@
     fold = folding(rank, width)
     tall = rank // fold
     me_node = ids_ref[ids_ref.shape[0] - 1]
-    gram_ref = beside[0]
-    for out in outs[:2]:
-        out[pieces * tall:, :] = gram_ref[...]
-    for out in outs[2:]:
-        out[pieces * tall:, :] = jnp.zeros(gram_ref.shape, F32)
     dst = iota((depth, depth), 1)
     src = iota((depth, depth), 0)
     a, rest = dst // (samp * width), dst % (samp * width)
@@ -372,14 +368,14 @@
 
 def finish_kernel(scale, per_node, width_cols, count, inv_ref, piece_ref, *refs):
     both, high = refs[:count], refs[count:2 * count]
-    low_ref, core_ref, coef_ref = refs[-3:]
+    low, core_ref, coef_ref = refs[2 * count:3 * count], refs[-2], refs[-1]
     rank = inv_ref.shape[0]
     inverse = inv_ref[...]
     at = 0
     for c in range(count):
         s = both[c][:rank, :].astype(F32) + both[c][rank:, :].astype(F32)
         rows = s.shape[1]
-        s = s + (high[c][...].astype(F32) + low_ref[:, at:at + rows].astype(F32))
+        s = s + (high[c][...].astype(F32) + low[c][...].astype(F32))
         core_ref[:, at:at + rows] = dot(inverse, s, ((1,), (0,)), HI)
         at += rows
     width = per_node * width_cols
@@ -404,7 +400,7 @@
         compiler_params=params(),
         cost_estimate=cost(12 * rank * rank * rows, 12 * rank * rows),
         name="finish",
-    )(inverse, piece, *both, *high, low)
+    )(inverse, piece, *both, *high, *low)
 
 
 def swap(value, axis, size, bit):
@@ -456,7 +452,8 @@
         out = sketch(jnp.stack(numbers), snapshots, ws, borrowed[b], UNIT, w_at, done)
         pairs[b], high = out[:2]
         done = (high,)
-        arrived[b[0] ^ last, b[1]] = swap(high, "samp", samp, last)
+        if k + 1 < len(blocks):
+            arrived[b[0] ^ last, b[1]] = swap(high, "samp", samp, last)
         for o in later:
             borrowed[o] = [swap(v, "samp", samp, d) for d, v in zip(near, out[2:])]
     own = [pairs[0, c] for c in range(2)]
@@ -467,42 +464,57 @@
 
     gram = own_gram(own[0], got_high[0], None, None)
     gram = own_gram(own[1], got_high[1], gram, 1.0 / total, done)
+    t = project(ids, parts([(0, 0), (0, 1)]), snapshots, None, [gram])
+    final = blocks[-1]
+    late = [(final[0] ^ last, final[1])]
+    high, t = lax.optimization_barrier((high, t))
+    arrived[late[0]] = swap(high, "samp", samp, last)
     gram = gram + swap(gram, "samp", samp, last)
-
-    t = project(ids, parts([(0, 0), (0, 1)]), snapshots, None)
-    t = project(ids, parts([(last, 0)]), snapshots, t)
-    late = [(last, 1)]
+    got_low = []
+    for c in range(2):
+        low, _ = lax.optimization_barrier((pairs[last, c][rank:], gram))
+        got_low.append(swap(low, "samp", samp, last))
+    bit = last // 2
+    while bit:
+        gram = gram + swap(gram, "samp", samp, bit)
+        bit //= 2
+    rounds = node.bit_length() - 1
+    before = gram
+    for k in range(rounds):
+        if k == min(PLACE[0], rounds - 1):
+            t = project(ids, parts([(last, 0)]), snapshots, t, [gram])
+            gram, t = lax.optimization_barrier((gram, t))
+        before = gram
+        gram = gram + swap(gram, "node", node, 1 << k)
+
     per_node = P1 // node
     width_cols = P2 // samp
     tall = rank // folding(rank, per_node * width_cols)
     messages = project(
-        ids, parts(late), snapshots, t, [gram],
+        ids, parts(late), snapshots, t, [before],
         functools.partial(tail, node, samp, per_node, width_cols),
-        [jax.ShapeDtypeStruct((node * tall + gram.shape[0], 128), F32)] * last,
+        [jax.ShapeDtypeStruct((node * tall, 128), F32)] * last,
         [pltpu.VMEM((node, tall, 128), F32)])
-
-    low = jnp.concatenate([pairs[last, c][rank:] for c in range(2)], axis=1)
-    low, _ = lax.optimization_barrier((low, gram))
-    got_low = swap(low, "samp", samp, last)
-
-    held = messages[0]
+    if PLACE[1]:
+        *messages, gram = lax.optimization_barrier((*messages, gram))
+
+    pieces = messages[0]
     for d in near:
-        held = held + swap(messages[d], "samp", samp, d)
-    edge = node * tall
-    pieces, gram = held[:edge], held[edge:]
-    rounds = node.bit_length() - 1
+        pieces = pieces + swap(messages[d], "samp", samp, d)
+    inverse = factor_inverse(gram, rank, (pieces,))
     for k in range(rounds):
-        if k == rounds - 1:
-            pieces, got_low = lax.optimization_barrier((pieces, got_low))
-        edge //= 2
-        got = swap(jnp.concatenate([pieces[edge:], gram], axis=0), "node", node, 1 << k)
-        pieces, gram = pieces[:edge] + got[:edge], gram + got[edge:]
+        if k == min(PLACE[2], rounds - 1):
+            pieces, inverse = lax.optimization_barrier((pieces, inverse))
+        for c in range(2):
+            if k == PLACE[3 + c]:
+                pieces, got_low[c] = lax.optimization_barrier((pieces, got_low[c]))
+        edge = pieces.shape[0] // 2
+        pieces = pieces[:edge] + swap(pieces[edge:], "node", node, 1 << k)
     spread = node // samp
     route = [
         (n * samp + s, (s * spread + n // samp) * samp + n % samp) for n in range(node) for s in range(samp)
     ]
     piece = lax.ppermute(pieces, ("node", "samp"), route)
-    inverse = factor_inverse(gram, rank)
     core, coef = finish(inverse, piece, own, got_high, got_low, 1.0 / total, per_node, width_cols)
     return (core.T, coef.T)
 

time: 88.4 us -> 88.6 us (level)
  the two profiles are of different devices: /device:TPU:3 before, /device:TPU:6 now
where the time goes in v9:
time: 88.6 us; the launch traced here: 88.3 us
  Pallas kernels  36.1 us (41%)
  waiting for transfers between devices  33.1 us (37%)
  starting transfers between devices  16.9 us (19%)
  local copies, waits for them, and re-layouts  1.07 us (1%)
    ppermute x19, waiting for transfers between devices, swap(): return lax.ppermute(value, axis, [(i, i ^ bit) for i in range(size)])  25.5 us
    ppermute x19, starting transfers between devices, swap(): return lax.ppermute(value, axis, [(i, i ^ bit) for i in range(size)])  15 us
    pallas_call x4, Pallas kernels, sketch(): pl.pallas_call(functools.partial(sketch_kernel, count, lent), grid_spec=p...  10.6 us
    pallas_call x3, Pallas kernels, project(): pl.pallas_call(functools.partial(project_kernel, count, wide, len(bases),...  10.6 us
    ppermute x1, waiting for transfers between devices, body(): piece = lax.ppermute(pieces, ('node', 'samp'), route)  7.55 us
    pallas_call x1, Pallas kernels, factor_inverse(): pl.pallas_call(functools.partial(factor_kernel, rank), in_specs=[HELD] +...  5.48 us
    pallas_call x2, Pallas kernels, lend(): pl.pallas_call(functools.partial(lend_kernel, size, stride, at), in_specs...  5.4 us
    pallas_call x1, Pallas kernels, finish(): pl.pallas_call(functools.partial(finish_kernel, scale, per_node, width_co...  2.48 us
  transfers between devices with their start and end apart: 20, of which 12 were waited for; matrix products, arithmetic and copies ran while one was open for 0% of the time, Pallas kernels for 37%

profile of v9, /device:TPU:6, one launch (start us, length us, event | category | flops | bytes accessed | tf_op | source)
XLA Modules:
  0.0 88.3 jit_solution(18112756878755565776)
XLA Ops:
  3.0 4.2 %lend.3 = (bf16[1024,512]{1,0:T(8,128)(2,1)}, bf16[1024,512]{1,0:T(8,128)(2,1)}, bf16[1024,512]{1,0:T(8,128)(2,1)}) custom-call(s32[3]{0:T(128)S(1)} %pad_add_fusion.ids_ref, bf16[8192,512]{1,0:T(8,128)(2,1)} %refs_2_.3, bf16[1280,512]{1,0:T(8,128)(2,1)S(1)} %lend.2.refs_0_), custom_call_target="tpu_custom_call" | custom-call | bytes 6291456 | tf_op jit(solution)/shard_map/lend/pallas_call | solution.py:74
  8.2 2.8 %sketch.4 = (bf16[320,1024]{1,0:T(8,128)(2,1)S(1)}, bf16[160,1024]{1,0:T(8,128)(2,1)}) custom-call(s32[1]{0:T(128)} %bitcast.ids_ref, bf16[8192,512]{1,0:T(8,128)(2,1)} %refs_2_.3, bf16[160,512]{1,0:T(8,128)(2,1)S(1)} %bitcast.13, bf16[1280,512]{1,0:T(8,128)(2,1)S(1)} %collective-permute-done.refs_1_.refs_2_.refs_3_, ...), custom_call_target="tpu_custom_call" | custom-call | flops 335544320 | bytes 3080192 | tf_op jit(solution)/shard_map/sketch/pallas_call | solution.py:108
  11.5 3.1 %sketch.5 = (bf16[320,1024]{1,0:T(8,128)(2,1)S(1)}, bf16[160,1024]{1,0:T(8,128)(2,1)}) custom-call(s32[1]{0:T(128)} %bitcast.1.ids_ref, bf16[8192,512]{1,0:T(8,128)(2,1)} %refs_2_.3, bf16[160,512]{1,0:T(8,128)(2,1)S(1)} %bitcast.14, bf16[1280,512]{1,0:T(8,128)(2,1)S(1)} %collective-permute-done.refs_1_.refs_2_.refs_3_, ...), custom_call_target="tpu_custom_call" | custom-call | flops 335544320 | bytes 3080192 | tf_op jit(solution)/shard_map/sketch/pallas_call | solution.py:108
  14.6 1.5 %collective-permute-start.5 = (bf16[160,1024]{1,0:T(8,128)(2,1)}, bf16[160,1024]{1,0:T(8,128)(2,1)S(1)}, u32[]{:S(2)}, u32[]{:S(2)}) collective-permute-start(bf16[160,1024]{1,0:T(8,128)(2,1)} %get-tuple-element.35.refs_3_), channel_id=1, source_target_pairs={{0,2},{1,3},{2,0},{3,1},{4,6},{5,7},{6,4},{7,5},{8,10},{9,11},{10,... | collective-permute-start | bytes 983048 | tf_op jit(solution)/shard_map/ppermute | solution.py:407
  16.2 2.4 %sketch.6 = (bf16[320,1024]{1,0:T(8,128)(2,1)S(1)}, bf16[160,1024]{1,0:T(8,128)(2,1)S(1)}) custom-call(s32[1]{0:T(128)} %bitcast.2.ids_ref, bf16[8192,512]{1,0:T(8,128)(2,1)} %refs_2_.3, bf16[160,512]{1,0:T(8,128)(2,1)S(1)} %bitcast.15, bf16[1280,512]{1,0:T(8,128)(2,1)S(1)} %collective-permute-done.refs_1_.refs_2_.refs_3_, ...), custom_call_target="tpu_custom_call" | custom-call | flops 335544320 | bytes 3080192 | tf_op jit(solution)/shard_map/sketch/pallas_call | solution.py:108
  19.2 2.4 %sketch.7 = (bf16[320,1024]{1,0:T(8,128)(2,1)S(1)}, bf16[160,1024]{1,0:T(8,128)(2,1)S(1)}) custom-call(s32[1]{0:T(128)} %bitcast.3.ids_ref, bf16[8192,512]{1,0:T(8,128)(2,1)} %refs_2_.3, bf16[160,512]{1,0:T(8,128)(2,1)S(1)} %bitcast.16, bf16[1280,512]{1,0:T(8,128)(2,1)S(1)} %collective-permute-done.refs_1_.refs_2_.refs_3_, ...), custom_call_target="tpu_custom_call" | custom-call | flops 335544320 | bytes 3080192 | tf_op jit(solution)/shard_map/sketch/pallas_call | solution.py:108
  22.5 6.3 %collective-permute-done.5.got_ref.refs_3_ = bf16[160,1024]{1,0:T(8,128)(2,1)S(1)} collective-permute-done((bf16[160,1024]{1,0:T(8,128)(2,1)}, bf16[160,1024]{1,0:T(8,128)(2,1)S(1)}, u32[]{:S(2)}, u32[]{:S(2)}) %collective-permute-start.5) | collective-permute-done | bytes 327712 | tf_op jit(solution)/shard_map/ppermute | solution.py:407
  30.2 4.0 %project.3.refs_4_ = f32[2,160,512]{2,1,0:T(8,128)S(1)} custom-call(s32[5]{0:T(128)S(1)} %stack.42.ids_ref, bf16[320,1024]{1,0:T(8,128)(2,1)S(1)} %get-tuple-element.38.own_ref.refs_0_, bf16[320,1024]{1,0:T(8,128)(2,1)S(1)} %get-tuple-element.39.own_ref.refs_1_, bf16[160,1024]{1,0:T(8,128)(2,1)S(1)} %collective-permute-done.4.got_ref.refs_2_, ...), custom_call_target="tpu_custom_call" | custom-call | flops 1342177280 | bytes 6160384 | tf_op jit(solution)/shard_map/project/pallas_call | solution.py:300
  34.2 1.6 %collective-permute-start.6 = (bf16[160,1024]{1,0:T(8,128)(2,1)S(1)}, bf16[160,1024]{1,0:T(8,128)(2,1)S(1)}, u32[]{:S(2)}, u32[]{:S(2)}) collective-permute-start(bf16[160,1024]{1,0:T(8,128)(2,1)S(1)} %get-tuple-element.40.refs_1_), channel_id=1, source_target_pairs={{0,2},{1,3},{2,0},{3,1},{4,6},{5,7},{6,4},{7,5},{8,10},{9,11},{10,... | collective-permute-start | bytes 983048 | tf_op jit(solution)/shard_map/ppermute | solution.py:407
  39.2 3.8 %collective-permute-done.9 = f32[128,128]{1,0:T(8,128)S(1)} collective-permute-done((f32[128,128]{1,0:T(8,128)S(1)}, f32[128,128]{1,0:T(8,128)S(1)}, u32[]{:S(2)}, u32[]{:S(2)}) %collective-permute-start.9) | collective-permute-done | bytes 65568 | tf_op jit(solution)/shard_map/ppermute | solution.py:407
  42.9 2.8 %project.4.refs_4_ = f32[2,160,512]{2,1,0:T(8,128)S(1)} custom-call(s32[5]{0:T(128)S(1)} %stack.42.ids_ref, bf16[320,1024]{1,0:T(8,128)(2,1)S(1)} %get-tuple-element.41.refs_0_, bf16[160,1024]{1,0:T(8,128)(2,1)S(1)} %collective-permute-done.10.refs_1_, bf16[8192,512]{1,0:T(8,128)(2,1)} %refs_2_.3, ...), custom_call_target="tpu_custom_call" | custom-call | flops 671088640 | bytes 3080192 | tf_op jit(solution)/shard_map/project/pallas_call | solution.py:300
  45.7 1.6 %collective-permute-start.11 = (f32[128,128]{1,0:T(8,128)S(1)}, f32[128,128]{1,0:T(8,128)S(1)}, u32[]{:S(2)}, u32[]{:S(2)}) collective-permute-start(f32[128,128]{1,0:T(8,128)S(1)} %add.47.refs_5_), channel_id=1, source_target_pairs={{0,8},{4,12},{8,0},{12,4},{16,24},{20,28},{24,16},{28,20},{1,9},{5... | collective-permute-start | bytes 196616 | tf_op jit(solution)/shard_map/ppermute | solution.py:407
  47.3 2.7 %collective-permute-done.11 = f32[128,128]{1,0:T(8,128)S(1)} collective-permute-done((f32[128,128]{1,0:T(8,128)S(1)}, f32[128,128]{1,0:T(8,128)S(1)}, u32[]{:S(2)}, u32[]{:S(2)}) %collective-permute-start.11) | collective-permute-done | bytes 65568 | tf_op jit(solution)/shard_map/ppermute | solution.py:407
  50.1 2.6 %collective-permute-start.12 = (f32[128,128]{1,0:T(8,128)S(1)}, f32[128,128]{1,0:T(8,128)S(1)}, u32[]{:S(2)}, u32[]{:S(2)}) collective-permute-start(f32[128,128]{1,0:T(8,128)S(1)} %add.48.refs_5_), channel_id=1, source_target_pairs={{0,16},{4,20},{8,24},{12,28},{16,0},{20,4},{24,8},{28,12},{1,17},{... | collective-permute-start | bytes 196616 | tf_op jit(solution)/shard_map/ppermute | solution.py:407
  52.7 3.8 %project.5 = (f32[640,128]{1,0:T(8,128)S(1)}, f32[640,128]{1,0:T(8,128)S(1)}) custom-call(s32[5]{0:T(128)S(1)} %stack.42.ids_ref, bf16[320,1024]{1,0:T(8,128)(2,1)S(1)} %get-tuple-element.32.refs_0_, bf16[160,1024]{1,0:T(8,128)(2,1)S(1)} %collective-permute-done.6.refs_1_, bf16[8192,512]{1,0:T(8,128)(2,1)} %refs_2_.3, ...), custom_call_target="tpu_custom_call" | custom-call | flops 671088640 | bytes 3080192 | tf_op jit(solution)/shard_map/project/pallas_call | solution.py:300
  58.9 5.5 %factor.1.inv_ref = f32[160,160]{1,0:T(8,128)S(1)} custom-call(f32[128,128]{1,0:T(8,128)S(1)} %add.49.g_ref, f32[640,128]{1,0:T(8,128)S(1)} %add.50.refs_0_), custom_call_target="tpu_custom_call" | custom-call | flops 6000000000 | bytes 102400 | tf_op jit(solution)/shard_map/factor/pallas_call | solution.py:245
  64.7 2.2 %collective-permute-done.15.refs_4_ = bf16[160,1024]{1,0:T(8,128)(2,1)S(1)} collective-permute-done((bf16[160,1024]{1,0:T(8,128)(2,1)S(1)}, bf16[160,1024]{1,0:T(8,128)(2,1)S(1)}, u32[]{:S(2)}, u32[]{:S(2)}) %collective-permute-start.15) | collective-permute-done | bytes 327712 | tf_op jit(solution)/shard_map/ppermute | solution.py:407
  66.9 1.6 %collective-permute-start.16 = (f32[160,128]{1,0:T(8,128)S(1)}, f32[160,128]{1,0:T(8,128)S(1)}, u32[]{:S(2)}, u32[]{:S(2)}) collective-permute-start(f32[160,128]{1,0:T(8,128)S(1)} %slice.28), channel_id=1, source_target_pairs={{0,8},{4,12},{8,0},{12,4},{16,24},{20,28},{24,16},{28,20},{1,9},{5... | collective-permute-start | bytes 245768 | tf_op jit(solution)/shard_map/ppermute | solution.py:407
  68.8 2.5 %collective-permute-done.16 = f32[160,128]{1,0:T(8,128)S(1)} collective-permute-done((f32[160,128]{1,0:T(8,128)S(1)}, f32[160,128]{1,0:T(8,128)S(1)}, u32[]{:S(2)}, u32[]{:S(2)}) %collective-permute-start.16) | collective-permute-done | bytes 81952 | tf_op jit(solution)/shard_map/ppermute | solution.py:407
  71.3 1.5 %collective-permute-start.17 = (f32[80,128]{1,0:T(8,128)S(1)}, f32[80,128]{1,0:T(8,128)S(1)}, u32[]{:S(2)}, u32[]{:S(2)}) collective-permute-start(f32[80,128]{1,0:T(8,128)S(1)} %slice.35), channel_id=1, source_target_pairs={{0,16},{4,20},{8,24},{12,28},{16,0},{20,4},{24,8},{28,12},{1,17},{... | collective-permute-start | bytes 122888 | tf_op jit(solution)/shard_map/ppermute | solution.py:407
  72.8 3.5 %collective-permute-done.17 = f32[80,128]{1,0:T(8,128)S(1)} collective-permute-done((f32[80,128]{1,0:T(8,128)S(1)}, f32[80,128]{1,0:T(8,128)S(1)}, u32[]{:S(2)}, u32[]{:S(2)}) %collective-permute-start.17) | collective-permute-done | bytes 40992 | tf_op jit(solution)/shard_map/ppermute | solution.py:407
  76.3 1.9 %collective-permute-start.18 = (f32[80,128]{1,0:T(8,128)S(1)}, f32[80,128]{1,0:T(8,128)S(1)}, u32[]{:S(2)}, u32[]{:S(2)}) collective-permute-start(f32[80,128]{1,0:T(8,128)S(1)} %slice_add_fusion.2), channel_id=1, source_target_pairs={{0,0},{1,8},{2,16},{3,24},{4,1},{5,9},{6,17},{7,25},{8,2},{9,10},{... | collective-permute-start | bytes 122888 | tf_op jit(solution)/shard_map/ppermute | solution.py:517
  78.2 7.6 %collective-permute-done.18.piece_ref = f32[80,128]{1,0:T(8,128)S(1)} collective-permute-done((f32[80,128]{1,0:T(8,128)S(1)}, f32[80,128]{1,0:T(8,128)S(1)}, u32[]{:S(2)}, u32[]{:S(2)}) %collective-permute-start.18) | collective-permute-done | bytes 40992 | tf_op jit(solution)/shard_map/ppermute | solution.py:517
  85.8 2.5 %finish.1 = (f32[160,2048]{1,0:T(8,128)}, f32[8,1280]{1,0:T(8,128)}) custom-call(f32[160,160]{1,0:T(8,128)S(1)} %factor.1.inv_ref, f32[80,128]{1,0:T(8,128)S(1)} %collective-permute-done.18.piece_ref, bf16[320,1024]{1,0:T(8,128)(2,1)S(1)} %get-tuple-element.38.own_ref.refs_0_, bf16[320,1024]{1,0:T(8,128)(2,1)S(1)} %get-tuple-element.39.own_ref.refs_1_, ...), custom_call_target="tpu_custom_call" | custom-call | flops 629145600 | bytes 3932160 | tf_op jit(solution)/shard_map/finish/pallas_call | solution.py:394
  (49 shorter events, 13.2 us)
Async XLA Ops:
  0.6 0.9 %copy-start = (bf16[512,160]{0,1:T(8,128)(2,1)S(1)}, bf16[512,160]{0,1:T(8,128)(2,1)}, u32[]{:S(2)}) copy-start(bf16[512,160]{0,1:T(8,128)(2,1)} %param.3) | copy-start | bytes 491524
  2.8 5.4 %collective-permute-start = (bf16[1280,512]{1,0:T(8,128)(2,1)S(1)}, bf16[1280,512]{1,0:T(8,128)(2,1)S(1)}, u32[]{:S(2)}, u32[]{:S(2)}) collective-permute-start(bf16[1280,512]{1,0:T(8,128)(2,1)S(1)} %lend.2.refs_0_), channel_id=1, source_target_pairs={{0,1},{1,0},{2,3},{3,2},{4,5},{5,4},{6,7},{7,6},{8,9},{9,8},{10,11... | collective-permute-start | bytes 3932168 | tf_op jit(solution)/shard_map/ppermute | solution.py:407
  3.0 5.3 %copy-start.1 = (bf16[512,160]{0,1:T(8,128)(2,1)S(1)}, bf16[512,160]{0,1:T(8,128)(2,1)}, u32[]{:S(2)}) copy-start(bf16[512,160]{0,1:T(8,128)(2,1)} %param.3) | copy-start | bytes 491524
  7.1 4.4 %collective-permute-start.1 = (bf16[1024,512]{1,0:T(8,128)(2,1)}, bf16[1024,512]{1,0:T(8,128)(2,1)}, u32[]{:S(2)}, u32[]{:S(2)}) collective-permute-start(bf16[1024,512]{1,0:T(8,128)(2,1)} %get-tuple-element.30), channel_id=1, source_target_pairs={{0,1},{1,0},{2,3},{3,2},{4,5},{5,4},{6,7},{7,6},{8,9},{9,8},{10,11... | collective-permute-start | bytes 3145736 | tf_op jit(solution)/shard_map/ppermute | solution.py:407
  7.7 8.5 %collective-permute-start.3 = (bf16[1024,512]{1,0:T(8,128)(2,1)}, bf16[1024,512]{1,0:T(8,128)(2,1)}, u32[]{:S(2)}, u32[]{:S(2)}) collective-permute-start(bf16[1024,512]{1,0:T(8,128)(2,1)} %get-tuple-element.34), channel_id=1, source_target_pairs={{0,1},{1,0},{2,3},{3,2},{4,5},{5,4},{6,7},{7,6},{8,9},{9,8},{10,11... | collective-permute-start | bytes 3145736 | tf_op jit(solution)/shard_map/ppermute | solution.py:407
  7.8 11.4 %collective-permute-start.2 = (bf16[1024,512]{1,0:T(8,128)(2,1)}, bf16[1024,512]{1,0:T(8,128)(2,1)}, u32[]{:S(2)}, u32[]{:S(2)}) collective-permute-start(bf16[1024,512]{1,0:T(8,128)(2,1)} %get-tuple-element.33), channel_id=1, source_target_pairs={{0,1},{1,0},{2,3},{3,2},{4,5},{5,4},{6,7},{7,6},{8,9},{9,8},{10,11... | collective-permute-start | bytes 3145736 | tf_op jit(solution)/shard_map/ppermute | solution.py:407
  11.0 10.8 %collective-permute-start.4 = (bf16[160,1024]{1,0:T(8,128)(2,1)}, bf16[160,1024]{1,0:T(8,128)(2,1)S(1)}, u32[]{:S(2)}, u32[]{:S(2)}) collective-permute-start(bf16[160,1024]{1,0:T(8,128)(2,1)} %get-tuple-element.31.refs_3_), channel_id=1, source_target_pairs={{0,2},{1,3},{2,0},{3,1},{4,6},{5,7},{6,4},{7,5},{8,10},{9,11},{10,... | collective-permute-start | bytes 983048 | tf_op jit(solution)/shard_map/ppermute | solution.py:407
  14.6 14.2 %collective-permute-start.5 = (bf16[160,1024]{1,0:T(8,128)(2,1)}, bf16[160,1024]{1,0:T(8,128)(2,1)S(1)}, u32[]{:S(2)}, u32[]{:S(2)}) collective-permute-start(bf16[160,1024]{1,0:T(8,128)(2,1)} %get-tuple-element.35.refs_3_), channel_id=1, source_target_pairs={{0,2},{1,3},{2,0},{3,1},{4,6},{5,7},{6,4},{7,5},{8,10},{9,11},{10,... | collective-permute-start | bytes 983048 | tf_op jit(solution)/shard_map/ppermute | solution.py:407
  18.6 24.3 %collective-permute-start.10 = (bf16[160,1024]{1,0:T(8,128)(2,1)S(1)}, bf16[160,1024]{1,0:T(8,128)(2,1)S(1)}, u32[]{:S(2)}, u32[]{:S(2)}) collective-permute-start(bf16[160,1024]{1,0:T(8,128)(2,1)S(1)} %get-tuple-element.36.refs_3_), channel_id=1, source_target_pairs={{0,2},{1,3},{2,0},{3,1},{4,6},{5,7},{6,4},{7,5},{8,10},{9,11},{10,... | collective-permute-start | bytes 983048 | tf_op jit(solution)/shard_map/ppermute | solution.py:407
  29.6 7.6 %collective-permute-start.7 = (f32[128,128]{1,0:T(8,128)S(1)}, f32[128,128]{1,0:T(8,128)S(1)}, u32[]{:S(2)}, u32[]{:S(2)}) collective-permute-start(f32[128,128]{1,0:T(8,128)S(1)} %gram.3.refs_8_), channel_id=1, source_target_pairs={{0,2},{1,3},{2,0},{3,1},{4,6},{5,7},{6,4},{7,5},{8,10},{9,11},{10,... | collective-permute-start | bytes 196616 | tf_op jit(solution)/shard_map/ppermute | solution.py:407
  34.2 18.5 %collective-permute-start.6 = (bf16[160,1024]{1,0:T(8,128)(2,1)S(1)}, bf16[160,1024]{1,0:T(8,128)(2,1)S(1)}, u32[]{:S(2)}, u32[]{:S(2)}) collective-permute-start(bf16[160,1024]{1,0:T(8,128)(2,1)S(1)} %get-tuple-element.40.refs_1_), channel_id=1, source_target_pairs={{0,2},{1,3},{2,0},{3,1},{4,6},{5,7},{6,4},{7,5},{8,10},{9,11},{10,... | collective-permute-start | bytes 983048 | tf_op jit(solution)/shard_map/ppermute | solution.py:407
  37.3 1.3 %collective-permute-start.8 = (f32[128,128]{1,0:T(8,128)S(1)}, f32[128,128]{1,0:T(8,128)S(1)}, u32[]{:S(2)}, u32[]{:S(2)}) collective-permute-start(f32[128,128]{1,0:T(8,128)S(1)} %add.45), channel_id=1, source_target_pairs={{0,1},{1,0},{2,3},{3,2},{4,5},{5,4},{6,7},{7,6},{8,9},{9,8},{10,11... | collective-permute-start | bytes 196616 | tf_op jit(solution)/shard_map/ppermute | solution.py:407
  38.6 4.3 %collective-permute-start.9 = (f32[128,128]{1,0:T(8,128)S(1)}, f32[128,128]{1,0:T(8,128)S(1)}, u32[]{:S(2)}, u32[]{:S(2)}) collective-permute-start(f32[128,128]{1,0:T(8,128)S(1)} %add.46), channel_id=1, source_target_pairs={{0,4},{4,0},{8,12},{12,8},{16,20},{20,16},{24,28},{28,24},{1,5},{5... | collective-permute-start | bytes 196616 | tf_op jit(solution)/shard_map/ppermute | solution.py:407
  45.7 4.3 %collective-permute-start.11 = (f32[128,128]{1,0:T(8,128)S(1)}, f32[128,128]{1,0:T(8,128)S(1)}, u32[]{:S(2)}, u32[]{:S(2)}) collective-permute-start(f32[128,128]{1,0:T(8,128)S(1)} %add.47.refs_5_), channel_id=1, source_target_pairs={{0,8},{4,12},{8,0},{12,4},{16,24},{20,28},{24,16},{28,20},{1,9},{5... | collective-permute-start | bytes 196616 | tf_op jit(solution)/shard_map/ppermute | solution.py:407
  50.1 6.5 %collective-permute-start.12 = (f32[128,128]{1,0:T(8,128)S(1)}, f32[128,128]{1,0:T(8,128)S(1)}, u32[]{:S(2)}, u32[]{:S(2)}) collective-permute-start(f32[128,128]{1,0:T(8,128)S(1)} %add.48.refs_5_), channel_id=1, source_target_pairs={{0,16},{4,20},{8,24},{12,28},{16,0},{20,4},{24,8},{28,12},{1,17},{... | collective-permute-start | bytes 196616 | tf_op jit(solution)/shard_map/ppermute | solution.py:407
  56.6 1.7 %collective-permute-start.13 = (f32[640,128]{1,0:T(8,128)S(1)}, f32[640,128]{1,0:T(8,128)S(1)}, u32[]{:S(2)}, u32[]{:S(2)}) collective-permute-start(f32[640,128]{1,0:T(8,128)S(1)} %get-tuple-element.48), channel_id=1, source_target_pairs={{0,1},{1,0},{2,3},{3,2},{4,5},{5,4},{6,7},{7,6},{8,9},{9,8},{10,11... | collective-permute-start | bytes 983048 | tf_op jit(solution)/shard_map/ppermute | solution.py:407
  56.7 10.2 %collective-permute-start.15 = (bf16[160,1024]{1,0:T(8,128)(2,1)S(1)}, bf16[160,1024]{1,0:T(8,128)(2,1)S(1)}, u32[]{:S(2)}, u32[]{:S(2)}) collective-permute-start(bf16[160,1024]{1,0:T(8,128)(2,1)S(1)} %slice.26), channel_id=1, source_target_pairs={{0,2},{1,3},{2,0},{3,1},{4,6},{5,7},{6,4},{7,5},{8,10},{9,11},{10,... | collective-permute-start | bytes 983048 | tf_op jit(solution)/shard_map/ppermute | solution.py:407
  58.3 6.3 %collective-permute-start.14 = (f32[320,128]{1,0:T(8,128)S(1)}, f32[320,128]{1,0:T(8,128)S(1)}, u32[]{:S(2)}, u32[]{:S(2)}) collective-permute-start(f32[320,128]{1,0:T(8,128)S(1)} %slice.33), channel_id=1, source_target_pairs={{0,4},{4,0},{8,12},{12,8},{16,20},{20,16},{24,28},{28,24},{1,5},{5... | collective-permute-start | bytes 491528 | tf_op jit(solution)/shard_map/ppermute | solution.py:407
  66.9 4.4 %collective-permute-start.16 = (f32[160,128]{1,0:T(8,128)S(1)}, f32[160,128]{1,0:T(8,128)S(1)}, u32[]{:S(2)}, u32[]{:S(2)}) collective-permute-start(f32[160,128]{1,0:T(8,128)S(1)} %slice.28), channel_id=1, source_target_pairs={{0,8},{4,12},{8,0},{12,4},{16,24},{20,28},{24,16},{28,20},{1,9},{5... | collective-permute-start | bytes 245768 | tf_op jit(solution)/shard_map/ppermute | solution.py:407
  68.5 9.8 %collective-permute-start.19 = (bf16[160,1024]{1,0:T(8,128)(2,1)S(1)}, bf16[160,1024]{1,0:T(8,128)(2,1)S(1)}, u32[]{:S(2)}, u32[]{:S(2)}) collective-permute-start(bf16[160,1024]{1,0:T(8,128)(2,1)S(1)} %slice.31), channel_id=1, source_target_pairs={{0,2},{1,3},{2,0},{3,1},{4,6},{5,7},{6,4},{7,5},{8,10},{9,11},{10,... | collective-permute-start | bytes 983048 | tf_op jit(solution)/shard_map/ppermute | solution.py:407
  71.3 5.0 %collective-permute-start.17 = (f32[80,128]{1,0:T(8,128)S(1)}, f32[80,128]{1,0:T(8,128)S(1)}, u32[]{:S(2)}, u32[]{:S(2)}) collective-permute-start(f32[80,128]{1,0:T(8,128)S(1)} %slice.35), channel_id=1, source_target_pairs={{0,16},{4,20},{8,24},{12,28},{16,0},{20,4},{24,8},{28,12},{1,17},{... | collective-permute-start | bytes 122888 | tf_op jit(solution)/shard_map/ppermute | solution.py:407
  76.3 9.5 %collective-permute-start.18 = (f32[80,128]{1,0:T(8,128)S(1)}, f32[80,128]{1,0:T(8,128)S(1)}, u32[]{:S(2)}, u32[]{:S(2)}) collective-permute-start(f32[80,128]{1,0:T(8,128)S(1)} %slice_add_fusion.2), channel_id=1, source_target_pairs={{0,0},{1,8},{2,16},{3,24},{4,1},{5,9},{6,17},{7,25},{8,2},{9,10},{... | collective-permute-start | bytes 122888 | tf_op jit(solution)/shard_map/ppermute | solution.py:517

commit v10 on v9

--- a/solution.py
+++ b/solution.py
@@ -1,6 +1,7 @@
 import functools
 import jax
 import jax.numpy as jnp
+import numpy as np
 from jax import lax
 from jax.experimental import pallas as pl
 from jax.experimental.pallas import tpu as pltpu
@@ -12,7 +13,7 @@
 UNIT = 1024
 LEND_PARTS = 4
 PROJECT_ROWS = 512
-PLACE = (1, True, 1, 1, -1)
+PLACE = (-1, True, 1, -1, 1, True)
 SKETCH_STEPS = 1
 FACTOR_COST = 6e9
 COST_CUT = 1
@@ -335,19 +336,23 @@
     return sum(1 << (count - 1 - b) for b in range(count) if (p >> b) & 1)
 
 
-def tail(pieces, samp, per_node, width_cols, t_ref, ids_ref, beside, *refs):
+def column_order(depth, samp, per_node, width_cols):
+    width = per_node * width_cols
+    dst = np.arange(depth)
+    a, rest = dst // (samp * width), dst % (samp * width)
+    s, rest = rest // width, rest % width
+    src = (a * per_node + rest // width_cols) * (samp * width_cols) + s * width_cols + rest % width_cols
+    return jnp.asarray(np.arange(depth)[:, None] == src[None, :], BF16)
+
+
+def tail(pieces, per_node, width_cols, t_ref, ids_ref, beside, *refs):
     outs, hold = refs[:-1], refs[-1]
     wide, rank, depth = t_ref.shape
     width = per_node * width_cols
     fold = folding(rank, width)
     tall = rank // fold
     me_node = ids_ref[ids_ref.shape[0] - 1]
-    dst = iota((depth, depth), 1)
-    src = iota((depth, depth), 0)
-    a, rest = dst // (samp * width), dst % (samp * width)
-    s, rest = rest // width, rest % width
-    want = (a * per_node + rest // width_cols) * (samp * width_cols) + s * width_cols + rest % width_cols
-    move = jnp.where(src == want, 1.0, 0.0).astype(BF16)
+    move = beside[0][...]
     bits = pieces.bit_length() - 1
     for w in range(wide):
         t = t_ref[w]
@@ -463,8 +468,11 @@
         return [(pairs[b], arrived[b], slot[b], borrowed[b]) for b in chosen]
 
     gram = own_gram(own[0], got_high[0], None, None)
+    t = project(ids, parts([(0, 0)]), snapshots, None, [gram])
+    if PLACE[5]:
+        t, gram = lax.optimization_barrier((t, gram))
     gram = own_gram(own[1], got_high[1], gram, 1.0 / total, done)
-    t = project(ids, parts([(0, 0), (0, 1)]), snapshots, None, [gram])
+    t = project(ids, parts([(0, 1)]), snapshots, t, [gram])
     final = blocks[-1]
     late = [(final[0] ^ last, final[1])]
     high, t = lax.optimization_barrier((high, t))
@@ -474,6 +482,9 @@
     for c in range(2):
         low, _ = lax.optimization_barrier((pairs[last, c][rank:], gram))
         got_low.append(swap(low, "samp", samp, last))
+    if PLACE[0] < 0:
+        t = project(ids, parts([(last, 0)]), snapshots, t)
+        gram, t = lax.optimization_barrier((gram, t))
     bit = last // 2
     while bit:
         gram = gram + swap(gram, "samp", samp, bit)
@@ -481,7 +492,7 @@
     rounds = node.bit_length() - 1
     before = gram
     for k in range(rounds):
-        if k == min(PLACE[0], rounds - 1):
+        if k == PLACE[0]:
             t = project(ids, parts([(last, 0)]), snapshots, t, [gram])
             gram, t = lax.optimization_barrier((gram, t))
         before = gram
@@ -491,12 +502,15 @@
     width_cols = P2 // samp
     tall = rank // folding(rank, per_node * width_cols)
     messages = project(
-        ids, parts(late), snapshots, t, [before],
-        functools.partial(tail, node, samp, per_node, width_cols),
+        ids, parts(late), snapshots, t, [column_order(snapshots.shape[1], samp, per_node, width_cols), before],
+        functools.partial(tail, node, per_node, width_cols),
         [jax.ShapeDtypeStruct((node * tall, 128), F32)] * last,
         [pltpu.VMEM((node, tall, 128), F32)])
     if PLACE[1]:
         *messages, gram = lax.optimization_barrier((*messages, gram))
+    for c in range(2):
+        if PLACE[3 + c] < 0:
+            *messages, got_low[c] = lax.optimization_barrier((*messages, got_low[c]))
 
     pieces = messages[0]
     for d in near:

time: 88.6 us -> 89.2 us (level)
  waiting for transfers between devices: 33.1 us -> 29.9 us
  Pallas kernels: 36.1 us -> 38.6 us
  starting transfers between devices: 16.9 us -> 18.2 us
    ppermute x19, waiting for transfers between devices: 25.5 us -> 22.3 us  [swap(): return lax.ppermute(value, axis, [(i, i ^ bit) for i in range(size)])]
    pallas_call x3 -> x4, Pallas kernels: 10.6 us -> 12.5 us  [project(): pl.pallas_call(functools.partial(project_kernel, count, wide, len(bases),...]
    ppermute x19, starting transfers between devices: 15 us -> 16.3 us  [swap(): return lax.ppermute(value, axis, [(i, i ^ bit) for i in range(size)])]
  transfers between devices with their start and end apart: 20 -> 20, of which waited for: 12 -> 10; matrix products, arithmetic and copies ran while one was open for 0% -> 0% of each run, Pallas kernels for 37% -> 39%
where the time goes in v10:
time: 89.2 us; the launch traced here: 88.8 us
  Pallas kernels  38.6 us (43%)
  waiting for transfers between devices  29.9 us (34%)
  starting transfers between devices  18.2 us (20%)
  local copies, waits for them, and re-layouts  1.08 us (1%)
    ppermute x19, waiting for transfers between devices, swap(): return lax.ppermute(value, axis, [(i, i ^ bit) for i in range(size)])  22.3 us
    ppermute x19, starting transfers between devices, swap(): return lax.ppermute(value, axis, [(i, i ^ bit) for i in range(size)])  16.3 us
    pallas_call x4, Pallas kernels, project(): pl.pallas_call(functools.partial(project_kernel, count, wide, len(bases),...  12.5 us
    pallas_call x4, Pallas kernels, sketch(): pl.pallas_call(functools.partial(sketch_kernel, count, lent), grid_spec=p...  11.3 us
    ppermute x1, waiting for transfers between devices, body(): piece = lax.ppermute(pieces, ('node', 'samp'), route)  7.57 us
    pallas_call x1, Pallas kernels, factor_inverse(): pl.pallas_call(functools.partial(factor_kernel, rank), in_specs=[HELD] +...  5.48 us
    pallas_call x2, Pallas kernels, lend(): pl.pallas_call(functools.partial(lend_kernel, size, stride, at), in_specs...  5.35 us
    pallas_call x1, Pallas kernels, finish(): pl.pallas_call(functools.partial(finish_kernel, scale, per_node, width_co...  2.45 us
  transfers between devices with their start and end apart: 20, of which 10 were waited for; matrix products, arithmetic and copies ran while one was open for 0% of the time, Pallas kernels for 39%

profile of v10, /device:TPU:6, one launch (start us, length us, event | category | flops | bytes accessed | tf_op | source)
XLA Modules:
  0.0 88.8 jit_solution(611221431231219916)
XLA Ops:
  3.0 4.1 %lend.3 = (bf16[1024,512]{1,0:T(8,128)(2,1)}, bf16[1024,512]{1,0:T(8,128)(2,1)}, bf16[1024,512]{1,0:T(8,128)(2,1)}) custom-call(s32[3]{0:T(128)S(1)} %pad_add_fusion.ids_ref, bf16[8192,512]{1,0:T(8,128)(2,1)} %refs_2_.7, bf16[1280,512]{1,0:T(8,128)(2,1)S(1)} %lend.2.refs_0_), custom_call_target="tpu_custom_call" | custom-call | bytes 6291456 | tf_op jit(solution)/shard_map/lend/pallas_call | solution.py:75
  8.2 2.8 %sketch.4 = (bf16[320,1024]{1,0:T(8,128)(2,1)S(1)}, bf16[160,1024]{1,0:T(8,128)(2,1)}) custom-call(s32[1]{0:T(128)} %bitcast.ids_ref, bf16[8192,512]{1,0:T(8,128)(2,1)} %refs_2_.7, bf16[160,512]{1,0:T(8,128)(2,1)S(1)} %bitcast.13, bf16[1280,512]{1,0:T(8,128)(2,1)S(1)} %collective-permute-done.refs_1_.refs_2_.refs_3_, ...), custom_call_target="tpu_custom_call" | custom-call | flops 335544320 | bytes 3080192 | tf_op jit(solution)/shard_map/sketch/pallas_call | solution.py:109
  11.5 3.1 %sketch.5 = (bf16[320,1024]{1,0:T(8,128)(2,1)S(1)}, bf16[160,1024]{1,0:T(8,128)(2,1)}) custom-call(s32[1]{0:T(128)} %bitcast.1.ids_ref, bf16[8192,512]{1,0:T(8,128)(2,1)} %refs_2_.7, bf16[160,512]{1,0:T(8,128)(2,1)S(1)} %bitcast.14, bf16[1280,512]{1,0:T(8,128)(2,1)S(1)} %collective-permute-done.refs_1_.refs_2_.refs_3_, ...), custom_call_target="tpu_custom_call" | custom-call | flops 335544320 | bytes 3080192 | tf_op jit(solution)/shard_map/sketch/pallas_call | solution.py:109
  16.1 3.1 %sketch.6 = (bf16[320,1024]{1,0:T(8,128)(2,1)S(1)}, bf16[160,1024]{1,0:T(8,128)(2,1)}) custom-call(s32[1]{0:T(128)} %bitcast.2.ids_ref, bf16[8192,512]{1,0:T(8,128)(2,1)} %refs_2_.7, bf16[160,512]{1,0:T(8,128)(2,1)S(1)} %bitcast.15, bf16[1280,512]{1,0:T(8,128)(2,1)S(1)} %collective-permute-done.refs_1_.refs_2_.refs_3_, ...), custom_call_target="tpu_custom_call" | custom-call | flops 335544320 | bytes 3080192 | tf_op jit(solution)/shard_map/sketch/pallas_call | solution.py:109
  19.8 2.4 %sketch.7 = (bf16[320,1024]{1,0:T(8,128)(2,1)S(1)}, bf16[160,1024]{1,0:T(8,128)(2,1)S(1)}) custom-call(s32[1]{0:T(128)} %bitcast.3.ids_ref, bf16[8192,512]{1,0:T(8,128)(2,1)} %refs_2_.7, bf16[160,512]{1,0:T(8,128)(2,1)S(1)} %bitcast.16, bf16[1280,512]{1,0:T(8,128)(2,1)S(1)} %collective-permute-done.refs_1_.refs_2_.refs_3_, ...), custom_call_target="tpu_custom_call" | custom-call | flops 335544320 | bytes 3080192 | tf_op jit(solution)/shard_map/sketch/pallas_call | solution.py:109
  22.9 2.9 %project.4.refs_4_ = f32[2,160,512]{2,1,0:T(8,128)S(1)} custom-call(s32[5]{0:T(128)S(1)} %stack.42.ids_ref, bf16[320,1024]{1,0:T(8,128)(2,1)S(1)} %get-tuple-element.44.own_ref.refs_0_, bf16[160,1024]{1,0:T(8,128)(2,1)S(1)} %collective-permute-done.5.got_ref.refs_1_.refs_2_, bf16[8192,512]{1,0:T(8,128)(2,1)} %refs_2_.7, ...), custom_call_target="tpu_custom_call" | custom-call | flops 671088640 | bytes 3080192 | tf_op jit(solution)/shard_map/project/pallas_call | solution.py:301
  25.8 2.9 %collective-permute-done.4.got_ref.refs_1_.refs_3_ = bf16[160,1024]{1,0:T(8,128)(2,1)S(1)} collective-permute-done((bf16[160,1024]{1,0:T(8,128)(2,1)}, bf16[160,1024]{1,0:T(8,128)(2,1)S(1)}, u32[]{:S(2)}, u32[]{:S(2)}) %collective-permute-start.4) | collective-permute-done | bytes 327712 | tf_op jit(solution)/shard_map/ppermute | solution.py:412
  30.1 2.9 %project.5.refs_4_ = f32[2,160,512]{2,1,0:T(8,128)S(1)} custom-call(s32[5]{0:T(128)S(1)} %stack.42.ids_ref, bf16[320,1024]{1,0:T(8,128)(2,1)S(1)} %get-tuple-element.43.own_ref.refs_0_.refs_1_, bf16[160,1024]{1,0:T(8,128)(2,1)S(1)} %collective-permute-done.4.got_ref.refs_1_.refs_3_, bf16[8192,512]{1,0:T(8,128)(2,1)} %refs_2_.7, ...), custom_call_target="tpu_custom_call" | custom-call | flops 671088640 | bytes 3080192 | tf_op jit(solution)/shard_map/project/pallas_call | solution.py:301
  34.7 2.5 %collective-permute-done.7 = f32[128,128]{1,0:T(8,128)S(1)} collective-permute-done((f32[128,128]{1,0:T(8,128)S(1)}, f32[128,128]{1,0:T(8,128)S(1)}, u32[]{:S(2)}, u32[]{:S(2)}) %collective-permute-start.7) | collective-permute-done | bytes 65568 | tf_op jit(solution)/shard_map/ppermute | solution.py:412
  37.8 2.9 %project.6.refs_4_ = f32[2,160,512]{2,1,0:T(8,128)S(1)} custom-call(s32[5]{0:T(128)S(1)} %stack.42.ids_ref, bf16[320,1024]{1,0:T(8,128)(2,1)S(1)} %copy-done.3, bf16[160,1024]{1,0:T(8,128)(2,1)} %collective-permute-done.8.refs_1_, bf16[8192,512]{1,0:T(8,128)(2,1)} %refs_2_.7, bf16[1280,512]{1,0:T(8,128)(2,1)S(1)} %collective-permute-done.refs_1_.refs_2_.refs_3_, ...), custom_call_target="tpu_custom_call" | custom-call | flops 671088640 | bytes 3080192 | tf_op jit(solution)/shard_map/project/pallas_call | solution.py:301
  42.1 4.3 %collective-permute-done.10 = f32[128,128]{1,0:T(8,128)S(1)} collective-permute-done((f32[128,128]{1,0:T(8,128)S(1)}, f32[128,128]{1,0:T(8,128)S(1)}, u32[]{:S(2)}, u32[]{:S(2)}) %collective-permute-start.10) | collective-permute-done | bytes 65568 | tf_op jit(solution)/shard_map/ppermute | solution.py:412
  46.3 1.6 %collective-permute-start.11 = (f32[128,128]{1,0:T(8,128)S(1)}, f32[128,128]{1,0:T(8,128)S(1)}, u32[]{:S(2)}, u32[]{:S(2)}) collective-permute-start(f32[128,128]{1,0:T(8,128)S(1)} %add.47), channel_id=1, source_target_pairs={{0,8},{4,12},{8,0},{12,4},{16,24},{20,28},{24,16},{28,20},{1,9},{5... | collective-permute-start | bytes 196616 | tf_op jit(solution)/shard_map/ppermute | solution.py:412
  48.0 2.7 %collective-permute-done.11 = f32[128,128]{1,0:T(8,128)S(1)} collective-permute-done((f32[128,128]{1,0:T(8,128)S(1)}, f32[128,128]{1,0:T(8,128)S(1)}, u32[]{:S(2)}, u32[]{:S(2)}) %collective-permute-start.11) | collective-permute-done | bytes 65568 | tf_op jit(solution)/shard_map/ppermute | solution.py:412
  50.7 2.7 %collective-permute-start.12 = (f32[128,128]{1,0:T(8,128)S(1)}, f32[128,128]{1,0:T(8,128)S(1)}, u32[]{:S(2)}, u32[]{:S(2)}) collective-permute-start(f32[128,128]{1,0:T(8,128)S(1)} %add.48.refs_6_), channel_id=1, source_target_pairs={{0,16},{4,20},{8,24},{12,28},{16,0},{20,4},{24,8},{28,12},{1,17},{... | collective-permute-start | bytes 196616 | tf_op jit(solution)/shard_map/ppermute | solution.py:412
  53.3 3.8 %project.7 = (f32[640,128]{1,0:T(8,128)S(1)}, f32[640,128]{1,0:T(8,128)S(1)}) custom-call(s32[5]{0:T(128)S(1)} %stack.42.ids_ref, bf16[320,1024]{1,0:T(8,128)(2,1)S(1)} %get-tuple-element.37.refs_0_, bf16[160,1024]{1,0:T(8,128)(2,1)S(1)} %collective-permute-done.6.refs_1_, bf16[8192,512]{1,0:T(8,128)(2,1)} %refs_2_.7, ...), custom_call_target="tpu_custom_call" | custom-call | flops 671088640 | bytes 3080192 | tf_op jit(solution)/shard_map/project/pallas_call | solution.py:301
  59.5 5.5 %factor.1.inv_ref = f32[160,160]{1,0:T(8,128)S(1)} custom-call(f32[128,128]{1,0:T(8,128)S(1)} %add.49.g_ref, f32[640,128]{1,0:T(8,128)S(1)} %add.50.refs_0_), custom_call_target="tpu_custom_call" | custom-call | flops 6000000000 | bytes 102400 | tf_op jit(solution)/shard_map/factor/pallas_call | solution.py:246
  65.3 2.1 %collective-permute-done.16.refs_5_ = bf16[160,1024]{1,0:T(8,128)(2,1)S(1)} collective-permute-done((bf16[160,1024]{1,0:T(8,128)(2,1)S(1)}, bf16[160,1024]{1,0:T(8,128)(2,1)S(1)}, u32[]{:S(2)}, u32[]{:S(2)}) %collective-permute-start.16) | collective-permute-done | bytes 327712 | tf_op jit(solution)/shard_map/ppermute | solution.py:412
  67.4 1.6 %collective-permute-start.17 = (f32[160,128]{1,0:T(8,128)S(1)}, f32[160,128]{1,0:T(8,128)S(1)}, u32[]{:S(2)}, u32[]{:S(2)}) collective-permute-start(f32[160,128]{1,0:T(8,128)S(1)} %slice.29), channel_id=1, source_target_pairs={{0,8},{4,12},{8,0},{12,4},{16,24},{20,28},{24,16},{28,20},{1,9},{5... | collective-permute-start | bytes 245768 | tf_op jit(solution)/shard_map/ppermute | solution.py:412
  69.0 2.9 %collective-permute-done.17 = f32[160,128]{1,0:T(8,128)S(1)} collective-permute-done((f32[160,128]{1,0:T(8,128)S(1)}, f32[160,128]{1,0:T(8,128)S(1)}, u32[]{:S(2)}, u32[]{:S(2)}) %collective-permute-start.17) | collective-permute-done | bytes 81952 | tf_op jit(solution)/shard_map/ppermute | solution.py:412
  71.9 1.6 %collective-permute-start.18 = (f32[80,128]{1,0:T(8,128)S(1)}, f32[80,128]{1,0:T(8,128)S(1)}, u32[]{:S(2)}, u32[]{:S(2)}) collective-permute-start(f32[80,128]{1,0:T(8,128)S(1)} %slice.35), channel_id=1, source_target_pairs={{0,16},{4,20},{8,24},{12,28},{16,0},{20,4},{24,8},{28,12},{1,17},{... | collective-permute-start | bytes 122888 | tf_op jit(solution)/shard_map/ppermute | solution.py:412
  73.5 3.4 %collective-permute-done.18 = f32[80,128]{1,0:T(8,128)S(1)} collective-permute-done((f32[80,128]{1,0:T(8,128)S(1)}, f32[80,128]{1,0:T(8,128)S(1)}, u32[]{:S(2)}, u32[]{:S(2)}) %collective-permute-start.18) | collective-permute-done | bytes 40992 | tf_op jit(solution)/shard_map/ppermute | solution.py:412
  76.9 1.9 %collective-permute-start.19 = (f32[80,128]{1,0:T(8,128)S(1)}, f32[80,128]{1,0:T(8,128)S(1)}, u32[]{:S(2)}, u32[]{:S(2)}) collective-permute-start(f32[80,128]{1,0:T(8,128)S(1)} %slice_add_fusion.2), channel_id=1, source_target_pairs={{0,0},{1,8},{2,16},{3,24},{4,1},{5,9},{6,17},{7,25},{8,2},{9,10},{... | collective-permute-start | bytes 122888 | tf_op jit(solution)/shard_map/ppermute | solution.py:531
  78.8 7.6 %collective-permute-done.19.piece_ref = f32[80,128]{1,0:T(8,128)S(1)} collective-permute-done((f32[80,128]{1,0:T(8,128)S(1)}, f32[80,128]{1,0:T(8,128)S(1)}, u32[]{:S(2)}, u32[]{:S(2)}) %collective-permute-start.19) | collective-permute-done | bytes 40992 | tf_op jit(solution)/shard_map/ppermute | solution.py:531
  86.4 2.5 %finish.1 = (f32[160,2048]{1,0:T(8,128)}, f32[8,1280]{1,0:T(8,128)}) custom-call(f32[160,160]{1,0:T(8,128)S(1)} %factor.1.inv_ref, f32[80,128]{1,0:T(8,128)S(1)} %collective-permute-done.19.piece_ref, bf16[320,1024]{1,0:T(8,128)(2,1)S(1)} %get-tuple-element.44.own_ref.refs_0_, bf16[320,1024]{1,0:T(8,128)(2,1)S(1)} %get-tuple-element.43.own_ref.refs_0_.refs_1_, ...), custom_call_target="tpu_custom_call" | custom-call | flops 629145600 | bytes 3932160 | tf_op jit(solution)/shard_map/finish/pallas_call | solution.py:399
  (56 shorter events, 14.4 us)
Async XLA Ops:
  2.8 5.4 %collective-permute-start = (bf16[1280,512]{1,0:T(8,128)(2,1)S(1)}, bf16[1280,512]{1,0:T(8,128)(2,1)S(1)}, u32[]{:S(2)}, u32[]{:S(2)}) collective-permute-start(bf16[1280,512]{1,0:T(8,128)(2,1)S(1)} %lend.2.refs_0_), channel_id=1, source_target_pairs={{0,1},{1,0},{2,3},{3,2},{4,5},{5,4},{6,7},{7,6},{8,9},{9,8},{10,11... | collective-permute-start | bytes 3932168 | tf_op jit(solution)/shard_map/ppermute | solution.py:412
  3.0 5.2 %copy-start.1 = (bf16[512,160]{0,1:T(8,128)(2,1)S(1)}, bf16[512,160]{0,1:T(8,128)(2,1)}, u32[]{:S(2)}) copy-start(bf16[512,160]{0,1:T(8,128)(2,1)} %param.4) | copy-start | bytes 491524
  7.1 4.4 %collective-permute-start.1 = (bf16[1024,512]{1,0:T(8,128)(2,1)}, bf16[1024,512]{1,0:T(8,128)(2,1)}, u32[]{:S(2)}, u32[]{:S(2)}) collective-permute-start(bf16[1024,512]{1,0:T(8,128)(2,1)} %get-tuple-element.35), channel_id=1, source_target_pairs={{0,1},{1,0},{2,3},{3,2},{4,5},{5,4},{6,7},{7,6},{8,9},{9,8},{10,11... | collective-permute-start | bytes 3145736 | tf_op jit(solution)/shard_map/ppermute | solution.py:412
  7.6 8.4 %collective-permute-start.3 = (bf16[1024,512]{1,0:T(8,128)(2,1)}, bf16[1024,512]{1,0:T(8,128)(2,1)}, u32[]{:S(2)}, u32[]{:S(2)}) collective-permute-start(bf16[1024,512]{1,0:T(8,128)(2,1)} %get-tuple-element.39), channel_id=1, source_target_pairs={{0,1},{1,0},{2,3},{3,2},{4,5},{5,4},{6,7},{7,6},{8,9},{9,8},{10,11... | collective-permute-start | bytes 3145736 | tf_op jit(solution)/shard_map/ppermute | solution.py:412
  7.7 12.1 %collective-permute-start.2 = (bf16[1024,512]{1,0:T(8,128)(2,1)}, bf16[1024,512]{1,0:T(8,128)(2,1)}, u32[]{:S(2)}, u32[]{:S(2)}) collective-permute-start(bf16[1024,512]{1,0:T(8,128)(2,1)} %get-tuple-element.38), channel_id=1, source_target_pairs={{0,1},{1,0},{2,3},{3,2},{4,5},{5,4},{6,7},{7,6},{8,9},{9,8},{10,11... | collective-permute-start | bytes 3145736 | tf_op jit(solution)/shard_map/ppermute | solution.py:412
  10.9 3.6 %copy-start.2 = (bf16[320,1024]{1,0:T(8,128)(2,1)}, bf16[320,1024]{1,0:T(8,128)(2,1)S(1)}, u32[]{:S(2)}) copy-start(bf16[320,1024]{1,0:T(8,128)(2,1)S(1)} %get-tuple-element.48.refs_0_) | copy-start | bytes 1966084
  10.9 11.2 %collective-permute-start.5 = (bf16[160,1024]{1,0:T(8,128)(2,1)}, bf16[160,1024]{1,0:T(8,128)(2,1)S(1)}, u32[]{:S(2)}, u32[]{:S(2)}) collective-permute-start(bf16[160,1024]{1,0:T(8,128)(2,1)} %get-tuple-element.36.refs_3_), channel_id=1, source_target_pairs={{0,2},{1,3},{2,0},{3,1},{4,6},{5,7},{6,4},{7,5},{8,10},{9,11},{10,... | collective-permute-start | bytes 983048 | tf_op jit(solution)/shard_map/ppermute | solution.py:412
  14.6 14.2 %collective-permute-start.4 = (bf16[160,1024]{1,0:T(8,128)(2,1)}, bf16[160,1024]{1,0:T(8,128)(2,1)S(1)}, u32[]{:S(2)}, u32[]{:S(2)}) collective-permute-start(bf16[160,1024]{1,0:T(8,128)(2,1)} %get-tuple-element.40.refs_3_), channel_id=1, source_target_pairs={{0,2},{1,3},{2,0},{3,1},{4,6},{5,7},{6,4},{7,5},{8,10},{9,11},{10,... | collective-permute-start | bytes 983048 | tf_op jit(solution)/shard_map/ppermute | solution.py:412
  19.2 18.6 %collective-permute-start.8 = (bf16[160,1024]{1,0:T(8,128)(2,1)}, bf16[160,1024]{1,0:T(8,128)(2,1)}, u32[]{:S(2)}, u32[]{:S(2)}) collective-permute-start(bf16[160,1024]{1,0:T(8,128)(2,1)} %get-tuple-element.41.refs_3_), channel_id=1, source_target_pairs={{0,2},{1,3},{2,0},{3,1},{4,6},{5,7},{6,4},{7,5},{8,10},{9,11},{10,... | collective-permute-start | bytes 983048 | tf_op jit(solution)/shard_map/ppermute | solution.py:412
  29.5 5.1 %copy-start.3 = (bf16[320,1024]{1,0:T(8,128)(2,1)S(1)}, bf16[320,1024]{1,0:T(8,128)(2,1)}, u32[]{:S(2)}) copy-start(bf16[320,1024]{1,0:T(8,128)(2,1)} %copy-done.2) | copy-start | bytes 1966084
  29.5 7.6 %collective-permute-start.7 = (f32[128,128]{1,0:T(8,128)S(1)}, f32[128,128]{1,0:T(8,128)S(1)}, u32[]{:S(2)}, u32[]{:S(2)}) collective-permute-start(f32[128,128]{1,0:T(8,128)S(1)} %gram.3.refs_5_), channel_id=1, source_target_pairs={{0,2},{1,3},{2,0},{3,1},{4,6},{5,7},{6,4},{7,5},{8,10},{9,11},{10,... | collective-permute-start | bytes 196616 | tf_op jit(solution)/shard_map/ppermute | solution.py:412
  33.1 20.3 %collective-permute-start.6 = (bf16[160,1024]{1,0:T(8,128)(2,1)S(1)}, bf16[160,1024]{1,0:T(8,128)(2,1)S(1)}, u32[]{:S(2)}, u32[]{:S(2)}) collective-permute-start(bf16[160,1024]{1,0:T(8,128)(2,1)S(1)} %get-tuple-element.47.refs_1_), channel_id=1, source_target_pairs={{0,2},{1,3},{2,0},{3,1},{4,6},{5,7},{6,4},{7,5},{8,10},{9,11},{10,... | collective-permute-start | bytes 983048 | tf_op jit(solution)/shard_map/ppermute | solution.py:412
  37.2 16.2 %copy-start.4 = (bf16[512,512]{1,0:T(8,128)(2,1)S(1)}, bf16[512,512]{1,0:T(8,128)(2,1)}, u32[]{:S(2)}) copy-start(bf16[512,512]{1,0:T(8,128)(2,1)} %constant.17.clone.refs_5_) | copy-start | bytes 1572868
  37.2 19.9 %collective-permute-start.13 = (bf16[160,1024]{1,0:T(8,128)(2,1)S(1)}, bf16[160,1024]{1,0:T(8,128)(2,1)S(1)}, u32[]{:S(2)}, u32[]{:S(2)}) collective-permute-start(bf16[160,1024]{1,0:T(8,128)(2,1)S(1)} %slice.24), channel_id=1, source_target_pairs={{0,2},{1,3},{2,0},{3,1},{4,6},{5,7},{6,4},{7,5},{8,10},{9,11},{10,... | collective-permute-start | bytes 983048 | tf_op jit(solution)/shard_map/ppermute | solution.py:412
  40.7 1.3 %collective-permute-start.9 = (f32[128,128]{1,0:T(8,128)S(1)}, f32[128,128]{1,0:T(8,128)S(1)}, u32[]{:S(2)}, u32[]{:S(2)}) collective-permute-start(f32[128,128]{1,0:T(8,128)S(1)} %add.45), channel_id=1, source_target_pairs={{0,1},{1,0},{2,3},{3,2},{4,5},{5,4},{6,7},{7,6},{8,9},{9,8},{10,11... | collective-permute-start | bytes 196616 | tf_op jit(solution)/shard_map/ppermute | solution.py:412
  42.0 4.3 %collective-permute-start.10 = (f32[128,128]{1,0:T(8,128)S(1)}, f32[128,128]{1,0:T(8,128)S(1)}, u32[]{:S(2)}, u32[]{:S(2)}) collective-permute-start(f32[128,128]{1,0:T(8,128)S(1)} %add.46), channel_id=1, source_target_pairs={{0,4},{4,0},{8,12},{12,8},{16,20},{20,16},{24,28},{28,24},{1,5},{5... | collective-permute-start | bytes 196616 | tf_op jit(solution)/shard_map/ppermute | solution.py:412
  46.3 4.3 %collective-permute-start.11 = (f32[128,128]{1,0:T(8,128)S(1)}, f32[128,128]{1,0:T(8,128)S(1)}, u32[]{:S(2)}, u32[]{:S(2)}) collective-permute-start(f32[128,128]{1,0:T(8,128)S(1)} %add.47), channel_id=1, source_target_pairs={{0,8},{4,12},{8,0},{12,4},{16,24},{20,28},{24,16},{28,20},{1,9},{5... | collective-permute-start | bytes 196616 | tf_op jit(solution)/shard_map/ppermute | solution.py:412
  50.7 6.4 %collective-permute-start.12 = (f32[128,128]{1,0:T(8,128)S(1)}, f32[128,128]{1,0:T(8,128)S(1)}, u32[]{:S(2)}, u32[]{:S(2)}) collective-permute-start(f32[128,128]{1,0:T(8,128)S(1)} %add.48.refs_6_), channel_id=1, source_target_pairs={{0,16},{4,20},{8,24},{12,28},{16,0},{20,4},{24,8},{28,12},{1,17},{... | collective-permute-start | bytes 196616 | tf_op jit(solution)/shard_map/ppermute | solution.py:412
  57.1 1.7 %collective-permute-start.14 = (f32[640,128]{1,0:T(8,128)S(1)}, f32[640,128]{1,0:T(8,128)S(1)}, u32[]{:S(2)}, u32[]{:S(2)}) collective-permute-start(f32[640,128]{1,0:T(8,128)S(1)} %get-tuple-element.58), channel_id=1, source_target_pairs={{0,1},{1,0},{2,3},{3,2},{4,5},{5,4},{6,7},{7,6},{8,9},{9,8},{10,11... | collective-permute-start | bytes 983048 | tf_op jit(solution)/shard_map/ppermute | solution.py:412
  57.2 10.2 %collective-permute-start.16 = (bf16[160,1024]{1,0:T(8,128)(2,1)S(1)}, bf16[160,1024]{1,0:T(8,128)(2,1)S(1)}, u32[]{:S(2)}, u32[]{:S(2)}) collective-permute-start(bf16[160,1024]{1,0:T(8,128)(2,1)S(1)} %slice.27), channel_id=1, source_target_pairs={{0,2},{1,3},{2,0},{3,1},{4,6},{5,7},{6,4},{7,5},{8,10},{9,11},{10,... | collective-permute-start | bytes 983048 | tf_op jit(solution)/shard_map/ppermute | solution.py:412
  58.9 6.4 %collective-permute-start.15 = (f32[320,128]{1,0:T(8,128)S(1)}, f32[320,128]{1,0:T(8,128)S(1)}, u32[]{:S(2)}, u32[]{:S(2)}) collective-permute-start(f32[320,128]{1,0:T(8,128)S(1)} %slice.33), channel_id=1, source_target_pairs={{0,4},{4,0},{8,12},{12,8},{16,20},{20,16},{24,28},{28,24},{1,5},{5... | collective-permute-start | bytes 491528 | tf_op jit(solution)/shard_map/ppermute | solution.py:412
  67.4 4.4 %collective-permute-start.17 = (f32[160,128]{1,0:T(8,128)S(1)}, f32[160,128]{1,0:T(8,128)S(1)}, u32[]{:S(2)}, u32[]{:S(2)}) collective-permute-start(f32[160,128]{1,0:T(8,128)S(1)} %slice.29), channel_id=1, source_target_pairs={{0,8},{4,12},{8,0},{12,4},{16,24},{20,28},{24,16},{28,20},{1,9},{5... | collective-permute-start | bytes 245768 | tf_op jit(solution)/shard_map/ppermute | solution.py:412
  71.9 5.0 %collective-permute-start.18 = (f32[80,128]{1,0:T(8,128)S(1)}, f32[80,128]{1,0:T(8,128)S(1)}, u32[]{:S(2)}, u32[]{:S(2)}) collective-permute-start(f32[80,128]{1,0:T(8,128)S(1)} %slice.35), channel_id=1, source_target_pairs={{0,16},{4,20},{8,24},{12,28},{16,0},{20,4},{24,8},{28,12},{1,17},{... | collective-permute-start | bytes 122888 | tf_op jit(solution)/shard_map/ppermute | solution.py:412
  76.9 9.5 %collective-permute-start.19 = (f32[80,128]{1,0:T(8,128)S(1)}, f32[80,128]{1,0:T(8,128)S(1)}, u32[]{:S(2)}, u32[]{:S(2)}) collective-permute-start(f32[80,128]{1,0:T(8,128)S(1)} %slice_add_fusion.2), channel_id=1, source_target_pairs={{0,0},{1,8},{2,16},{3,24},{4,1},{5,9},{6,17},{7,25},{8,2},{9,10},{... | collective-permute-start | bytes 122888 | tf_op jit(solution)/shard_map/ppermute | solution.py:531
  (1 other events, 0.9 us)

commit v11 on v10

--- a/solution.py
+++ b/solution.py
@@ -13,7 +13,7 @@
 UNIT = 1024
 LEND_PARTS = 4
 PROJECT_ROWS = 512
-PLACE = (-1, True, 1, -1, 1, True)
+PLACE = (False, 1, -1, True, False)
 SKETCH_STEPS = 1
 FACTOR_COST = 6e9
 COST_CUT = 1
@@ -469,7 +469,7 @@
 
     gram = own_gram(own[0], got_high[0], None, None)
     t = project(ids, parts([(0, 0)]), snapshots, None, [gram])
-    if PLACE[5]:
+    if PLACE[3]:
         t, gram = lax.optimization_barrier((t, gram))
     gram = own_gram(own[1], got_high[1], gram, 1.0 / total, done)
     t = project(ids, parts([(0, 1)]), snapshots, t, [gram])
@@ -482,53 +482,37 @@
     for c in range(2):
         low, _ = lax.optimization_barrier((pairs[last, c][rank:], gram))
         got_low.append(swap(low, "samp", samp, last))
-    if PLACE[0] < 0:
-        t = project(ids, parts([(last, 0)]), snapshots, t)
-        gram, t = lax.optimization_barrier((gram, t))
+    t = project(ids, parts([(last, 0)]), snapshots, t, [gram] if PLACE[4] else ())
+    gram, t = lax.optimization_barrier((gram, t))
     bit = last // 2
     while bit:
         gram = gram + swap(gram, "samp", samp, bit)
         bit //= 2
-    rounds = node.bit_length() - 1
-    before = gram
-    for k in range(rounds):
-        if k == PLACE[0]:
-            t = project(ids, parts([(last, 0)]), snapshots, t, [gram])
-            gram, t = lax.optimization_barrier((gram, t))
-        before = gram
-        gram = gram + swap(gram, "node", node, 1 << k)
-
     per_node = P1 // node
     width_cols = P2 // samp
     tall = rank // folding(rank, per_node * width_cols)
     messages = project(
-        ids, parts(late), snapshots, t, [column_order(snapshots.shape[1], samp, per_node, width_cols), before],
+        ids, parts(late), snapshots, t, [column_order(snapshots.shape[1], samp, per_node, width_cols)] + ([gram] if PLACE[0] else []),
         functools.partial(tail, node, per_node, width_cols),
         [jax.ShapeDtypeStruct((node * tall, 128), F32)] * last,
         [pltpu.VMEM((node, tall, 128), F32)])
-    if PLACE[1]:
-        *messages, gram = lax.optimization_barrier((*messages, gram))
-    for c in range(2):
-        if PLACE[3 + c] < 0:
-            *messages, got_low[c] = lax.optimization_barrier((*messages, got_low[c]))
 
     pieces = messages[0]
     for d in near:
         pieces = pieces + swap(messages[d], "samp", samp, d)
-    inverse = factor_inverse(gram, rank, (pieces,))
-    for k in range(rounds):
-        if k == min(PLACE[2], rounds - 1):
-            pieces, inverse = lax.optimization_barrier((pieces, inverse))
+    for k in range(node.bit_length() - 1):
         for c in range(2):
-            if k == PLACE[3 + c]:
+            if k == PLACE[1 + c]:
                 pieces, got_low[c] = lax.optimization_barrier((pieces, got_low[c]))
         edge = pieces.shape[0] // 2
-        pieces = pieces[:edge] + swap(pieces[edge:], "node", node, 1 << k)
+        got = swap(jnp.concatenate([pieces[edge:], gram], axis=0), "node", node, 1 << k)
+        pieces, gram = pieces[:edge] + got[:edge], gram + got[edge:]
     spread = node // samp
     route = [
         (n * samp + s, (s * spread + n // samp) * samp + n % samp) for n in range(node) for s in range(samp)
     ]
     piece = lax.ppermute(pieces, ("node", "samp"), route)
+    inverse = factor_inverse(gram, rank)
     core, coef = finish(inverse, piece, own, got_high, got_low, 1.0 / total, per_node, width_cols)
     return (core.T, coef.T)
 

time: 89.2 us -> 86.4 us (0.969)
  the two profiles are of different devices: /device:TPU:6 before, /device:TPU:3 now
where the time goes in v11:
time: 86.4 us; the launch traced here: 86 us
  Pallas kernels  37.9 us (44%)
  waiting for transfers between devices  25.2 us (29%)
  starting transfers between devices  20.7 us (24%)
  local copies, waits for them, and re-layouts  1.07 us (1%)
  between operations  0.91 us (1%)
    ppermute x16, waiting for transfers between devices, swap(): return lax.ppermute(value, axis, [(i, i ^ bit) for i in range(size)])  25.2 us
    pallas_call x4, Pallas kernels, project(): pl.pallas_call(functools.partial(project_kernel, count, wide, len(bases),...  12.4 us
    ppermute x16, starting transfers between devices, swap(): return lax.ppermute(value, axis, [(i, i ^ bit) for i in range(size)])  12 us
    pallas_call x4, Pallas kernels, sketch(): pl.pallas_call(functools.partial(sketch_kernel, count, lent), grid_spec=p...  10.6 us
    ppermute x1, starting transfers between devices, body(): piece = lax.ppermute(pieces, ('node', 'samp'), route)  8.79 us
    pallas_call x1, Pallas kernels, factor_inverse(): pl.pallas_call(functools.partial(factor_kernel, rank), in_specs=[HELD] +...  5.49 us
    pallas_call x2, Pallas kernels, lend(): pl.pallas_call(functools.partial(lend_kernel, size, stride, at), in_specs...  5.39 us
    pallas_call x1, Pallas kernels, finish(): pl.pallas_call(functools.partial(finish_kernel, scale, per_node, width_co...  2.49 us
  transfers between devices with their start and end apart: 17, of which 8 were waited for; matrix products, arithmetic and copies ran while one was open for 0% of the time, Pallas kernels for 35%

profile of v11, /device:TPU:3, one launch (start us, length us, event | category | flops | bytes accessed | tf_op | source)
XLA Modules:
  0.0 86.0 jit_solution(10842252078117192143)
XLA Ops:
  3.6 4.2 %lend.3 = (bf16[1024,512]{1,0:T(8,128)(2,1)}, bf16[1024,512]{1,0:T(8,128)(2,1)}, bf16[1024,512]{1,0:T(8,128)(2,1)}) custom-call(s32[3]{0:T(128)S(1)} %pad_add_fusion.ids_ref, bf16[8192,512]{1,0:T(8,128)(2,1)} %refs_2_.7, bf16[1280,512]{1,0:T(8,128)(2,1)S(1)} %lend.2.refs_0_), custom_call_target="tpu_custom_call" | custom-call | bytes 6291456 | tf_op jit(solution)/shard_map/lend/pallas_call | solution.py:75
  8.4 2.8 %sketch.4 = (bf16[320,1024]{1,0:T(8,128)(2,1)S(1)}, bf16[160,1024]{1,0:T(8,128)(2,1)}) custom-call(s32[1]{0:T(128)} %bitcast.8.ids_ref, bf16[8192,512]{1,0:T(8,128)(2,1)} %refs_2_.7, bf16[160,512]{1,0:T(8,128)(2,1)S(1)} %bitcast.13, bf16[1280,512]{1,0:T(8,128)(2,1)S(1)} %collective-permute-done.refs_1_.refs_2_.refs_3_, ...), custom_call_target="tpu_custom_call" | custom-call | flops 335544320 | bytes 3080192 | tf_op jit(solution)/shard_map/sketch/pallas_call | solution.py:109
  11.2 3.1 %sketch.5 = (bf16[320,1024]{1,0:T(8,128)(2,1)S(1)}, bf16[160,1024]{1,0:T(8,128)(2,1)}) custom-call(s32[1]{0:T(128)} %bitcast.7.ids_ref, bf16[8192,512]{1,0:T(8,128)(2,1)} %refs_2_.7, bf16[160,512]{1,0:T(8,128)(2,1)S(1)} %bitcast.14, bf16[1280,512]{1,0:T(8,128)(2,1)S(1)} %collective-permute-done.refs_1_.refs_2_.refs_3_, ...), custom_call_target="tpu_custom_call" | custom-call | flops 335544320 | bytes 3080192 | tf_op jit(solution)/shard_map/sketch/pallas_call | solution.py:109
  14.3 1.5 %collective-permute-start.4 = (bf16[160,1024]{1,0:T(8,128)(2,1)}, bf16[160,1024]{1,0:T(8,128)(2,1)S(1)}, u32[]{:S(2)}, u32[]{:S(2)}) collective-permute-start(bf16[160,1024]{1,0:T(8,128)(2,1)} %get-tuple-element.31.refs_3_), channel_id=1, source_target_pairs={{0,2},{1,3},{2,0},{3,1},{4,6},{5,7},{6,4},{7,5},{8,10},{9,11},{10,... | collective-permute-start | bytes 983048 | tf_op jit(solution)/shard_map/ppermute | solution.py:412
  15.9 2.4 %sketch.6 = (bf16[320,1024]{1,0:T(8,128)(2,1)S(1)}, bf16[160,1024]{1,0:T(8,128)(2,1)S(1)}) custom-call(s32[1]{0:T(128)} %bitcast.6.ids_ref, bf16[8192,512]{1,0:T(8,128)(2,1)} %refs_2_.7, bf16[160,512]{1,0:T(8,128)(2,1)S(1)} %bitcast.15, bf16[1280,512]{1,0:T(8,128)(2,1)S(1)} %collective-permute-done.refs_1_.refs_2_.refs_3_, ...), custom_call_target="tpu_custom_call" | custom-call | flops 335544320 | bytes 3080192 | tf_op jit(solution)/shard_map/sketch/pallas_call | solution.py:109
  18.4 2.4 %sketch.7 = (bf16[320,1024]{1,0:T(8,128)(2,1)S(1)}, bf16[160,1024]{1,0:T(8,128)(2,1)S(1)}) custom-call(s32[1]{0:T(128)} %bitcast.ids_ref, bf16[8192,512]{1,0:T(8,128)(2,1)} %refs_2_.7, bf16[160,512]{1,0:T(8,128)(2,1)S(1)} %bitcast.16, bf16[1280,512]{1,0:T(8,128)(2,1)S(1)} %collective-permute-done.refs_1_.refs_2_.refs_3_, ...), custom_call_target="tpu_custom_call" | custom-call | flops 335544320 | bytes 3080192 | tf_op jit(solution)/shard_map/sketch/pallas_call | solution.py:109
  21.5 2.9 %project.4.refs_4_ = f32[2,160,512]{2,1,0:T(8,128)S(1)} custom-call(s32[5]{0:T(128)S(1)} %stack.47.ids_ref, bf16[320,1024]{1,0:T(8,128)(2,1)S(1)} %get-tuple-element.34.own_ref.refs_0_, bf16[160,1024]{1,0:T(8,128)(2,1)S(1)} %collective-permute-done.5.got_ref.refs_1_.refs_2_, bf16[8192,512]{1,0:T(8,128)(2,1)} %refs_2_.7, ...), custom_call_target="tpu_custom_call" | custom-call | flops 671088640 | bytes 3080192 | tf_op jit(solution)/shard_map/project/pallas_call | solution.py:301
  24.4 2.9 %collective-permute-done.4.got_ref.refs_1_.refs_3_ = bf16[160,1024]{1,0:T(8,128)(2,1)S(1)} collective-permute-done((bf16[160,1024]{1,0:T(8,128)(2,1)}, bf16[160,1024]{1,0:T(8,128)(2,1)S(1)}, u32[]{:S(2)}, u32[]{:S(2)}) %collective-permute-start.4) | collective-permute-done | bytes 327712 | tf_op jit(solution)/shard_map/ppermute | solution.py:412
  28.1 2.9 %project.5.refs_4_ = f32[2,160,512]{2,1,0:T(8,128)S(1)} custom-call(s32[5]{0:T(128)S(1)} %stack.47.ids_ref, bf16[320,1024]{1,0:T(8,128)(2,1)S(1)} %get-tuple-element.33.own_ref.refs_0_.refs_1_, bf16[160,1024]{1,0:T(8,128)(2,1)S(1)} %collective-permute-done.4.got_ref.refs_1_.refs_3_, bf16[8192,512]{1,0:T(8,128)(2,1)} %refs_2_.7, ...), custom_call_target="tpu_custom_call" | custom-call | flops 671088640 | bytes 3080192 | tf_op jit(solution)/shard_map/project/pallas_call | solution.py:301
  32.6 1.8 %collective-permute-done.7.refs_1_ = bf16[160,1024]{1,0:T(8,128)(2,1)S(1)} collective-permute-done((bf16[160,1024]{1,0:T(8,128)(2,1)S(1)}, bf16[160,1024]{1,0:T(8,128)(2,1)S(1)}, u32[]{:S(2)}, u32[]{:S(2)}) %collective-permute-start.7) | collective-permute-done | bytes 327712 | tf_op jit(solution)/shard_map/ppermute | solution.py:412
  34.4 2.8 %project.6.refs_4_ = f32[2,160,512]{2,1,0:T(8,128)S(1)} custom-call(s32[5]{0:T(128)S(1)} %stack.47.ids_ref, bf16[320,1024]{1,0:T(8,128)(2,1)S(1)} %get-tuple-element.37.refs_0_, bf16[160,1024]{1,0:T(8,128)(2,1)S(1)} %collective-permute-done.7.refs_1_, bf16[8192,512]{1,0:T(8,128)(2,1)} %refs_2_.7, ...), custom_call_target="tpu_custom_call" | custom-call | flops 671088640 | bytes 3080192 | tf_op jit(solution)/shard_map/project/pallas_call | solution.py:301
  37.1 5.3 %collective-permute-done.6 = f32[128,128]{1,0:T(8,128)S(1)} collective-permute-done((f32[128,128]{1,0:T(8,128)S(1)}, f32[128,128]{1,0:T(8,128)S(1)}, u32[]{:S(2)}, u32[]{:S(2)}) %collective-permute-start.6) | collective-permute-done | bytes 65568 | tf_op jit(solution)/shard_map/ppermute | solution.py:412
  42.4 3.8 %project.7 = (f32[640,128]{1,0:T(8,128)S(1)}, f32[640,128]{1,0:T(8,128)S(1)}) custom-call(s32[5]{0:T(128)S(1)} %stack.47.ids_ref, bf16[320,1024]{1,0:T(8,128)(2,1)S(1)} %get-tuple-element.41.refs_0_, bf16[160,1024]{1,0:T(8,128)(2,1)S(1)} %collective-permute-done.9.refs_1_, bf16[8192,512]{1,0:T(8,128)(2,1)} %refs_2_.7, ...), custom_call_target="tpu_custom_call" | custom-call | flops 671088640 | bytes 3080192 | tf_op jit(solution)/shard_map/project/pallas_call | solution.py:301
  46.2 1.7 %collective-permute-start.10 = (f32[640,128]{1,0:T(8,128)S(1)}, f32[640,128]{1,0:T(8,128)S(1)}, u32[]{:S(2)}, u32[]{:S(2)}) collective-permute-start(f32[640,128]{1,0:T(8,128)S(1)} %get-tuple-element.45), channel_id=1, source_target_pairs={{0,1},{1,0},{2,3},{3,2},{4,5},{5,4},{6,7},{7,6},{8,9},{9,8},{10,11... | collective-permute-start | bytes 983048 | tf_op jit(solution)/shard_map/ppermute | solution.py:412
  49.4 1.3 %collective-permute-start.11 = (f32[448,128]{1,0:T(8,128)S(1)}, f32[448,128]{1,0:T(8,128)S(1)}, u32[]{:S(2)}, u32[]{:S(2)}) collective-permute-start(f32[448,128]{1,0:T(8,128)S(1)} %pad_maximum_fusion), channel_id=1, source_target_pairs={{0,4},{4,0},{8,12},{12,8},{16,20},{20,16},{24,28},{28,24},{1,5},{5... | collective-permute-start | bytes 688136 | tf_op jit(solution)/shard_map/ppermute | solution.py:412
  51.0 5.2 %collective-permute-done.11 = f32[448,128]{1,0:T(8,128)S(1)} collective-permute-done((f32[448,128]{1,0:T(8,128)S(1)}, f32[448,128]{1,0:T(8,128)S(1)}, u32[]{:S(2)}, u32[]{:S(2)}) %collective-permute-start.11) | collective-permute-done | bytes 229408 | tf_op jit(solution)/shard_map/ppermute | solution.py:412
  56.3 3.1 %collective-permute-done.12.refs_4_ = bf16[160,1024]{1,0:T(8,128)(2,1)S(1)} collective-permute-done((bf16[160,1024]{1,0:T(8,128)(2,1)S(1)}, bf16[160,1024]{1,0:T(8,128)(2,1)S(1)}, u32[]{:S(2)}, u32[]{:S(2)}) %collective-permute-start.12) | collective-permute-done | bytes 327712 | tf_op jit(solution)/shard_map/ppermute | solution.py:412
  59.4 1.4 %collective-permute-start.13 = (f32[288,128]{1,0:T(8,128)S(1)}, f32[288,128]{1,0:T(8,128)S(1)}, u32[]{:S(2)}, u32[]{:S(2)}) collective-permute-start(f32[288,128]{1,0:T(8,128)S(1)} %pad_maximum_fusion.1), channel_id=1, source_target_pairs={{0,8},{4,12},{8,0},{12,4},{16,24},{20,28},{24,16},{28,20},{1,9},{5... | collective-permute-start | bytes 442376 | tf_op jit(solution)/shard_map/ppermute | solution.py:412
  60.8 2.7 %collective-permute-done.13 = f32[288,128]{1,0:T(8,128)S(1)} collective-permute-done((f32[288,128]{1,0:T(8,128)S(1)}, f32[288,128]{1,0:T(8,128)S(1)}, u32[]{:S(2)}, u32[]{:S(2)}) %collective-permute-start.13) | collective-permute-done | bytes 147488 | tf_op jit(solution)/shard_map/ppermute | solution.py:412
  63.5 2.4 %collective-permute-start.14 = (f32[208,128]{1,0:T(8,128)S(1)}, f32[208,128]{1,0:T(8,128)S(1)}, u32[]{:S(2)}, u32[]{:S(2)}) collective-permute-start(f32[208,128]{1,0:T(8,128)S(1)} %pad_maximum_fusion.2), channel_id=1, source_target_pairs={{0,16},{4,20},{8,24},{12,28},{16,0},{20,4},{24,8},{28,12},{1,17},{... | collective-permute-start | bytes 319496 | tf_op jit(solution)/shard_map/ppermute | solution.py:412
  66.3 2.9 %collective-permute-done.14 = f32[208,128]{1,0:T(8,128)S(1)} collective-permute-done((f32[208,128]{1,0:T(8,128)S(1)}, f32[208,128]{1,0:T(8,128)S(1)}, u32[]{:S(2)}, u32[]{:S(2)}) %collective-permute-start.14) | collective-permute-done | bytes 106528 | tf_op jit(solution)/shard_map/ppermute | solution.py:412
  69.2 8.8 %collective-permute-start.15 = (f32[80,128]{1,0:T(8,128)S(1)}, f32[80,128]{1,0:T(8,128)S(1)}, u32[]{:S(2)}, u32[]{:S(2)}) collective-permute-start(f32[80,128]{1,0:T(8,128)S(1)} %slice_add_fusion.5), channel_id=1, source_target_pairs={{0,0},{1,8},{2,16},{3,24},{4,1},{5,9},{6,17},{7,25},{8,2},{9,10},{... | collective-permute-start | bytes 122888 | tf_op jit(solution)/shard_map/ppermute | solution.py:514
  78.0 5.5 %factor.1.inv_ref = f32[160,160]{1,0:T(8,128)S(1)} custom-call(f32[128,128]{1,0:T(8,128)S(1)} %slice_add_fusion.2.g_ref), custom_call_target="tpu_custom_call" | custom-call | flops 6000000000 | bytes 102400 | tf_op jit(solution)/shard_map/factor/pallas_call | solution.py:246
  83.5 2.5 %finish.1 = (f32[160,2048]{1,0:T(8,128)}, f32[8,1280]{1,0:T(8,128)}) custom-call(f32[160,160]{1,0:T(8,128)S(1)} %factor.1.inv_ref, f32[80,128]{1,0:T(8,128)S(1)} %collective-permute-done.15.piece_ref, bf16[320,1024]{1,0:T(8,128)(2,1)S(1)} %get-tuple-element.34.own_ref.refs_0_, bf16[320,1024]{1,0:T(8,128)(2,1)S(1)} %get-tuple-element.33.own_ref.refs_0_.refs_1_, ...), custom_call_target="tpu_custom_call" | custom-call | flops 629145600 | bytes 3932160 | tf_op jit(solution)/shard_map/finish/pallas_call | solution.py:399
  (49 shorter events, 9.0 us)
Async XLA Ops:
  0.6 0.9 %copy-start = (bf16[512,160]{0,1:T(8,128)(2,1)S(1)}, bf16[512,160]{0,1:T(8,128)(2,1)}, u32[]{:S(2)}) copy-start(bf16[512,160]{0,1:T(8,128)(2,1)} %param.4) | copy-start | bytes 491524
  2.8 5.7 %collective-permute-start = (bf16[1280,512]{1,0:T(8,128)(2,1)S(1)}, bf16[1280,512]{1,0:T(8,128)(2,1)S(1)}, u32[]{:S(2)}, u32[]{:S(2)}) collective-permute-start(bf16[1280,512]{1,0:T(8,128)(2,1)S(1)} %lend.2.refs_0_), channel_id=1, source_target_pairs={{0,1},{1,0},{2,3},{3,2},{4,5},{5,4},{6,7},{7,6},{8,9},{9,8},{10,11... | collective-permute-start | bytes 3932168 | tf_op jit(solution)/shard_map/ppermute | solution.py:412
  3.6 4.8 %copy-start.1 = (bf16[512,160]{0,1:T(8,128)(2,1)S(1)}, bf16[512,160]{0,1:T(8,128)(2,1)}, u32[]{:S(2)}) copy-start(bf16[512,160]{0,1:T(8,128)(2,1)} %param.4) | copy-start | bytes 491524
  7.8 3.5 %collective-permute-start.3 = (bf16[1024,512]{1,0:T(8,128)(2,1)}, bf16[1024,512]{1,0:T(8,128)(2,1)}, u32[]{:S(2)}, u32[]{:S(2)}) collective-permute-start(bf16[1024,512]{1,0:T(8,128)(2,1)} %get-tuple-element.29), channel_id=1, source_target_pairs={{0,1},{1,0},{2,3},{3,2},{4,5},{5,4},{6,7},{7,6},{8,9},{9,8},{10,11... | collective-permute-start | bytes 3145736 | tf_op jit(solution)/shard_map/ppermute | solution.py:412
  7.9 8.0 %collective-permute-start.2 = (bf16[1024,512]{1,0:T(8,128)(2,1)}, bf16[1024,512]{1,0:T(8,128)(2,1)}, u32[]{:S(2)}, u32[]{:S(2)}) collective-permute-start(bf16[1024,512]{1,0:T(8,128)(2,1)} %get-tuple-element.28), channel_id=1, source_target_pairs={{0,1},{1,0},{2,3},{3,2},{4,5},{5,4},{6,7},{7,6},{8,9},{9,8},{10,11... | collective-permute-start | bytes 3145736 | tf_op jit(solution)/shard_map/ppermute | solution.py:412
  8.4 10.0 %collective-permute-start.1 = (bf16[1024,512]{1,0:T(8,128)(2,1)}, bf16[1024,512]{1,0:T(8,128)(2,1)}, u32[]{:S(2)}, u32[]{:S(2)}) collective-permute-start(bf16[1024,512]{1,0:T(8,128)(2,1)} %get-tuple-element.27), channel_id=1, source_target_pairs={{0,1},{1,0},{2,3},{3,2},{4,5},{5,4},{6,7},{7,6},{8,9},{9,8},{10,11... | collective-permute-start | bytes 3145736 | tf_op jit(solution)/shard_map/ppermute | solution.py:412
  11.2 9.5 %collective-permute-start.5 = (bf16[160,1024]{1,0:T(8,128)(2,1)}, bf16[160,1024]{1,0:T(8,128)(2,1)S(1)}, u32[]{:S(2)}, u32[]{:S(2)}) collective-permute-start(bf16[160,1024]{1,0:T(8,128)(2,1)} %get-tuple-element.30.refs_3_), channel_id=1, source_target_pairs={{0,2},{1,3},{2,0},{3,1},{4,6},{5,7},{6,4},{7,5},{8,10},{9,11},{10,... | collective-permute-start | bytes 983048 | tf_op jit(solution)/shard_map/ppermute | solution.py:412
  14.3 13.0 %collective-permute-start.4 = (bf16[160,1024]{1,0:T(8,128)(2,1)}, bf16[160,1024]{1,0:T(8,128)(2,1)S(1)}, u32[]{:S(2)}, u32[]{:S(2)}) collective-permute-start(bf16[160,1024]{1,0:T(8,128)(2,1)} %get-tuple-element.31.refs_3_), channel_id=1, source_target_pairs={{0,2},{1,3},{2,0},{3,1},{4,6},{5,7},{6,4},{7,5},{8,10},{9,11},{10,... | collective-permute-start | bytes 983048 | tf_op jit(solution)/shard_map/ppermute | solution.py:412
  18.3 16.1 %collective-permute-start.7 = (bf16[160,1024]{1,0:T(8,128)(2,1)S(1)}, bf16[160,1024]{1,0:T(8,128)(2,1)S(1)}, u32[]{:S(2)}, u32[]{:S(2)}) collective-permute-start(bf16[160,1024]{1,0:T(8,128)(2,1)S(1)} %get-tuple-element.32.refs_3_), channel_id=1, source_target_pairs={{0,2},{1,3},{2,0},{3,1},{4,6},{5,7},{6,4},{7,5},{8,10},{9,11},{10,... | collective-permute-start | bytes 983048 | tf_op jit(solution)/shard_map/ppermute | solution.py:412
  31.1 11.3 %collective-permute-start.9 = (bf16[160,1024]{1,0:T(8,128)(2,1)S(1)}, bf16[160,1024]{1,0:T(8,128)(2,1)S(1)}, u32[]{:S(2)}, u32[]{:S(2)}) collective-permute-start(bf16[160,1024]{1,0:T(8,128)(2,1)S(1)} %get-tuple-element.42.refs_1_), channel_id=1, source_target_pairs={{0,2},{1,3},{2,0},{3,1},{4,6},{5,7},{6,4},{7,5},{8,10},{9,11},{10,... | collective-permute-start | bytes 983048 | tf_op jit(solution)/shard_map/ppermute | solution.py:412
  31.4 10.9 %collective-permute-start.6 = (f32[128,128]{1,0:T(8,128)S(1)}, f32[128,128]{1,0:T(8,128)S(1)}, u32[]{:S(2)}, u32[]{:S(2)}) collective-permute-start(f32[128,128]{1,0:T(8,128)S(1)} %gram.3.refs_5_), channel_id=1, source_target_pairs={{0,2},{1,3},{2,0},{3,1},{4,6},{5,7},{6,4},{7,5},{8,10},{9,11},{10,... | collective-permute-start | bytes 196616 | tf_op jit(solution)/shard_map/ppermute | solution.py:412
  34.4 8.1 %copy-start.2 = (bf16[512,512]{1,0:T(8,128)(2,1)S(1)}, bf16[512,512]{1,0:T(8,128)(2,1)}, u32[]{:S(2)}) copy-start(bf16[512,512]{1,0:T(8,128)(2,1)} %constant.17.clone.refs_5_) | copy-start | bytes 1572868
  46.2 3.1 %collective-permute-start.10 = (f32[640,128]{1,0:T(8,128)S(1)}, f32[640,128]{1,0:T(8,128)S(1)}, u32[]{:S(2)}, u32[]{:S(2)}) collective-permute-start(f32[640,128]{1,0:T(8,128)S(1)} %get-tuple-element.45), channel_id=1, source_target_pairs={{0,1},{1,0},{2,3},{3,2},{4,5},{5,4},{6,7},{7,6},{8,9},{9,8},{10,11... | collective-permute-start | bytes 983048 | tf_op jit(solution)/shard_map/ppermute | solution.py:412
  47.9 1.3 %collective-permute-start.8 = (f32[128,128]{1,0:T(8,128)S(1)}, f32[128,128]{1,0:T(8,128)S(1)}, u32[]{:S(2)}, u32[]{:S(2)}) collective-permute-start(f32[128,128]{1,0:T(8,128)S(1)} %add.45), channel_id=1, source_target_pairs={{0,1},{1,0},{2,3},{3,2},{4,5},{5,4},{6,7},{7,6},{8,9},{9,8},{10,11... | collective-permute-start | bytes 196616 | tf_op jit(solution)/shard_map/ppermute | solution.py:412
  49.4 6.9 %collective-permute-start.11 = (f32[448,128]{1,0:T(8,128)S(1)}, f32[448,128]{1,0:T(8,128)S(1)}, u32[]{:S(2)}, u32[]{:S(2)}) collective-permute-start(f32[448,128]{1,0:T(8,128)S(1)} %pad_maximum_fusion), channel_id=1, source_target_pairs={{0,4},{4,0},{8,12},{12,8},{16,20},{20,16},{24,28},{28,24},{1,5},{5... | collective-permute-start | bytes 688136 | tf_op jit(solution)/shard_map/ppermute | solution.py:412
  50.7 8.7 %collective-permute-start.12 = (bf16[160,1024]{1,0:T(8,128)(2,1)S(1)}, bf16[160,1024]{1,0:T(8,128)(2,1)S(1)}, u32[]{:S(2)}, u32[]{:S(2)}) collective-permute-start(bf16[160,1024]{1,0:T(8,128)(2,1)S(1)} %slice.46), channel_id=1, source_target_pairs={{0,2},{1,3},{2,0},{3,1},{4,6},{5,7},{6,4},{7,5},{8,10},{9,11},{10,... | collective-permute-start | bytes 983048 | tf_op jit(solution)/shard_map/ppermute | solution.py:412
  59.4 4.1 %collective-permute-start.13 = (f32[288,128]{1,0:T(8,128)S(1)}, f32[288,128]{1,0:T(8,128)S(1)}, u32[]{:S(2)}, u32[]{:S(2)}) collective-permute-start(f32[288,128]{1,0:T(8,128)S(1)} %pad_maximum_fusion.1), channel_id=1, source_target_pairs={{0,8},{4,12},{8,0},{12,4},{16,24},{20,28},{24,16},{28,20},{1,9},{5... | collective-permute-start | bytes 442376 | tf_op jit(solution)/shard_map/ppermute | solution.py:412
  63.5 5.7 %collective-permute-start.14 = (f32[208,128]{1,0:T(8,128)S(1)}, f32[208,128]{1,0:T(8,128)S(1)}, u32[]{:S(2)}, u32[]{:S(2)}) collective-permute-start(f32[208,128]{1,0:T(8,128)S(1)} %pad_maximum_fusion.2), channel_id=1, source_target_pairs={{0,16},{4,20},{8,24},{12,28},{16,0},{20,4},{24,8},{28,12},{1,17},{... | collective-permute-start | bytes 319496 | tf_op jit(solution)/shard_map/ppermute | solution.py:412
  65.9 17.6 %collective-permute-start.16 = (bf16[160,1024]{1,0:T(8,128)(2,1)S(1)}, bf16[160,1024]{1,0:T(8,128)(2,1)S(1)}, u32[]{:S(2)}, u32[]{:S(2)}) collective-permute-start(bf16[160,1024]{1,0:T(8,128)(2,1)S(1)} %slice.55), channel_id=1, source_target_pairs={{0,2},{1,3},{2,0},{3,1},{4,6},{5,7},{6,4},{7,5},{8,10},{9,11},{10,... | collective-permute-start | bytes 983048 | tf_op jit(solution)/shard_map/ppermute | solution.py:412
  69.2 14.3 %collective-permute-start.15 = (f32[80,128]{1,0:T(8,128)S(1)}, f32[80,128]{1,0:T(8,128)S(1)}, u32[]{:S(2)}, u32[]{:S(2)}) collective-permute-start(f32[80,128]{1,0:T(8,128)S(1)} %slice_add_fusion.5), channel_id=1, source_target_pairs={{0,0},{1,8},{2,16},{3,24},{4,1},{5,9},{6,17},{7,25},{8,2},{9,10},{... | collective-permute-start | bytes 122888 | tf_op jit(solution)/shard_map/ppermute | solution.py:514

commit v12 on v11

--- a/solution.py
+++ b/solution.py
@@ -11,7 +11,7 @@
 P2 = 32
 BAND = 32
 UNIT = 1024
-LEND_PARTS = 4
+LEND_STEPS = 2
 PROJECT_ROWS = 512
 PLACE = (False, 1, -1, True, False)
 SKETCH_STEPS = 1
@@ -41,47 +41,42 @@
     return pl.CostEstimate(flops=int(flops) // COST_CUT, bytes_accessed=int(moved) // COST_CUT, transcendentals=0)
 
 
-def lend_kernel(size, stride, at, ids_ref, x_ref, *refs):
-    count = ids_ref.shape[0]
-    extra = 1 if at is not None else 0
-    outs, sems = refs[-1 - count:-1], refs[-1]
-    copies = []
+def lend_kernel(count, at, ids_ref, *refs):
+    outs = refs[-count:]
+    rows = refs[0].shape[0]
     for k in range(count):
-        first = pl.multiple_of(ids_ref[k] * size, size)
-        for part in range(size // stride):
-            copies.append(pltpu.make_async_copy(
-                x_ref.at[pl.ds(first + part * stride, stride)],
-                outs[k].at[pl.ds(part * stride, stride)],
-                sems.at[len(copies)]))
-    if extra:
-        copies.append(pltpu.make_async_copy(
-            refs[0], outs[0].at[pl.ds(at, refs[0].shape[0])], sems.at[len(copies)]))
-    for copy in copies:
-        copy.start()
-    for copy in copies:
-        copy.wait()
+        outs[k][:rows, :] = refs[k][...]
+    if at is not None:
+        outs[0][at:, :] = refs[count][...]
 
 
 def lend(ids, x, size, w=None, after=()):
     count = ids.shape[0]
     depth = x.shape[1]
-    stride = size // LEND_PARTS
-    at, height = None, size
+    steps = LEND_STEPS if w is None else 1
+    rows = size // steps
+    at, height, more, shapes = None, size, [], (rows, depth)
     if w is not None:
         rank = w.shape[0]
         at = -(-size // rank) * rank
         height = at + rank
-    more = [] if w is None else [w]
+        more, shapes = [w], (height, depth)
     return pl.pallas_call(
-        functools.partial(lend_kernel, size, stride, at),
-        in_specs=[pl.BlockSpec(memory_space=pltpu.SMEM)] + [UNREAD] * (1 + len(more) + len(after)),
-        out_specs=[HELD] * count,
+        functools.partial(lend_kernel, count, at),
+        grid_spec=pltpu.PrefetchScalarGridSpec(
+            num_scalar_prefetch=1,
+            grid=(steps,),
+            in_specs=[
+                pl.BlockSpec((rows, depth), lambda i, ids, k=k: (ids[k] * steps + i, 0))
+                for k in range(count)
+            ] + [pl.BlockSpec(v.shape, lambda i, ids: (0, 0)) for v in more] + [UNREAD] * len(after),
+            out_specs=[pl.BlockSpec(shapes, lambda i, ids: (i, 0))] * count,
+        ),
         out_shape=[jax.ShapeDtypeStruct((height, depth), BF16)] * count,
-        scratch_shapes=[pltpu.SemaphoreType.DMA((LEND_PARTS * count + len(more),))],
         compiler_params=params(),
         cost_estimate=cost(0, 4 * count * height * depth),
         name="lend",
-    )(ids, x, *more, *after)
+    )(ids, *([x] * count), *more, *after)
 
 
 def sketch_kernel(count, lent, ids_ref, x_ref, *refs):

time: 86.4 us -> 85.9 us (level)
  no operation moved by 1% of the time
where the time goes in v12:
time: 85.9 us; the launch traced here: 85.5 us
  Pallas kernels  37.5 us (44%)
  waiting for transfers between devices  25.1 us (29%)
  starting transfers between devices  20.7 us (24%)
  local copies, waits for them, and re-layouts  1.07 us (1%)
  between operations  0.9 us (1%)
    ppermute x16, waiting for transfers between devices, swap(): return lax.ppermute(value, axis, [(i, i ^ bit) for i in range(size)])  25.1 us
    pallas_call x4, Pallas kernels, project(): pl.pallas_call(functools.partial(project_kernel, count, wide, len(bases),...  12.4 us
    ppermute x16, starting transfers between devices, swap(): return lax.ppermute(value, axis, [(i, i ^ bit) for i in range(size)])  11.9 us
    pallas_call x4, Pallas kernels, sketch(): pl.pallas_call(functools.partial(sketch_kernel, count, lent), grid_spec=p...  10.6 us
    ppermute x1, starting transfers between devices, body(): piece = lax.ppermute(pieces, ('node', 'samp'), route)  8.79 us
    pallas_call x1, Pallas kernels, factor_inverse(): pl.pallas_call(functools.partial(factor_kernel, rank), in_specs=[HELD] +...  5.49 us
    pallas_call x2, Pallas kernels, lend(): pl.pallas_call(functools.partial(lend_kernel, count, at), grid_spec=pltpu...  4.99 us
    pallas_call x1, Pallas kernels, finish(): pl.pallas_call(functools.partial(finish_kernel, scale, per_node, width_co...  2.49 us
  transfers between devices with their start and end apart: 17, of which 8 were waited for; matrix products, arithmetic and copies ran while one was open for 0% of the time, Pallas kernels for 35%

profile of v12, /device:TPU:3, one launch (start us, length us, event | category | flops | bytes accessed | tf_op | source)
XLA Modules:
  0.0 85.5 jit_solution(6202348783742002303)
XLA Ops:
  3.7 3.7 %lend.3 = (bf16[1024,512]{1,0:T(8,128)(2,1)}, bf16[1024,512]{1,0:T(8,128)(2,1)}, bf16[1024,512]{1,0:T(8,128)(2,1)}) custom-call(s32[3]{0:T(128)S(1)} %pad_add_fusion.ids_ref, bf16[8192,512]{1,0:T(8,128)(2,1)} %refs_2_.9, bf16[8192,512]{1,0:T(8,128)(2,1)} %refs_2_.9, bf16[8192,512]{1,0:T(8,128)(2,1)} %refs_2_.9, bf16[1280,512]{1,0:T(8,128)(2,1)S(1)} %lend.2.refs_3_), custom_call_target="tpu_custom_call" | custom-call | bytes 6291456 | tf_op jit(solution)/shard_map/lend/pallas_call | solution.py:64
  7.9 2.8 %sketch.4 = (bf16[320,1024]{1,0:T(8,128)(2,1)S(1)}, bf16[160,1024]{1,0:T(8,128)(2,1)}) custom-call(s32[1]{0:T(128)} %bitcast.8.ids_ref, bf16[8192,512]{1,0:T(8,128)(2,1)} %refs_2_.9, bf16[160,512]{1,0:T(8,128)(2,1)S(1)} %bitcast.13, bf16[1280,512]{1,0:T(8,128)(2,1)S(1)} %collective-permute-done.refs_1_.refs_2_.refs_3_, ...), custom_call_target="tpu_custom_call" | custom-call | flops 335544320 | bytes 3080192 | tf_op jit(solution)/shard_map/sketch/pallas_call | solution.py:104
  10.7 3.1 %sketch.5 = (bf16[320,1024]{1,0:T(8,128)(2,1)S(1)}, bf16[160,1024]{1,0:T(8,128)(2,1)}) custom-call(s32[1]{0:T(128)} %bitcast.7.ids_ref, bf16[8192,512]{1,0:T(8,128)(2,1)} %refs_2_.9, bf16[160,512]{1,0:T(8,128)(2,1)S(1)} %bitcast.14, bf16[1280,512]{1,0:T(8,128)(2,1)S(1)} %collective-permute-done.refs_1_.refs_2_.refs_3_, ...), custom_call_target="tpu_custom_call" | custom-call | flops 335544320 | bytes 3080192 | tf_op jit(solution)/shard_map/sketch/pallas_call | solution.py:104
  13.8 1.5 %collective-permute-start.4 = (bf16[160,1024]{1,0:T(8,128)(2,1)}, bf16[160,1024]{1,0:T(8,128)(2,1)S(1)}, u32[]{:S(2)}, u32[]{:S(2)}) collective-permute-start(bf16[160,1024]{1,0:T(8,128)(2,1)} %get-tuple-element.31.refs_3_), channel_id=1, source_target_pairs={{0,2},{1,3},{2,0},{3,1},{4,6},{5,7},{6,4},{7,5},{8,10},{9,11},{10,... | collective-permute-start | bytes 983048 | tf_op jit(solution)/shard_map/ppermute | solution.py:407
  15.4 2.4 %sketch.6 = (bf16[320,1024]{1,0:T(8,128)(2,1)S(1)}, bf16[160,1024]{1,0:T(8,128)(2,1)S(1)}) custom-call(s32[1]{0:T(128)} %bitcast.6.ids_ref, bf16[8192,512]{1,0:T(8,128)(2,1)} %refs_2_.9, bf16[160,512]{1,0:T(8,128)(2,1)S(1)} %bitcast.15, bf16[1280,512]{1,0:T(8,128)(2,1)S(1)} %collective-permute-done.refs_1_.refs_2_.refs_3_, ...), custom_call_target="tpu_custom_call" | custom-call | flops 335544320 | bytes 3080192 | tf_op jit(solution)/shard_map/sketch/pallas_call | solution.py:104
  17.8 2.4 %sketch.7 = (bf16[320,1024]{1,0:T(8,128)(2,1)S(1)}, bf16[160,1024]{1,0:T(8,128)(2,1)S(1)}) custom-call(s32[1]{0:T(128)} %bitcast.ids_ref, bf16[8192,512]{1,0:T(8,128)(2,1)} %refs_2_.9, bf16[160,512]{1,0:T(8,128)(2,1)S(1)} %bitcast.16, bf16[1280,512]{1,0:T(8,128)(2,1)S(1)} %collective-permute-done.refs_1_.refs_2_.refs_3_, ...), custom_call_target="tpu_custom_call" | custom-call | flops 335544320 | bytes 3080192 | tf_op jit(solution)/shard_map/sketch/pallas_call | solution.py:104
  20.9 2.9 %project.4.refs_4_ = f32[2,160,512]{2,1,0:T(8,128)S(1)} custom-call(s32[5]{0:T(128)S(1)} %stack.47.ids_ref, bf16[320,1024]{1,0:T(8,128)(2,1)S(1)} %get-tuple-element.34.own_ref.refs_0_, bf16[160,1024]{1,0:T(8,128)(2,1)S(1)} %collective-permute-done.5.got_ref.refs_1_.refs_2_, bf16[8192,512]{1,0:T(8,128)(2,1)} %refs_2_.9, ...), custom_call_target="tpu_custom_call" | custom-call | flops 671088640 | bytes 3080192 | tf_op jit(solution)/shard_map/project/pallas_call | solution.py:296
  23.9 2.8 %collective-permute-done.4.got_ref.refs_1_.refs_3_ = bf16[160,1024]{1,0:T(8,128)(2,1)S(1)} collective-permute-done((bf16[160,1024]{1,0:T(8,128)(2,1)}, bf16[160,1024]{1,0:T(8,128)(2,1)S(1)}, u32[]{:S(2)}, u32[]{:S(2)}) %collective-permute-start.4) | collective-permute-done | bytes 327712 | tf_op jit(solution)/shard_map/ppermute | solution.py:407
  27.5 2.9 %project.5.refs_4_ = f32[2,160,512]{2,1,0:T(8,128)S(1)} custom-call(s32[5]{0:T(128)S(1)} %stack.47.ids_ref, bf16[320,1024]{1,0:T(8,128)(2,1)S(1)} %get-tuple-element.33.own_ref.refs_0_.refs_1_, bf16[160,1024]{1,0:T(8,128)(2,1)S(1)} %collective-permute-done.4.got_ref.refs_1_.refs_3_, bf16[8192,512]{1,0:T(8,128)(2,1)} %refs_2_.9, ...), custom_call_target="tpu_custom_call" | custom-call | flops 671088640 | bytes 3080192 | tf_op jit(solution)/shard_map/project/pallas_call | solution.py:296
  32.0 1.8 %collective-permute-done.7.refs_1_ = bf16[160,1024]{1,0:T(8,128)(2,1)S(1)} collective-permute-done((bf16[160,1024]{1,0:T(8,128)(2,1)S(1)}, bf16[160,1024]{1,0:T(8,128)(2,1)S(1)}, u32[]{:S(2)}, u32[]{:S(2)}) %collective-permute-start.7) | collective-permute-done | bytes 327712 | tf_op jit(solution)/shard_map/ppermute | solution.py:407
  33.8 2.8 %project.6.refs_4_ = f32[2,160,512]{2,1,0:T(8,128)S(1)} custom-call(s32[5]{0:T(128)S(1)} %stack.47.ids_ref, bf16[320,1024]{1,0:T(8,128)(2,1)S(1)} %get-tuple-element.37.refs_0_, bf16[160,1024]{1,0:T(8,128)(2,1)S(1)} %collective-permute-done.7.refs_1_, bf16[8192,512]{1,0:T(8,128)(2,1)} %refs_2_.9, ...), custom_call_target="tpu_custom_call" | custom-call | flops 671088640 | bytes 3080192 | tf_op jit(solution)/shard_map/project/pallas_call | solution.py:296
  36.5 5.3 %collective-permute-done.6 = f32[128,128]{1,0:T(8,128)S(1)} collective-permute-done((f32[128,128]{1,0:T(8,128)S(1)}, f32[128,128]{1,0:T(8,128)S(1)}, u32[]{:S(2)}, u32[]{:S(2)}) %collective-permute-start.6) | collective-permute-done | bytes 65568 | tf_op jit(solution)/shard_map/ppermute | solution.py:407
  41.8 3.8 %project.7 = (f32[640,128]{1,0:T(8,128)S(1)}, f32[640,128]{1,0:T(8,128)S(1)}) custom-call(s32[5]{0:T(128)S(1)} %stack.47.ids_ref, bf16[320,1024]{1,0:T(8,128)(2,1)S(1)} %get-tuple-element.41.refs_0_, bf16[160,1024]{1,0:T(8,128)(2,1)S(1)} %collective-permute-done.9.refs_1_, bf16[8192,512]{1,0:T(8,128)(2,1)} %refs_2_.9, ...), custom_call_target="tpu_custom_call" | custom-call | flops 671088640 | bytes 3080192 | tf_op jit(solution)/shard_map/project/pallas_call | solution.py:296
  45.6 1.8 %collective-permute-start.10 = (f32[640,128]{1,0:T(8,128)S(1)}, f32[640,128]{1,0:T(8,128)S(1)}, u32[]{:S(2)}, u32[]{:S(2)}) collective-permute-start(f32[640,128]{1,0:T(8,128)S(1)} %get-tuple-element.45), channel_id=1, source_target_pairs={{0,1},{1,0},{2,3},{3,2},{4,5},{5,4},{6,7},{7,6},{8,9},{9,8},{10,11... | collective-permute-start | bytes 983048 | tf_op jit(solution)/shard_map/ppermute | solution.py:407
  48.9 1.3 %collective-permute-start.11 = (f32[448,128]{1,0:T(8,128)S(1)}, f32[448,128]{1,0:T(8,128)S(1)}, u32[]{:S(2)}, u32[]{:S(2)}) collective-permute-start(f32[448,128]{1,0:T(8,128)S(1)} %pad_maximum_fusion), channel_id=1, source_target_pairs={{0,4},{4,0},{8,12},{12,8},{16,20},{20,16},{24,28},{28,24},{1,5},{5... | collective-permute-start | bytes 688136 | tf_op jit(solution)/shard_map/ppermute | solution.py:407
  50.5 5.2 %collective-permute-done.11 = f32[448,128]{1,0:T(8,128)S(1)} collective-permute-done((f32[448,128]{1,0:T(8,128)S(1)}, f32[448,128]{1,0:T(8,128)S(1)}, u32[]{:S(2)}, u32[]{:S(2)}) %collective-permute-start.11) | collective-permute-done | bytes 229408 | tf_op jit(solution)/shard_map/ppermute | solution.py:407
  55.8 3.1 %collective-permute-done.12.refs_4_ = bf16[160,1024]{1,0:T(8,128)(2,1)S(1)} collective-permute-done((bf16[160,1024]{1,0:T(8,128)(2,1)S(1)}, bf16[160,1024]{1,0:T(8,128)(2,1)S(1)}, u32[]{:S(2)}, u32[]{:S(2)}) %collective-permute-start.12) | collective-permute-done | bytes 327712 | tf_op jit(solution)/shard_map/ppermute | solution.py:407
  58.9 1.4 %collective-permute-start.13 = (f32[288,128]{1,0:T(8,128)S(1)}, f32[288,128]{1,0:T(8,128)S(1)}, u32[]{:S(2)}, u32[]{:S(2)}) collective-permute-start(f32[288,128]{1,0:T(8,128)S(1)} %pad_maximum_fusion.1), channel_id=1, source_target_pairs={{0,8},{4,12},{8,0},{12,4},{16,24},{20,28},{24,16},{28,20},{1,9},{5... | collective-permute-start | bytes 442376 | tf_op jit(solution)/shard_map/ppermute | solution.py:407
  60.3 2.7 %collective-permute-done.13 = f32[288,128]{1,0:T(8,128)S(1)} collective-permute-done((f32[288,128]{1,0:T(8,128)S(1)}, f32[288,128]{1,0:T(8,128)S(1)}, u32[]{:S(2)}, u32[]{:S(2)}) %collective-permute-start.13) | collective-permute-done | bytes 147488 | tf_op jit(solution)/shard_map/ppermute | solution.py:407
  63.0 2.4 %collective-permute-start.14 = (f32[208,128]{1,0:T(8,128)S(1)}, f32[208,128]{1,0:T(8,128)S(1)}, u32[]{:S(2)}, u32[]{:S(2)}) collective-permute-start(f32[208,128]{1,0:T(8,128)S(1)} %pad_maximum_fusion.2), channel_id=1, source_target_pairs={{0,16},{4,20},{8,24},{12,28},{16,0},{20,4},{24,8},{28,12},{1,17},{... | collective-permute-start | bytes 319496 | tf_op jit(solution)/shard_map/ppermute | solution.py:407
  65.7 2.9 %collective-permute-done.14 = f32[208,128]{1,0:T(8,128)S(1)} collective-permute-done((f32[208,128]{1,0:T(8,128)S(1)}, f32[208,128]{1,0:T(8,128)S(1)}, u32[]{:S(2)}, u32[]{:S(2)}) %collective-permute-start.14) | collective-permute-done | bytes 106528 | tf_op jit(solution)/shard_map/ppermute | solution.py:407
  68.7 8.8 %collective-permute-start.15 = (f32[80,128]{1,0:T(8,128)S(1)}, f32[80,128]{1,0:T(8,128)S(1)}, u32[]{:S(2)}, u32[]{:S(2)}) collective-permute-start(f32[80,128]{1,0:T(8,128)S(1)} %slice_add_fusion.5), channel_id=1, source_target_pairs={{0,0},{1,8},{2,16},{3,24},{4,1},{5,9},{6,17},{7,25},{8,2},{9,10},{... | collective-permute-start | bytes 122888 | tf_op jit(solution)/shard_map/ppermute | solution.py:509
  77.5 5.5 %factor.1.inv_ref = f32[160,160]{1,0:T(8,128)S(1)} custom-call(f32[128,128]{1,0:T(8,128)S(1)} %slice_add_fusion.2.g_ref), custom_call_target="tpu_custom_call" | custom-call | flops 6000000000 | bytes 102400 | tf_op jit(solution)/shard_map/factor/pallas_call | solution.py:241
  83.0 2.5 %finish.1 = (f32[160,2048]{1,0:T(8,128)}, f32[8,1280]{1,0:T(8,128)}) custom-call(f32[160,160]{1,0:T(8,128)S(1)} %factor.1.inv_ref, f32[80,128]{1,0:T(8,128)S(1)} %collective-permute-done.15.piece_ref, bf16[320,1024]{1,0:T(8,128)(2,1)S(1)} %get-tuple-element.34.own_ref.refs_0_, bf16[320,1024]{1,0:T(8,128)(2,1)S(1)} %get-tuple-element.33.own_ref.refs_0_.refs_1_, ...), custom_call_target="tpu_custom_call" | custom-call | flops 629145600 | bytes 3932160 | tf_op jit(solution)/shard_map/finish/pallas_call | solution.py:394
  (49 shorter events, 9.0 us)
Async XLA Ops:
  0.6 0.9 %copy-start = (bf16[512,160]{0,1:T(8,128)(2,1)S(1)}, bf16[512,160]{0,1:T(8,128)(2,1)}, u32[]{:S(2)}) copy-start(bf16[512,160]{0,1:T(8,128)(2,1)} %param.4) | copy-start | bytes 491524
  2.9 5.0 %collective-permute-start = (bf16[1280,512]{1,0:T(8,128)(2,1)S(1)}, bf16[1280,512]{1,0:T(8,128)(2,1)S(1)}, u32[]{:S(2)}, u32[]{:S(2)}) collective-permute-start(bf16[1280,512]{1,0:T(8,128)(2,1)S(1)} %lend.2.refs_3_), channel_id=1, source_target_pairs={{0,1},{1,0},{2,3},{3,2},{4,5},{5,4},{6,7},{7,6},{8,9},{9,8},{10,11... | collective-permute-start | bytes 3932168 | tf_op jit(solution)/shard_map/ppermute | solution.py:407
  3.7 4.2 %copy-start.1 = (bf16[512,160]{0,1:T(8,128)(2,1)S(1)}, bf16[512,160]{0,1:T(8,128)(2,1)}, u32[]{:S(2)}) copy-start(bf16[512,160]{0,1:T(8,128)(2,1)} %param.4) | copy-start | bytes 491524
  7.4 3.3 %collective-permute-start.3 = (bf16[1024,512]{1,0:T(8,128)(2,1)}, bf16[1024,512]{1,0:T(8,128)(2,1)}, u32[]{:S(2)}, u32[]{:S(2)}) collective-permute-start(bf16[1024,512]{1,0:T(8,128)(2,1)} %get-tuple-element.29), channel_id=1, source_target_pairs={{0,1},{1,0},{2,3},{3,2},{4,5},{5,4},{6,7},{7,6},{8,9},{9,8},{10,11... | collective-permute-start | bytes 3145736 | tf_op jit(solution)/shard_map/ppermute | solution.py:407
  7.4 8.0 %collective-permute-start.2 = (bf16[1024,512]{1,0:T(8,128)(2,1)}, bf16[1024,512]{1,0:T(8,128)(2,1)}, u32[]{:S(2)}, u32[]{:S(2)}) collective-permute-start(bf16[1024,512]{1,0:T(8,128)(2,1)} %get-tuple-element.28), channel_id=1, source_target_pairs={{0,1},{1,0},{2,3},{3,2},{4,5},{5,4},{6,7},{7,6},{8,9},{9,8},{10,11... | collective-permute-start | bytes 3145736 | tf_op jit(solution)/shard_map/ppermute | solution.py:407
  7.9 9.9 %collective-permute-start.1 = (bf16[1024,512]{1,0:T(8,128)(2,1)}, bf16[1024,512]{1,0:T(8,128)(2,1)}, u32[]{:S(2)}, u32[]{:S(2)}) collective-permute-start(bf16[1024,512]{1,0:T(8,128)(2,1)} %get-tuple-element.27), channel_id=1, source_target_pairs={{0,1},{1,0},{2,3},{3,2},{4,5},{5,4},{6,7},{7,6},{8,9},{9,8},{10,11... | collective-permute-start | bytes 3145736 | tf_op jit(solution)/shard_map/ppermute | solution.py:407
  10.7 9.5 %collective-permute-start.5 = (bf16[160,1024]{1,0:T(8,128)(2,1)}, bf16[160,1024]{1,0:T(8,128)(2,1)S(1)}, u32[]{:S(2)}, u32[]{:S(2)}) collective-permute-start(bf16[160,1024]{1,0:T(8,128)(2,1)} %get-tuple-element.30.refs_3_), channel_id=1, source_target_pairs={{0,2},{1,3},{2,0},{3,1},{4,6},{5,7},{6,4},{7,5},{8,10},{9,11},{10,... | collective-permute-start | bytes 983048 | tf_op jit(solution)/shard_map/ppermute | solution.py:407
  13.8 12.9 %collective-permute-start.4 = (bf16[160,1024]{1,0:T(8,128)(2,1)}, bf16[160,1024]{1,0:T(8,128)(2,1)S(1)}, u32[]{:S(2)}, u32[]{:S(2)}) collective-permute-start(bf16[160,1024]{1,0:T(8,128)(2,1)} %get-tuple-element.31.refs_3_), channel_id=1, source_target_pairs={{0,2},{1,3},{2,0},{3,1},{4,6},{5,7},{6,4},{7,5},{8,10},{9,11},{10,... | collective-permute-start | bytes 983048 | tf_op jit(solution)/shard_map/ppermute | solution.py:407
  17.7 16.0 %collective-permute-start.7 = (bf16[160,1024]{1,0:T(8,128)(2,1)S(1)}, bf16[160,1024]{1,0:T(8,128)(2,1)S(1)}, u32[]{:S(2)}, u32[]{:S(2)}) collective-permute-start(bf16[160,1024]{1,0:T(8,128)(2,1)S(1)} %get-tuple-element.32.refs_3_), channel_id=1, source_target_pairs={{0,2},{1,3},{2,0},{3,1},{4,6},{5,7},{6,4},{7,5},{8,10},{9,11},{10,... | collective-permute-start | bytes 983048 | tf_op jit(solution)/shard_map/ppermute | solution.py:407
  30.5 11.3 %collective-permute-start.9 = (bf16[160,1024]{1,0:T(8,128)(2,1)S(1)}, bf16[160,1024]{1,0:T(8,128)(2,1)S(1)}, u32[]{:S(2)}, u32[]{:S(2)}) collective-permute-start(bf16[160,1024]{1,0:T(8,128)(2,1)S(1)} %get-tuple-element.42.refs_1_), channel_id=1, source_target_pairs={{0,2},{1,3},{2,0},{3,1},{4,6},{5,7},{6,4},{7,5},{8,10},{9,11},{10,... | collective-permute-start | bytes 983048 | tf_op jit(solution)/shard_map/ppermute | solution.py:407
  30.9 10.9 %collective-permute-start.6 = (f32[128,128]{1,0:T(8,128)S(1)}, f32[128,128]{1,0:T(8,128)S(1)}, u32[]{:S(2)}, u32[]{:S(2)}) collective-permute-start(f32[128,128]{1,0:T(8,128)S(1)} %gram.3.refs_5_), channel_id=1, source_target_pairs={{0,2},{1,3},{2,0},{3,1},{4,6},{5,7},{6,4},{7,5},{8,10},{9,11},{10,... | collective-permute-start | bytes 196616 | tf_op jit(solution)/shard_map/ppermute | solution.py:407
  33.8 8.1 %copy-start.2 = (bf16[512,512]{1,0:T(8,128)(2,1)S(1)}, bf16[512,512]{1,0:T(8,128)(2,1)}, u32[]{:S(2)}) copy-start(bf16[512,512]{1,0:T(8,128)(2,1)} %constant.17.clone.refs_5_) | copy-start | bytes 1572868
  45.6 3.2 %collective-permute-start.10 = (f32[640,128]{1,0:T(8,128)S(1)}, f32[640,128]{1,0:T(8,128)S(1)}, u32[]{:S(2)}, u32[]{:S(2)}) collective-permute-start(f32[640,128]{1,0:T(8,128)S(1)} %get-tuple-element.45), channel_id=1, source_target_pairs={{0,1},{1,0},{2,3},{3,2},{4,5},{5,4},{6,7},{7,6},{8,9},{9,8},{10,11... | collective-permute-start | bytes 983048 | tf_op jit(solution)/shard_map/ppermute | solution.py:407
  47.4 1.3 %collective-permute-start.8 = (f32[128,128]{1,0:T(8,128)S(1)}, f32[128,128]{1,0:T(8,128)S(1)}, u32[]{:S(2)}, u32[]{:S(2)}) collective-permute-start(f32[128,128]{1,0:T(8,128)S(1)} %add.45), channel_id=1, source_target_pairs={{0,1},{1,0},{2,3},{3,2},{4,5},{5,4},{6,7},{7,6},{8,9},{9,8},{10,11... | collective-permute-start | bytes 196616 | tf_op jit(solution)/shard_map/ppermute | solution.py:407
  48.9 6.9 %collective-permute-start.11 = (f32[448,128]{1,0:T(8,128)S(1)}, f32[448,128]{1,0:T(8,128)S(1)}, u32[]{:S(2)}, u32[]{:S(2)}) collective-permute-start(f32[448,128]{1,0:T(8,128)S(1)} %pad_maximum_fusion), channel_id=1, source_target_pairs={{0,4},{4,0},{8,12},{12,8},{16,20},{20,16},{24,28},{28,24},{1,5},{5... | collective-permute-start | bytes 688136 | tf_op jit(solution)/shard_map/ppermute | solution.py:407
  50.2 8.7 %collective-permute-start.12 = (bf16[160,1024]{1,0:T(8,128)(2,1)S(1)}, bf16[160,1024]{1,0:T(8,128)(2,1)S(1)}, u32[]{:S(2)}, u32[]{:S(2)}) collective-permute-start(bf16[160,1024]{1,0:T(8,128)(2,1)S(1)} %slice.46), channel_id=1, source_target_pairs={{0,2},{1,3},{2,0},{3,1},{4,6},{5,7},{6,4},{7,5},{8,10},{9,11},{10,... | collective-permute-start | bytes 983048 | tf_op jit(solution)/shard_map/ppermute | solution.py:407
  58.9 4.1 %collective-permute-start.13 = (f32[288,128]{1,0:T(8,128)S(1)}, f32[288,128]{1,0:T(8,128)S(1)}, u32[]{:S(2)}, u32[]{:S(2)}) collective-permute-start(f32[288,128]{1,0:T(8,128)S(1)} %pad_maximum_fusion.1), channel_id=1, source_target_pairs={{0,8},{4,12},{8,0},{12,4},{16,24},{20,28},{24,16},{28,20},{1,9},{5... | collective-permute-start | bytes 442376 | tf_op jit(solution)/shard_map/ppermute | solution.py:407
  63.0 5.7 %collective-permute-start.14 = (f32[208,128]{1,0:T(8,128)S(1)}, f32[208,128]{1,0:T(8,128)S(1)}, u32[]{:S(2)}, u32[]{:S(2)}) collective-permute-start(f32[208,128]{1,0:T(8,128)S(1)} %pad_maximum_fusion.2), channel_id=1, source_target_pairs={{0,16},{4,20},{8,24},{12,28},{16,0},{20,4},{24,8},{28,12},{1,17},{... | collective-permute-start | bytes 319496 | tf_op jit(solution)/shard_map/ppermute | solution.py:407
  65.4 17.6 %collective-permute-start.16 = (bf16[160,1024]{1,0:T(8,128)(2,1)S(1)}, bf16[160,1024]{1,0:T(8,128)(2,1)S(1)}, u32[]{:S(2)}, u32[]{:S(2)}) collective-permute-start(bf16[160,1024]{1,0:T(8,128)(2,1)S(1)} %slice.55), channel_id=1, source_target_pairs={{0,2},{1,3},{2,0},{3,1},{4,6},{5,7},{6,4},{7,5},{8,10},{9,11},{10,... | collective-permute-start | bytes 983048 | tf_op jit(solution)/shard_map/ppermute | solution.py:407
  68.7 14.3 %collective-permute-start.15 = (f32[80,128]{1,0:T(8,128)S(1)}, f32[80,128]{1,0:T(8,128)S(1)}, u32[]{:S(2)}, u32[]{:S(2)}) collective-permute-start(f32[80,128]{1,0:T(8,128)S(1)} %slice_add_fusion.5), channel_id=1, source_target_pairs={{0,0},{1,8},{2,16},{3,24},{4,1},{5,9},{6,17},{7,25},{8,2},{9,10},{... | collective-permute-start | bytes 122888 | tf_op jit(solution)/shard_map/ppermute | solution.py:509

commit v13 on v12

--- a/solution.py
+++ b/solution.py
@@ -14,7 +14,7 @@
 LEND_STEPS = 2
 PROJECT_ROWS = 512
 PLACE = (False, 1, -1, True, False)
-SKETCH_STEPS = 1
+SKETCH_STEPS = 2
 FACTOR_COST = 6e9
 COST_CUT = 1
 F32 = jnp.float32
@@ -441,13 +441,13 @@
     for v in borrowed[blocks[0]]:
         w_at = v.shape[0] - rank
         ws.append(v)
-    borrow(blocks[1:], done)
+    borrow(blocks[1:3], done)
 
     pairs, arrived, done = {}, {}, ()
     ids = jnp.stack([block_of(*b) for b in blocks] + [me_n])
     slot = {b: k for k, b in enumerate(blocks)}
     for k, b in enumerate(blocks):
-        later = ()
+        later = blocks[3:] if k == 0 else ()
         numbers = [block_of(*b)] + [block_of(o[0] ^ d, o[1]) for o in later for d in near]
         out = sketch(jnp.stack(numbers), snapshots, ws, borrowed[b], UNIT, w_at, done)
         pairs[b], high = out[:2]

time: 85.9 us -> 87.2 us (1.015)
  local copies, waits for them, and re-layouts: 1.07 us -> 2.76 us
    unnamed x6 -> x14, local copies, waits for them, and re-layouts: 0.92 us -> 2.61 us
  transfers between devices with their start and end apart: 17 -> 17, of which waited for: 8 -> 9; matrix products, arithmetic and copies ran while one was open for 0% -> 0% of each run, Pallas kernels for 35% -> 34%
where the time goes in v13:
time: 87.2 us; the launch traced here: 86.8 us
  Pallas kernels  37.3 us (43%)
  waiting for transfers between devices  25.1 us (29%)
  starting transfers between devices  20.5 us (24%)
  local copies, waits for them, and re-layouts  2.76 us (3%)
  between operations  0.89 us (1%)
    ppermute x16, waiting for transfers between devices, swap(): return lax.ppermute(value, axis, [(i, i ^ bit) for i in range(size)])  25.1 us
    pallas_call x4, Pallas kernels, project(): pl.pallas_call(functools.partial(project_kernel, count, wide, len(bases),...  12.2 us
    ppermute x16, starting transfers between devices, swap(): return lax.ppermute(value, axis, [(i, i ^ bit) for i in range(size)])  11.7 us
    pallas_call x4, Pallas kernels, sketch(): pl.pallas_call(functools.partial(sketch_kernel, count, lent), grid_spec=p...  11.2 us
    ppermute x1, starting transfers between devices, body(): piece = lax.ppermute(pieces, ('node', 'samp'), route)  8.78 us
    pallas_call x1, Pallas kernels, factor_inverse(): pl.pallas_call(functools.partial(factor_kernel, rank), in_specs=[HELD] +...  5.48 us
    pallas_call x2, Pallas kernels, lend(): pl.pallas_call(functools.partial(lend_kernel, count, at), grid_spec=pltpu...  4.48 us
    unnamed x14, local copies, waits for them, and re-layouts  2.61 us
  transfers between devices with their start and end apart: 17, of which 9 were waited for; matrix products, arithmetic and copies ran while one was open for 0% of the time, Pallas kernels for 34%

profile of v13, /device:TPU:3, one launch (start us, length us, event | category | flops | bytes accessed | tf_op | source)
XLA Modules:
  0.0 86.8 jit_solution(6880770966221713743)
XLA Ops:
  1.6 1.3 %lend.2.refs_2_ = bf16[1280,512]{1,0:T(8,128)(2,1)S(1)} custom-call(s32[1]{0:T(128)} %bitcast.2.ids_ref, bf16[8192,512]{1,0:T(8,128)(2,1)} %refs_2_.7, bf16[160,512]{1,0:T(8,128)(2,1)S(1)} %bitcast.12), custom_call_target="tpu_custom_call" | custom-call | bytes 2621440 | tf_op jit(solution)/shard_map/lend/pallas_call | solution.py:64
  3.7 3.2 %lend.3 = (bf16[1024,512]{1,0:T(8,128)(2,1)}, bf16[1024,512]{1,0:T(8,128)(2,1)}) custom-call(s32[2]{0:T(128)S(1)} %pad_add_fusion.1.ids_ref, bf16[8192,512]{1,0:T(8,128)(2,1)} %refs_2_.7, bf16[8192,512]{1,0:T(8,128)(2,1)} %refs_2_.7, bf16[1280,512]{1,0:T(8,128)(2,1)S(1)} %lend.2.refs_2_), custom_call_target="tpu_custom_call" | custom-call | bytes 4194304 | tf_op jit(solution)/shard_map/lend/pallas_call | solution.py:64
  7.4 3.7 %sketch.4 = (bf16[320,1024]{1,0:T(8,128)(2,1)S(1)}, bf16[160,1024]{1,0:T(8,128)(2,1)}, bf16[1024,512]{1,0:T(8,128)(2,1)}) custom-call(s32[2]{0:T(128)S(1)} %pad_add_fusion.ids_ref, bf16[8192,512]{1,0:T(8,128)(2,1)} %refs_2_.7, bf16[160,512]{1,0:T(8,128)(2,1)S(1)} %bitcast.13, bf16[1280,512]{1,0:T(8,128)(2,1)S(1)} %collective-permute-done.refs_1_.refs_2_.refs_3_, ...), custom_call_target="tpu_custom_call" | custom-call | flops 335544320 | bytes 5177344 | tf_op jit(solution)/shard_map/sketch/pallas_call | solution.py:104
  12.0 3.0 %sketch.5 = (bf16[320,1024]{1,0:T(8,128)(2,1)S(1)}, bf16[160,1024]{1,0:T(8,128)(2,1)}) custom-call(s32[1]{0:T(128)} %bitcast.8.ids_ref, bf16[8192,512]{1,0:T(8,128)(2,1)} %refs_2_.7, bf16[160,512]{1,0:T(8,128)(2,1)S(1)} %bitcast.14, bf16[1280,512]{1,0:T(8,128)(2,1)S(1)} %collective-permute-done.refs_1_.refs_2_.refs_3_, ...), custom_call_target="tpu_custom_call" | custom-call | flops 335544320 | bytes 3080192 | tf_op jit(solution)/shard_map/sketch/pallas_call | solution.py:104
  15.9 1.4 %collective-permute-start.4 = (bf16[160,1024]{1,0:T(8,128)(2,1)}, bf16[160,1024]{1,0:T(8,128)(2,1)S(1)}, u32[]{:S(2)}, u32[]{:S(2)}) collective-permute-start(bf16[160,1024]{1,0:T(8,128)(2,1)} %get-tuple-element.31.refs_3_), channel_id=1, source_target_pairs={{0,2},{1,3},{2,0},{3,1},{4,6},{5,7},{6,4},{7,5},{8,10},{9,11},{10,... | collective-permute-start | bytes 983048 | tf_op jit(solution)/shard_map/ppermute | solution.py:407
  17.4 2.3 %sketch.6 = (bf16[320,1024]{1,0:T(8,128)(2,1)S(1)}, bf16[160,1024]{1,0:T(8,128)(2,1)S(1)}) custom-call(s32[1]{0:T(128)} %bitcast.5.ids_ref, bf16[8192,512]{1,0:T(8,128)(2,1)} %refs_2_.7, bf16[160,512]{1,0:T(8,128)(2,1)S(1)} %bitcast.15, bf16[1280,512]{1,0:T(8,128)(2,1)S(1)} %collective-permute-done.refs_1_.refs_2_.refs_3_, ...), custom_call_target="tpu_custom_call" | custom-call | flops 335544320 | bytes 3080192 | tf_op jit(solution)/shard_map/sketch/pallas_call | solution.py:104
  21.7 2.9 %project.4.refs_4_ = f32[2,160,512]{2,1,0:T(8,128)S(1)} custom-call(s32[5]{0:T(128)S(1)} %stack.51.ids_ref, bf16[320,1024]{1,0:T(8,128)(2,1)S(1)} %get-tuple-element.34.own_ref.refs_0_, bf16[160,1024]{1,0:T(8,128)(2,1)S(1)} %collective-permute-done.5.got_ref.refs_1_.refs_2_, bf16[8192,512]{1,0:T(8,128)(2,1)} %refs_2_.7, ...), custom_call_target="tpu_custom_call" | custom-call | flops 671088640 | bytes 3080192 | tf_op jit(solution)/shard_map/project/pallas_call | solution.py:296
  24.7 2.2 %sketch.7 = (bf16[320,1024]{1,0:T(8,128)(2,1)S(1)}, bf16[160,1024]{1,0:T(8,128)(2,1)S(1)}) custom-call(s32[1]{0:T(128)} %bitcast.ids_ref, bf16[8192,512]{1,0:T(8,128)(2,1)} %refs_2_.7, bf16[160,512]{1,0:T(8,128)(2,1)S(1)} %bitcast.16, bf16[1280,512]{1,0:T(8,128)(2,1)S(1)} %collective-permute-done.refs_1_.refs_2_.refs_3_, ...), custom_call_target="tpu_custom_call" | custom-call | flops 335544320 | bytes 3080192 | tf_op jit(solution)/shard_map/sketch/pallas_call | solution.py:104
  28.8 2.8 %project.5.refs_4_ = f32[2,160,512]{2,1,0:T(8,128)S(1)} custom-call(s32[5]{0:T(128)S(1)} %stack.51.ids_ref, bf16[320,1024]{1,0:T(8,128)(2,1)S(1)} %get-tuple-element.33.own_ref.refs_0_.refs_1_, bf16[160,1024]{1,0:T(8,128)(2,1)S(1)} %collective-permute-done.4.got_ref.refs_1_.refs_3_, bf16[8192,512]{1,0:T(8,128)(2,1)} %refs_2_.7, ...), custom_call_target="tpu_custom_call" | custom-call | flops 671088640 | bytes 3080192 | tf_op jit(solution)/shard_map/project/pallas_call | solution.py:296
  33.1 1.9 %collective-permute-done.7.refs_1_ = bf16[160,1024]{1,0:T(8,128)(2,1)S(1)} collective-permute-done((bf16[160,1024]{1,0:T(8,128)(2,1)S(1)}, bf16[160,1024]{1,0:T(8,128)(2,1)S(1)}, u32[]{:S(2)}, u32[]{:S(2)}) %collective-permute-start.7) | collective-permute-done | bytes 327712 | tf_op jit(solution)/shard_map/ppermute | solution.py:407
  35.1 2.8 %project.6.refs_4_ = f32[2,160,512]{2,1,0:T(8,128)S(1)} custom-call(s32[5]{0:T(128)S(1)} %stack.51.ids_ref, bf16[320,1024]{1,0:T(8,128)(2,1)S(1)} %copy-done.5, bf16[160,1024]{1,0:T(8,128)(2,1)S(1)} %collective-permute-done.7.refs_1_, bf16[8192,512]{1,0:T(8,128)(2,1)} %refs_2_.7, bf16[1280,512]{1,0:T(8,128)(2,1)S(1)} %collective-permute-done.refs_1_.refs_2_.refs_3_, ...), custom_call_target="tpu_custom_call" | custom-call | flops 671088640 | bytes 3080192 | tf_op jit(solution)/shard_map/project/pallas_call | solution.py:296
  37.8 5.4 %collective-permute-done.6 = f32[128,128]{1,0:T(8,128)S(1)} collective-permute-done((f32[128,128]{1,0:T(8,128)S(1)}, f32[128,128]{1,0:T(8,128)S(1)}, u32[]{:S(2)}, u32[]{:S(2)}) %collective-permute-start.6) | collective-permute-done | bytes 65568 | tf_op jit(solution)/shard_map/ppermute | solution.py:407
  43.3 3.8 %project.7 = (f32[640,128]{1,0:T(8,128)S(1)}, f32[640,128]{1,0:T(8,128)S(1)}) custom-call(s32[5]{0:T(128)S(1)} %stack.51.ids_ref, bf16[320,1024]{1,0:T(8,128)(2,1)S(1)} %copy-done.3, bf16[160,1024]{1,0:T(8,128)(2,1)S(1)} %collective-permute-done.9.refs_1_, bf16[8192,512]{1,0:T(8,128)(2,1)} %refs_2_.7, ...), custom_call_target="tpu_custom_call" | custom-call | flops 671088640 | bytes 3080192 | tf_op jit(solution)/shard_map/project/pallas_call | solution.py:296
  47.1 1.6 %collective-permute-start.10 = (f32[640,128]{1,0:T(8,128)S(1)}, f32[640,128]{1,0:T(8,128)S(1)}, u32[]{:S(2)}, u32[]{:S(2)}) collective-permute-start(f32[640,128]{1,0:T(8,128)S(1)} %get-tuple-element.45), channel_id=1, source_target_pairs={{0,1},{1,0},{2,3},{3,2},{4,5},{5,4},{6,7},{7,6},{8,9},{9,8},{10,11... | collective-permute-start | bytes 983048 | tf_op jit(solution)/shard_map/ppermute | solution.py:407
  50.2 1.3 %collective-permute-start.11 = (f32[448,128]{1,0:T(8,128)S(1)}, f32[448,128]{1,0:T(8,128)S(1)}, u32[]{:S(2)}, u32[]{:S(2)}) collective-permute-start(f32[448,128]{1,0:T(8,128)S(1)} %pad_maximum_fusion), channel_id=1, source_target_pairs={{0,4},{4,0},{8,12},{12,8},{16,20},{20,16},{24,28},{28,24},{1,5},{5... | collective-permute-start | bytes 688136 | tf_op jit(solution)/shard_map/ppermute | solution.py:407
  51.8 5.2 %collective-permute-done.11 = f32[448,128]{1,0:T(8,128)S(1)} collective-permute-done((f32[448,128]{1,0:T(8,128)S(1)}, f32[448,128]{1,0:T(8,128)S(1)}, u32[]{:S(2)}, u32[]{:S(2)}) %collective-permute-start.11) | collective-permute-done | bytes 229408 | tf_op jit(solution)/shard_map/ppermute | solution.py:407
  57.1 3.1 %collective-permute-done.12.refs_4_ = bf16[160,1024]{1,0:T(8,128)(2,1)S(1)} collective-permute-done((bf16[160,1024]{1,0:T(8,128)(2,1)S(1)}, bf16[160,1024]{1,0:T(8,128)(2,1)S(1)}, u32[]{:S(2)}, u32[]{:S(2)}) %collective-permute-start.12) | collective-permute-done | bytes 327712 | tf_op jit(solution)/shard_map/ppermute | solution.py:407
  60.2 1.3 %collective-permute-start.13 = (f32[288,128]{1,0:T(8,128)S(1)}, f32[288,128]{1,0:T(8,128)S(1)}, u32[]{:S(2)}, u32[]{:S(2)}) collective-permute-start(f32[288,128]{1,0:T(8,128)S(1)} %pad_maximum_fusion.1), channel_id=1, source_target_pairs={{0,8},{4,12},{8,0},{12,4},{16,24},{20,28},{24,16},{28,20},{1,9},{5... | collective-permute-start | bytes 442376 | tf_op jit(solution)/shard_map/ppermute | solution.py:407
  61.6 2.7 %collective-permute-done.13 = f32[288,128]{1,0:T(8,128)S(1)} collective-permute-done((f32[288,128]{1,0:T(8,128)S(1)}, f32[288,128]{1,0:T(8,128)S(1)}, u32[]{:S(2)}, u32[]{:S(2)}) %collective-permute-start.13) | collective-permute-done | bytes 147488 | tf_op jit(solution)/shard_map/ppermute | solution.py:407
  64.4 2.4 %collective-permute-start.14 = (f32[208,128]{1,0:T(8,128)S(1)}, f32[208,128]{1,0:T(8,128)S(1)}, u32[]{:S(2)}, u32[]{:S(2)}) collective-permute-start(f32[208,128]{1,0:T(8,128)S(1)} %pad_maximum_fusion.2), channel_id=1, source_target_pairs={{0,16},{4,20},{8,24},{12,28},{16,0},{20,4},{24,8},{28,12},{1,17},{... | collective-permute-start | bytes 319496 | tf_op jit(solution)/shard_map/ppermute | solution.py:407
  67.1 2.9 %collective-permute-done.14 = f32[208,128]{1,0:T(8,128)S(1)} collective-permute-done((f32[208,128]{1,0:T(8,128)S(1)}, f32[208,128]{1,0:T(8,128)S(1)}, u32[]{:S(2)}, u32[]{:S(2)}) %collective-permute-start.14) | collective-permute-done | bytes 106528 | tf_op jit(solution)/shard_map/ppermute | solution.py:407
  70.0 8.8 %collective-permute-start.15 = (f32[80,128]{1,0:T(8,128)S(1)}, f32[80,128]{1,0:T(8,128)S(1)}, u32[]{:S(2)}, u32[]{:S(2)}) collective-permute-start(f32[80,128]{1,0:T(8,128)S(1)} %slice_add_fusion.5), channel_id=1, source_target_pairs={{0,0},{1,8},{2,16},{3,24},{4,1},{5,9},{6,17},{7,25},{8,2},{9,10},{... | collective-permute-start | bytes 122888 | tf_op jit(solution)/shard_map/ppermute | solution.py:509
  78.8 5.5 %factor.1.inv_ref = f32[160,160]{1,0:T(8,128)S(1)} custom-call(f32[128,128]{1,0:T(8,128)S(1)} %slice_add_fusion.2.g_ref), custom_call_target="tpu_custom_call" | custom-call | flops 6000000000 | bytes 102400 | tf_op jit(solution)/shard_map/factor/pallas_call | solution.py:241
  84.4 2.5 %finish.1 = (f32[160,2048]{1,0:T(8,128)}, f32[8,1280]{1,0:T(8,128)}) custom-call(f32[160,160]{1,0:T(8,128)S(1)} %factor.1.inv_ref, f32[80,128]{1,0:T(8,128)S(1)} %collective-permute-done.15.piece_ref, bf16[320,1024]{1,0:T(8,128)(2,1)S(1)} %get-tuple-element.34.own_ref.refs_0_, bf16[320,1024]{1,0:T(8,128)(2,1)S(1)} %get-tuple-element.33.own_ref.refs_0_.refs_1_, ...), custom_call_target="tpu_custom_call" | custom-call | flops 629145600 | bytes 3932160 | tf_op jit(solution)/shard_map/finish/pallas_call | solution.py:394
  (58 shorter events, 11.9 us)
Async XLA Ops:
  0.6 0.9 %copy-start = (bf16[512,160]{0,1:T(8,128)(2,1)S(1)}, bf16[512,160]{0,1:T(8,128)(2,1)}, u32[]{:S(2)}) copy-start(bf16[512,160]{0,1:T(8,128)(2,1)} %param.4) | copy-start | bytes 491524
  2.9 4.6 %collective-permute-start = (bf16[1280,512]{1,0:T(8,128)(2,1)S(1)}, bf16[1280,512]{1,0:T(8,128)(2,1)S(1)}, u32[]{:S(2)}, u32[]{:S(2)}) collective-permute-start(bf16[1280,512]{1,0:T(8,128)(2,1)S(1)} %lend.2.refs_2_), channel_id=1, source_target_pairs={{0,1},{1,0},{2,3},{3,2},{4,5},{5,4},{6,7},{7,6},{8,9},{9,8},{10,11... | collective-permute-start | bytes 3932168 | tf_op jit(solution)/shard_map/ppermute | solution.py:407
  3.7 3.8 %copy-start.1 = (bf16[512,160]{0,1:T(8,128)(2,1)S(1)}, bf16[512,160]{0,1:T(8,128)(2,1)}, u32[]{:S(2)}) copy-start(bf16[512,160]{0,1:T(8,128)(2,1)} %param.4) | copy-start | bytes 491524
  6.9 5.2 %collective-permute-start.3 = (bf16[1024,512]{1,0:T(8,128)(2,1)}, bf16[1024,512]{1,0:T(8,128)(2,1)}, u32[]{:S(2)}, u32[]{:S(2)}) collective-permute-start(bf16[1024,512]{1,0:T(8,128)(2,1)} %get-tuple-element.29), channel_id=1, source_target_pairs={{0,1},{1,0},{2,3},{3,2},{4,5},{5,4},{6,7},{7,6},{8,9},{9,8},{10,11... | collective-permute-start | bytes 3145736 | tf_op jit(solution)/shard_map/ppermute | solution.py:407
  6.9 10.5 %collective-permute-start.2 = (bf16[1024,512]{1,0:T(8,128)(2,1)}, bf16[1024,512]{1,0:T(8,128)(2,1)}, u32[]{:S(2)}, u32[]{:S(2)}) collective-permute-start(bf16[1024,512]{1,0:T(8,128)(2,1)} %get-tuple-element.28), channel_id=1, source_target_pairs={{0,1},{1,0},{2,3},{3,2},{4,5},{5,4},{6,7},{7,6},{8,9},{9,8},{10,11... | collective-permute-start | bytes 3145736 | tf_op jit(solution)/shard_map/ppermute | solution.py:407
  11.2 0.8 copy-start.4
  12.0 12.7 %collective-permute-start.1 = (bf16[1024,512]{1,0:T(8,128)(2,1)}, bf16[1024,512]{1,0:T(8,128)(2,1)S(1)}, u32[]{:S(2)}, u32[]{:S(2)}) collective-permute-start(bf16[1024,512]{1,0:T(8,128)(2,1)} %get-tuple-element.27), channel_id=1, source_target_pairs={{0,1},{1,0},{2,3},{3,2},{4,5},{5,4},{6,7},{7,6},{8,9},{9,8},{10,11... | collective-permute-start | bytes 3145736 | tf_op jit(solution)/shard_map/ppermute | solution.py:407
  12.0 9.0 %collective-permute-start.5 = (bf16[160,1024]{1,0:T(8,128)(2,1)}, bf16[160,1024]{1,0:T(8,128)(2,1)S(1)}, u32[]{:S(2)}, u32[]{:S(2)}) collective-permute-start(bf16[160,1024]{1,0:T(8,128)(2,1)} %get-tuple-element.30.refs_3_), channel_id=1, source_target_pairs={{0,2},{1,3},{2,0},{3,1},{4,6},{5,7},{6,4},{7,5},{8,10},{9,11},{10,... | collective-permute-start | bytes 983048 | tf_op jit(solution)/shard_map/ppermute | solution.py:407
  15.0 0.8 copy-start.2
  15.9 12.2 %collective-permute-start.4 = (bf16[160,1024]{1,0:T(8,128)(2,1)}, bf16[160,1024]{1,0:T(8,128)(2,1)S(1)}, u32[]{:S(2)}, u32[]{:S(2)}) collective-permute-start(bf16[160,1024]{1,0:T(8,128)(2,1)} %get-tuple-element.31.refs_3_), channel_id=1, source_target_pairs={{0,2},{1,3},{2,0},{3,1},{4,6},{5,7},{6,4},{7,5},{8,10},{9,11},{10,... | collective-permute-start | bytes 983048 | tf_op jit(solution)/shard_map/ppermute | solution.py:407
  19.7 15.4 %collective-permute-start.7 = (bf16[160,1024]{1,0:T(8,128)(2,1)S(1)}, bf16[160,1024]{1,0:T(8,128)(2,1)S(1)}, u32[]{:S(2)}, u32[]{:S(2)}) collective-permute-start(bf16[160,1024]{1,0:T(8,128)(2,1)S(1)} %get-tuple-element.32.refs_3_), channel_id=1, source_target_pairs={{0,2},{1,3},{2,0},{3,1},{4,6},{5,7},{6,4},{7,5},{8,10},{9,11},{10,... | collective-permute-start | bytes 983048 | tf_op jit(solution)/shard_map/ppermute | solution.py:407
  28.8 6.2 %copy-start.5 = (bf16[320,1024]{1,0:T(8,128)(2,1)S(1)}, bf16[320,1024]{1,0:T(8,128)(2,1)}, u32[]{:S(2)}) copy-start(bf16[320,1024]{1,0:T(8,128)(2,1)} %copy-done.4) | copy-start | bytes 1966084
  31.6 11.7 %collective-permute-start.9 = (bf16[160,1024]{1,0:T(8,128)(2,1)S(1)}, bf16[160,1024]{1,0:T(8,128)(2,1)S(1)}, u32[]{:S(2)}, u32[]{:S(2)}) collective-permute-start(bf16[160,1024]{1,0:T(8,128)(2,1)S(1)} %get-tuple-element.42.refs_1_), channel_id=1, source_target_pairs={{0,2},{1,3},{2,0},{3,1},{4,6},{5,7},{6,4},{7,5},{8,10},{9,11},{10,... | collective-permute-start | bytes 983048 | tf_op jit(solution)/shard_map/ppermute | solution.py:407
  32.0 11.3 %collective-permute-start.6 = (f32[128,128]{1,0:T(8,128)S(1)}, f32[128,128]{1,0:T(8,128)S(1)}, u32[]{:S(2)}, u32[]{:S(2)}) collective-permute-start(f32[128,128]{1,0:T(8,128)S(1)} %gram.3.refs_5_), channel_id=1, source_target_pairs={{0,2},{1,3},{2,0},{3,1},{4,6},{5,7},{6,4},{7,5},{8,10},{9,11},{10,... | collective-permute-start | bytes 196616 | tf_op jit(solution)/shard_map/ppermute | solution.py:407
  35.1 8.2 %copy-start.3 = (bf16[320,1024]{1,0:T(8,128)(2,1)S(1)}, bf16[320,1024]{1,0:T(8,128)(2,1)}, u32[]{:S(2)}) copy-start(bf16[320,1024]{1,0:T(8,128)(2,1)} %copy-done.2) | copy-start | bytes 1966084
  35.1 8.2 %copy-start.6 = (bf16[512,512]{1,0:T(8,128)(2,1)S(1)}, bf16[512,512]{1,0:T(8,128)(2,1)}, u32[]{:S(2)}) copy-start(bf16[512,512]{1,0:T(8,128)(2,1)} %constant.17.clone.refs_5_) | copy-start | bytes 1572868
  47.1 3.0 %collective-permute-start.10 = (f32[640,128]{1,0:T(8,128)S(1)}, f32[640,128]{1,0:T(8,128)S(1)}, u32[]{:S(2)}, u32[]{:S(2)}) collective-permute-start(f32[640,128]{1,0:T(8,128)S(1)} %get-tuple-element.45), channel_id=1, source_target_pairs={{0,1},{1,0},{2,3},{3,2},{4,5},{5,4},{6,7},{7,6},{8,9},{9,8},{10,11... | collective-permute-start | bytes 983048 | tf_op jit(solution)/shard_map/ppermute | solution.py:407
  48.7 1.3 %collective-permute-start.8 = (f32[128,128]{1,0:T(8,128)S(1)}, f32[128,128]{1,0:T(8,128)S(1)}, u32[]{:S(2)}, u32[]{:S(2)}) collective-permute-start(f32[128,128]{1,0:T(8,128)S(1)} %add.45), channel_id=1, source_target_pairs={{0,1},{1,0},{2,3},{3,2},{4,5},{5,4},{6,7},{7,6},{8,9},{9,8},{10,11... | collective-permute-start | bytes 196616 | tf_op jit(solution)/shard_map/ppermute | solution.py:407
  50.2 6.9 %collective-permute-start.11 = (f32[448,128]{1,0:T(8,128)S(1)}, f32[448,128]{1,0:T(8,128)S(1)}, u32[]{:S(2)}, u32[]{:S(2)}) collective-permute-start(f32[448,128]{1,0:T(8,128)S(1)} %pad_maximum_fusion), channel_id=1, source_target_pairs={{0,4},{4,0},{8,12},{12,8},{16,20},{20,16},{24,28},{28,24},{1,5},{5... | collective-permute-start | bytes 688136 | tf_op jit(solution)/shard_map/ppermute | solution.py:407
  51.5 8.7 %collective-permute-start.12 = (bf16[160,1024]{1,0:T(8,128)(2,1)S(1)}, bf16[160,1024]{1,0:T(8,128)(2,1)S(1)}, u32[]{:S(2)}, u32[]{:S(2)}) collective-permute-start(bf16[160,1024]{1,0:T(8,128)(2,1)S(1)} %slice.46), channel_id=1, source_target_pairs={{0,2},{1,3},{2,0},{3,1},{4,6},{5,7},{6,4},{7,5},{8,10},{9,11},{10,... | collective-permute-start | bytes 983048 | tf_op jit(solution)/shard_map/ppermute | solution.py:407
  60.2 4.1 %collective-permute-start.13 = (f32[288,128]{1,0:T(8,128)S(1)}, f32[288,128]{1,0:T(8,128)S(1)}, u32[]{:S(2)}, u32[]{:S(2)}) collective-permute-start(f32[288,128]{1,0:T(8,128)S(1)} %pad_maximum_fusion.1), channel_id=1, source_target_pairs={{0,8},{4,12},{8,0},{12,4},{16,24},{20,28},{24,16},{28,20},{1,9},{5... | collective-permute-start | bytes 442376 | tf_op jit(solution)/shard_map/ppermute | solution.py:407
  64.4 5.7 %collective-permute-start.14 = (f32[208,128]{1,0:T(8,128)S(1)}, f32[208,128]{1,0:T(8,128)S(1)}, u32[]{:S(2)}, u32[]{:S(2)}) collective-permute-start(f32[208,128]{1,0:T(8,128)S(1)} %pad_maximum_fusion.2), channel_id=1, source_target_pairs={{0,16},{4,20},{8,24},{12,28},{16,0},{20,4},{24,8},{28,12},{1,17},{... | collective-permute-start | bytes 319496 | tf_op jit(solution)/shard_map/ppermute | solution.py:407
  66.7 17.6 %collective-permute-start.16 = (bf16[160,1024]{1,0:T(8,128)(2,1)S(1)}, bf16[160,1024]{1,0:T(8,128)(2,1)S(1)}, u32[]{:S(2)}, u32[]{:S(2)}) collective-permute-start(bf16[160,1024]{1,0:T(8,128)(2,1)S(1)} %slice.55), channel_id=1, source_target_pairs={{0,2},{1,3},{2,0},{3,1},{4,6},{5,7},{6,4},{7,5},{8,10},{9,11},{10,... | collective-permute-start | bytes 983048 | tf_op jit(solution)/shard_map/ppermute | solution.py:407
  70.0 14.3 %collective-permute-start.15 = (f32[80,128]{1,0:T(8,128)S(1)}, f32[80,128]{1,0:T(8,128)S(1)}, u32[]{:S(2)}, u32[]{:S(2)}) collective-permute-start(f32[80,128]{1,0:T(8,128)S(1)} %slice_add_fusion.5), channel_id=1, source_target_pairs={{0,0},{1,8},{2,16},{3,24},{4,1},{5,9},{6,17},{7,25},{8,2},{9,10},{... | collective-permute-start | bytes 122888 | tf_op jit(solution)/shard_map/ppermute | solution.py:509

commit v14 on v12

--- a/solution.py
+++ b/solution.py
@@ -366,7 +366,7 @@
             outs[w][p * tall:(p + 1) * tall, :] = hold[me_node ^ reverse_bits(p, bits)]
 
 
-def finish_kernel(scale, per_node, width_cols, count, inv_ref, piece_ref, *refs):
+def finish_kernel(scale, per_node, width_cols, count, inv_ref, piece_ref, piece2_ref, *refs):
     both, high = refs[:count], refs[count:2 * count]
     low, core_ref, coef_ref = refs[2 * count:3 * count], refs[-2], refs[-1]
     rank = inv_ref.shape[0]
@@ -380,14 +380,14 @@
         at += rows
     width = per_node * width_cols
     fold = folding(rank, width)
-    total = piece_ref[...]
+    total = piece_ref[...] + piece2_ref[...]
     total = jnp.concatenate([total[:, f * width:(f + 1) * width] for f in range(fold)], axis=0)
     out = dot(total, inverse, ((0,), (1,)), HI) * scale
     coef_ref[...] = jnp.concatenate(
         [out[p * width_cols:(p + 1) * width_cols, :] for p in range(per_node)], axis=1)
 
 
-def finish(inverse, piece, both, high, low, scale, per_node, width_cols):
+def finish(inverse, pieces, both, high, low, scale, per_node, width_cols):
     rank = inverse.shape[0]
     count = len(both)
     rows = sum(v.shape[1] for v in high)
@@ -400,7 +400,7 @@
         compiler_params=params(),
         cost_estimate=cost(12 * rank * rank * rows, 12 * rank * rows),
         name="finish",
-    )(inverse, piece, *both, *high, *low)
+    )(inverse, *pieces, *both, *high, *low)
 
 
 def swap(value, axis, size, bit):
@@ -495,20 +495,28 @@
     pieces = messages[0]
     for d in near:
         pieces = pieces + swap(messages[d], "samp", samp, d)
-    for k in range(node.bit_length() - 1):
+    bit = 1
+    for k in range(node.bit_length() - 2):
         for c in range(2):
             if k == PLACE[1 + c]:
                 pieces, got_low[c] = lax.optimization_barrier((pieces, got_low[c]))
         edge = pieces.shape[0] // 2
-        got = swap(jnp.concatenate([pieces[edge:], gram], axis=0), "node", node, 1 << k)
+        got = swap(jnp.concatenate([pieces[edge:], gram], axis=0), "node", node, bit)
         pieces, gram = pieces[:edge] + got[:edge], gram + got[edge:]
+        bit *= 2
+
+    gram = gram + swap(gram, "node", node, bit)
     spread = node // samp
-    route = [
-        (n * samp + s, (s * spread + n // samp) * samp + n % samp) for n in range(node) for s in range(samp)
-    ]
-    piece = lax.ppermute(pieces, ("node", "samp"), route)
+    landed = []
+    for k, value in ((0, pieces[:tall]), (bit, pieces[tall:])):
+        route = []
+        for n in range(node):
+            a, s_to = (n ^ k) // samp, (n ^ k) % samp
+            for s_from in range(samp):
+                route.append((n * samp + s_from, (s_from * spread + a) * samp + s_to))
+        landed.append(lax.ppermute(value, ("node", "samp"), route))
     inverse = factor_inverse(gram, rank)
-    core, coef = finish(inverse, piece, own, got_high, got_low, 1.0 / total, per_node, width_cols)
+    core, coef = finish(inverse, landed, own, got_high, got_low, 1.0 / total, per_node, width_cols)
     return (core.T, coef.T)
 
 

time: 85.9 us -> 81.1 us (0.944)
  starting transfers between devices: 20.7 us -> 18.3 us
  waiting for transfers between devices: 25.1 us -> 22.8 us
    ppermute x16, waiting for transfers between devices: 25.1 us -> 21.8 us  [swap(): return lax.ppermute(value, axis, [(i, i ^ bit) for i in range(size)])]
    ppermute x1 -> x2, starting transfers between devices: 8.79 us -> 6.35 us  [body(): landed.append(lax.ppermute(value, ('node', 'samp'), route))]
    ppermute x1 -> x2, waiting for transfers between devices: 0.01 us -> 0.99 us  [body(): landed.append(lax.ppermute(value, ('node', 'samp'), route))]
  transfers between devices with their start and end apart: 17 -> 18, of which waited for: 8 -> 8; matrix products, arithmetic and copies ran while one was open for 0% -> 0% of each run, Pallas kernels for 35% -> 37%
where the time goes in v14:
time: 81.1 us; the launch traced here: 80.7 us
  Pallas kernels  37.5 us (46%)
  waiting for transfers between devices  22.8 us (28%)
  starting transfers between devices  18.3 us (23%)
  local copies, waits for them, and re-layouts  1.07 us (1%)
  between operations  0.87 us (1%)
    ppermute x16, waiting for transfers between devices, swap(): return lax.ppermute(value, axis, [(i, i ^ bit) for i in range(size)])  21.8 us
    pallas_call x4, Pallas kernels, project(): pl.pallas_call(functools.partial(project_kernel, count, wide, len(bases),...  12.4 us
    ppermute x16, starting transfers between devices, swap(): return lax.ppermute(value, axis, [(i, i ^ bit) for i in range(size)])  11.9 us
    pallas_call x4, Pallas kernels, sketch(): pl.pallas_call(functools.partial(sketch_kernel, count, lent), grid_spec=p...  10.6 us
    ppermute x2, starting transfers between devices, body(): landed.append(lax.ppermute(value, ('node', 'samp'), route))  6.35 us
    pallas_call x1, Pallas kernels, factor_inverse(): pl.pallas_call(functools.partial(factor_kernel, rank), in_specs=[HELD] +...  5.48 us
    pallas_call x2, Pallas kernels, lend(): pl.pallas_call(functools.partial(lend_kernel, count, at), grid_spec=pltpu...  4.99 us
    pallas_call x1, Pallas kernels, finish(): pl.pallas_call(functools.partial(finish_kernel, scale, per_node, width_co...  2.46 us
  transfers between devices with their start and end apart: 18, of which 8 were waited for; matrix products, arithmetic and copies ran while one was open for 0% of the time, Pallas kernels for 37%

profile of v14, /device:TPU:3, one launch (start us, length us, event | category | flops | bytes accessed | tf_op | source)
XLA Modules:
  0.0 80.7 jit_solution(11259276470596729969)
XLA Ops:
  1.6 1.3 %lend.2.refs_3_ = bf16[1280,512]{1,0:T(8,128)(2,1)S(1)} custom-call(s32[1]{0:T(128)} %bitcast.2.ids_ref, bf16[8192,512]{1,0:T(8,128)(2,1)} %refs_2_.9, bf16[160,512]{1,0:T(8,128)(2,1)S(1)} %bitcast.12), custom_call_target="tpu_custom_call" | custom-call | bytes 2621440 | tf_op jit(solution)/shard_map/lend/pallas_call | solution.py:64
  3.7 3.7 %lend.3 = (bf16[1024,512]{1,0:T(8,128)(2,1)}, bf16[1024,512]{1,0:T(8,128)(2,1)}, bf16[1024,512]{1,0:T(8,128)(2,1)}) custom-call(s32[3]{0:T(128)S(1)} %pad_add_fusion.ids_ref, bf16[8192,512]{1,0:T(8,128)(2,1)} %refs_2_.9, bf16[8192,512]{1,0:T(8,128)(2,1)} %refs_2_.9, bf16[8192,512]{1,0:T(8,128)(2,1)} %refs_2_.9, bf16[1280,512]{1,0:T(8,128)(2,1)S(1)} %lend.2.refs_3_), custom_call_target="tpu_custom_call" | custom-call | bytes 6291456 | tf_op jit(solution)/shard_map/lend/pallas_call | solution.py:64
  7.9 2.8 %sketch.4 = (bf16[320,1024]{1,0:T(8,128)(2,1)S(1)}, bf16[160,1024]{1,0:T(8,128)(2,1)}) custom-call(s32[1]{0:T(128)} %bitcast.8.ids_ref, bf16[8192,512]{1,0:T(8,128)(2,1)} %refs_2_.9, bf16[160,512]{1,0:T(8,128)(2,1)S(1)} %bitcast.13, bf16[1280,512]{1,0:T(8,128)(2,1)S(1)} %collective-permute-done.refs_1_.refs_2_.refs_3_, ...), custom_call_target="tpu_custom_call" | custom-call | flops 335544320 | bytes 3080192 | tf_op jit(solution)/shard_map/sketch/pallas_call | solution.py:104
  10.7 3.1 %sketch.5 = (bf16[320,1024]{1,0:T(8,128)(2,1)S(1)}, bf16[160,1024]{1,0:T(8,128)(2,1)}) custom-call(s32[1]{0:T(128)} %bitcast.7.ids_ref, bf16[8192,512]{1,0:T(8,128)(2,1)} %refs_2_.9, bf16[160,512]{1,0:T(8,128)(2,1)S(1)} %bitcast.14, bf16[1280,512]{1,0:T(8,128)(2,1)S(1)} %collective-permute-done.refs_1_.refs_2_.refs_3_, ...), custom_call_target="tpu_custom_call" | custom-call | flops 335544320 | bytes 3080192 | tf_op jit(solution)/shard_map/sketch/pallas_call | solution.py:104
  13.8 1.5 %collective-permute-start.4 = (bf16[160,1024]{1,0:T(8,128)(2,1)}, bf16[160,1024]{1,0:T(8,128)(2,1)S(1)}, u32[]{:S(2)}, u32[]{:S(2)}) collective-permute-start(bf16[160,1024]{1,0:T(8,128)(2,1)} %get-tuple-element.31.refs_3_), channel_id=1, source_target_pairs={{0,2},{1,3},{2,0},{3,1},{4,6},{5,7},{6,4},{7,5},{8,10},{9,11},{10,... | collective-permute-start | bytes 983048 | tf_op jit(solution)/shard_map/ppermute | solution.py:407
  15.4 2.4 %sketch.6 = (bf16[320,1024]{1,0:T(8,128)(2,1)S(1)}, bf16[160,1024]{1,0:T(8,128)(2,1)S(1)}) custom-call(s32[1]{0:T(128)} %bitcast.6.ids_ref, bf16[8192,512]{1,0:T(8,128)(2,1)} %refs_2_.9, bf16[160,512]{1,0:T(8,128)(2,1)S(1)} %bitcast.15, bf16[1280,512]{1,0:T(8,128)(2,1)S(1)} %collective-permute-done.refs_1_.refs_2_.refs_3_, ...), custom_call_target="tpu_custom_call" | custom-call | flops 335544320 | bytes 3080192 | tf_op jit(solution)/shard_map/sketch/pallas_call | solution.py:104
  17.8 2.4 %sketch.7 = (bf16[320,1024]{1,0:T(8,128)(2,1)S(1)}, bf16[160,1024]{1,0:T(8,128)(2,1)S(1)}) custom-call(s32[1]{0:T(128)} %bitcast.ids_ref, bf16[8192,512]{1,0:T(8,128)(2,1)} %refs_2_.9, bf16[160,512]{1,0:T(8,128)(2,1)S(1)} %bitcast.16, bf16[1280,512]{1,0:T(8,128)(2,1)S(1)} %collective-permute-done.refs_1_.refs_2_.refs_3_, ...), custom_call_target="tpu_custom_call" | custom-call | flops 335544320 | bytes 3080192 | tf_op jit(solution)/shard_map/sketch/pallas_call | solution.py:104
  20.9 2.9 %project.4.refs_4_ = f32[2,160,512]{2,1,0:T(8,128)S(1)} custom-call(s32[5]{0:T(128)S(1)} %stack.47.ids_ref, bf16[320,1024]{1,0:T(8,128)(2,1)S(1)} %get-tuple-element.34.own_ref.refs_0_, bf16[160,1024]{1,0:T(8,128)(2,1)S(1)} %collective-permute-done.5.got_ref.refs_1_.refs_2_, bf16[8192,512]{1,0:T(8,128)(2,1)} %refs_2_.9, ...), custom_call_target="tpu_custom_call" | custom-call | flops 671088640 | bytes 3080192 | tf_op jit(solution)/shard_map/project/pallas_call | solution.py:296
  23.9 2.8 %collective-permute-done.4.got_ref.refs_1_.refs_3_ = bf16[160,1024]{1,0:T(8,128)(2,1)S(1)} collective-permute-done((bf16[160,1024]{1,0:T(8,128)(2,1)}, bf16[160,1024]{1,0:T(8,128)(2,1)S(1)}, u32[]{:S(2)}, u32[]{:S(2)}) %collective-permute-start.4) | collective-permute-done | bytes 327712 | tf_op jit(solution)/shard_map/ppermute | solution.py:407
  27.5 3.0 %project.5.refs_4_ = f32[2,160,512]{2,1,0:T(8,128)S(1)} custom-call(s32[5]{0:T(128)S(1)} %stack.47.ids_ref, bf16[320,1024]{1,0:T(8,128)(2,1)S(1)} %get-tuple-element.33.own_ref.refs_0_.refs_1_, bf16[160,1024]{1,0:T(8,128)(2,1)S(1)} %collective-permute-done.4.got_ref.refs_1_.refs_3_, bf16[8192,512]{1,0:T(8,128)(2,1)} %refs_2_.9, ...), custom_call_target="tpu_custom_call" | custom-call | flops 671088640 | bytes 3080192 | tf_op jit(solution)/shard_map/project/pallas_call | solution.py:296
  32.0 1.8 %collective-permute-done.7.refs_1_ = bf16[160,1024]{1,0:T(8,128)(2,1)S(1)} collective-permute-done((bf16[160,1024]{1,0:T(8,128)(2,1)S(1)}, bf16[160,1024]{1,0:T(8,128)(2,1)S(1)}, u32[]{:S(2)}, u32[]{:S(2)}) %collective-permute-start.7) | collective-permute-done | bytes 327712 | tf_op jit(solution)/shard_map/ppermute | solution.py:407
  33.8 2.8 %project.6.refs_4_ = f32[2,160,512]{2,1,0:T(8,128)S(1)} custom-call(s32[5]{0:T(128)S(1)} %stack.47.ids_ref, bf16[320,1024]{1,0:T(8,128)(2,1)S(1)} %get-tuple-element.37.refs_0_, bf16[160,1024]{1,0:T(8,128)(2,1)S(1)} %collective-permute-done.7.refs_1_, bf16[8192,512]{1,0:T(8,128)(2,1)} %refs_2_.9, ...), custom_call_target="tpu_custom_call" | custom-call | flops 671088640 | bytes 3080192 | tf_op jit(solution)/shard_map/project/pallas_call | solution.py:296
  36.5 5.3 %collective-permute-done.6 = f32[128,128]{1,0:T(8,128)S(1)} collective-permute-done((f32[128,128]{1,0:T(8,128)S(1)}, f32[128,128]{1,0:T(8,128)S(1)}, u32[]{:S(2)}, u32[]{:S(2)}) %collective-permute-start.6) | collective-permute-done | bytes 65568 | tf_op jit(solution)/shard_map/ppermute | solution.py:407
  41.8 3.8 %project.7 = (f32[640,128]{1,0:T(8,128)S(1)}, f32[640,128]{1,0:T(8,128)S(1)}) custom-call(s32[5]{0:T(128)S(1)} %stack.47.ids_ref, bf16[320,1024]{1,0:T(8,128)(2,1)S(1)} %get-tuple-element.41.refs_0_, bf16[160,1024]{1,0:T(8,128)(2,1)S(1)} %collective-permute-done.9.refs_1_, bf16[8192,512]{1,0:T(8,128)(2,1)} %refs_2_.9, ...), custom_call_target="tpu_custom_call" | custom-call | flops 671088640 | bytes 3080192 | tf_op jit(solution)/shard_map/project/pallas_call | solution.py:296
  45.6 1.8 %collective-permute-start.10 = (f32[640,128]{1,0:T(8,128)S(1)}, f32[640,128]{1,0:T(8,128)S(1)}, u32[]{:S(2)}, u32[]{:S(2)}) collective-permute-start(f32[640,128]{1,0:T(8,128)S(1)} %get-tuple-element.45), channel_id=1, source_target_pairs={{0,1},{1,0},{2,3},{3,2},{4,5},{5,4},{6,7},{7,6},{8,9},{9,8},{10,11... | collective-permute-start | bytes 983048 | tf_op jit(solution)/shard_map/ppermute | solution.py:407
  48.8 1.3 %collective-permute-start.11 = (f32[448,128]{1,0:T(8,128)S(1)}, f32[448,128]{1,0:T(8,128)S(1)}, u32[]{:S(2)}, u32[]{:S(2)}) collective-permute-start(f32[448,128]{1,0:T(8,128)S(1)} %pad_maximum_fusion), channel_id=1, source_target_pairs={{0,4},{4,0},{8,12},{12,8},{16,20},{20,16},{24,28},{28,24},{1,5},{5... | collective-permute-start | bytes 688136 | tf_op jit(solution)/shard_map/ppermute | solution.py:407
  50.5 5.2 %collective-permute-done.11 = f32[448,128]{1,0:T(8,128)S(1)} collective-permute-done((f32[448,128]{1,0:T(8,128)S(1)}, f32[448,128]{1,0:T(8,128)S(1)}, u32[]{:S(2)}, u32[]{:S(2)}) %collective-permute-start.11) | collective-permute-done | bytes 229408 | tf_op jit(solution)/shard_map/ppermute | solution.py:407
  55.8 3.1 %collective-permute-done.12.refs_4_ = bf16[160,1024]{1,0:T(8,128)(2,1)S(1)} collective-permute-done((bf16[160,1024]{1,0:T(8,128)(2,1)S(1)}, bf16[160,1024]{1,0:T(8,128)(2,1)S(1)}, u32[]{:S(2)}, u32[]{:S(2)}) %collective-permute-start.12) | collective-permute-done | bytes 327712 | tf_op jit(solution)/shard_map/ppermute | solution.py:407
  58.9 1.4 %collective-permute-start.13 = (f32[288,128]{1,0:T(8,128)S(1)}, f32[288,128]{1,0:T(8,128)S(1)}, u32[]{:S(2)}, u32[]{:S(2)}) collective-permute-start(f32[288,128]{1,0:T(8,128)S(1)} %pad_maximum_fusion.1), channel_id=1, source_target_pairs={{0,8},{4,12},{8,0},{12,4},{16,24},{20,28},{24,16},{28,20},{1,9},{5... | collective-permute-start | bytes 442376 | tf_op jit(solution)/shard_map/ppermute | solution.py:407
  60.6 2.3 %collective-permute-done.13 = f32[288,128]{1,0:T(8,128)S(1)} collective-permute-done((f32[288,128]{1,0:T(8,128)S(1)}, f32[288,128]{1,0:T(8,128)S(1)}, u32[]{:S(2)}, u32[]{:S(2)}) %collective-permute-start.13) | collective-permute-done | bytes 147488 | tf_op jit(solution)/shard_map/ppermute | solution.py:407
  63.0 2.4 %collective-permute-start.14 = (f32[128,128]{1,0:T(8,128)S(1)}, f32[128,128]{1,0:T(8,128)S(1)}, u32[]{:S(2)}, u32[]{:S(2)}) collective-permute-start(f32[128,128]{1,0:T(8,128)S(1)} %slice_add_fusion.2), channel_id=1, source_target_pairs={{0,16},{4,20},{8,24},{12,28},{16,0},{20,4},{24,8},{28,12},{1,17},{... | collective-permute-start | bytes 196616 | tf_op jit(solution)/shard_map/ppermute | solution.py:407
  65.4 5.8 %collective-permute-start.15 = (f32[80,128]{1,0:T(8,128)S(1)}, f32[80,128]{1,0:T(8,128)S(1)}, u32[]{:S(2)}, u32[]{:S(2)}) collective-permute-start(f32[80,128]{1,0:T(8,128)S(1)} %get-tuple-element.53), channel_id=1, source_target_pairs={{0,0},{1,8},{2,16},{3,24},{4,1},{5,9},{6,17},{7,25},{8,2},{9,10},{... | collective-permute-start | bytes 122888 | tf_op jit(solution)/shard_map/ppermute | solution.py:517
  71.7 5.5 %factor.1.inv_ref = f32[160,160]{1,0:T(8,128)S(1)} custom-call(f32[128,128]{1,0:T(8,128)S(1)} %add.48.g_ref), custom_call_target="tpu_custom_call" | custom-call | flops 6000000000 | bytes 102400 | tf_op jit(solution)/shard_map/factor/pallas_call | solution.py:241
  78.2 2.5 %finish.1 = (f32[160,2048]{1,0:T(8,128)}, f32[8,1280]{1,0:T(8,128)}) custom-call(f32[160,160]{1,0:T(8,128)S(1)} %factor.1.inv_ref, f32[80,128]{1,0:T(8,128)S(1)} %collective-permute-done.15.piece_ref, f32[80,128]{1,0:T(8,128)S(1)} %collective-permute-done.16.piece2_ref, bf16[320,1024]{1,0:T(8,128)(2,1)S(1)} %get-tuple-element.34.own_ref.refs_0_, ...), custom_call_target="tpu_custom_call" | custom-call | flops 629145600 | bytes 3932160 | tf_op jit(solution)/shard_map/finish/pallas_call | solution.py:394
  (49 shorter events, 9.2 us)
Async XLA Ops:
  0.6 0.9 %copy-start = (bf16[512,160]{0,1:T(8,128)(2,1)S(1)}, bf16[512,160]{0,1:T(8,128)(2,1)}, u32[]{:S(2)}) copy-start(bf16[512,160]{0,1:T(8,128)(2,1)} %param.4) | copy-start | bytes 491524
  2.9 5.0 %collective-permute-start = (bf16[1280,512]{1,0:T(8,128)(2,1)S(1)}, bf16[1280,512]{1,0:T(8,128)(2,1)S(1)}, u32[]{:S(2)}, u32[]{:S(2)}) collective-permute-start(bf16[1280,512]{1,0:T(8,128)(2,1)S(1)} %lend.2.refs_3_), channel_id=1, source_target_pairs={{0,1},{1,0},{2,3},{3,2},{4,5},{5,4},{6,7},{7,6},{8,9},{9,8},{10,11... | collective-permute-start | bytes 3932168 | tf_op jit(solution)/shard_map/ppermute | solution.py:407
  3.7 4.2 %copy-start.1 = (bf16[512,160]{0,1:T(8,128)(2,1)S(1)}, bf16[512,160]{0,1:T(8,128)(2,1)}, u32[]{:S(2)}) copy-start(bf16[512,160]{0,1:T(8,128)(2,1)} %param.4) | copy-start | bytes 491524
  7.4 3.3 %collective-permute-start.3 = (bf16[1024,512]{1,0:T(8,128)(2,1)}, bf16[1024,512]{1,0:T(8,128)(2,1)}, u32[]{:S(2)}, u32[]{:S(2)}) collective-permute-start(bf16[1024,512]{1,0:T(8,128)(2,1)} %get-tuple-element.29), channel_id=1, source_target_pairs={{0,1},{1,0},{2,3},{3,2},{4,5},{5,4},{6,7},{7,6},{8,9},{9,8},{10,11... | collective-permute-start | bytes 3145736 | tf_op jit(solution)/shard_map/ppermute | solution.py:407
  7.4 8.0 %collective-permute-start.2 = (bf16[1024,512]{1,0:T(8,128)(2,1)}, bf16[1024,512]{1,0:T(8,128)(2,1)}, u32[]{:S(2)}, u32[]{:S(2)}) collective-permute-start(bf16[1024,512]{1,0:T(8,128)(2,1)} %get-tuple-element.28), channel_id=1, source_target_pairs={{0,1},{1,0},{2,3},{3,2},{4,5},{5,4},{6,7},{7,6},{8,9},{9,8},{10,11... | collective-permute-start | bytes 3145736 | tf_op jit(solution)/shard_map/ppermute | solution.py:407
  7.9 9.9 %collective-permute-start.1 = (bf16[1024,512]{1,0:T(8,128)(2,1)}, bf16[1024,512]{1,0:T(8,128)(2,1)}, u32[]{:S(2)}, u32[]{:S(2)}) collective-permute-start(bf16[1024,512]{1,0:T(8,128)(2,1)} %get-tuple-element.27), channel_id=1, source_target_pairs={{0,1},{1,0},{2,3},{3,2},{4,5},{5,4},{6,7},{7,6},{8,9},{9,8},{10,11... | collective-permute-start | bytes 3145736 | tf_op jit(solution)/shard_map/ppermute | solution.py:407
  10.7 9.5 %collective-permute-start.5 = (bf16[160,1024]{1,0:T(8,128)(2,1)}, bf16[160,1024]{1,0:T(8,128)(2,1)S(1)}, u32[]{:S(2)}, u32[]{:S(2)}) collective-permute-start(bf16[160,1024]{1,0:T(8,128)(2,1)} %get-tuple-element.30.refs_3_), channel_id=1, source_target_pairs={{0,2},{1,3},{2,0},{3,1},{4,6},{5,7},{6,4},{7,5},{8,10},{9,11},{10,... | collective-permute-start | bytes 983048 | tf_op jit(solution)/shard_map/ppermute | solution.py:407
  13.8 12.9 %collective-permute-start.4 = (bf16[160,1024]{1,0:T(8,128)(2,1)}, bf16[160,1024]{1,0:T(8,128)(2,1)S(1)}, u32[]{:S(2)}, u32[]{:S(2)}) collective-permute-start(bf16[160,1024]{1,0:T(8,128)(2,1)} %get-tuple-element.31.refs_3_), channel_id=1, source_target_pairs={{0,2},{1,3},{2,0},{3,1},{4,6},{5,7},{6,4},{7,5},{8,10},{9,11},{10,... | collective-permute-start | bytes 983048 | tf_op jit(solution)/shard_map/ppermute | solution.py:407
  17.7 16.0 %collective-permute-start.7 = (bf16[160,1024]{1,0:T(8,128)(2,1)S(1)}, bf16[160,1024]{1,0:T(8,128)(2,1)S(1)}, u32[]{:S(2)}, u32[]{:S(2)}) collective-permute-start(bf16[160,1024]{1,0:T(8,128)(2,1)S(1)} %get-tuple-element.32.refs_3_), channel_id=1, source_target_pairs={{0,2},{1,3},{2,0},{3,1},{4,6},{5,7},{6,4},{7,5},{8,10},{9,11},{10,... | collective-permute-start | bytes 983048 | tf_op jit(solution)/shard_map/ppermute | solution.py:407
  30.5 11.3 %collective-permute-start.9 = (bf16[160,1024]{1,0:T(8,128)(2,1)S(1)}, bf16[160,1024]{1,0:T(8,128)(2,1)S(1)}, u32[]{:S(2)}, u32[]{:S(2)}) collective-permute-start(bf16[160,1024]{1,0:T(8,128)(2,1)S(1)} %get-tuple-element.42.refs_1_), channel_id=1, source_target_pairs={{0,2},{1,3},{2,0},{3,1},{4,6},{5,7},{6,4},{7,5},{8,10},{9,11},{10,... | collective-permute-start | bytes 983048 | tf_op jit(solution)/shard_map/ppermute | solution.py:407
  30.8 10.9 %collective-permute-start.6 = (f32[128,128]{1,0:T(8,128)S(1)}, f32[128,128]{1,0:T(8,128)S(1)}, u32[]{:S(2)}, u32[]{:S(2)}) collective-permute-start(f32[128,128]{1,0:T(8,128)S(1)} %gram.3.refs_5_), channel_id=1, source_target_pairs={{0,2},{1,3},{2,0},{3,1},{4,6},{5,7},{6,4},{7,5},{8,10},{9,11},{10,... | collective-permute-start | bytes 196616 | tf_op jit(solution)/shard_map/ppermute | solution.py:407
  33.8 8.0 %copy-start.2 = (bf16[512,512]{1,0:T(8,128)(2,1)S(1)}, bf16[512,512]{1,0:T(8,128)(2,1)}, u32[]{:S(2)}) copy-start(bf16[512,512]{1,0:T(8,128)(2,1)} %constant.17.clone.refs_5_) | copy-start | bytes 1572868
  45.6 3.2 %collective-permute-start.10 = (f32[640,128]{1,0:T(8,128)S(1)}, f32[640,128]{1,0:T(8,128)S(1)}, u32[]{:S(2)}, u32[]{:S(2)}) collective-permute-start(f32[640,128]{1,0:T(8,128)S(1)} %get-tuple-element.45), channel_id=1, source_target_pairs={{0,1},{1,0},{2,3},{3,2},{4,5},{5,4},{6,7},{7,6},{8,9},{9,8},{10,11... | collective-permute-start | bytes 983048 | tf_op jit(solution)/shard_map/ppermute | solution.py:407
  47.4 1.3 %collective-permute-start.8 = (f32[128,128]{1,0:T(8,128)S(1)}, f32[128,128]{1,0:T(8,128)S(1)}, u32[]{:S(2)}, u32[]{:S(2)}) collective-permute-start(f32[128,128]{1,0:T(8,128)S(1)} %add.42), channel_id=1, source_target_pairs={{0,1},{1,0},{2,3},{3,2},{4,5},{5,4},{6,7},{7,6},{8,9},{9,8},{10,11... | collective-permute-start | bytes 196616 | tf_op jit(solution)/shard_map/ppermute | solution.py:407
  48.8 6.9 %collective-permute-start.11 = (f32[448,128]{1,0:T(8,128)S(1)}, f32[448,128]{1,0:T(8,128)S(1)}, u32[]{:S(2)}, u32[]{:S(2)}) collective-permute-start(f32[448,128]{1,0:T(8,128)S(1)} %pad_maximum_fusion), channel_id=1, source_target_pairs={{0,4},{4,0},{8,12},{12,8},{16,20},{20,16},{24,28},{28,24},{1,5},{5... | collective-permute-start | bytes 688136 | tf_op jit(solution)/shard_map/ppermute | solution.py:407
  50.2 8.7 %collective-permute-start.12 = (bf16[160,1024]{1,0:T(8,128)(2,1)S(1)}, bf16[160,1024]{1,0:T(8,128)(2,1)S(1)}, u32[]{:S(2)}, u32[]{:S(2)}) collective-permute-start(bf16[160,1024]{1,0:T(8,128)(2,1)S(1)} %slice.40), channel_id=1, source_target_pairs={{0,2},{1,3},{2,0},{3,1},{4,6},{5,7},{6,4},{7,5},{8,10},{9,11},{10,... | collective-permute-start | bytes 983048 | tf_op jit(solution)/shard_map/ppermute | solution.py:407
  58.9 4.1 %collective-permute-start.13 = (f32[288,128]{1,0:T(8,128)S(1)}, f32[288,128]{1,0:T(8,128)S(1)}, u32[]{:S(2)}, u32[]{:S(2)}) collective-permute-start(f32[288,128]{1,0:T(8,128)S(1)} %pad_maximum_fusion.1), channel_id=1, source_target_pairs={{0,8},{4,12},{8,0},{12,4},{16,24},{20,28},{24,16},{28,20},{1,9},{5... | collective-permute-start | bytes 442376 | tf_op jit(solution)/shard_map/ppermute | solution.py:407
  60.3 17.0 %collective-permute-start.17 = (bf16[160,1024]{1,0:T(8,128)(2,1)S(1)}, bf16[160,1024]{1,0:T(8,128)(2,1)S(1)}, u32[]{:S(2)}, u32[]{:S(2)}) collective-permute-start(bf16[160,1024]{1,0:T(8,128)(2,1)S(1)} %slice.47), channel_id=1, source_target_pairs={{0,2},{1,3},{2,0},{3,1},{4,6},{5,7},{6,4},{7,5},{8,10},{9,11},{10,... | collective-permute-start | bytes 983048 | tf_op jit(solution)/shard_map/ppermute | solution.py:407
  63.0 8.8 %collective-permute-start.14 = (f32[128,128]{1,0:T(8,128)S(1)}, f32[128,128]{1,0:T(8,128)S(1)}, u32[]{:S(2)}, u32[]{:S(2)}) collective-permute-start(f32[128,128]{1,0:T(8,128)S(1)} %slice_add_fusion.2), channel_id=1, source_target_pairs={{0,16},{4,20},{8,24},{12,28},{16,0},{20,4},{24,8},{28,12},{1,17},{... | collective-permute-start | bytes 196616 | tf_op jit(solution)/shard_map/ppermute | solution.py:407
  65.4 11.9 %collective-permute-start.15 = (f32[80,128]{1,0:T(8,128)S(1)}, f32[80,128]{1,0:T(8,128)S(1)}, u32[]{:S(2)}, u32[]{:S(2)}) collective-permute-start(f32[80,128]{1,0:T(8,128)S(1)} %get-tuple-element.53), channel_id=1, source_target_pairs={{0,0},{1,8},{2,16},{3,24},{4,1},{5,9},{6,17},{7,25},{8,2},{9,10},{... | collective-permute-start | bytes 122888 | tf_op jit(solution)/shard_map/ppermute | solution.py:517
  71.2 7.1 %collective-permute-start.16 = (f32[80,128]{1,0:T(8,128)S(1)}, f32[80,128]{1,0:T(8,128)S(1)}, u32[]{:S(2)}, u32[]{:S(2)}) collective-permute-start(f32[80,128]{1,0:T(8,128)S(1)} %get-tuple-element.52), channel_id=1, source_target_pairs={{0,4},{1,12},{2,20},{3,28},{4,5},{5,13},{6,21},{7,29},{8,6},{9,14}... | collective-permute-start | bytes 122888 | tf_op jit(solution)/shard_map/ppermute | solution.py:517

commit v15 on v14

--- a/solution.py
+++ b/solution.py
@@ -13,7 +13,7 @@
 UNIT = 1024
 LEND_STEPS = 2
 PROJECT_ROWS = 512
-PLACE = (False, 1, -1, True, False)
+PLACE = (False, -1, -1, True, False)
 SKETCH_STEPS = 1
 FACTOR_COST = 6e9
 COST_CUT = 1

time: 81.1 us -> 79.4 us (0.979)
  the two profiles are of different devices: /device:TPU:3 before, /device:TPU:17 now
where the time goes in v15:
time: 79.4 us; the launch traced here: 78.9 us
  Pallas kernels  37.5 us (47%)
  starting transfers between devices  20 us (25%)
  waiting for transfers between devices  19.3 us (24%)
  local copies, waits for them, and re-layouts  1.08 us (1%)
  between operations  0.9 us (1%)
    ppermute x16, waiting for transfers between devices, swap(): return lax.ppermute(value, axis, [(i, i ^ bit) for i in range(size)])  16.7 us
    pallas_call x4, Pallas kernels, project(): pl.pallas_call(functools.partial(project_kernel, count, wide, len(bases),...  12.4 us
    ppermute x16, starting transfers between devices, swap(): return lax.ppermute(value, axis, [(i, i ^ bit) for i in range(size)])  11.7 us
    pallas_call x4, Pallas kernels, sketch(): pl.pallas_call(functools.partial(sketch_kernel, count, lent), grid_spec=p...  10.6 us
    ppermute x2, starting transfers between devices, body(): landed.append(lax.ppermute(value, ('node', 'samp'), route))  8.32 us
    pallas_call x1, Pallas kernels, factor_inverse(): pl.pallas_call(functools.partial(factor_kernel, rank), in_specs=[HELD] +...  5.48 us
    pallas_call x2, Pallas kernels, lend(): pl.pallas_call(functools.partial(lend_kernel, count, at), grid_spec=pltpu...  4.99 us
    ppermute x2, waiting for transfers between devices, body(): landed.append(lax.ppermute(value, ('node', 'samp'), route))  2.61 us
  transfers between devices with their start and end apart: 18, of which 7 were waited for; matrix products, arithmetic and copies ran while one was open for 0% of the time, Pallas kernels for 38%

profile of v15, /device:TPU:17, one launch (start us, length us, event | category | flops | bytes accessed | tf_op | source)
XLA Modules:
  0.0 78.9 jit_solution(7148837156843976832)
XLA Ops:
  1.6 1.3 %lend.2.refs_3_ = bf16[1280,512]{1,0:T(8,128)(2,1)S(1)} custom-call(s32[1]{0:T(128)} %bitcast.2.ids_ref, bf16[8192,512]{1,0:T(8,128)(2,1)} %refs_2_.9, bf16[160,512]{1,0:T(8,128)(2,1)S(1)} %bitcast.12), custom_call_target="tpu_custom_call" | custom-call | bytes 2621440 | tf_op jit(solution)/shard_map/lend/pallas_call | solution.py:64
  3.7 3.7 %lend.3 = (bf16[1024,512]{1,0:T(8,128)(2,1)}, bf16[1024,512]{1,0:T(8,128)(2,1)}, bf16[1024,512]{1,0:T(8,128)(2,1)}) custom-call(s32[3]{0:T(128)S(1)} %pad_add_fusion.ids_ref, bf16[8192,512]{1,0:T(8,128)(2,1)} %refs_2_.9, bf16[8192,512]{1,0:T(8,128)(2,1)} %refs_2_.9, bf16[8192,512]{1,0:T(8,128)(2,1)} %refs_2_.9, bf16[1280,512]{1,0:T(8,128)(2,1)S(1)} %lend.2.refs_3_), custom_call_target="tpu_custom_call" | custom-call | bytes 6291456 | tf_op jit(solution)/shard_map/lend/pallas_call | solution.py:64
  7.9 2.8 %sketch.4 = (bf16[320,1024]{1,0:T(8,128)(2,1)S(1)}, bf16[160,1024]{1,0:T(8,128)(2,1)}) custom-call(s32[1]{0:T(128)} %bitcast.8.ids_ref, bf16[8192,512]{1,0:T(8,128)(2,1)} %refs_2_.9, bf16[160,512]{1,0:T(8,128)(2,1)S(1)} %bitcast.13, bf16[1280,512]{1,0:T(8,128)(2,1)S(1)} %collective-permute-done.refs_1_.refs_2_.refs_3_, ...), custom_call_target="tpu_custom_call" | custom-call | flops 335544320 | bytes 3080192 | tf_op jit(solution)/shard_map/sketch/pallas_call | solution.py:104
  11.9 3.1 %sketch.5 = (bf16[320,1024]{1,0:T(8,128)(2,1)S(1)}, bf16[160,1024]{1,0:T(8,128)(2,1)}) custom-call(s32[1]{0:T(128)} %bitcast.7.ids_ref, bf16[8192,512]{1,0:T(8,128)(2,1)} %refs_2_.9, bf16[160,512]{1,0:T(8,128)(2,1)S(1)} %bitcast.14, bf16[1280,512]{1,0:T(8,128)(2,1)S(1)} %collective-permute-done.refs_1_.refs_2_.refs_3_, ...), custom_call_target="tpu_custom_call" | custom-call | flops 335544320 | bytes 3080192 | tf_op jit(solution)/shard_map/sketch/pallas_call | solution.py:104
  15.4 2.4 %sketch.6 = (bf16[320,1024]{1,0:T(8,128)(2,1)S(1)}, bf16[160,1024]{1,0:T(8,128)(2,1)S(1)}) custom-call(s32[1]{0:T(128)} %bitcast.6.ids_ref, bf16[8192,512]{1,0:T(8,128)(2,1)} %refs_2_.9, bf16[160,512]{1,0:T(8,128)(2,1)S(1)} %bitcast.15, bf16[1280,512]{1,0:T(8,128)(2,1)S(1)} %collective-permute-done.refs_1_.refs_2_.refs_3_, ...), custom_call_target="tpu_custom_call" | custom-call | flops 335544320 | bytes 3080192 | tf_op jit(solution)/shard_map/sketch/pallas_call | solution.py:104
  19.0 2.4 %sketch.7 = (bf16[320,1024]{1,0:T(8,128)(2,1)S(1)}, bf16[160,1024]{1,0:T(8,128)(2,1)S(1)}) custom-call(s32[1]{0:T(128)} %bitcast.ids_ref, bf16[8192,512]{1,0:T(8,128)(2,1)} %refs_2_.9, bf16[160,512]{1,0:T(8,128)(2,1)S(1)} %bitcast.16, bf16[1280,512]{1,0:T(8,128)(2,1)S(1)} %collective-permute-done.refs_1_.refs_2_.refs_3_, ...), custom_call_target="tpu_custom_call" | custom-call | flops 335544320 | bytes 3080192 | tf_op jit(solution)/shard_map/sketch/pallas_call | solution.py:104
  22.1 2.9 %project.4.refs_4_ = f32[2,160,512]{2,1,0:T(8,128)S(1)} custom-call(s32[5]{0:T(128)S(1)} %stack.47.ids_ref, bf16[320,1024]{1,0:T(8,128)(2,1)S(1)} %get-tuple-element.32.own_ref.refs_0_, bf16[160,1024]{1,0:T(8,128)(2,1)S(1)} %collective-permute-done.5.got_ref.refs_1_.refs_2_, bf16[8192,512]{1,0:T(8,128)(2,1)} %refs_2_.9, ...), custom_call_target="tpu_custom_call" | custom-call | flops 671088640 | bytes 3080192 | tf_op jit(solution)/shard_map/project/pallas_call | solution.py:296
  25.1 1.7 %collective-permute-done.4.got_ref.refs_1_.refs_3_ = bf16[160,1024]{1,0:T(8,128)(2,1)S(1)} collective-permute-done((bf16[160,1024]{1,0:T(8,128)(2,1)}, bf16[160,1024]{1,0:T(8,128)(2,1)S(1)}, u32[]{:S(2)}, u32[]{:S(2)}) %collective-permute-start.4) | collective-permute-done | bytes 327712 | tf_op jit(solution)/shard_map/ppermute | solution.py:407
  27.5 2.9 %project.5.refs_4_ = f32[2,160,512]{2,1,0:T(8,128)S(1)} custom-call(s32[5]{0:T(128)S(1)} %stack.47.ids_ref, bf16[320,1024]{1,0:T(8,128)(2,1)S(1)} %get-tuple-element.31.own_ref.refs_0_.refs_1_, bf16[160,1024]{1,0:T(8,128)(2,1)S(1)} %collective-permute-done.4.got_ref.refs_1_.refs_3_, bf16[8192,512]{1,0:T(8,128)(2,1)} %refs_2_.9, ...), custom_call_target="tpu_custom_call" | custom-call | flops 671088640 | bytes 3080192 | tf_op jit(solution)/shard_map/project/pallas_call | solution.py:296
  30.5 1.3 %collective-permute-start.9 = (bf16[160,1024]{1,0:T(8,128)(2,1)S(1)}, bf16[160,1024]{1,0:T(8,128)(2,1)S(1)}, u32[]{:S(2)}, u32[]{:S(2)}) collective-permute-start(bf16[160,1024]{1,0:T(8,128)(2,1)S(1)} %get-tuple-element.40.refs_1_), channel_id=1, source_target_pairs={{0,2},{1,3},{2,0},{3,1},{4,6},{5,7},{6,4},{7,5},{8,10},{9,11},{10,... | collective-permute-start | bytes 983048 | tf_op jit(solution)/shard_map/ppermute | solution.py:407
  32.0 1.8 %collective-permute-done.7.refs_1_ = bf16[160,1024]{1,0:T(8,128)(2,1)S(1)} collective-permute-done((bf16[160,1024]{1,0:T(8,128)(2,1)S(1)}, bf16[160,1024]{1,0:T(8,128)(2,1)S(1)}, u32[]{:S(2)}, u32[]{:S(2)}) %collective-permute-start.7) | collective-permute-done | bytes 327712 | tf_op jit(solution)/shard_map/ppermute | solution.py:407
  33.8 2.8 %project.6.refs_4_ = f32[2,160,512]{2,1,0:T(8,128)S(1)} custom-call(s32[5]{0:T(128)S(1)} %stack.47.ids_ref, bf16[320,1024]{1,0:T(8,128)(2,1)S(1)} %get-tuple-element.35.refs_0_, bf16[160,1024]{1,0:T(8,128)(2,1)S(1)} %collective-permute-done.7.refs_1_, bf16[8192,512]{1,0:T(8,128)(2,1)} %refs_2_.9, ...), custom_call_target="tpu_custom_call" | custom-call | flops 671088640 | bytes 3080192 | tf_op jit(solution)/shard_map/project/pallas_call | solution.py:296
  36.5 5.3 %collective-permute-done.6 = f32[128,128]{1,0:T(8,128)S(1)} collective-permute-done((f32[128,128]{1,0:T(8,128)S(1)}, f32[128,128]{1,0:T(8,128)S(1)}, u32[]{:S(2)}, u32[]{:S(2)}) %collective-permute-start.6) | collective-permute-done | bytes 65568 | tf_op jit(solution)/shard_map/ppermute | solution.py:407
  41.8 3.8 %project.7 = (f32[640,128]{1,0:T(8,128)S(1)}, f32[640,128]{1,0:T(8,128)S(1)}) custom-call(s32[5]{0:T(128)S(1)} %stack.47.ids_ref, bf16[320,1024]{1,0:T(8,128)(2,1)S(1)} %get-tuple-element.39.refs_0_, bf16[160,1024]{1,0:T(8,128)(2,1)S(1)} %collective-permute-done.9.refs_1_, bf16[8192,512]{1,0:T(8,128)(2,1)} %refs_2_.9, ...), custom_call_target="tpu_custom_call" | custom-call | flops 671088640 | bytes 3080192 | tf_op jit(solution)/shard_map/project/pallas_call | solution.py:296
  45.6 1.8 %collective-permute-start.10 = (f32[640,128]{1,0:T(8,128)S(1)}, f32[640,128]{1,0:T(8,128)S(1)}, u32[]{:S(2)}, u32[]{:S(2)}) collective-permute-start(f32[640,128]{1,0:T(8,128)S(1)} %get-tuple-element.43), channel_id=1, source_target_pairs={{0,1},{1,0},{2,3},{3,2},{4,5},{5,4},{6,7},{7,6},{8,9},{9,8},{10,11... | collective-permute-start | bytes 983048 | tf_op jit(solution)/shard_map/ppermute | solution.py:407
  47.5 1.3 %collective-permute-done.8 = f32[128,128]{1,0:T(8,128)S(1)} collective-permute-done((f32[128,128]{1,0:T(8,128)S(1)}, f32[128,128]{1,0:T(8,128)S(1)}, u32[]{:S(2)}, u32[]{:S(2)}) %collective-permute-start.8) | collective-permute-done | bytes 65568 | tf_op jit(solution)/shard_map/ppermute | solution.py:407
  48.9 1.3 %collective-permute-start.11 = (f32[448,128]{1,0:T(8,128)S(1)}, f32[448,128]{1,0:T(8,128)S(1)}, u32[]{:S(2)}, u32[]{:S(2)}) collective-permute-start(f32[448,128]{1,0:T(8,128)S(1)} %pad_maximum_fusion), channel_id=1, source_target_pairs={{0,4},{4,0},{8,12},{12,8},{16,20},{20,16},{24,28},{28,24},{1,5},{5... | collective-permute-start | bytes 688136 | tf_op jit(solution)/shard_map/ppermute | solution.py:407
  50.2 5.6 %collective-permute-done.11 = f32[448,128]{1,0:T(8,128)S(1)} collective-permute-done((f32[448,128]{1,0:T(8,128)S(1)}, f32[448,128]{1,0:T(8,128)S(1)}, u32[]{:S(2)}, u32[]{:S(2)}) %collective-permute-start.11) | collective-permute-done | bytes 229408 | tf_op jit(solution)/shard_map/ppermute | solution.py:407
  55.8 1.4 %collective-permute-start.12 = (f32[288,128]{1,0:T(8,128)S(1)}, f32[288,128]{1,0:T(8,128)S(1)}, u32[]{:S(2)}, u32[]{:S(2)}) collective-permute-start(f32[288,128]{1,0:T(8,128)S(1)} %pad_maximum_fusion.1), channel_id=1, source_target_pairs={{0,8},{4,12},{8,0},{12,4},{16,24},{20,28},{24,16},{28,20},{1,9},{5... | collective-permute-start | bytes 442376 | tf_op jit(solution)/shard_map/ppermute | solution.py:407
  57.2 1.3 %collective-permute-start.17 = (bf16[160,1024]{1,0:T(8,128)(2,1)S(1)}, bf16[160,1024]{1,0:T(8,128)(2,1)S(1)}, u32[]{:S(2)}, u32[]{:S(2)}) collective-permute-start(bf16[160,1024]{1,0:T(8,128)(2,1)S(1)} %slice.47), channel_id=1, source_target_pairs={{0,2},{1,3},{2,0},{3,1},{4,6},{5,7},{6,4},{7,5},{8,10},{9,11},{10,... | collective-permute-start | bytes 983048 | tf_op jit(solution)/shard_map/ppermute | solution.py:407
  60.0 7.8 %collective-permute-start.14 = (f32[80,128]{1,0:T(8,128)S(1)}, f32[80,128]{1,0:T(8,128)S(1)}, u32[]{:S(2)}, u32[]{:S(2)}) collective-permute-start(f32[80,128]{1,0:T(8,128)S(1)} %get-tuple-element.49), channel_id=1, source_target_pairs={{0,0},{1,8},{2,16},{3,24},{4,1},{5,9},{6,17},{7,25},{8,2},{9,10},{... | collective-permute-start | bytes 122888 | tf_op jit(solution)/shard_map/ppermute | solution.py:517
  68.3 5.5 %factor.1.inv_ref = f32[160,160]{1,0:T(8,128)S(1)} custom-call(f32[128,128]{1,0:T(8,128)S(1)} %add.48.g_ref), custom_call_target="tpu_custom_call" | custom-call | flops 6000000000 | bytes 102400 | tf_op jit(solution)/shard_map/factor/pallas_call | solution.py:241
  73.9 2.6 %collective-permute-done.15.piece2_ref = f32[80,128]{1,0:T(8,128)S(1)} collective-permute-done((f32[80,128]{1,0:T(8,128)S(1)}, f32[80,128]{1,0:T(8,128)S(1)}, u32[]{:S(2)}, u32[]{:S(2)}) %collective-permute-start.15) | collective-permute-done | bytes 40992 | tf_op jit(solution)/shard_map/ppermute | solution.py:517
  76.5 2.5 %finish.1 = (f32[160,2048]{1,0:T(8,128)}, f32[8,1280]{1,0:T(8,128)}) custom-call(f32[160,160]{1,0:T(8,128)S(1)} %factor.1.inv_ref, f32[80,128]{1,0:T(8,128)S(1)} %collective-permute-done.14.piece_ref, f32[80,128]{1,0:T(8,128)S(1)} %collective-permute-done.15.piece2_ref, bf16[320,1024]{1,0:T(8,128)(2,1)S(1)} %get-tuple-element.32.own_ref.refs_0_, ...), custom_call_target="tpu_custom_call" | custom-call | flops 629145600 | bytes 3932160 | tf_op jit(solution)/shard_map/finish/pallas_call | solution.py:394
  (49 shorter events, 9.1 us)
Async XLA Ops:
  0.6 0.9 %copy-start = (bf16[512,160]{0,1:T(8,128)(2,1)S(1)}, bf16[512,160]{0,1:T(8,128)(2,1)}, u32[]{:S(2)}) copy-start(bf16[512,160]{0,1:T(8,128)(2,1)} %param.4) | copy-start | bytes 491524
  2.9 5.0 %collective-permute-start = (bf16[1280,512]{1,0:T(8,128)(2,1)S(1)}, bf16[1280,512]{1,0:T(8,128)(2,1)S(1)}, u32[]{:S(2)}, u32[]{:S(2)}) collective-permute-start(bf16[1280,512]{1,0:T(8,128)(2,1)S(1)} %lend.2.refs_3_), channel_id=1, source_target_pairs={{0,1},{1,0},{2,3},{3,2},{4,5},{5,4},{6,7},{7,6},{8,9},{9,8},{10,11... | collective-permute-start | bytes 3932168 | tf_op jit(solution)/shard_map/ppermute | solution.py:407
  3.7 4.2 %copy-start.1 = (bf16[512,160]{0,1:T(8,128)(2,1)S(1)}, bf16[512,160]{0,1:T(8,128)(2,1)}, u32[]{:S(2)}) copy-start(bf16[512,160]{0,1:T(8,128)(2,1)} %param.4) | copy-start | bytes 491524
  7.4 4.6 %collective-permute-start.3 = (bf16[1024,512]{1,0:T(8,128)(2,1)}, bf16[1024,512]{1,0:T(8,128)(2,1)}, u32[]{:S(2)}, u32[]{:S(2)}) collective-permute-start(bf16[1024,512]{1,0:T(8,128)(2,1)} %get-tuple-element.27), channel_id=1, source_target_pairs={{0,1},{1,0},{2,3},{3,2},{4,5},{5,4},{6,7},{7,6},{8,9},{9,8},{10,11... | collective-permute-start | bytes 3145736 | tf_op jit(solution)/shard_map/ppermute | solution.py:407
  7.4 8.0 %collective-permute-start.2 = (bf16[1024,512]{1,0:T(8,128)(2,1)}, bf16[1024,512]{1,0:T(8,128)(2,1)}, u32[]{:S(2)}, u32[]{:S(2)}) collective-permute-start(bf16[1024,512]{1,0:T(8,128)(2,1)} %get-tuple-element.26), channel_id=1, source_target_pairs={{0,1},{1,0},{2,3},{3,2},{4,5},{5,4},{6,7},{7,6},{8,9},{9,8},{10,11... | collective-permute-start | bytes 3145736 | tf_op jit(solution)/shard_map/ppermute | solution.py:407
  7.9 11.1 %collective-permute-start.1 = (bf16[1024,512]{1,0:T(8,128)(2,1)}, bf16[1024,512]{1,0:T(8,128)(2,1)}, u32[]{:S(2)}, u32[]{:S(2)}) collective-permute-start(bf16[1024,512]{1,0:T(8,128)(2,1)} %get-tuple-element.25), channel_id=1, source_target_pairs={{0,1},{1,0},{2,3},{3,2},{4,5},{5,4},{6,7},{7,6},{8,9},{9,8},{10,11... | collective-permute-start | bytes 3145736 | tf_op jit(solution)/shard_map/ppermute | solution.py:407
  10.7 10.7 %collective-permute-start.5 = (bf16[160,1024]{1,0:T(8,128)(2,1)}, bf16[160,1024]{1,0:T(8,128)(2,1)S(1)}, u32[]{:S(2)}, u32[]{:S(2)}) collective-permute-start(bf16[160,1024]{1,0:T(8,128)(2,1)} %get-tuple-element.28.refs_3_), channel_id=1, source_target_pairs={{0,2},{1,3},{2,0},{3,1},{4,6},{5,7},{6,4},{7,5},{8,10},{9,11},{10,... | collective-permute-start | bytes 983048 | tf_op jit(solution)/shard_map/ppermute | solution.py:407
  15.0 11.7 %collective-permute-start.4 = (bf16[160,1024]{1,0:T(8,128)(2,1)}, bf16[160,1024]{1,0:T(8,128)(2,1)S(1)}, u32[]{:S(2)}, u32[]{:S(2)}) collective-permute-start(bf16[160,1024]{1,0:T(8,128)(2,1)} %get-tuple-element.29.refs_3_), channel_id=1, source_target_pairs={{0,2},{1,3},{2,0},{3,1},{4,6},{5,7},{6,4},{7,5},{8,10},{9,11},{10,... | collective-permute-start | bytes 983048 | tf_op jit(solution)/shard_map/ppermute | solution.py:407
  17.7 16.0 %collective-permute-start.7 = (bf16[160,1024]{1,0:T(8,128)(2,1)S(1)}, bf16[160,1024]{1,0:T(8,128)(2,1)S(1)}, u32[]{:S(2)}, u32[]{:S(2)}) collective-permute-start(bf16[160,1024]{1,0:T(8,128)(2,1)S(1)} %get-tuple-element.30.refs_3_), channel_id=1, source_target_pairs={{0,2},{1,3},{2,0},{3,1},{4,6},{5,7},{6,4},{7,5},{8,10},{9,11},{10,... | collective-permute-start | bytes 983048 | tf_op jit(solution)/shard_map/ppermute | solution.py:407
  30.5 11.3 %collective-permute-start.9 = (bf16[160,1024]{1,0:T(8,128)(2,1)S(1)}, bf16[160,1024]{1,0:T(8,128)(2,1)S(1)}, u32[]{:S(2)}, u32[]{:S(2)}) collective-permute-start(bf16[160,1024]{1,0:T(8,128)(2,1)S(1)} %get-tuple-element.40.refs_1_), channel_id=1, source_target_pairs={{0,2},{1,3},{2,0},{3,1},{4,6},{5,7},{6,4},{7,5},{8,10},{9,11},{10,... | collective-permute-start | bytes 983048 | tf_op jit(solution)/shard_map/ppermute | solution.py:407
  31.7 10.0 %collective-permute-start.6 = (f32[128,128]{1,0:T(8,128)S(1)}, f32[128,128]{1,0:T(8,128)S(1)}, u32[]{:S(2)}, u32[]{:S(2)}) collective-permute-start(f32[128,128]{1,0:T(8,128)S(1)} %gram.3.refs_5_), channel_id=1, source_target_pairs={{0,2},{1,3},{2,0},{3,1},{4,6},{5,7},{6,4},{7,5},{8,10},{9,11},{10,... | collective-permute-start | bytes 196616 | tf_op jit(solution)/shard_map/ppermute | solution.py:407
  33.8 8.1 %copy-start.2 = (bf16[512,512]{1,0:T(8,128)(2,1)S(1)}, bf16[512,512]{1,0:T(8,128)(2,1)}, u32[]{:S(2)}) copy-start(bf16[512,512]{1,0:T(8,128)(2,1)} %constant.17.clone.refs_5_) | copy-start | bytes 1572868
  45.6 3.2 %collective-permute-start.10 = (f32[640,128]{1,0:T(8,128)S(1)}, f32[640,128]{1,0:T(8,128)S(1)}, u32[]{:S(2)}, u32[]{:S(2)}) collective-permute-start(f32[640,128]{1,0:T(8,128)S(1)} %get-tuple-element.43), channel_id=1, source_target_pairs={{0,1},{1,0},{2,3},{3,2},{4,5},{5,4},{6,7},{7,6},{8,9},{9,8},{10,11... | collective-permute-start | bytes 983048 | tf_op jit(solution)/shard_map/ppermute | solution.py:407
  47.4 1.3 %collective-permute-start.8 = (f32[128,128]{1,0:T(8,128)S(1)}, f32[128,128]{1,0:T(8,128)S(1)}, u32[]{:S(2)}, u32[]{:S(2)}) collective-permute-start(f32[128,128]{1,0:T(8,128)S(1)} %add.42), channel_id=1, source_target_pairs={{0,1},{1,0},{2,3},{3,2},{4,5},{5,4},{6,7},{7,6},{8,9},{9,8},{10,11... | collective-permute-start | bytes 196616 | tf_op jit(solution)/shard_map/ppermute | solution.py:407
  48.9 6.9 %collective-permute-start.11 = (f32[448,128]{1,0:T(8,128)S(1)}, f32[448,128]{1,0:T(8,128)S(1)}, u32[]{:S(2)}, u32[]{:S(2)}) collective-permute-start(f32[448,128]{1,0:T(8,128)S(1)} %pad_maximum_fusion), channel_id=1, source_target_pairs={{0,4},{4,0},{8,12},{12,8},{16,20},{20,16},{24,28},{28,24},{1,5},{5... | collective-permute-start | bytes 688136 | tf_op jit(solution)/shard_map/ppermute | solution.py:407
  55.8 4.1 %collective-permute-start.12 = (f32[288,128]{1,0:T(8,128)S(1)}, f32[288,128]{1,0:T(8,128)S(1)}, u32[]{:S(2)}, u32[]{:S(2)}) collective-permute-start(f32[288,128]{1,0:T(8,128)S(1)} %pad_maximum_fusion.1), channel_id=1, source_target_pairs={{0,8},{4,12},{8,0},{12,4},{16,24},{20,28},{24,16},{28,20},{1,9},{5... | collective-permute-start | bytes 442376 | tf_op jit(solution)/shard_map/ppermute | solution.py:407
  57.2 16.6 %collective-permute-start.17 = (bf16[160,1024]{1,0:T(8,128)(2,1)S(1)}, bf16[160,1024]{1,0:T(8,128)(2,1)S(1)}, u32[]{:S(2)}, u32[]{:S(2)}) collective-permute-start(bf16[160,1024]{1,0:T(8,128)(2,1)S(1)} %slice.47), channel_id=1, source_target_pairs={{0,2},{1,3},{2,0},{3,1},{4,6},{5,7},{6,4},{7,5},{8,10},{9,11},{10,... | collective-permute-start | bytes 983048 | tf_op jit(solution)/shard_map/ppermute | solution.py:407
  58.5 15.3 %collective-permute-start.16 = (bf16[160,1024]{1,0:T(8,128)(2,1)S(1)}, bf16[160,1024]{1,0:T(8,128)(2,1)S(1)}, u32[]{:S(2)}, u32[]{:S(2)}) collective-permute-start(bf16[160,1024]{1,0:T(8,128)(2,1)S(1)} %slice.46), channel_id=1, source_target_pairs={{0,2},{1,3},{2,0},{3,1},{4,6},{5,7},{6,4},{7,5},{8,10},{9,11},{10,... | collective-permute-start | bytes 983048 | tf_op jit(solution)/shard_map/ppermute | solution.py:407
  59.9 8.4 %collective-permute-start.13 = (f32[128,128]{1,0:T(8,128)S(1)}, f32[128,128]{1,0:T(8,128)S(1)}, u32[]{:S(2)}, u32[]{:S(2)}) collective-permute-start(f32[128,128]{1,0:T(8,128)S(1)} %slice_add_fusion.2), channel_id=1, source_target_pairs={{0,16},{4,20},{8,24},{12,28},{16,0},{20,4},{24,8},{28,12},{1,17},{... | collective-permute-start | bytes 196616 | tf_op jit(solution)/shard_map/ppermute | solution.py:407
  60.0 13.9 %collective-permute-start.14 = (f32[80,128]{1,0:T(8,128)S(1)}, f32[80,128]{1,0:T(8,128)S(1)}, u32[]{:S(2)}, u32[]{:S(2)}) collective-permute-start(f32[80,128]{1,0:T(8,128)S(1)} %get-tuple-element.49), channel_id=1, source_target_pairs={{0,0},{1,8},{2,16},{3,24},{4,1},{5,9},{6,17},{7,25},{8,2},{9,10},{... | collective-permute-start | bytes 122888 | tf_op jit(solution)/shard_map/ppermute | solution.py:517
  67.8 8.6 %collective-permute-start.15 = (f32[80,128]{1,0:T(8,128)S(1)}, f32[80,128]{1,0:T(8,128)S(1)}, u32[]{:S(2)}, u32[]{:S(2)}) collective-permute-start(f32[80,128]{1,0:T(8,128)S(1)} %get-tuple-element.48), channel_id=1, source_target_pairs={{0,4},{1,12},{2,20},{3,28},{4,5},{5,13},{6,21},{7,29},{8,6},{9,14}... | collective-permute-start | bytes 122888 | tf_op jit(solution)/shard_map/ppermute | solution.py:517

commit v16 on v15

--- a/solution.py
+++ b/solution.py
@@ -14,7 +14,7 @@
 LEND_STEPS = 2
 PROJECT_ROWS = 512
 PLACE = (False, -1, -1, True, False)
-SKETCH_STEPS = 1
+SKETCH_STEPS = 2
 FACTOR_COST = 6e9
 COST_CUT = 1
 F32 = jnp.float32

time: 79.4 us -> 79.3 us (level)
  no operation moved by 1% of the time
where the time goes in v16:
time: 79.3 us; the launch traced here: 78.9 us
  Pallas kernels  37.2 us (47%)
  starting transfers between devices  20 us (25%)
  waiting for transfers between devices  19.6 us (25%)
  local copies, waits for them, and re-layouts  1.08 us (1%)
  between operations  0.9 us (1%)
    ppermute x16, waiting for transfers between devices, swap(): return lax.ppermute(value, axis, [(i, i ^ bit) for i in range(size)])  16.9 us
    pallas_call x4, Pallas kernels, project(): pl.pallas_call(functools.partial(project_kernel, count, wide, len(bases),...  12.4 us
    ppermute x16, starting transfers between devices, swap(): return lax.ppermute(value, axis, [(i, i ^ bit) for i in range(size)])  11.7 us
    pallas_call x4, Pallas kernels, sketch(): pl.pallas_call(functools.partial(sketch_kernel, count, lent), grid_spec=p...  10.3 us
    ppermute x2, starting transfers between devices, body(): landed.append(lax.ppermute(value, ('node', 'samp'), route))  8.32 us
    pallas_call x1, Pallas kernels, factor_inverse(): pl.pallas_call(functools.partial(factor_kernel, rank), in_specs=[HELD] +...  5.48 us
    pallas_call x2, Pallas kernels, lend(): pl.pallas_call(functools.partial(lend_kernel, count, at), grid_spec=pltpu...  4.99 us
    ppermute x2, waiting for transfers between devices, body(): landed.append(lax.ppermute(value, ('node', 'samp'), route))  2.6 us
  transfers between devices with their start and end apart: 18, of which 7 were waited for; matrix products, arithmetic and copies ran while one was open for 0% of the time, Pallas kernels for 38%

profile of v16, /device:TPU:17, one launch (start us, length us, event | category | flops | bytes accessed | tf_op | source)
XLA Modules:
  0.0 78.9 jit_solution(4781236060403623863)
XLA Ops:
  1.6 1.3 %lend.2.refs_3_ = bf16[1280,512]{1,0:T(8,128)(2,1)S(1)} custom-call(s32[1]{0:T(128)} %bitcast.2.ids_ref, bf16[8192,512]{1,0:T(8,128)(2,1)} %refs_2_.9, bf16[160,512]{1,0:T(8,128)(2,1)S(1)} %bitcast.12), custom_call_target="tpu_custom_call" | custom-call | bytes 2621440 | tf_op jit(solution)/shard_map/lend/pallas_call | solution.py:64
  3.7 3.7 %lend.3 = (bf16[1024,512]{1,0:T(8,128)(2,1)}, bf16[1024,512]{1,0:T(8,128)(2,1)}, bf16[1024,512]{1,0:T(8,128)(2,1)}) custom-call(s32[3]{0:T(128)S(1)} %pad_add_fusion.ids_ref, bf16[8192,512]{1,0:T(8,128)(2,1)} %refs_2_.9, bf16[8192,512]{1,0:T(8,128)(2,1)} %refs_2_.9, bf16[8192,512]{1,0:T(8,128)(2,1)} %refs_2_.9, bf16[1280,512]{1,0:T(8,128)(2,1)S(1)} %lend.2.refs_3_), custom_call_target="tpu_custom_call" | custom-call | bytes 6291456 | tf_op jit(solution)/shard_map/lend/pallas_call | solution.py:64
  7.9 2.8 %sketch.4 = (bf16[320,1024]{1,0:T(8,128)(2,1)S(1)}, bf16[160,1024]{1,0:T(8,128)(2,1)}) custom-call(s32[1]{0:T(128)} %bitcast.8.ids_ref, bf16[8192,512]{1,0:T(8,128)(2,1)} %refs_2_.9, bf16[160,512]{1,0:T(8,128)(2,1)S(1)} %bitcast.13, bf16[1280,512]{1,0:T(8,128)(2,1)S(1)} %collective-permute-done.refs_1_.refs_2_.refs_3_, ...), custom_call_target="tpu_custom_call" | custom-call | flops 335544320 | bytes 3080192 | tf_op jit(solution)/shard_map/sketch/pallas_call | solution.py:104
  11.9 2.9 %sketch.5 = (bf16[320,1024]{1,0:T(8,128)(2,1)S(1)}, bf16[160,1024]{1,0:T(8,128)(2,1)}) custom-call(s32[1]{0:T(128)} %bitcast.7.ids_ref, bf16[8192,512]{1,0:T(8,128)(2,1)} %refs_2_.9, bf16[160,512]{1,0:T(8,128)(2,1)S(1)} %bitcast.14, bf16[1280,512]{1,0:T(8,128)(2,1)S(1)} %collective-permute-done.refs_1_.refs_2_.refs_3_, ...), custom_call_target="tpu_custom_call" | custom-call | flops 335544320 | bytes 3080192 | tf_op jit(solution)/shard_map/sketch/pallas_call | solution.py:104
  15.2 2.3 %sketch.6 = (bf16[320,1024]{1,0:T(8,128)(2,1)S(1)}, bf16[160,1024]{1,0:T(8,128)(2,1)S(1)}) custom-call(s32[1]{0:T(128)} %bitcast.6.ids_ref, bf16[8192,512]{1,0:T(8,128)(2,1)} %refs_2_.9, bf16[160,512]{1,0:T(8,128)(2,1)S(1)} %bitcast.15, bf16[1280,512]{1,0:T(8,128)(2,1)S(1)} %collective-permute-done.refs_1_.refs_2_.refs_3_, ...), custom_call_target="tpu_custom_call" | custom-call | flops 335544320 | bytes 3080192 | tf_op jit(solution)/shard_map/sketch/pallas_call | solution.py:104
  17.5 1.3 %collective-permute-start.7 = (bf16[160,1024]{1,0:T(8,128)(2,1)S(1)}, bf16[160,1024]{1,0:T(8,128)(2,1)S(1)}, u32[]{:S(2)}, u32[]{:S(2)}) collective-permute-start(bf16[160,1024]{1,0:T(8,128)(2,1)S(1)} %get-tuple-element.30.refs_3_), channel_id=1, source_target_pairs={{0,2},{1,3},{2,0},{3,1},{4,6},{5,7},{6,4},{7,5},{8,10},{9,11},{10,... | collective-permute-start | bytes 983048 | tf_op jit(solution)/shard_map/ppermute | solution.py:407
  18.8 2.3 %sketch.7 = (bf16[320,1024]{1,0:T(8,128)(2,1)S(1)}, bf16[160,1024]{1,0:T(8,128)(2,1)S(1)}) custom-call(s32[1]{0:T(128)} %bitcast.ids_ref, bf16[8192,512]{1,0:T(8,128)(2,1)} %refs_2_.9, bf16[160,512]{1,0:T(8,128)(2,1)S(1)} %bitcast.16, bf16[1280,512]{1,0:T(8,128)(2,1)S(1)} %collective-permute-done.refs_1_.refs_2_.refs_3_, ...), custom_call_target="tpu_custom_call" | custom-call | flops 335544320 | bytes 3080192 | tf_op jit(solution)/shard_map/sketch/pallas_call | solution.py:104
  21.8 2.9 %project.4.refs_4_ = f32[2,160,512]{2,1,0:T(8,128)S(1)} custom-call(s32[5]{0:T(128)S(1)} %stack.47.ids_ref, bf16[320,1024]{1,0:T(8,128)(2,1)S(1)} %get-tuple-element.32.own_ref.refs_0_, bf16[160,1024]{1,0:T(8,128)(2,1)S(1)} %collective-permute-done.5.got_ref.refs_1_.refs_2_, bf16[8192,512]{1,0:T(8,128)(2,1)} %refs_2_.9, ...), custom_call_target="tpu_custom_call" | custom-call | flops 671088640 | bytes 3080192 | tf_op jit(solution)/shard_map/project/pallas_call | solution.py:296
  24.8 1.9 %collective-permute-done.4.got_ref.refs_1_.refs_3_ = bf16[160,1024]{1,0:T(8,128)(2,1)S(1)} collective-permute-done((bf16[160,1024]{1,0:T(8,128)(2,1)}, bf16[160,1024]{1,0:T(8,128)(2,1)S(1)}, u32[]{:S(2)}, u32[]{:S(2)}) %collective-permute-start.4) | collective-permute-done | bytes 327712 | tf_op jit(solution)/shard_map/ppermute | solution.py:407
  27.5 2.9 %project.5.refs_4_ = f32[2,160,512]{2,1,0:T(8,128)S(1)} custom-call(s32[5]{0:T(128)S(1)} %stack.47.ids_ref, bf16[320,1024]{1,0:T(8,128)(2,1)S(1)} %get-tuple-element.31.own_ref.refs_0_.refs_1_, bf16[160,1024]{1,0:T(8,128)(2,1)S(1)} %collective-permute-done.4.got_ref.refs_1_.refs_3_, bf16[8192,512]{1,0:T(8,128)(2,1)} %refs_2_.9, ...), custom_call_target="tpu_custom_call" | custom-call | flops 671088640 | bytes 3080192 | tf_op jit(solution)/shard_map/project/pallas_call | solution.py:296
  30.4 1.3 %collective-permute-start.9 = (bf16[160,1024]{1,0:T(8,128)(2,1)S(1)}, bf16[160,1024]{1,0:T(8,128)(2,1)S(1)}, u32[]{:S(2)}, u32[]{:S(2)}) collective-permute-start(bf16[160,1024]{1,0:T(8,128)(2,1)S(1)} %get-tuple-element.40.refs_1_), channel_id=1, source_target_pairs={{0,2},{1,3},{2,0},{3,1},{4,6},{5,7},{6,4},{7,5},{8,10},{9,11},{10,... | collective-permute-start | bytes 983048 | tf_op jit(solution)/shard_map/ppermute | solution.py:407
  32.0 1.8 %collective-permute-done.7.refs_1_ = bf16[160,1024]{1,0:T(8,128)(2,1)S(1)} collective-permute-done((bf16[160,1024]{1,0:T(8,128)(2,1)S(1)}, bf16[160,1024]{1,0:T(8,128)(2,1)S(1)}, u32[]{:S(2)}, u32[]{:S(2)}) %collective-permute-start.7) | collective-permute-done | bytes 327712 | tf_op jit(solution)/shard_map/ppermute | solution.py:407
  33.7 2.8 %project.6.refs_4_ = f32[2,160,512]{2,1,0:T(8,128)S(1)} custom-call(s32[5]{0:T(128)S(1)} %stack.47.ids_ref, bf16[320,1024]{1,0:T(8,128)(2,1)S(1)} %get-tuple-element.35.refs_0_, bf16[160,1024]{1,0:T(8,128)(2,1)S(1)} %collective-permute-done.7.refs_1_, bf16[8192,512]{1,0:T(8,128)(2,1)} %refs_2_.9, ...), custom_call_target="tpu_custom_call" | custom-call | flops 671088640 | bytes 3080192 | tf_op jit(solution)/shard_map/project/pallas_call | solution.py:296
  36.5 5.3 %collective-permute-done.6 = f32[128,128]{1,0:T(8,128)S(1)} collective-permute-done((f32[128,128]{1,0:T(8,128)S(1)}, f32[128,128]{1,0:T(8,128)S(1)}, u32[]{:S(2)}, u32[]{:S(2)}) %collective-permute-start.6) | collective-permute-done | bytes 65568 | tf_op jit(solution)/shard_map/ppermute | solution.py:407
  41.8 3.8 %project.7 = (f32[640,128]{1,0:T(8,128)S(1)}, f32[640,128]{1,0:T(8,128)S(1)}) custom-call(s32[5]{0:T(128)S(1)} %stack.47.ids_ref, bf16[320,1024]{1,0:T(8,128)(2,1)S(1)} %get-tuple-element.39.refs_0_, bf16[160,1024]{1,0:T(8,128)(2,1)S(1)} %collective-permute-done.9.refs_1_, bf16[8192,512]{1,0:T(8,128)(2,1)} %refs_2_.9, ...), custom_call_target="tpu_custom_call" | custom-call | flops 671088640 | bytes 3080192 | tf_op jit(solution)/shard_map/project/pallas_call | solution.py:296
  45.6 1.8 %collective-permute-start.10 = (f32[640,128]{1,0:T(8,128)S(1)}, f32[640,128]{1,0:T(8,128)S(1)}, u32[]{:S(2)}, u32[]{:S(2)}) collective-permute-start(f32[640,128]{1,0:T(8,128)S(1)} %get-tuple-element.43), channel_id=1, source_target_pairs={{0,1},{1,0},{2,3},{3,2},{4,5},{5,4},{6,7},{7,6},{8,9},{9,8},{10,11... | collective-permute-start | bytes 983048 | tf_op jit(solution)/shard_map/ppermute | solution.py:407
  48.8 1.3 %collective-permute-start.11 = (f32[448,128]{1,0:T(8,128)S(1)}, f32[448,128]{1,0:T(8,128)S(1)}, u32[]{:S(2)}, u32[]{:S(2)}) collective-permute-start(f32[448,128]{1,0:T(8,128)S(1)} %pad_maximum_fusion), channel_id=1, source_target_pairs={{0,4},{4,0},{8,12},{12,8},{16,20},{20,16},{24,28},{28,24},{1,5},{5... | collective-permute-start | bytes 688136 | tf_op jit(solution)/shard_map/ppermute | solution.py:407
  50.1 5.6 %collective-permute-done.11 = f32[448,128]{1,0:T(8,128)S(1)} collective-permute-done((f32[448,128]{1,0:T(8,128)S(1)}, f32[448,128]{1,0:T(8,128)S(1)}, u32[]{:S(2)}, u32[]{:S(2)}) %collective-permute-start.11) | collective-permute-done | bytes 229408 | tf_op jit(solution)/shard_map/ppermute | solution.py:407
  55.8 1.4 %collective-permute-start.12 = (f32[288,128]{1,0:T(8,128)S(1)}, f32[288,128]{1,0:T(8,128)S(1)}, u32[]{:S(2)}, u32[]{:S(2)}) collective-permute-start(f32[288,128]{1,0:T(8,128)S(1)} %pad_maximum_fusion.1), channel_id=1, source_target_pairs={{0,8},{4,12},{8,0},{12,4},{16,24},{20,28},{24,16},{28,20},{1,9},{5... | collective-permute-start | bytes 442376 | tf_op jit(solution)/shard_map/ppermute | solution.py:407
  57.2 1.3 %collective-permute-start.17 = (bf16[160,1024]{1,0:T(8,128)(2,1)S(1)}, bf16[160,1024]{1,0:T(8,128)(2,1)S(1)}, u32[]{:S(2)}, u32[]{:S(2)}) collective-permute-start(bf16[160,1024]{1,0:T(8,128)(2,1)S(1)} %slice.47), channel_id=1, source_target_pairs={{0,2},{1,3},{2,0},{3,1},{4,6},{5,7},{6,4},{7,5},{8,10},{9,11},{10,... | collective-permute-start | bytes 983048 | tf_op jit(solution)/shard_map/ppermute | solution.py:407
  60.0 7.8 %collective-permute-start.14 = (f32[80,128]{1,0:T(8,128)S(1)}, f32[80,128]{1,0:T(8,128)S(1)}, u32[]{:S(2)}, u32[]{:S(2)}) collective-permute-start(f32[80,128]{1,0:T(8,128)S(1)} %get-tuple-element.49), channel_id=1, source_target_pairs={{0,0},{1,8},{2,16},{3,24},{4,1},{5,9},{6,17},{7,25},{8,2},{9,10},{... | collective-permute-start | bytes 122888 | tf_op jit(solution)/shard_map/ppermute | solution.py:517
  68.3 5.5 %factor.1.inv_ref = f32[160,160]{1,0:T(8,128)S(1)} custom-call(f32[128,128]{1,0:T(8,128)S(1)} %add.48.g_ref), custom_call_target="tpu_custom_call" | custom-call | flops 6000000000 | bytes 102400 | tf_op jit(solution)/shard_map/factor/pallas_call | solution.py:241
  73.9 2.6 %collective-permute-done.15.piece2_ref = f32[80,128]{1,0:T(8,128)S(1)} collective-permute-done((f32[80,128]{1,0:T(8,128)S(1)}, f32[80,128]{1,0:T(8,128)S(1)}, u32[]{:S(2)}, u32[]{:S(2)}) %collective-permute-start.15) | collective-permute-done | bytes 40992 | tf_op jit(solution)/shard_map/ppermute | solution.py:517
  76.5 2.5 %finish.1 = (f32[160,2048]{1,0:T(8,128)}, f32[8,1280]{1,0:T(8,128)}) custom-call(f32[160,160]{1,0:T(8,128)S(1)} %factor.1.inv_ref, f32[80,128]{1,0:T(8,128)S(1)} %collective-permute-done.14.piece_ref, f32[80,128]{1,0:T(8,128)S(1)} %collective-permute-done.15.piece2_ref, bf16[320,1024]{1,0:T(8,128)(2,1)S(1)} %get-tuple-element.32.own_ref.refs_0_, ...), custom_call_target="tpu_custom_call" | custom-call | flops 629145600 | bytes 3932160 | tf_op jit(solution)/shard_map/finish/pallas_call | solution.py:394
  (49 shorter events, 9.1 us)
Async XLA Ops:
  0.6 0.9 %copy-start = (bf16[512,160]{0,1:T(8,128)(2,1)S(1)}, bf16[512,160]{0,1:T(8,128)(2,1)}, u32[]{:S(2)}) copy-start(bf16[512,160]{0,1:T(8,128)(2,1)} %param.4) | copy-start | bytes 491524
  2.9 5.0 %collective-permute-start = (bf16[1280,512]{1,0:T(8,128)(2,1)S(1)}, bf16[1280,512]{1,0:T(8,128)(2,1)S(1)}, u32[]{:S(2)}, u32[]{:S(2)}) collective-permute-start(bf16[1280,512]{1,0:T(8,128)(2,1)S(1)} %lend.2.refs_3_), channel_id=1, source_target_pairs={{0,1},{1,0},{2,3},{3,2},{4,5},{5,4},{6,7},{7,6},{8,9},{9,8},{10,11... | collective-permute-start | bytes 3932168 | tf_op jit(solution)/shard_map/ppermute | solution.py:407
  3.7 4.2 %copy-start.1 = (bf16[512,160]{0,1:T(8,128)(2,1)S(1)}, bf16[512,160]{0,1:T(8,128)(2,1)}, u32[]{:S(2)}) copy-start(bf16[512,160]{0,1:T(8,128)(2,1)} %param.4) | copy-start | bytes 491524
  7.4 4.5 %collective-permute-start.3 = (bf16[1024,512]{1,0:T(8,128)(2,1)}, bf16[1024,512]{1,0:T(8,128)(2,1)}, u32[]{:S(2)}, u32[]{:S(2)}) collective-permute-start(bf16[1024,512]{1,0:T(8,128)(2,1)} %get-tuple-element.27), channel_id=1, source_target_pairs={{0,1},{1,0},{2,3},{3,2},{4,5},{5,4},{6,7},{7,6},{8,9},{9,8},{10,11... | collective-permute-start | bytes 3145736 | tf_op jit(solution)/shard_map/ppermute | solution.py:407
  7.4 7.8 %collective-permute-start.2 = (bf16[1024,512]{1,0:T(8,128)(2,1)}, bf16[1024,512]{1,0:T(8,128)(2,1)}, u32[]{:S(2)}, u32[]{:S(2)}) collective-permute-start(bf16[1024,512]{1,0:T(8,128)(2,1)} %get-tuple-element.26), channel_id=1, source_target_pairs={{0,1},{1,0},{2,3},{3,2},{4,5},{5,4},{6,7},{7,6},{8,9},{9,8},{10,11... | collective-permute-start | bytes 3145736 | tf_op jit(solution)/shard_map/ppermute | solution.py:407
  7.9 10.9 %collective-permute-start.1 = (bf16[1024,512]{1,0:T(8,128)(2,1)}, bf16[1024,512]{1,0:T(8,128)(2,1)}, u32[]{:S(2)}, u32[]{:S(2)}) collective-permute-start(bf16[1024,512]{1,0:T(8,128)(2,1)} %get-tuple-element.25), channel_id=1, source_target_pairs={{0,1},{1,0},{2,3},{3,2},{4,5},{5,4},{6,7},{7,6},{8,9},{9,8},{10,11... | collective-permute-start | bytes 3145736 | tf_op jit(solution)/shard_map/ppermute | solution.py:407
  10.7 10.4 %collective-permute-start.5 = (bf16[160,1024]{1,0:T(8,128)(2,1)}, bf16[160,1024]{1,0:T(8,128)(2,1)S(1)}, u32[]{:S(2)}, u32[]{:S(2)}) collective-permute-start(bf16[160,1024]{1,0:T(8,128)(2,1)} %get-tuple-element.28.refs_3_), channel_id=1, source_target_pairs={{0,2},{1,3},{2,0},{3,1},{4,6},{5,7},{6,4},{7,5},{8,10},{9,11},{10,... | collective-permute-start | bytes 983048 | tf_op jit(solution)/shard_map/ppermute | solution.py:407
  14.9 11.9 %collective-permute-start.4 = (bf16[160,1024]{1,0:T(8,128)(2,1)}, bf16[160,1024]{1,0:T(8,128)(2,1)S(1)}, u32[]{:S(2)}, u32[]{:S(2)}) collective-permute-start(bf16[160,1024]{1,0:T(8,128)(2,1)} %get-tuple-element.29.refs_3_), channel_id=1, source_target_pairs={{0,2},{1,3},{2,0},{3,1},{4,6},{5,7},{6,4},{7,5},{8,10},{9,11},{10,... | collective-permute-start | bytes 983048 | tf_op jit(solution)/shard_map/ppermute | solution.py:407
  17.5 16.2 %collective-permute-start.7 = (bf16[160,1024]{1,0:T(8,128)(2,1)S(1)}, bf16[160,1024]{1,0:T(8,128)(2,1)S(1)}, u32[]{:S(2)}, u32[]{:S(2)}) collective-permute-start(bf16[160,1024]{1,0:T(8,128)(2,1)S(1)} %get-tuple-element.30.refs_3_), channel_id=1, source_target_pairs={{0,2},{1,3},{2,0},{3,1},{4,6},{5,7},{6,4},{7,5},{8,10},{9,11},{10,... | collective-permute-start | bytes 983048 | tf_op jit(solution)/shard_map/ppermute | solution.py:407
  30.4 11.3 %collective-permute-start.9 = (bf16[160,1024]{1,0:T(8,128)(2,1)S(1)}, bf16[160,1024]{1,0:T(8,128)(2,1)S(1)}, u32[]{:S(2)}, u32[]{:S(2)}) collective-permute-start(bf16[160,1024]{1,0:T(8,128)(2,1)S(1)} %get-tuple-element.40.refs_1_), channel_id=1, source_target_pairs={{0,2},{1,3},{2,0},{3,1},{4,6},{5,7},{6,4},{7,5},{8,10},{9,11},{10,... | collective-permute-start | bytes 983048 | tf_op jit(solution)/shard_map/ppermute | solution.py:407
  31.7 10.0 %collective-permute-start.6 = (f32[128,128]{1,0:T(8,128)S(1)}, f32[128,128]{1,0:T(8,128)S(1)}, u32[]{:S(2)}, u32[]{:S(2)}) collective-permute-start(f32[128,128]{1,0:T(8,128)S(1)} %gram.3.refs_5_), channel_id=1, source_target_pairs={{0,2},{1,3},{2,0},{3,1},{4,6},{5,7},{6,4},{7,5},{8,10},{9,11},{10,... | collective-permute-start | bytes 196616 | tf_op jit(solution)/shard_map/ppermute | solution.py:407
  33.7 8.1 %copy-start.2 = (bf16[512,512]{1,0:T(8,128)(2,1)S(1)}, bf16[512,512]{1,0:T(8,128)(2,1)}, u32[]{:S(2)}) copy-start(bf16[512,512]{1,0:T(8,128)(2,1)} %constant.17.clone.refs_5_) | copy-start | bytes 1572868
  45.6 3.2 %collective-permute-start.10 = (f32[640,128]{1,0:T(8,128)S(1)}, f32[640,128]{1,0:T(8,128)S(1)}, u32[]{:S(2)}, u32[]{:S(2)}) collective-permute-start(f32[640,128]{1,0:T(8,128)S(1)} %get-tuple-element.43), channel_id=1, source_target_pairs={{0,1},{1,0},{2,3},{3,2},{4,5},{5,4},{6,7},{7,6},{8,9},{9,8},{10,11... | collective-permute-start | bytes 983048 | tf_op jit(solution)/shard_map/ppermute | solution.py:407
  47.4 1.3 %collective-permute-start.8 = (f32[128,128]{1,0:T(8,128)S(1)}, f32[128,128]{1,0:T(8,128)S(1)}, u32[]{:S(2)}, u32[]{:S(2)}) collective-permute-start(f32[128,128]{1,0:T(8,128)S(1)} %add.42), channel_id=1, source_target_pairs={{0,1},{1,0},{2,3},{3,2},{4,5},{5,4},{6,7},{7,6},{8,9},{9,8},{10,11... | collective-permute-start | bytes 196616 | tf_op jit(solution)/shard_map/ppermute | solution.py:407
  48.8 6.9 %collective-permute-start.11 = (f32[448,128]{1,0:T(8,128)S(1)}, f32[448,128]{1,0:T(8,128)S(1)}, u32[]{:S(2)}, u32[]{:S(2)}) collective-permute-start(f32[448,128]{1,0:T(8,128)S(1)} %pad_maximum_fusion), channel_id=1, source_target_pairs={{0,4},{4,0},{8,12},{12,8},{16,20},{20,16},{24,28},{28,24},{1,5},{5... | collective-permute-start | bytes 688136 | tf_op jit(solution)/shard_map/ppermute | solution.py:407
  55.8 4.1 %collective-permute-start.12 = (f32[288,128]{1,0:T(8,128)S(1)}, f32[288,128]{1,0:T(8,128)S(1)}, u32[]{:S(2)}, u32[]{:S(2)}) collective-permute-start(f32[288,128]{1,0:T(8,128)S(1)} %pad_maximum_fusion.1), channel_id=1, source_target_pairs={{0,8},{4,12},{8,0},{12,4},{16,24},{20,28},{24,16},{28,20},{1,9},{5... | collective-permute-start | bytes 442376 | tf_op jit(solution)/shard_map/ppermute | solution.py:407
  57.2 16.6 %collective-permute-start.17 = (bf16[160,1024]{1,0:T(8,128)(2,1)S(1)}, bf16[160,1024]{1,0:T(8,128)(2,1)S(1)}, u32[]{:S(2)}, u32[]{:S(2)}) collective-permute-start(bf16[160,1024]{1,0:T(8,128)(2,1)S(1)} %slice.47), channel_id=1, source_target_pairs={{0,2},{1,3},{2,0},{3,1},{4,6},{5,7},{6,4},{7,5},{8,10},{9,11},{10,... | collective-permute-start | bytes 983048 | tf_op jit(solution)/shard_map/ppermute | solution.py:407
  58.5 15.3 %collective-permute-start.16 = (bf16[160,1024]{1,0:T(8,128)(2,1)S(1)}, bf16[160,1024]{1,0:T(8,128)(2,1)S(1)}, u32[]{:S(2)}, u32[]{:S(2)}) collective-permute-start(bf16[160,1024]{1,0:T(8,128)(2,1)S(1)} %slice.46), channel_id=1, source_target_pairs={{0,2},{1,3},{2,0},{3,1},{4,6},{5,7},{6,4},{7,5},{8,10},{9,11},{10,... | collective-permute-start | bytes 983048 | tf_op jit(solution)/shard_map/ppermute | solution.py:407
  59.9 8.4 %collective-permute-start.13 = (f32[128,128]{1,0:T(8,128)S(1)}, f32[128,128]{1,0:T(8,128)S(1)}, u32[]{:S(2)}, u32[]{:S(2)}) collective-permute-start(f32[128,128]{1,0:T(8,128)S(1)} %slice_add_fusion.2), channel_id=1, source_target_pairs={{0,16},{4,20},{8,24},{12,28},{16,0},{20,4},{24,8},{28,12},{1,17},{... | collective-permute-start | bytes 196616 | tf_op jit(solution)/shard_map/ppermute | solution.py:407
  60.0 13.9 %collective-permute-start.14 = (f32[80,128]{1,0:T(8,128)S(1)}, f32[80,128]{1,0:T(8,128)S(1)}, u32[]{:S(2)}, u32[]{:S(2)}) collective-permute-start(f32[80,128]{1,0:T(8,128)S(1)} %get-tuple-element.49), channel_id=1, source_target_pairs={{0,0},{1,8},{2,16},{3,24},{4,1},{5,9},{6,17},{7,25},{8,2},{9,10},{... | collective-permute-start | bytes 122888 | tf_op jit(solution)/shard_map/ppermute | solution.py:517
  67.8 8.6 %collective-permute-start.15 = (f32[80,128]{1,0:T(8,128)S(1)}, f32[80,128]{1,0:T(8,128)S(1)}, u32[]{:S(2)}, u32[]{:S(2)}) collective-permute-start(f32[80,128]{1,0:T(8,128)S(1)} %get-tuple-element.48), channel_id=1, source_target_pairs={{0,4},{1,12},{2,20},{3,28},{4,5},{5,13},{6,21},{7,29},{8,6},{9,14}... | collective-permute-start | bytes 122888 | tf_op jit(solution)/shard_map/ppermute | solution.py:517
